TPU v7x, 32 devices: a whole 2x2x4 slice. The times are simulated.
32 devices in a mesh: src: 8 (over z, y), tgt: 4 (over x, core).
Axes of the slice: x: 2, y: 2, z: 4, core: 2. Of those that a mesh axis runs over, the one named last changes fastest.
Arguments:
- source_points: float32 [3, 32768], P(None, 'src'), may hold values from -3.5 to 3.5, as said below
- target_points: float32 [3, 16384], P(None, 'tgt'), may hold values from -3.5 to 3.5, as said below
- source_weight: float32 [32768], P('src'), may hold values from 0.1 to 3
- target_weight: float32 [16384], P('tgt'), may hold values from 0.1 to 3
- target_start: float32 [16384], P('tgt'), may hold values from -1.2 to 1.2
- tile_source: int32 [8, 4, 12], P('src', 'tgt'), may hold values from 0 to 7, as said below
- tile_target: int32 [8, 4, 12], P('src', 'tgt'), may hold values from 0 to 7, as said below
- tile_count: int32 [8, 4], P('src', 'tgt'), may hold values from 8 to 12, as said below
Outputs:
- source_potential: float32 [32768], P('src')
- target_potential: float32 [16384], P('tgt')
- source_gradient: float32 [3, 32768], P(None, ('src', 'tgt'))
- target_gradient: float32 [3, 16384], P(None, 'tgt')
Inputs may be any that keep to these rules, and one draw needn't show every extreme that they name: `source_points`: coordinates are cluster centres plus offsets. `target_points`: coordinates are cluster centres plus offsets. `tile_source`: within one block pair the live slots name distinct cluster pairs; the first 8 slots name every source cluster of the block once and every target cluster of the block once; slots from tile_count on hold 0. `tile_target`: as for tile_source. `tile_count`: some block pair uses all 12 slots.
All inputs are finite; a program needn't handle non-finite values.
Results may differ from a plain program's by a relative error of at most 0.0003.
Values sent between devices are 32-bit elements; how exact they have to be, the bound alone decides.
No kernel may reach another device: no remote copies, remote signals or barrier semaphores. Data moves between devices by JAX's collectives and lax.ppermute only.
A program may use at most 64 MiB of HBM per device.

v0:
```python
import jax
import jax.numpy as jnp
from jax import lax
from jax.sharding import PartitionSpec as P

CLUSTER = 512
ITERS = 2


EPSILON = 0.02
FLOOR = -1e30


def tile_offsets(xs, ys):
    return [xs[c][:, None] - ys[c][None, :] for c in range(3)]


def tile_cost(offsets):
    return 0.5 * (offsets[0] * offsets[0] + offsets[1] * offsets[1] + offsets[2] * offsets[2])


def combine_parts(first, second):
    top = jnp.maximum(first[0], second[0])
    total = first[1] * jnp.exp(first[0] - top) + second[1] * jnp.exp(second[0] - top)
    return (top, total)


def reduce_rows(tops, totals):
    largest = lax.pmax(tops, "tgt")
    return (largest, lax.psum(totals * jnp.exp(tops - largest), "tgt"))


def reduce_cols(tops, totals):
    largest = lax.pmax(tops, "src")
    return (largest, lax.psum(totals * jnp.exp(tops - largest), "src"))


def body(
    source_points,
    target_points,
    source_weight,
    target_weight,
    target_start,
    tile_source,
    tile_target,
    tile_count,
):
    width_src = source_points.shape[1]
    width_tgt = target_points.shape[1]
    slots = tile_source.shape[2]
    pairs_src = tile_source[0, 0]
    pairs_tgt = tile_target[0, 0]
    live_count = tile_count[0, 0]
    log_source = jnp.log(source_weight)
    log_target = jnp.log(target_weight)

    def tile_points(slot):
        srow = pairs_src[slot] * CLUSTER
        tcol = pairs_tgt[slot] * CLUSTER
        xs = lax.dynamic_slice_in_dim(source_points, srow, CLUSTER, 1)
        ys = lax.dynamic_slice_in_dim(target_points, tcol, CLUSTER, 1)
        return (srow, tcol, tile_offsets(xs, ys))

    def run_tiles(step, init):
        return lax.fori_loop(0, slots, step, init)

    def row_pass(target_pot):

        def step(slot, carry):
            tops, totals = carry
            srow, tcol, offs = tile_points(slot)
            lb = lax.dynamic_slice_in_dim(log_target, tcol, CLUSTER)
            gs = lax.dynamic_slice_in_dim(target_pot, tcol, CLUSTER)
            scores = lb[None, :] + (gs[None, :] - tile_cost(offs)) / EPSILON
            part_top = jnp.max(scores, axis=1)
            part_total = jnp.sum(jnp.exp(scores - part_top[:, None]), axis=1)
            live = slot < live_count
            part_top = jnp.where(live, part_top, FLOOR)
            part_total = jnp.where(live, part_total, 0.0)
            old = (
                lax.dynamic_slice_in_dim(tops, srow, CLUSTER),
                lax.dynamic_slice_in_dim(totals, srow, CLUSTER),
            )
            new = combine_parts(old, (part_top, part_total))
            tops = lax.dynamic_update_slice_in_dim(tops, new[0], srow, 0)
            totals = lax.dynamic_update_slice_in_dim(totals, new[1], srow, 0)
            return (tops, totals)

        init = (jnp.full((width_src,), FLOOR, jnp.float32), jnp.zeros((width_src,), jnp.float32))
        tops, totals = run_tiles(step, init)
        tops, totals = reduce_rows(tops, totals)
        return -EPSILON * (tops + jnp.log(totals))

    def col_pass(source_pot):

        def step(slot, carry):
            tops, totals = carry
            srow, tcol, offs = tile_points(slot)
            la = lax.dynamic_slice_in_dim(log_source, srow, CLUSTER)
            fs = lax.dynamic_slice_in_dim(source_pot, srow, CLUSTER)
            scores = la[:, None] + (fs[:, None] - tile_cost(offs)) / EPSILON
            part_top = jnp.max(scores, axis=0)
            part_total = jnp.sum(jnp.exp(scores - part_top[None, :]), axis=0)
            live = slot < live_count
            part_top = jnp.where(live, part_top, FLOOR)
            part_total = jnp.where(live, part_total, 0.0)
            old = (
                lax.dynamic_slice_in_dim(tops, tcol, CLUSTER),
                lax.dynamic_slice_in_dim(totals, tcol, CLUSTER),
            )
            new = combine_parts(old, (part_top, part_total))
            tops = lax.dynamic_update_slice_in_dim(tops, new[0], tcol, 0)
            totals = lax.dynamic_update_slice_in_dim(totals, new[1], tcol, 0)
            return (tops, totals)

        init = (jnp.full((width_tgt,), FLOOR, jnp.float32), jnp.zeros((width_tgt,), jnp.float32))
        tops, totals = run_tiles(step, init)
        tops, totals = reduce_cols(tops, totals)
        return -EPSILON * (tops + jnp.log(totals))

    target_pot = target_start
    source_pot = source_weight
    for turn in range(ITERS):
        source_pot = row_pass(target_pot)
        target_pot = col_pass(source_pot)

    def grad_step(slot, carry):
        grad_src, grad_tgt = carry
        srow, tcol, offs = tile_points(slot)
        la = lax.dynamic_slice_in_dim(log_source, srow, CLUSTER)
        lb = lax.dynamic_slice_in_dim(log_target, tcol, CLUSTER)
        fs = lax.dynamic_slice_in_dim(source_pot, srow, CLUSTER)
        gs = lax.dynamic_slice_in_dim(target_pot, tcol, CLUSTER)
        plan = jnp.exp(
            la[:, None] + lb[None, :] + (fs[:, None] + gs[None, :] - tile_cost(offs)) / EPSILON
        )
        plan = jnp.where(slot < live_count, plan, 0.0)
        src_part = jnp.stack([jnp.sum(plan * offs[c], axis=1) for c in range(3)])
        tgt_part = jnp.stack([-jnp.sum(plan * offs[c], axis=0) for c in range(3)])
        grad_src = lax.dynamic_update_slice_in_dim(
            grad_src, lax.dynamic_slice_in_dim(grad_src, srow, CLUSTER, 1) + src_part, srow, 1
        )
        grad_tgt = lax.dynamic_update_slice_in_dim(
            grad_tgt, lax.dynamic_slice_in_dim(grad_tgt, tcol, CLUSTER, 1) + tgt_part, tcol, 1
        )
        return (grad_src, grad_tgt)

    init = (jnp.zeros((3, width_src), jnp.float32), jnp.zeros((3, width_tgt), jnp.float32))
    grad_src, grad_tgt = run_tiles(grad_step, init)
    whole_grad = lax.psum(grad_src, "tgt")
    share = width_src // lax.axis_size("tgt")
    own_grad = lax.dynamic_slice_in_dim(whole_grad, lax.axis_index("tgt") * share, share, 1)
    target_grad = lax.psum(grad_tgt, "src")
    return (source_pot, target_pot, own_grad, target_grad)


def solution(mesh):
    return jax.shard_map(
        body,
        mesh=mesh,
        in_specs=(
            P(None, "src"),
            P(None, "tgt"),
            P("src"),
            P("tgt"),
            P("tgt"),
            P("src", "tgt", None),
            P("src", "tgt", None),
            P("src", "tgt"),
        ),
        out_specs=(P("src"), P("tgt"), P(None, ("src", "tgt")), P(None, "tgt")),
        check_vma=False,
    )
```

profile of v0, /device:TPU:0, one launch (start us, length us, event | category | flops | bytes accessed | tf_op | source)
XLA Modules:
  0.0 591.6 jit_solution(7122815364865898730)
XLA Ops:
  2.0 78.2 %while.75 = (s32[]{:T(128)}, f32[4096]{0:T(1024)S(1)}, f32[4096]{0:T(1024)S(1)}, s32[12]{0:T(128)S(1)}, s32[]{:T(128)}, /*index=5*/s32[12]{0:T(128)S(1)}, f32[40...) while((s32[]{:T(128)}, f32[4096]{0:T(1024)S(1)}, ...), condition=%wide.region_3.4_spmd, body=%wide.region_0.3_spmd.sunk | while | flops 7080973 | bytes 84295 | solution.py:65
  4.5 0.9 constant_dynamic-slice_fusion.15
  11.0 0.9 constant_dynamic-slice_fusion.15
  17.6 0.9 constant_dynamic-slice_fusion.15
  24.1 1.0 constant_dynamic-slice_fusion.15
  30.7 0.9 constant_dynamic-slice_fusion.15
  37.2 0.9 constant_dynamic-slice_fusion.15
  43.7 0.9 constant_dynamic-slice_fusion.15
  50.2 0.9 constant_dynamic-slice_fusion.15
  56.7 0.9 constant_dynamic-slice_fusion.15
  63.2 0.9 constant_dynamic-slice_fusion.15
  69.7 0.9 constant_dynamic-slice_fusion.15
  76.2 0.9 constant_dynamic-slice_fusion.15
  80.3 12.6 %pmax.28 = f32[4096]{0:T(1024)S(1)} all-reduce(f32[4096]{0:T(1024)S(1)} %get-tuple-element.884), channel_id=1, replica_groups=mesh['src'=8,'tgt'=4] {'tgt'}, use_global_device_ids=true, to_apply=%region_4.5 | all-reduce | flops 4096 | bytes 32768 | tf_op jit(solution)/shard_map/pmax | solution.py:29
  92.9 10.1 %psum.42 = f32[4096]{0:T(1024)S(1)} all-reduce(f32[4096]{0:T(1024)S(1)} %exponential_multiply_fusion.3), channel_id=1, replica_groups=mesh['src'=8,'tgt'=4] {'tgt'}, use_global_device_ids=true, to_apply=%region_5.6 | all-reduce | flops 4096 | bytes 32768 | tf_op jit(solution)/shard_map/psum | solution.py:30
  103.8 67.9 %while.76 = (s32[]{:T(128)}, f32[4096]{0:T(1024)S(1)}, f32[4096]{0:T(1024)S(1)}, s32[12]{0:T(128)S(1)}, s32[]{:T(128)}, /*index=5*/s32[12]{0:T(128)S(1)}, f32[40...) while((s32[]{:T(128)}, f32[4096]{0:T(1024)S(1)}, ...), condition=%wide.region_9.10_spmd, body=%wide.region_6.9_spmd.sunk | while | flops 7080973 | bytes 84295 | solution.py:65
  123.2 1.0 constant_dynamic-slice_fusion.16
  171.7 37.5 %pmax.29 = f32[4096]{0:T(1024)S(1)} all-reduce(f32[4096]{0:T(1024)S(1)} %get-tuple-element.886), channel_id=1, replica_groups=mesh['src'=8,'tgt'=4] {'src'}, use_global_device_ids=true, to_apply=%region_10.11 | all-reduce | flops 4096 | bytes 32768 | tf_op jit(solution)/shard_map/pmax | solution.py:34
  209.2 33.0 %psum.43 = f32[4096]{0:T(1024)S(1)} all-reduce(f32[4096]{0:T(1024)S(1)} %exponential_multiply_fusion.2), channel_id=1, replica_groups=mesh['src'=8,'tgt'=4] {'src'}, use_global_device_ids=true, to_apply=%region_11.12 | all-reduce | flops 4096 | bytes 32768 | tf_op jit(solution)/shard_map/psum | solution.py:35
  242.2 70.1 %while.77 = (s32[]{:T(128)}, f32[4096]{0:T(1024)S(1)}, f32[4096]{0:T(1024)S(1)}, s32[12]{0:T(128)S(1)}, s32[]{:T(128)}, /*index=5*/s32[12]{0:T(128)S(1)}, f32[40...) while((s32[]{:T(128)}, f32[4096]{0:T(1024)S(1)}, ...), condition=%wide.region_15.16_spmd, body=%wide.region_12.15_spmd.sunk | while | flops 7080973 | bytes 84295 | solution.py:65
  244.8 0.9 constant_dynamic-slice_fusion.17
  250.6 0.9 constant_dynamic-slice_fusion.17
  256.4 0.9 constant_dynamic-slice_fusion.17
  262.3 1.0 constant_dynamic-slice_fusion.17
  268.2 0.9 constant_dynamic-slice_fusion.17
  274.0 0.9 constant_dynamic-slice_fusion.17
  279.8 0.9 constant_dynamic-slice_fusion.17
  285.6 0.9 constant_dynamic-slice_fusion.17
  291.4 0.9 constant_dynamic-slice_fusion.17
  297.3 0.9 constant_dynamic-slice_fusion.17
  303.1 0.9 constant_dynamic-slice_fusion.17
  309.0 0.9 constant_dynamic-slice_fusion.17
  312.3 10.1 %pmax.30 = f32[4096]{0:T(1024)S(1)} all-reduce(f32[4096]{0:T(1024)S(1)} %get-tuple-element.888), channel_id=1, replica_groups=mesh['src'=8,'tgt'=4] {'tgt'}, use_global_device_ids=true, to_apply=%region_16.17 | all-reduce | flops 4096 | bytes 32768 | tf_op jit(solution)/shard_map/pmax | solution.py:29
  322.4 10.1 %psum.44 = f32[4096]{0:T(1024)S(1)} all-reduce(f32[4096]{0:T(1024)S(1)} %exponential_multiply_fusion.1), channel_id=1, replica_groups=mesh['src'=8,'tgt'=4] {'tgt'}, use_global_device_ids=true, to_apply=%region_17.18 | all-reduce | flops 4096 | bytes 32768 | tf_op jit(solution)/shard_map/psum | solution.py:30
  332.6 67.9 %while.78 = (s32[]{:T(128)}, f32[4096]{0:T(1024)S(1)}, f32[4096]{0:T(1024)S(1)}, s32[12]{0:T(128)S(1)}, s32[]{:T(128)}, /*index=5*/s32[12]{0:T(128)S(1)}, f32[40...) while((s32[]{:T(128)}, f32[4096]{0:T(1024)S(1)}, ...), condition=%wide.region_21.22_spmd, body=%wide.region_18.21_spmd.sunk | while | flops 7080973 | bytes 84295 | solution.py:65
  335.1 0.9 constant_dynamic-slice_fusion.18
  340.8 0.9 constant_dynamic-slice_fusion.18
  346.4 0.9 constant_dynamic-slice_fusion.18
  352.1 1.0 constant_dynamic-slice_fusion.18
  357.7 0.9 constant_dynamic-slice_fusion.18
  363.4 0.9 constant_dynamic-slice_fusion.18
  369.1 0.9 constant_dynamic-slice_fusion.18
  374.7 0.9 constant_dynamic-slice_fusion.18
  380.4 0.9 constant_dynamic-slice_fusion.18
  386.0 0.9 constant_dynamic-slice_fusion.18
  391.7 0.9 constant_dynamic-slice_fusion.18
  397.3 0.9 constant_dynamic-slice_fusion.18
  400.5 33.0 %pmax.31 = f32[4096]{0:T(1024)S(1)} all-reduce(f32[4096]{0:T(1024)S(1)} %get-tuple-element.890), channel_id=1, replica_groups=mesh['src'=8,'tgt'=4] {'src'}, use_global_device_ids=true, to_apply=%region_22.23 | all-reduce | flops 4096 | bytes 32768 | tf_op jit(solution)/shard_map/pmax | solution.py:34
  433.5 33.0 %psum.45 = f32[4096]{0:T(1024)S(1)} all-reduce(f32[4096]{0:T(1024)S(1)} %exponential_multiply_fusion), channel_id=1, replica_groups=mesh['src'=8,'tgt'=4] {'src'}, use_global_device_ids=true, to_apply=%region_23.24 | all-reduce | flops 4096 | bytes 32768 | tf_op jit(solution)/shard_map/psum | solution.py:35
  466.6 79.7 %while.79 = (s32[]{:T(128)}, f32[3,4096]{1,0:T(4,128)S(1)}, f32[3,4096]{1,0:T(4,128)S(1)}, s32[12]{0:T(128)S(1)}, s32[]{:T(128)}, /*index=5*/f32[4096]{0:T(1024)...) while((s32[]{:T(128)}, f32[3,4096]{1,0:T(4,128)S(1)}, ...), condition=%wide.region_31.32_spmd, body=%wide.region_24.31_spmd.sunk | while | flops 6299149 | bytes 131435 | solution.py:65
  471.8 1.3 fusion.36
  478.4 1.3 fusion.36
  485.1 1.3 fusion.36
  491.7 1.3 fusion.36
  498.4 1.3 fusion.36
  505.0 1.3 fusion.36
  511.6 1.3 fusion.36
  518.3 1.3 fusion.36
  524.9 1.3 fusion.36
  531.6 1.3 fusion.36
  538.2 1.3 fusion.36
  544.8 1.3 fusion.36
  546.3 10.7 %psum.46 = f32[3,4096]{1,0:T(4,128)S(1)} all-reduce(f32[3,4096]{1,0:T(4,128)S(1)} %get-tuple-element.892), channel_id=1, replica_groups=mesh['src'=8,'tgt'=4] {'tgt'}, use_global_device_ids=true, to_apply=%region_32.33 | all-reduce | flops 12288 | bytes 98304 | tf_op jit(solution)/shard_map/psum | solution.py:150
  557.7 33.9 %psum.47 = f32[3,4096]{1,0:T(4,128)} all-reduce(f32[3,4096]{1,0:T(4,128)S(1)} %get-tuple-element.893), channel_id=1, replica_groups=mesh['src'=8,'tgt'=4] {'src'}, use_global_device_ids=true, to_apply=%region_33.34 | all-reduce | flops 12288 | bytes 98304 | tf_op jit(solution)/shard_map/psum | solution.py:153
  (522 shorter events, 197.0 us)
Async XLA Ops:
  1.4 0.7 copy-start.3
  1.4 0.7 copy-start.4
  103.0 0.7 copy-start.2
  546.2 10.8 %copy-start = (f32[4096]{0:T(1024)}, f32[4096]{0:T(1024)S(1)}, u32[]{:S(2)}) copy-start(f32[4096]{0:T(1024)S(1)} %get-tuple-element.1724) | copy-start | bytes 49156
  546.3 10.8 %copy-start.1 = (f32[4096]{0:T(1024)}, f32[4096]{0:T(1024)S(1)}, u32[]{:S(2)}) copy-start(f32[4096]{0:T(1024)S(1)} %get-tuple-element.1725) | copy-start | bytes 49156
where the time goes:
time: 599 us; the launch traced here: 592 us
  blocking collectives  224 us (37%)
  local copies, waits for them, and re-layouts  157 us (26%)
  loops' own time  120 us (20%)
  other arithmetic  89.1 us (15%)
    another operation x5, loops' own time, run_tiles(): return lax.fori_loop(0, slots, step, init)  120 us
    pmax x2, blocking collectives, reduce_cols(): largest = lax.pmax(tops, 'src')  70.5 us
    psum x2, blocking collectives, reduce_cols(): return (largest, lax.psum(totals * jnp.exp(tops - largest), 'src'))  66 us
    slice x72, local copies, waits for them, and re-layouts, tile_offsets(): return [xs[c][:, None] - ys[c][None, :] for c in range(3)]  65 us
    dynamic_slice x60, local copies, waits for them, and re-layouts, tile_points(): tcol = pairs_tgt[slot] * CLUSTER  35.3 us
    dynamic_slice x60, local copies, waits for them, and re-layouts, tile_points(): srow = pairs_src[slot] * CLUSTER  35.3 us
    psum x1, blocking collectives, body(): target_grad = lax.psum(grad_tgt, 'src')  33.9 us
    pmax x2, blocking collectives, reduce_rows(): largest = lax.pmax(tops, 'tgt')  22.7 us

commit v1 on v0

v1 whole, which is shorter than its diff:
```python
import functools
import math

import jax
import jax.numpy as jnp
from jax import lax
from jax.experimental import pallas as pl
from jax.experimental.pallas import tpu as pltpu
from jax.sharding import PartitionSpec as P

CLUSTER = 512
EPSILON = 0.02
KAPPA = math.log2(math.e) / EPSILON
LOG2E = math.log2(math.e)
FLOOR = -1e30
CHUNK = 128
DEPTH = 32
F32 = jnp.float32
BF16 = jnp.bfloat16


def log2(value):
    return jnp.log(value) * LOG2E


def split(value):
    high = value.astype(BF16).astype(F32)
    rest = value - high
    middle = rest.astype(BF16).astype(F32)
    return (high, middle, rest - middle)


def half_square(points):
    return 0.5 * (points[0:1] * points[0:1] + points[1:2] * points[1:2] + points[2:3] * points[2:3])


def place(scratch, parts, order):
    scratch[...] = jnp.zeros_like(scratch)
    for at, which in enumerate(order):
        scratch[3 * at : 3 * at + 3, :] = parts[which]


SOURCE_ORDER = (0, 0, 1, 0, 2, 1)
TARGET_ORDER = (0, 1, 0, 2, 0, 1)


def with_rows(out, static, first, second):
    out[0:16, :] = static[0:16, :]
    low = static[16:32, :].astype(F32)
    row = lax.broadcasted_iota(jnp.int32, low.shape, 0)
    for at, part in enumerate(tuple(first) + tuple(second)):
        low = jnp.where(row == 2 + at, part, low)
    out[16:32, :] = low.astype(BF16)


ONES = (1.0, 1.0, 1.0)
ZEROS = (0.0, 0.0, 0.0)


def scores(left, right):
    return lax.dot_general(left, right, (((0,), (0,)), ((), ())), preferred_element_type=F32)


def start_of(index):
    return pl.multiple_of(index * CLUSTER, CLUSTER)


def lse_tiles(count, red_at, kept_at, red, kept, top, total, columns=None, sums=None):
    top[...] = jnp.full_like(top, FLOOR)
    total[...] = jnp.zeros_like(total)
    if sums is not None:
        sums[...] = jnp.zeros_like(sums)

    def step(slot, carry):
        r = start_of(red_at[0, 0, slot])
        k = start_of(kept_at[0, 0, slot])
        here = pl.ds(k, CLUSTER)
        right = kept[:, here]
        m = top[:, here]
        t = total[:, here]
        acc = None if sums is None else [sums[c, :, here] for c in range(3)]
        for at in range(CLUSTER // CHUNK):
            start = pl.multiple_of(r + at * CHUNK, CHUNK)
            s = scores(red[:, pl.ds(start, CHUNK)], right)
            s = s.reshape(CHUNK // 8, 8, CLUSTER)
            new = jnp.maximum(m, jnp.max(s, axis=0))
            old = jnp.exp2(m - new)
            p = jnp.exp2(s - new[None])
            t = t * old + jnp.sum(p, axis=0)
            if acc is not None:
                for c in range(3):
                    col = columns[pl.ds(start, CHUNK), 128 * c : 128 * (c + 1)]
                    col = jnp.concatenate([col] * (CLUSTER // 128), axis=1).reshape(s.shape)
                    acc[c] = acc[c] * old + jnp.sum(p * col, axis=0)
            m = new
        top[:, here] = m
        total[:, here] = t
        if acc is not None:
            for c in range(3):
                sums[c, :, here] = acc[c]
        return carry

    lax.fori_loop(0, count, step, 0)


def finish(top, total):
    m = top[...]
    largest = jnp.max(m, axis=0, keepdims=True)
    scale = jnp.exp2(m - largest)
    whole = jnp.sum(total[...] * scale, axis=0, keepdims=True)
    return largest + log2(whole), scale, whole


def combine(parts):
    largest = functools.reduce(jnp.maximum, parts)
    terms = [jnp.exp2(part - largest) for part in parts]
    whole = functools.reduce(jnp.add, terms)
    return largest + log2(whole), [term / whole for term in terms]


def rows_of(refs):
    return [refs[at] for at in range(refs.shape[0])]


def spread_columns(columns, static):
    pieces = static[1]
    row = lax.broadcasted_iota(jnp.int32, (DEPTH, 384), 0)
    lane = lax.broadcasted_iota(jnp.int32, (DEPTH, 384), 1) // 128
    pick = functools.reduce(jnp.logical_or, [row == lane + first for first in pieces])
    pick = jnp.where(pick, 1.0, 0.0).astype(BF16)

    def step(at, carry):
        here = pl.ds(start_of(at), CLUSTER)
        columns[here, :] = scores(static[0][:, here], pick)
        return carry

    lax.fori_loop(0, columns.shape[0] // CLUSTER, step, 0)


def fetch(pairs, sems):
    copies = [pltpu.make_async_copy(src, dst, sems.at[at]) for at, (src, dst) in enumerate(pairs)]
    for copy in copies:
        copy.start()
    return copies


def first_row_kernel(
    ys_in, tw_in, g0_in, xs_in, sw_in, t_src_in, t_tgt_in, count_in,
    xc_out, yc_out, part_out, xs, ys, sw, tw,
    g0, t_src, t_tgt, count, sems, stack, red, kept, top, total,
):
    copies = fetch(
        [
            (ys_in, ys), (tw_in, tw), (g0_in, g0), (xs_in, xs), (sw_in, sw),
            (t_src_in, t_src), (t_tgt_in, t_tgt), (count_in, count),
        ],
        sems,
    )
    for copy in copies[:3]:
        copy.wait()
    place(stack, split(ys[...] * KAPPA), TARGET_ORDER)
    yc_out[...] = stack[...].astype(BF16)
    potential = log2(tw[...]) + KAPPA * (g0[...] - half_square(ys[...]))
    with_rows(red, yc_out, split(potential), ONES)
    for copy in copies[3:]:
        copy.wait()
    place(stack, split(xs[...]), SOURCE_ORDER)
    xc_out[...] = stack[...].astype(BF16)
    with_rows(kept, xc_out, ONES, ZEROS)
    lse_tiles(count[0, 0], t_tgt, t_src, red, kept, top, total)
    part_out[...] = finish(top, total)[0]


def pass_kernel(
    parts, red_static, kept_static, weight, red_in, kept_in, count_in, part_out, red_at, kept_at, count, sems, red, kept, top, total
):
    copies = fetch([(red_in, red_at), (kept_in, kept_at), (count_in, count)], sems)
    potential = log2(weight[...]) - combine(rows_of(parts))[0]
    with_rows(red, red_static, split(potential), ONES)
    with_rows(kept, kept_static, ONES, ZEROS)
    for copy in copies:
        copy.wait()
    lse_tiles(count[0, 0], red_at, kept_at, red, kept, top, total)
    part_out[...] = finish(top, total)[0]


def last_col_kernel(
    parts, xs, xc, yc, sw, t_src_in, t_tgt_in, count_in, f_out, u_out, part_out,
    t_src, t_tgt, count, sems, red, kept, top, total, sums, columns,
):
    copies = fetch([(t_src_in, t_src), (t_tgt_in, t_tgt), (count_in, count)], sems)
    u = -combine(rows_of(parts))[0]
    u_out[...] = u
    f_out[...] = u * (1.0 / KAPPA) + half_square(xs[...])
    with_rows(red, xc, split(log2(sw[...]) + u), ONES)
    with_rows(kept, yc, ONES, ZEROS)
    spread_columns(columns, (xc, (0, 6, 12)))
    for copy in copies:
        copy.wait()
    lse_tiles(count[0, 0], t_src, t_tgt, red, kept, top, total, columns, sums)
    part, scale, whole = finish(top, total)
    part_out[0:1, :] = part
    for c in range(3):
        part_out[c + 1 : c + 2, :] = jnp.sum(sums[c] * scale, axis=0, keepdims=True) / whole


def gradient_kernel(
    parts, u, xs, ys, xc, yc, sw, tw, t_src_in, t_tgt_in, count_in, g_out, target_out, source_out,
    t_src, t_tgt, count, sems, red, kept, sums, columns,
):
    copies = fetch([(t_src_in, t_src), (t_tgt_in, t_tgt), (count_in, count)], sems)
    lse, shares = combine([parts[at, 0:1, :] for at in range(parts.shape[0])])
    v = -lse
    g_out[...] = v * (1.0 / KAPPA) + half_square(ys[...])
    for c in range(3):
        mean = functools.reduce(jnp.add, [w * parts[at, c + 1 : c + 2, :] for at, w in enumerate(shares)])
        target_out[c : c + 1, :] = tw[...] * (ys[c : c + 1, :] - mean)
    with_rows(red, yc, split(log2(tw[...]) + v), ONES)
    with_rows(kept, xc, ONES, split(log2(sw[...]) + u[...]))
    spread_columns(columns, (yc, (0, 3, 9)))
    sums[...] = jnp.zeros_like(sums)
    for copy in copies:
        copy.wait()

    def step(slot, carry):
        r = start_of(t_tgt[0, 0, slot])
        k = start_of(t_src[0, 0, slot])
        here = pl.ds(k, CLUSTER)
        right = kept[:, here]
        acc = [sums[c, :, here] for c in range(4)]
        for at in range(CLUSTER // CHUNK):
            start = pl.multiple_of(r + at * CHUNK, CHUNK)
            s = scores(red[:, pl.ds(start, CHUNK)], right)
            p = jnp.exp2(s.reshape(CHUNK // 8, 8, CLUSTER))
            acc[3] = acc[3] + jnp.sum(p, axis=0)
            for c in range(3):
                col = columns[pl.ds(start, CHUNK), 128 * c : 128 * (c + 1)]
                col = jnp.concatenate([col] * (CLUSTER // 128), axis=1).reshape(p.shape)
                acc[c] = acc[c] + jnp.sum(p * col, axis=0)
        for c in range(4):
            sums[c, :, here] = acc[c]
        return carry

    lax.fori_loop(0, count[0, 0], step, 0)
    mass = jnp.sum(sums[3], axis=0, keepdims=True)
    for c in range(3):
        moved = jnp.sum(sums[c], axis=0, keepdims=True) * (1.0 / KAPPA)
        whole = xs[c : c + 1, :] * mass - moved
        for at in range(source_out.shape[0]):
            width = source_out.shape[2]
            source_out[at, c : c + 1, :] = whole[:, at * width : (at + 1) * width]


VMEM = pl.BlockSpec(memory_space=pltpu.VMEM)
HBM = pl.BlockSpec(memory_space=pltpu.HBM)


def call(kernel, ins, far, outs, scratch):
    return pl.pallas_call(
        kernel,
        out_shape=outs,
        in_specs=[VMEM] * len(ins) + [HBM] * len(far),
        out_specs=[VMEM] * len(outs),
        scratch_shapes=scratch,
        compiler_params=pltpu.CompilerParams(vmem_limit_bytes=48 * 1024 * 1024),
    )(*ins, *far)


def body(source_points, target_points, source_weight, target_weight, target_start, tile_source, tile_target, tile_count):
    ns, nt = source_points.shape[1], target_points.shape[1]
    sw, tw, g0 = (a.reshape(1, -1) for a in (source_weight, target_weight, target_start))
    tiles = (tile_source, tile_target, tile_count)

    def row(n, k=1):
        return jax.ShapeDtypeStruct((k, n), F32)

    def work(red, kept):
        return [pltpu.VMEM((DEPTH, red), BF16), pltpu.VMEM((DEPTH, kept), BF16)]

    def state(kept):
        return [pltpu.VMEM((8, kept), F32), pltpu.VMEM((8, kept), F32)]

    def lists(copies):
        return [pltpu.SMEM(a.shape, jnp.int32) for a in tiles] + [pltpu.SemaphoreType.DMA((copies,))]

    xc, yc, part, xs, ys, sw, tw = call(
        first_row_kernel,
        (),
        (target_points, tw, g0, source_points, sw, *tiles),
        [
            jax.ShapeDtypeStruct((DEPTH, ns), BF16),
            jax.ShapeDtypeStruct((DEPTH, nt), BF16),
            row(ns), row(ns, 3), row(nt, 3), row(ns), row(nt),
        ],
        [pltpu.VMEM((1, nt), F32)] + lists(8) + [pltpu.VMEM((DEPTH, ns), F32)] + work(nt, ns) + state(ns),
    )
    (part,) = call(
        pass_kernel,
        (lax.all_gather(part, "tgt"), xc, yc, sw),
        tiles,
        [row(nt)],
        lists(3) + work(ns, nt) + state(nt),
    )
    (part,) = call(
        pass_kernel,
        (lax.all_gather(part, "src"), yc, xc, tw),
        (tile_target, tile_source, tile_count),
        [row(ns)],
        lists(3) + work(nt, ns) + state(ns),
    )
    f, u, part = call(
        last_col_kernel,
        (lax.all_gather(part, "tgt"), xs, xc, yc, sw),
        tiles,
        [row(ns), row(ns), row(nt, 4)],
        lists(3) + work(ns, nt) + state(nt) + [pltpu.VMEM((3, 8, nt), F32), pltpu.VMEM((ns, 384), F32)],
    )
    n = lax.axis_size("tgt")
    g, target_grad, source_parts = call(
        gradient_kernel,
        (lax.all_gather(part, "src"), u, xs, ys, xc, yc, sw, tw),
        tiles,
        [row(nt), row(nt, 3), jax.ShapeDtypeStruct((n, 3, ns // n), F32)],
        lists(3) + work(nt, ns) + [pltpu.VMEM((4, 8, ns), F32), pltpu.VMEM((nt, 384), F32)],
    )
    own_grad = jnp.sum(lax.all_to_all(source_parts, "tgt", 0, 0), axis=0)
    return (f.reshape(-1), g.reshape(-1), own_grad, target_grad)


def solution(mesh):
    return jax.shard_map(
        body,
        mesh=mesh,
        in_specs=(
            P(None, "src"),
            P(None, "tgt"),
            P("src"),
            P("tgt"),
            P("tgt"),
            P("src", "tgt", None),
            P("src", "tgt", None),
            P("src", "tgt"),
        ),
        out_specs=(P("src"), P("tgt"), P(None, ("src", "tgt")), P(None, "tgt")),
        check_vma=False,
    )
```

time: 599 us -> 123 us (0.21)
  local copies, waits for them, and re-layouts: 157 us -> 4.48 us
  blocking collectives: 224 us -> 82.2 us
  loops' own time: 120 us -> 0 us
  other arithmetic: 89.1 us -> 0.62 us
  Pallas kernels: 0 us -> 32.6 us
    psum x6 -> x0, blocking collectives: 131 us -> none  [the longest x2 66 us: reduce_cols(): return (largest, lax.psum(totals * jnp.exp(tops - largest), 'src'))]
    another operation x5 -> x0, loops' own time: 120 us -> none  [run_tiles(): return lax.fori_loop(0, slots, step, init)]
    pmax x4 -> x0, blocking collectives: 93.3 us -> none  [the longest x2 70.5 us: reduce_cols(): largest = lax.pmax(tops, 'src')]
    dynamic_slice x265 -> x0, local copies, waits for them, and re-layouts: 90.3 us -> none  [the longest x60 35.3 us: tile_points(): tcol = pairs_tgt[slot] * CLUSTER]
    all_gather x0 -> x4, blocking collectives: none -> 75.7 us  [the longest x2 64.1 us: body(): lax.all_gather(part, 'src')]
    slice x72 -> x0, local copies, waits for them, and re-layouts: 65 us -> none  [tile_offsets(): return [xs[c][:, None] - ys[c][None, :] for c in range(3)]]
    reduce_sum x60 -> x1, other arithmetic: 49 us -> 0.62 us  [body(): own_grad = jnp.sum(lax.all_to_all(source_parts, 'tgt', 0, 0), axis=0)]
    pallas_call x0 -> x5, Pallas kernels: none -> 32.6 us  [call(): pl.pallas_call(kernel, out_shape=outs, in_specs=[VMEM] * len(ins) + [HBM]...]
where the time goes in v1:
time: 123 us; the launch traced here: 121 us
  blocking collectives  82.2 us (67%)
  Pallas kernels  32.6 us (27%)
  local copies, waits for them, and re-layouts  4.48 us (4%)
  between operations  1.34 us (1%)
    all_gather x2, blocking collectives, body(): lax.all_gather(part, 'src')  64.1 us
    pallas_call x5, Pallas kernels, call(): pl.pallas_call(kernel, out_shape=outs, in_specs=[VMEM] * len(ins) + [HBM]...  32.6 us
    all_gather x2, blocking collectives, body(): lax.all_gather(part, 'tgt')  11.6 us
    all_to_all x1, blocking collectives, body(): own_grad = jnp.sum(lax.all_to_all(source_parts, 'tgt', 0, 0), axis=0)  6.49 us
    unnamed x14, local copies, waits for them, and re-layouts  4.48 us

profile of v1, /device:TPU:0, one launch (start us, length us, event | category | flops | bytes accessed | tf_op | source)
XLA Modules:
  0.0 121.2 jit_solution(13585205282064178013)
XLA Ops:
  1.3 0.0 copy-start.5
  1.3 0.0 copy-start.6
  1.3 0.6 copy-done.5
  1.9 0.0 copy-done.6
  2.0 0.0 copy-start
  2.0 0.8 copy-done
  2.8 0.0 copy-start.1
  2.8 0.8 copy-done.1
  3.6 0.0 copy-start.2
  3.6 0.7 copy-done.2
  4.4 0.0 copy-start.3
  4.4 0.7 copy-done.3
  5.1 0.0 copy-start.4
  5.1 0.7 copy-done.4
  5.8 5.1 %shard_map.111 = (bf16[32,4096]{1,0:T(8,128)(2,1)S(1)}, bf16[32,4096]{1,0:T(8,128)(2,1)S(1)}, f32[1,4096]{1,0:T(1,128)S(1)}, f32[3,4096]{1,0:T(4,128)S(1)}, f32[...) custom-call(f32[3,4096]{1,0:T(4,128)S(1)} %copy-done, f32[1,4096]{1,0:T(1,128)S(1)} %bitcast.13, ...), custom_call_target="tpu_custom_call" | custom-call | tf_op jit(solution)/shard_map/pallas_call | solution.py:259
  10.9 6.4 %all-gather.4.parts = f32[4,1,4096]{2,1,0:T(1,128)S(1)} all-gather(f32[1,1,4096]{2,1,0:T(1,128)S(1)} %bitcast.12), channel_id=2, replica_groups=mesh['src'=8,'tgt'=4] {'tgt'}, dimensions={0}, use_global_device_ids=true | all-gather | bytes 81920 | tf_op jit(solution)/shard_map/all_gather | solution.py:299
  17.3 4.7 %shard_map.112 = f32[1,4096]{1,0:T(1,128)S(1)} custom-call(f32[4,1,4096]{2,1,0:T(1,128)S(1)} %all-gather.4.parts, bf16[32,4096]{1,0:T(8,128)(2,1)S(1)} %get-tuple-element.18.red_static.kept_static.xc, bf16[32,4096]{1,0:T(8,128)(2,1)S(1)} %get-tuple-element.19.kept_static.red_static.yc, f32[1,4096]{1,0:T(1,128)S(1)} %get-tuple-element.20.weight.sw, ...), custom_call_target="tpu_custom_call" | custom-call | tf_op jit(solution)/shard_map/pallas_call | solution.py:259
  22.0 32.8 %all-gather.5.parts = f32[8,1,4096]{2,1,0:T(1,128)S(1)} all-gather(f32[1,1,4096]{2,1,0:T(1,128)S(1)} %bitcast.10), channel_id=3, replica_groups=mesh['src'=8,'tgt'=4] {'src'}, dimensions={0}, use_global_device_ids=true | all-gather | bytes 147456 | tf_op jit(solution)/shard_map/all_gather | solution.py:306
  54.8 4.7 %shard_map.113 = f32[1,4096]{1,0:T(1,128)S(1)} custom-call(f32[8,1,4096]{2,1,0:T(1,128)S(1)} %all-gather.5.parts, bf16[32,4096]{1,0:T(8,128)(2,1)S(1)} %get-tuple-element.19.kept_static.red_static.yc, bf16[32,4096]{1,0:T(8,128)(2,1)S(1)} %get-tuple-element.18.red_static.kept_static.xc, f32[1,4096]{1,0:T(1,128)S(1)} %get-tuple-element.21.weight.tw, ...), custom_call_target="tpu_custom_call" | custom-call | tf_op jit(solution)/shard_map/pallas_call | solution.py:259
  59.6 5.2 %all-gather.6.parts = f32[4,1,4096]{2,1,0:T(1,128)S(1)} all-gather(f32[1,1,4096]{2,1,0:T(1,128)S(1)} %bitcast.11), channel_id=4, replica_groups=mesh['src'=8,'tgt'=4] {'tgt'}, dimensions={0}, use_global_device_ids=true | all-gather | bytes 81920 | tf_op jit(solution)/shard_map/all_gather | solution.py:313
  64.8 9.3 %shard_map.114 = (f32[1,4096]{1,0:T(1,128)}, f32[1,4096]{1,0:T(1,128)S(1)}, f32[4,4096]{1,0:T(4,128)S(1)}) custom-call(f32[4,1,4096]{2,1,0:T(1,128)S(1)} %all-gather.6.parts, f32[3,4096]{1,0:T(4,128)S(1)} %get-tuple-element.22.xs, bf16[32,4096]{1,0:T(8,128)(2,1)S(1)} %get-tuple-element.18.red_static.kept_static.xc, ...), custom_call_target="tpu_custom_call" | custom-call | tf_op jit(solution)/shard_map/pallas_call | solution.py:259
  74.1 31.3 %all-gather.7.parts = f32[8,4,4096]{2,1,0:T(4,128)S(1)} all-gather(f32[1,4,4096]{2,1,0:T(4,128)S(1)} %bitcast.9), channel_id=5, replica_groups=mesh['src'=8,'tgt'=4] {'src'}, dimensions={0}, use_global_device_ids=true | all-gather | bytes 589824 | tf_op jit(solution)/shard_map/all_gather | solution.py:321
  105.4 8.7 %shard_map.115 = (f32[1,4096]{1,0:T(1,128)}, f32[3,4096]{1,0:T(4,128)}, f32[4,3,1024]{2,1,0:T(4,128)S(1)}) custom-call(f32[8,4,4096]{2,1,0:T(4,128)S(1)} %all-gather.7.parts, f32[1,4096]{1,0:T(1,128)S(1)} %get-tuple-element.25.u, f32[3,4096]{1,0:T(4,128)S(1)} %get-tuple-element.22.xs, f32[3,4096]{1,0:T(4,128)S(1)} %get-tuple-element.26.ys, ...), custom_call_target="tpu_custom_call" | custom-call | tf_op jit(solution)/shard_map/pallas_call | solution.py:259
  114.1 6.5 %all_to_all.5 = f32[4,3,1024]{2,1,0:T(4,128)S(1)} all-to-all(f32[4,3,1024]{2,1,0:T(4,128)S(1)} %get-tuple-element.28), channel_id=1, replica_groups=mesh['src'=8,'tgt'=4] {'tgt'}, dimensions={0} | all-to-all | bytes 98304 | tf_op jit(solution)/shard_map/all_to_all | solution.py:326
  120.6 0.6 reduce_sum.9
Async XLA Ops:
  1.3 0.7 copy-start.5
  1.3 0.7 copy-start.6
  2.0 0.8 copy-start
  2.8 0.8 copy-start.1
  3.6 0.7 copy-start.2
  4.4 0.7 copy-start.3
  5.1 0.7 copy-start.4

commit v2 on v1

v2 whole, which is shorter than its diff:
```python
import functools
import math

import jax
import jax.numpy as jnp
from jax import lax
from jax.experimental import pallas as pl
from jax.experimental.pallas import tpu as pltpu
from jax.sharding import PartitionSpec as P

CLUSTER = 512
EPSILON = 0.02
KAPPA = math.log2(math.e) / EPSILON
LOG2E = math.log2(math.e)
DEPTH = 32
F32 = jnp.float32
BF16 = jnp.bfloat16


def log2(value):
    return jnp.log(value) * LOG2E


def split(value):
    high = value.astype(BF16).astype(F32)
    rest = value - high
    middle = rest.astype(BF16).astype(F32)
    return (high, middle, rest - middle)


def half_square(points):
    return 0.5 * (points[0:1] * points[0:1] + points[1:2] * points[1:2] + points[2:3] * points[2:3])


def place(scratch, parts, order):
    scratch[...] = jnp.zeros_like(scratch)
    for at, which in enumerate(order):
        scratch[3 * at : 3 * at + 3, :] = parts[which]


SOURCE_ORDER = (0, 0, 1, 0, 2, 1)
TARGET_ORDER = (0, 1, 0, 2, 0, 1)


def with_rows(out, static, first, second):
    out[0:16, :] = static[0:16, :]
    low = static[16:32, :].astype(F32)
    row = lax.broadcasted_iota(jnp.int32, low.shape, 0)
    for at, part in enumerate(tuple(first) + tuple(second)):
        low = jnp.where(row == 2 + at, part, low)
    out[16:32, :] = low.astype(BF16)


ONES = (1.0, 1.0, 1.0)
ZEROS = (0.0, 0.0, 0.0)


def scores(left, right):
    return lax.dot_general(left, right, (((0,), (0,)), ((), ())), preferred_element_type=F32)


def start_of(index):
    return pl.multiple_of(index * CLUSTER, CLUSTER)


def grouped(value):
    return value.reshape(value.shape[0] // 8, 8, value.shape[1])


def each_tile(tiles, left, right, chunk, unroll, visit, first, more):
    count, red_at, kept_at = tiles
    turned = left.shape[1] == DEPTH
    once = right.shape[1] // CLUSTER

    def tile(slot, done):
        r = start_of(red_at[0, 0, slot])
        here = pl.ds(start_of(kept_at[0, 0, slot]), CLUSTER)
        kept = right[:, here]
        state = None
        for at in range(CLUSTER // chunk):
            rows = pl.ds(pl.multiple_of(r + at * chunk, chunk), chunk)
            if turned:
                s = jnp.dot(left[rows, :], kept, preferred_element_type=F32)
            else:
                s = scores(left[:, rows], kept)
            state = visit(grouped(s), state, rows)
        done(here, state)

    def several(at, carry):
        for k in range(unroll):
            tile(at * unroll + k, first)
        return carry

    def one(slot, carry):
        tile(slot, more)
        return carry

    lax.fori_loop(0, once // unroll, several, 0)
    lax.fori_loop(once, count[0, 0], one, 0)


def weighed(p, columns, rows):
    for c in range(3):
        col = columns[rows, 128 * c : 128 * (c + 1)]
        col = jnp.concatenate([col] * (CLUSTER // 128), axis=1).reshape(p.shape)
        yield jnp.sum(p * col, axis=0)


def lse_tiles(tiles, left, right, top, sums, chunk, unroll, columns=None):
    def visit(s, state, rows):
        largest = jnp.max(s, axis=0)
        new = largest if state is None else jnp.maximum(state[0], largest)
        p = jnp.exp2(s - new[None])
        totals = [jnp.sum(p, axis=0)]
        if columns is not None:
            totals += weighed(p, columns, rows)
        if state is not None:
            scale = jnp.exp2(state[0] - new)
            totals = [old * scale + total for old, total in zip(state[1:], totals)]
        return [new] + totals

    def first(here, state):
        top[:, here] = state[0]
        for c, total in enumerate(state[1:]):
            sums[c, :, here] = total

    def more(here, state):
        old = top[:, here]
        new = jnp.maximum(old, state[0])
        before, now = jnp.exp2(old - new), jnp.exp2(state[0] - new)
        top[:, here] = new
        for c, total in enumerate(state[1:]):
            sums[c, :, here] = sums[c, :, here] * before + total * now

    each_tile(tiles, left, right, chunk, unroll, visit, first, more)
    m = top[...]
    largest = jnp.max(m, axis=0, keepdims=True)
    scale = jnp.exp2(m - largest)
    whole, *others = [jnp.sum(sums[c] * scale, axis=0, keepdims=True) for c in range(sums.shape[0])]
    return [largest + log2(whole)] + [other / whole for other in others]


def combine(parts):
    largest = functools.reduce(jnp.maximum, parts)
    terms = [jnp.exp2(part - largest) for part in parts]
    whole = functools.reduce(jnp.add, terms)
    return largest + log2(whole), [term / whole for term in terms]


def rows_of(refs):
    return [refs[at] for at in range(refs.shape[0])]


def spread_columns(columns, points, start):
    def step(at, carry):
        here = pl.ds(start_of(at), CLUSTER)
        block = points[0:8, here].T
        for c in range(3):
            columns[here, 128 * c : 128 * (c + 1)] = jnp.broadcast_to(block[:, start + c : start + c + 1], (CLUSTER, 128))
        return carry

    lax.fori_loop(0, columns.shape[0] // CLUSTER, step, 0)


def fetch(lists_in, lists, sem):
    copy = pltpu.make_async_copy(lists_in, lists, sem)
    copy.start()
    return copy


class List:
    def __init__(self, ref, first):
        self.ref, self.first = ref, first

    def __getitem__(self, at):
        return self.ref[self.first + at[-1]]


def lists_of(ref):
    slots = (ref.shape[0] - 1) // 2
    return List(ref, 2 * slots), List(ref, 0), List(ref, slots)


def turn(out, operand):
    out[...] = operand[...].T


def repeat(out, value):
    for at in range(out.shape[0]):
        out[at] = value


def first_row_kernel(points, lists_in, xc_out, yc_out, part_out, lists, sem, stack, red, turned, kept, top, total):
    copy = fetch(lists_in, lists, sem)
    xs, ys = points[0:3, :], points[3:6, :]
    place(stack, split(ys * KAPPA), TARGET_ORDER)
    yc_out[...] = stack[...].astype(BF16)
    potential = log2(points[7:8, :]) + KAPPA * (points[8:9, :] - half_square(ys))
    with_rows(red, yc_out, split(potential), ONES)
    turn(turned, red)
    place(stack, split(xs), SOURCE_ORDER)
    xc_out[...] = stack[...].astype(BF16)
    with_rows(kept, xc_out, ONES, ZEROS)
    copy.wait()
    count, t_src, t_tgt = lists_of(lists)
    part_out[...] = lse_tiles((count, t_tgt, t_src), turned, kept, top, total, 128, 4)[0]


def col_kernel(parts, points, xc, yc, lists_in, part_out, lists, sem, red, turned, kept, top, total):
    copy = fetch(lists_in, lists, sem)
    potential = log2(points[6:7, :]) - combine([parts[at] for at in range(parts.shape[0])])[0]
    with_rows(red, xc, split(potential), ONES)
    turn(turned, red)
    with_rows(kept, yc, ONES, ZEROS)
    copy.wait()
    count, t_src, t_tgt = lists_of(lists)
    repeat(part_out, lse_tiles((count, t_src, t_tgt), turned, kept, top, total, 128, 2)[0])


def row_kernel(parts, points, xc, yc, lists_in, part_out, lists, sem, red, turned, kept, top, total):
    copy = fetch(lists_in, lists, sem)
    potential = log2(points[7:8, :]) - combine([parts[at] for at in range(parts.shape[0])])[0]
    with_rows(red, yc, split(potential), ONES)
    turn(turned, red)
    with_rows(kept, xc, ONES, ZEROS)
    copy.wait()
    count, t_src, t_tgt = lists_of(lists)
    part_out[...] = lse_tiles((count, t_tgt, t_src), turned, kept, top, total, 256, 2)[0]


def last_col_kernel(
    parts, points, xc, yc, lists_in, f_out, u_out, part_out, lists, sem, red, turned, kept, top, total, columns
):
    copy = fetch(lists_in, lists, sem)
    u = -combine([parts[at] for at in range(parts.shape[0])])[0]
    u_out[...] = u
    f_out[...] = u * (1.0 / KAPPA) + half_square(points[0:3, :])
    with_rows(red, xc, split(log2(points[6:7, :]) + u), ONES)
    with_rows(kept, yc, ONES, ZEROS)
    turn(turned, red)
    spread_columns(columns, points, 0)
    copy.wait()
    count, t_src, t_tgt = lists_of(lists)
    cut(part_out, lse_tiles((count, t_src, t_tgt), turned, kept, top, total, 128, 2, columns))


def cut(out, rows):
    width = out.shape[2]
    for r, row in enumerate(rows):
        for at in range(out.shape[0]):
            out[at, r : r + 1, :] = row[:, at * width : (at + 1) * width]


def combine_kernel(parts, out):
    n = parts.shape[0]
    lse, shares = combine([parts[at, 0:1, :] for at in range(n)])
    means = [functools.reduce(jnp.add, [shares[at] * parts[at, c : c + 1, :] for at in range(n)]) for c in (1, 2, 3)]
    for at in range(n):
        for r, row in enumerate([lse] + means):
            out[at, r : r + 1, :] = row


def gradient_kernel(
    parts, u, points, xc, yc, lists_in, g_out, target_out, source_out, lists, sem, red, turned, kept, sums, columns
):
    copy = fetch(lists_in, lists, sem)
    joined = [jnp.concatenate([parts[at, r : r + 1, :] for at in range(parts.shape[0])], axis=1) for r in range(4)]
    xs, ys = points[0:3, :], points[3:6, :]
    v = -joined[0]
    g_out[...] = v * (1.0 / KAPPA) + half_square(ys)
    for c in range(3):
        target_out[c : c + 1, :] = points[7:8, :] * (ys[c : c + 1, :] - joined[c + 1])
    with_rows(red, yc, split(log2(points[7:8, :]) + v), ONES)
    with_rows(kept, xc, ONES, split(log2(points[6:7, :]) + u[...]))
    turn(turned, red)
    spread_columns(columns, points, 3)
    copy.wait()
    count, t_src, t_tgt = lists_of(lists)

    def visit(s, state, rows):
        p = jnp.exp2(s)
        totals = [jnp.sum(p, axis=0)] + list(weighed(p, columns, rows))
        return totals if state is None else [old + new for old, new in zip(state, totals)]

    def first(here, state):
        for c, value in enumerate(state):
            sums[c, :, here] = value

    def more(here, state):
        for c, value in enumerate(state):
            sums[c, :, here] += value

    each_tile((count, t_tgt, t_src), turned, kept, 128, 2, visit, first, more)
    mass, *moved = [jnp.sum(sums[c], axis=0, keepdims=True) for c in range(4)]
    cut(source_out, [xs[c : c + 1, :] * mass - moved[c] for c in range(3)])


VMEM = pl.BlockSpec(memory_space=pltpu.VMEM)
HBM = pl.BlockSpec(memory_space=pltpu.HBM)


def call(kernel, ins, lists, outs, scratch):
    return pl.pallas_call(
        kernel,
        out_shape=outs,
        in_specs=[VMEM] * len(ins) + [HBM] * len(lists),
        out_specs=[VMEM] * len(outs),
        scratch_shapes=scratch,
        compiler_params=pltpu.CompilerParams(vmem_limit_bytes=48 * 1024 * 1024),
    )(*ins, *lists)


def body(source_points, target_points, source_weight, target_weight, target_start, tile_source, tile_target, tile_count):
    ns, nt = source_points.shape[1], target_points.shape[1]
    n_src, n_tgt = lax.axis_size("src"), lax.axis_size("tgt")
    points = jnp.concatenate(
        [source_points, target_points] + [a.reshape(1, -1) for a in (source_weight, target_weight, target_start)]
    )
    lists = (jnp.concatenate([a.reshape(-1) for a in (tile_source, tile_target, tile_count)]),)

    def rows(n, *k):
        return jax.ShapeDtypeStruct((*k, n), F32)

    def split_rows(n):
        return jax.ShapeDtypeStruct((DEPTH, n), BF16)

    def work(red, kept):
        whole = [pltpu.SMEM(lists[0].shape, jnp.int32), pltpu.SemaphoreType.DMA, pltpu.VMEM((DEPTH, red), BF16)]
        whole += [pltpu.VMEM((red, DEPTH), BF16)]
        return whole + [pltpu.VMEM((DEPTH, kept), BF16)]

    def state(kept, totals=1):
        return [pltpu.VMEM((8, kept), F32), pltpu.VMEM((totals, 8, kept), F32)]

    first = work(nt, ns)
    xc, yc, part = call(
        first_row_kernel,
        (points,),
        lists,
        [split_rows(ns), split_rows(nt), rows(ns, 1)],
        first[:2] + [pltpu.VMEM((DEPTH, ns), F32)] + first[2:] + state(ns),
    )
    known = (points, xc, yc)
    (part,) = call(
        col_kernel, (lax.all_gather(part, "tgt"), *known), lists, [rows(nt, n_src, 1)], work(ns, nt) + state(nt)
    )
    (part,) = call(
        row_kernel, (lax.all_to_all(part, "src", 0, 0), *known), lists, [rows(ns, 1)], work(nt, ns) + state(ns)
    )
    f, u, part = call(
        last_col_kernel,
        (lax.all_gather(part, "tgt"), *known),
        lists,
        [rows(ns, 1), rows(ns, 1), rows(nt // n_src, n_src, 4)],
        work(ns, nt) + state(nt, 4) + [pltpu.VMEM((ns, 384), F32)],
    )
    (part,) = call(combine_kernel, (lax.all_to_all(part, "src", 0, 0),), (), [rows(nt // n_src, n_src, 4)], [])
    g, target_grad, part = call(
        gradient_kernel,
        (lax.all_to_all(part, "src", 0, 0), u, *known),
        lists,
        [rows(nt, 1), rows(nt, 3), rows(ns // n_tgt, n_tgt, 3)],
        work(nt, ns) + [pltpu.VMEM((4, 8, ns), F32), pltpu.VMEM((nt, 384), F32)],
    )
    own_grad = jnp.sum(lax.all_to_all(part, "tgt", 0, 0), axis=0)
    return (f.reshape(-1), g.reshape(-1), own_grad, target_grad)


def solution(mesh):
    return jax.shard_map(
        body,
        mesh=mesh,
        in_specs=(
            P(None, "src"),
            P(None, "tgt"),
            P("src"),
            P("tgt"),
            P("tgt"),
            P("src", "tgt", None),
            P("src", "tgt", None),
            P("src", "tgt"),
        ),
        out_specs=(P("src"), P("tgt"), P(None, ("src", "tgt")), P(None, "tgt")),
        check_vma=False,
    )
```

time: 123 us -> 86.9 us (0.71)
  blocking collectives: 82.2 us -> 50.1 us
  local copies, waits for them, and re-layouts: 4.48 us -> 2.37 us
  Pallas kernels: 32.6 us -> 30.9 us
    all_gather x2 -> x0, blocking collectives: 64.1 us -> none  [body(): lax.all_gather(part, 'src')]
    all_to_all x1 -> x4, blocking collectives: 6.49 us -> 39.1 us  [the longest x3 32.6 us: body(): lax.all_to_all(part, 'src', 0, 0)]
    unnamed x14 -> x4, local copies, waits for them, and re-layouts: 4.48 us -> 0.66 us
    concatenate x0 -> x1, local copies, waits for them, and re-layouts: none -> 1.71 us  [body(): jnp.concatenate([source_points, target_points] + [a.reshape(1, -1) for a...]
    pallas_call x5 -> x6, Pallas kernels: 32.6 us -> 30.9 us  [call(): pl.pallas_call(kernel, out_shape=outs, in_specs=[VMEM] * len(ins) + [HBM]...]
where the time goes in v2:
time: 86.9 us; the launch traced here: 85.5 us
  blocking collectives  50.1 us (58%)
  Pallas kernels  30.9 us (36%)
  local copies, waits for them, and re-layouts  2.37 us (3%)
  between operations  1.35 us (2%)
    all_to_all x3, blocking collectives, body(): lax.all_to_all(part, 'src', 0, 0)  32.6 us
    pallas_call x6, Pallas kernels, call(): pl.pallas_call(kernel, out_shape=outs, in_specs=[VMEM] * len(ins) + [HBM]...  30.9 us
    all_gather x2, blocking collectives, body(): lax.all_gather(part, 'tgt')  11.1 us
    all_to_all x1, blocking collectives, body(): own_grad = jnp.sum(lax.all_to_all(part, 'tgt', 0, 0), axis=0)  6.49 us

profile of v2, /device:TPU:0, one launch (start us, length us, event | category | flops | bytes accessed | tf_op | source)
XLA Modules:
  0.0 85.5 jit_solution(1237076700486332730)
XLA Ops:
  1.3 0.0 copy-start
  1.3 0.0 copy-start.1
  1.3 0.6 copy-done
  1.9 0.0 copy-done.1
  1.9 0.1 pad_add_fusion.lists_in
  2.0 1.7 %concatenate.6.points = f32[9,4096]{1,0:T(8,128)S(1)} concatenate(f32[3,4096]{1,0:T(4,128)} %param.8, f32[3,4096]{1,0:T(4,128)} %param.9, f32[1,4096]{1,0:T(1,128)} %bitcast.13, f32[1,4096]{1,0:T(1,128)} %bitcast.14, f32[1,4096]{1,0:T(1,128)} %bitcast.15), dimensions={0} | concatenate | bytes 294912 | tf_op jit(solution)/shard_map/concatenate | solution.py:316
  3.7 3.9 %shard_map.111 = (bf16[32,4096]{1,0:T(8,128)(2,1)S(1)}, bf16[32,4096]{1,0:T(8,128)(2,1)S(1)}, f32[1,4096]{1,0:T(1,128)S(1)}) custom-call(f32[9,4096]{1,0:T(8,128)S(1)} %concatenate.6.points, s32[25]{0:T(128)S(1)} %pad_add_fusion.lists_in), custom_call_target="tpu_custom_call" | custom-call | tf_op jit(solution)/shard_map/pallas_call | solution.py:303
  7.6 5.8 %all-gather.2.parts = f32[4,1,4096]{2,1,0:T(1,128)S(1)} all-gather(f32[1,1,4096]{2,1,0:T(1,128)S(1)} %bitcast.12), channel_id=2, replica_groups=mesh['src'=8,'tgt'=4] {'tgt'}, dimensions={0}, use_global_device_ids=true | all-gather | bytes 81920 | tf_op jit(solution)/shard_map/all_gather | solution.py:345
  13.5 3.9 %shard_map.112 = f32[8,1,4096]{2,1,0:T(1,128)S(1)} custom-call(f32[4,1,4096]{2,1,0:T(1,128)S(1)} %all-gather.2.parts, f32[9,4096]{1,0:T(8,128)S(1)} %concatenate.6.points, bf16[32,4096]{1,0:T(8,128)(2,1)S(1)} %get-tuple-element.14.xc, bf16[32,4096]{1,0:T(8,128)(2,1)S(1)} %get-tuple-element.15.yc, s32[25]{0:T(128)S(1)} %pad_add_fusion.lists_in), custom_call_target="tpu_custom_call" | custom-call | tf_op jit(solution)/shard_map/pallas_call | solution.py:303
  17.4 14.0 %all_to_all.20.parts = f32[8,1,4096]{2,1,0:T(1,128)S(1)} all-to-all(f32[8,1,4096]{2,1,0:T(1,128)S(1)} %shard_map.112), channel_id=1, replica_groups=mesh['src'=8,'tgt'=4] {'src'}, dimensions={0} | all-to-all | bytes 262144 | tf_op jit(solution)/shard_map/all_to_all | solution.py:348
  31.3 4.2 %shard_map.113 = f32[1,4096]{1,0:T(1,128)S(1)} custom-call(f32[8,1,4096]{2,1,0:T(1,128)S(1)} %all_to_all.20.parts, f32[9,4096]{1,0:T(8,128)S(1)} %concatenate.6.points, bf16[32,4096]{1,0:T(8,128)(2,1)S(1)} %get-tuple-element.14.xc, bf16[32,4096]{1,0:T(8,128)(2,1)S(1)} %get-tuple-element.15.yc, s32[25]{0:T(128)S(1)} %pad_add_fusion.lists_in), custom_call_target="tpu_custom_call" | custom-call | tf_op jit(solution)/shard_map/pallas_call | solution.py:303
  35.5 5.2 %all-gather.3.parts = f32[4,1,4096]{2,1,0:T(1,128)S(1)} all-gather(f32[1,1,4096]{2,1,0:T(1,128)S(1)} %bitcast.11), channel_id=3, replica_groups=mesh['src'=8,'tgt'=4] {'tgt'}, dimensions={0}, use_global_device_ids=true | all-gather | bytes 81920 | tf_op jit(solution)/shard_map/all_gather | solution.py:352
  40.8 9.8 %shard_map.114 = (f32[1,4096]{1,0:T(1,128)}, f32[1,4096]{1,0:T(1,128)S(1)}, f32[8,4,512]{2,1,0:T(4,128)S(1)}) custom-call(f32[4,1,4096]{2,1,0:T(1,128)S(1)} %all-gather.3.parts, f32[9,4096]{1,0:T(8,128)S(1)} %concatenate.6.points, bf16[32,4096]{1,0:T(8,128)(2,1)S(1)} %get-tuple-element.14.xc, bf16[32,4096]{1,0:T(8,128)(2,1)S(1)} %get-tuple-element.15.yc, ...), custom_call_target="tpu_custom_call" | custom-call | tf_op jit(solution)/shard_map/pallas_call | solution.py:303
  50.6 9.3 %all_to_all.21.parts = f32[8,4,512]{2,1,0:T(4,128)S(1)} all-to-all(f32[8,4,512]{2,1,0:T(4,128)S(1)} %get-tuple-element.17), channel_id=1, replica_groups=mesh['src'=8,'tgt'=4] {'src'}, dimensions={0} | all-to-all | bytes 131072 | tf_op jit(solution)/shard_map/all_to_all | solution.py:357
  60.0 9.3 %all_to_all.22.parts = f32[8,4,512]{2,1,0:T(4,128)S(1)} all-to-all(f32[8,4,512]{2,1,0:T(4,128)S(1)} %shard_map.115), channel_id=1, replica_groups=mesh['src'=8,'tgt'=4] {'src'}, dimensions={0} | all-to-all | bytes 131072 | tf_op jit(solution)/shard_map/all_to_all | solution.py:360
  69.3 9.1 %shard_map.116 = (f32[1,4096]{1,0:T(1,128)}, f32[3,4096]{1,0:T(4,128)}, f32[4,3,1024]{2,1,0:T(4,128)S(1)}) custom-call(f32[8,4,512]{2,1,0:T(4,128)S(1)} %all_to_all.22.parts, f32[1,4096]{1,0:T(1,128)S(1)} %get-tuple-element.18.u, f32[9,4096]{1,0:T(8,128)S(1)} %concatenate.6.points, bf16[32,4096]{1,0:T(8,128)(2,1)S(1)} %get-tuple-element.14.xc, ...), custom_call_target="tpu_custom_call" | custom-call | tf_op jit(solution)/shard_map/pallas_call | solution.py:303
  78.4 6.5 %all_to_all.23 = f32[4,3,1024]{2,1,0:T(4,128)S(1)} all-to-all(f32[4,3,1024]{2,1,0:T(4,128)S(1)} %get-tuple-element.20), channel_id=1, replica_groups=mesh['src'=8,'tgt'=4] {'tgt'}, dimensions={0} | all-to-all | bytes 98304 | tf_op jit(solution)/shard_map/all_to_all | solution.py:365
  84.9 0.6 reduce_sum.9
  (1 shorter events, 0.0 us)
Async XLA Ops:
  1.3 0.7 copy-start
  1.3 0.7 copy-start.1

commit v3 on v2

v3 whole, which is shorter than its diff:
```python
import functools
import math

import jax
import jax.numpy as jnp
from jax import lax
from jax.experimental import pallas as pl
from jax.experimental.pallas import tpu as pltpu
from jax.sharding import PartitionSpec as P

CLUSTER = 512
EPSILON = 0.02
KAPPA = math.log2(math.e) / EPSILON
LOG2E = math.log2(math.e)
DEPTH = 32
FLOOR = -1e30
F32 = jnp.float32
BF16 = jnp.bfloat16


def log2(value):
    return jnp.log(value) * LOG2E


def split(value):
    high = value.astype(BF16).astype(F32)
    rest = value - high
    middle = rest.astype(BF16).astype(F32)
    return (high, middle, rest - middle)


def half_square(points):
    return 0.5 * (points[0:1] * points[0:1] + points[1:2] * points[1:2] + points[2:3] * points[2:3])


SOURCE_ORDER = (0, 1, 2, 0, 0, 1)
TARGET_ORDER = (0, 0, 0, 1, 2, 1)
TARGET_PARTS = (0, 9, 12)
ONE = 15


def place(scratch, parts, order):
    scratch[...] = jnp.zeros_like(scratch)
    for at, which in enumerate(order[:5]):
        scratch[3 * at : 3 * at + 3, :] = parts[which]
    scratch[ONE : ONE + 1, :] = jnp.ones_like(parts[0][0:1])
    scratch[16:19, :] = parts[order[5]]


def with_rows(out, static, first, second):
    out[0:16, :] = static[0:16, :]
    low = static[16:32, :].astype(F32)
    row = lax.broadcasted_iota(jnp.int32, low.shape, 0)
    for at, part in enumerate(tuple(first) + tuple(second)):
        low = jnp.where(row == 3 + at, part, low)
    out[16:32, :] = low.astype(BF16)


def pieces(potential):
    return split(potential - 1.0)


ONES = (1.0, 1.0, 1.0)
ZEROS = (0.0, 0.0, 0.0)


def scores(left, right):
    return lax.dot_general(left, right, (((0,), (0,)), ((), ())), preferred_element_type=F32)


def start_of(index):
    return pl.multiple_of(index * CLUSTER, CLUSTER)


def grouped(value):
    return value.reshape(value.shape[0] // 8, 8, value.shape[1])


def each_tile(tiles, left, right, visit, first, more, chunk=128, unroll=2, ahead=0, halves=False):
    slots = tiles.slots
    once = right.shape[1] // CLUSTER

    def product(left_rows, kept):
        if not halves:
            return jnp.dot(left_rows, kept, preferred_element_type=F32)
        half = CLUSTER // 2
        both = [jnp.dot(left_rows, kept[:, at * half : (at + 1) * half], preferred_element_type=F32) for at in (0, 1)]
        return jnp.concatenate(both, axis=1)

    def tile_group(group):
        steps = []
        for which, slot in enumerate(group):
            r, k = tiles.starts(slot)
            for at in range(CLUSTER // chunk):
                steps.append((which, pl.ds(k, CLUSTER), pl.ds(pl.multiple_of(r + at * chunk, chunk), chunk)))
        states = [None] * len(group)
        scores = [None] * len(steps)

        def start(n):
            if n < len(steps):
                which, here, rows = steps[n]
                scores[n] = grouped(product(left[rows, :], right[:, here]))

        for n in range(ahead):
            start(n)
        for n, (which, here, rows) in enumerate(steps):
            start(n + ahead)
            states[which] = visit(scores[n], states[which], rows)
        return [(steps[which * (CLUSTER // chunk)][1], state) for which, state in enumerate(states)]

    def several(at, carry):
        for here, state in tile_group([at * unroll + k for k in range(unroll)]):
            first(here, state)
        return carry

    def others(at, carry):
        group = [jnp.minimum(once + at * 2 + k, slots - 1) for k in range(2)]
        live = [once + at * 2 + k < tiles.count() for k in range(2)]
        for alive, (here, state) in zip(live, tile_group(group)):
            more(here, state, alive)
        return carry

    lax.fori_loop(0, once // unroll, several, 0)
    lax.fori_loop(0, lax.div(tiles.count() - once + 1, 2), others, 0)


def lse_tiles(tiles, left, right, top, total, **how):
    def visit(s, state, rows):
        largest = jnp.max(s, axis=0)
        if state is None:
            return largest, jnp.sum(jnp.exp2(s - largest[None]), axis=0)
        new = jnp.maximum(state[0], largest)
        return new, state[1] * jnp.exp2(state[0] - new) + jnp.sum(jnp.exp2(s - new[None]), axis=0)

    def first(here, state):
        top[:, here], total[:, here] = state

    def more(here, state, live):
        old, m = top[:, here], jnp.where(live, state[0], FLOOR)
        new = jnp.maximum(old, m)
        top[:, here] = new
        total[:, here] = total[:, here] * jnp.exp2(old - new) + state[1] * jnp.exp2(m - new)

    each_tile(tiles, left, right, visit, first, more, **how)
    m = top[...]
    largest = jnp.max(m, axis=0, keepdims=True)
    return largest + log2(jnp.sum(total[...] * jnp.exp2(m - largest), axis=0, keepdims=True))


def moments(p, static, rows):
    p = p.reshape(p.shape[0] * 8, p.shape[2])
    high = p.astype(BF16)
    low = (p - high.astype(F32)).astype(BF16)
    weights = static[0:16, rows]
    half = CLUSTER // 2
    both = []
    for at in (0, 1):
        here = slice(at * half, (at + 1) * half)
        both.append(sum(jnp.dot(weights, part[:, here], preferred_element_type=F32) for part in (high, low)))
    return jnp.concatenate(both, axis=1)


def joined(sums, parts):
    return [functools.reduce(jnp.add, [sums[at + c : at + c + 1, :] for at in parts]) for c in range(3)]


def weighed(p, columns, rows):
    for c in range(3):
        col = columns[rows, 128 * c : 128 * (c + 1)]
        col = jnp.concatenate([col] * (CLUSTER // 128), axis=1).reshape(p.shape)
        yield jnp.sum(p * col, axis=0)


def mean_tiles(tiles, left, right, columns, top, sums, **how):
    def visit(s, state, rows):
        largest = jnp.max(s, axis=0)
        new = largest if state is None else jnp.maximum(state[0], largest)
        p = jnp.exp2(s - new[None])
        totals = [jnp.sum(p, axis=0)] + list(weighed(p, columns, rows))
        if state is not None:
            scale = jnp.exp2(state[0] - new)
            totals = [old * scale + total for old, total in zip(state[1:], totals)]
        return [new] + totals

    def first(here, state):
        top[:, here] = state[0]
        for c, total in enumerate(state[1:]):
            sums[c, :, here] = total

    def more(here, state, live):
        old, m = top[:, here], jnp.where(live, state[0], FLOOR)
        new = jnp.maximum(old, m)
        before, now = jnp.exp2(old - new), jnp.exp2(m - new)
        top[:, here] = new
        for c, total in enumerate(state[1:]):
            sums[c, :, here] = sums[c, :, here] * before + total * now

    each_tile(tiles, left, right, visit, first, more, **how)
    m = top[...]
    largest = jnp.max(m, axis=0, keepdims=True)
    scale = jnp.exp2(m - largest)
    mass, *others = [jnp.sum(sums[c] * scale, axis=0, keepdims=True) for c in range(4)]
    return [largest + log2(mass)] + [other / mass for other in others]


def spread_columns(columns, points, start):
    def step(at, carry):
        here = pl.ds(start_of(at), CLUSTER)
        block = points[0:8, here].T
        for c in range(3):
            columns[here, 128 * c : 128 * (c + 1)] = jnp.broadcast_to(block[:, start + c : start + c + 1], (CLUSTER, 128))
        return carry

    lax.fori_loop(0, columns.shape[0] // CLUSTER, step, 0)


def plan_tiles(tiles, left, right, static, parts, sums, **how):
    def visit(s, state, rows):
        total = moments(jnp.exp2(s), static, rows)
        return total if state is None else state + total

    def first(here, state):
        sums[:, here] = state

    def more(here, state, live):
        sums[:, here] += jnp.where(live, state, 0.0)

    each_tile(tiles, left, right, visit, first, more, **how)
    return [sums[ONE : ONE + 1, :]] + joined(sums, parts)


def combine(parts):
    largest = functools.reduce(jnp.maximum, parts)
    terms = [jnp.exp2(part - largest) for part in parts]
    whole = functools.reduce(jnp.add, terms)
    return largest + log2(whole), [term / whole for term in terms]


def rows_of(refs):
    return [refs[at] for at in range(refs.shape[0])]


class Tiles:
    def __init__(self, ref, points, kept_source):
        self.ref, self.slots, self.kept_source = ref, ref.shape[-1], kept_source
        self.sources, self.targets = points

    def count(self):
        return lax.div(self.ref[0, 0, 0], self.sources * self.targets)

    def starts(self, slot):
        packed = self.ref[0, 0, slot]
        source = start_of(lax.rem(packed, self.sources))
        target = start_of(lax.rem(lax.div(packed, self.sources), self.targets))
        return (target, source) if self.kept_source else (source, target)


def fetch(lists_in, lists, sem):
    copy = pltpu.make_async_copy(lists_in, lists, sem)
    copy.start()
    return copy


def turn(out, operand):
    out[...] = operand[...].T


def repeat(out, value):
    for at in range(out.shape[0]):
        out[at] = value


def sides(xc, yc):
    return xc.shape[1] // CLUSTER, yc.shape[1] // CLUSTER


def first_row_kernel(points, lists_in, xc_out, yc_out, part_out, lists, sem, stack, red, turned, kept, top, total):
    copy = fetch(lists_in, lists, sem)
    xs, ys = points[0:3, :], points[3:6, :]
    place(stack, split(ys * KAPPA), TARGET_ORDER)
    yc_out[...] = stack[...].astype(BF16)
    potential = log2(points[7:8, :]) + KAPPA * (points[8:9, :] - half_square(ys))
    with_rows(red, yc_out, pieces(potential), ONES)
    turn(turned, red)
    place(stack, split(xs), SOURCE_ORDER)
    xc_out[...] = stack[...].astype(BF16)
    with_rows(kept, xc_out, ONES, ZEROS)
    copy.wait()
    part_out[...] = lse_tiles(Tiles(lists, sides(kept, red), True), turned, kept, top, total, unroll=4, ahead=1)


def col_kernel(parts, points, xc, yc, lists_in, part_out, lists, sem, red, turned, kept, top, total):
    copy = fetch(lists_in, lists, sem)
    potential = log2(points[6:7, :]) - combine([ref[...] for ref in parts])[0]
    with_rows(red, xc, pieces(potential), ONES)
    turn(turned, red)
    with_rows(kept, yc, ONES, ZEROS)
    copy.wait()
    repeat(part_out, lse_tiles(Tiles(lists, sides(xc, yc), False), turned, kept, top, total, halves=True))


def row_kernel(parts, points, xc, yc, lists_in, part_out, lists, sem, red, turned, kept, top, total):
    copy = fetch(lists_in, lists, sem)
    potential = log2(points[7:8, :]) - combine([parts[at] for at in range(parts.shape[0])])[0]
    with_rows(red, yc, pieces(potential), ONES)
    turn(turned, red)
    with_rows(kept, xc, ONES, ZEROS)
    copy.wait()
    part_out[...] = lse_tiles(Tiles(lists, sides(xc, yc), True), turned, kept, top, total, unroll=8)


def last_col_kernel(
    parts, points, xc, yc, lists_in, f_out, u_out, part_out, lists, sem, red, turned, kept, top, sums, columns, f, sem_out
):
    copy = fetch(lists_in, lists, sem)
    u = -combine([ref[...] for ref in parts])[0]
    u_out[...] = u
    f[...] = u * (1.0 / KAPPA) + half_square(points[0:3, :])
    back = fetch(f, f_out, sem_out)
    with_rows(red, xc, pieces(log2(points[6:7, :]) + u), ONES)
    turn(turned, red)
    with_rows(kept, yc, ONES, ZEROS)
    copy.wait()
    tiles = Tiles(lists, sides(xc, yc), False)
    spread_columns(columns, points, 0)
    cut(part_out, mean_tiles(tiles, turned, kept, columns, top, sums))
    back.wait()


def cut(out, rows):
    width = out.shape[2]
    for r, row in enumerate(rows):
        for at in range(out.shape[0]):
            out[at, r : r + 1, :] = row[:, at * width : (at + 1) * width]


def combine_kernel(parts, out):
    n = parts.shape[0]
    lse, shares = combine([parts[at, 0:1, :] for at in range(n)])
    means = [functools.reduce(jnp.add, [shares[at] * parts[at, c : c + 1, :] for at in range(n)]) for c in (1, 2, 3)]
    for at in range(n):
        for r, row in enumerate([lse] + means):
            out[at, r : r + 1, :] = row


def gradient_kernel(
    parts, u, points, xc, yc, lists_in, g_out, target_out, *rest, shares
):
    source_out, (lists, sem, red, turned, kept, sums, g, target, whole, sems) = rest[:shares], rest[shares:]
    copy = fetch(lists_in, lists, sem)
    lse, *means = [jnp.concatenate([parts[at, r : r + 1, :] for at in range(parts.shape[0])], axis=1) for r in range(4)]
    xs, ys = points[0:3, :], points[3:6, :]
    g[...] = half_square(ys) - lse * (1.0 / KAPPA)
    for c in range(3):
        target[c : c + 1, :] = points[7:8, :] * (ys[c : c + 1, :] - means[c])
    back = [fetch(g, g_out, sems.at[0]), fetch(target, target_out, sems.at[1])]
    with_rows(red, yc, pieces(log2(points[7:8, :]) - lse), ONES)
    turn(turned, red)
    with_rows(kept, xc, ONES, split(log2(points[6:7, :]) + u[...]))
    copy.wait()
    tiles = Tiles(lists, sides(xc, yc), True)
    mass, *moved = plan_tiles(tiles, turned, kept, yc, TARGET_PARTS, sums)
    for c in range(3):
        whole[c : c + 1, :] = xs[c : c + 1, :] * mass - moved[c] * (1.0 / KAPPA)
    place_tgt = lax.axis_index("tgt")
    for k, out in enumerate(source_out):
        width = out.shape[1]
        at = pl.multiple_of(peer(place_tgt, k, shares) * width, width)
        out[...] = whole[:, pl.ds(at, width)]
    for one in back:
        one.wait()


VMEM = pl.BlockSpec(memory_space=pltpu.VMEM)
HBM = pl.BlockSpec(memory_space=pltpu.HBM)


def call(kernel, ins, lists, outs, scratch, far=()):
    return pl.pallas_call(
        kernel,
        out_shape=outs,
        in_specs=[VMEM] * len(ins) + [HBM] * len(lists),
        out_specs=[HBM if at in far else VMEM for at in range(len(outs))],
        scratch_shapes=scratch,
        compiler_params=pltpu.CompilerParams(vmem_limit_bytes=48 * 1024 * 1024),
    )(*ins, *lists)


def peer(i, k, n):
    return i ^ k if n & (n - 1) == 0 else (i + k) % n


def exchange(values, axis):
    n = lax.axis_size(axis)
    return values[:1] + [
        lax.ppermute(values[k], axis, [(i, peer(i, k, n)) for i in range(n)]) for k in range(1, n)
    ]


def body(source_points, target_points, source_weight, target_weight, target_start, tile_source, tile_target, tile_count):
    ns, nt = source_points.shape[1], target_points.shape[1]
    n_src, n_tgt = lax.axis_size("src"), lax.axis_size("tgt")
    points = jnp.concatenate(
        [source_points, target_points] + [a.reshape(1, -1) for a in (source_weight, target_weight, target_start)]
    )
    lists = ((tile_count[:, :, None] * (nt // CLUSTER) + tile_target) * (ns // CLUSTER) + tile_source,)

    def rows(n, *k):
        return jax.ShapeDtypeStruct((*k, n), F32)

    def split_rows(n):
        return jax.ShapeDtypeStruct((DEPTH, n), BF16)

    def work(red, kept):
        return [
            pltpu.SMEM(lists[0].shape, jnp.int32),
            pltpu.SemaphoreType.DMA,
            pltpu.VMEM((DEPTH, red), BF16),
            pltpu.VMEM((red, DEPTH), BF16),
            pltpu.VMEM((DEPTH, kept), BF16),
        ]

    def state(kept):
        return [pltpu.VMEM((8, kept), F32), pltpu.VMEM((8, kept), F32)]

    first = work(nt, ns)
    xc, yc, part = call(
        first_row_kernel,
        (points,),
        lists,
        [split_rows(ns), split_rows(nt), rows(ns, 1)],
        first[:2] + [pltpu.VMEM((DEPTH, ns), F32)] + first[2:] + state(ns),
    )
    known = (points, xc, yc)
    parts = exchange([part] * n_tgt, "tgt")
    (part,) = call(
        lambda *refs: col_kernel(refs[:n_tgt], *refs[n_tgt:]),
        (*parts, *known),
        lists,
        [rows(nt, n_src, 1)],
        work(ns, nt) + state(nt),
    )
    (part,) = call(
        row_kernel, (lax.all_to_all(part, "src", 0, 0), *known), lists, [rows(ns, 1)], work(nt, ns) + state(ns)
    )
    parts = exchange([part] * n_tgt, "tgt")
    f, u, part = call(
        lambda *refs: last_col_kernel(refs[:n_tgt], *refs[n_tgt:]),
        (*parts, *known),
        lists,
        [rows(ns, 1), rows(ns, 1), rows(nt // n_src, n_src, 4)],
        work(ns, nt)
        + [
            pltpu.VMEM((8, nt), F32),
            pltpu.VMEM((4, 8, nt), F32),
            pltpu.VMEM((ns, 384), F32),
            pltpu.VMEM((1, ns), F32),
            pltpu.SemaphoreType.DMA,
        ],
        far=(0,),
    )
    (part,) = call(combine_kernel, (lax.all_to_all(part, "src", 0, 0),), (), [rows(nt // n_src, n_src, 4)], [])
    g, target_grad, *parts = call(
        functools.partial(gradient_kernel, shares=n_tgt),
        (lax.all_to_all(part, "src", 0, 0), u, *known),
        lists,
        [rows(nt, 1), rows(nt, 3)] + [rows(ns // n_tgt, 3)] * n_tgt,
        work(nt, ns)
        + [
            pltpu.VMEM((16, ns), F32),
            pltpu.VMEM((1, nt), F32),
            pltpu.VMEM((3, nt), F32),
            pltpu.VMEM((3, ns), F32),
            pltpu.SemaphoreType.DMA((2,)),
        ],
        far=(0, 1),
    )
    own_grad = functools.reduce(jnp.add, exchange(parts, "tgt"))
    return (f.reshape(-1), g.reshape(-1), own_grad, target_grad)


def solution(mesh):
    return jax.shard_map(
        body,
        mesh=mesh,
        in_specs=(
            P(None, "src"),
            P(None, "tgt"),
            P("src"),
            P("tgt"),
            P("tgt"),
            P("src", "tgt", None),
            P("src", "tgt", None),
            P("src", "tgt"),
        ),
        out_specs=(P("src"), P("tgt"), P(None, ("src", "tgt")), P(None, "tgt")),
        check_vma=False,
    )
```

time: 86.9 us -> 81.3 us (0.936); the launches traced: 85.5 us -> 81.4 us
  blocking collectives: 50.1 us -> 33.3 us
  starting transfers between devices: 0 us -> 9.22 us
  waiting for transfers between devices: 0 us -> 7.46 us
  Pallas kernels: 30.9 us -> 27.1 us
    all_gather x2 -> x0, blocking collectives: 11.1 us -> none  [body(): lax.all_gather(part, 'tgt')]
    ppermute x0 -> x9, starting transfers between devices: none -> 9.22 us  [exchange(): lax.ppermute(values[k], axis, [(i, peer(i, k, n)) for i in range(n)])]
    ppermute x0 -> x9, waiting for transfers between devices: none -> 7.46 us  [exchange(): lax.ppermute(values[k], axis, [(i, peer(i, k, n)) for i in range(n)])]
    all_to_all x1 -> x0, blocking collectives: 6.49 us -> none  [body(): own_grad = jnp.sum(lax.all_to_all(part, 'tgt', 0, 0), axis=0)]
    pallas_call x6, Pallas kernels: 30.9 us -> 27.1 us  [call(): pl.pallas_call(kernel, out_shape=outs, in_specs=[VMEM] * len(ins) + [HBM]...]
  transfers between devices with their start and end apart: 0 -> 9, of which waited for: 0 -> 6; matrix products, arithmetic and copies ran while one was open for 0% -> 0% of each run, Pallas kernels for 0% -> 0%
where the time goes in v3:
time: 81.3 us; the launch traced here: 81.4 us
  blocking collectives  33.3 us (41%)
  Pallas kernels  27.1 us (33%)
  starting transfers between devices  9.22 us (11%)
  waiting for transfers between devices  7.46 us (9%)
  local copies, waits for them, and re-layouts  2.37 us (3%)
  between operations  1.37 us (2%)
    all_to_all x3, blocking collectives, body(): lax.all_to_all(part, 'src', 0, 0)  33.3 us
    pallas_call x6, Pallas kernels, call(): pl.pallas_call(kernel, out_shape=outs, in_specs=[VMEM] * len(ins) + [HBM]...  27.1 us
    ppermute x9, starting transfers between devices, exchange(): lax.ppermute(values[k], axis, [(i, peer(i, k, n)) for i in range(n)])  9.22 us
    ppermute x9, waiting for transfers between devices, exchange(): lax.ppermute(values[k], axis, [(i, peer(i, k, n)) for i in range(n)])  7.46 us
    concatenate x1, local copies, waits for them, and re-layouts, body(): jnp.concatenate([source_points, target_points] + [a.reshape(1, -1) for a...  1.71 us
  transfers between devices with their start and end apart: 9, of which 6 were waited for; matrix products, arithmetic and copies ran while one was open for 0% of the time, Pallas kernels for 0%

profile of v3, /device:TPU:0, one launch (start us, length us, event | category | flops | bytes accessed | tf_op | source)
XLA Modules:
  0.0 81.4 jit_solution(13998542870921207444)
XLA Ops:
  1.3 0.0 copy-start
  1.3 0.0 copy-start.1
  1.3 0.6 copy-done
  1.9 0.0 copy-done.1
  2.0 1.7 %concatenate.3.points.refs_4_ = f32[9,4096]{1,0:T(8,128)S(1)} concatenate(f32[3,4096]{1,0:T(4,128)} %param.8, f32[3,4096]{1,0:T(4,128)} %param.9, f32[1,4096]{1,0:T(1,128)} %bitcast.6, f32[1,4096]{1,0:T(1,128)} %bitcast.7, f32[1,4096]{1,0:T(1,128)} %bitcast.8), dimensions={0} | concatenate | bytes 294912 | tf_op jit(solution)/shard_map/concatenate | solution.py:403
  3.7 3.0 %shard_map.111 = (bf16[32,4096]{1,0:T(8,128)(2,1)S(1)}, bf16[32,4096]{1,0:T(8,128)(2,1)S(1)}, f32[1,4096]{1,0:T(1,128)S(1)}) custom-call(f32[9,4096]{1,0:T(8,128)S(1)} %concatenate.3.points.refs_4_, s32[1,1,12]{2,1,0:T(1,128)S(1)} %multiply_add_fusion.lists_in.refs_7_), custom_call_target="tpu_custom_call" | custom-call | tf_op jit(solution)/shard_map/pallas_call | solution.py:379
  6.6 2.4 %collective-permute-start.2 = (f32[1,4096]{1,0:T(1,128)S(1)}, f32[1,4096]{1,0:T(1,128)S(1)}, u32[]{:S(2)}, u32[]{:S(2)}) collective-permute-start(f32[1,4096]{1,0:T(1,128)S(1)} %get-tuple-element.16.refs_0_), channel_id=1, source_target_pairs={{0,3},{1,2},{2,1},{3,0},{4,7},{5,6},{6,5},{7,4},{8,11},{9,10},{10,... | collective-permute-start | bytes 49160 | tf_op jit(solution)/shard_map/ppermute | solution.py:396
  9.1 1.2 %collective-permute-start.1 = (f32[1,4096]{1,0:T(1,128)S(1)}, f32[1,4096]{1,0:T(1,128)S(1)}, u32[]{:S(2)}, u32[]{:S(2)}) collective-permute-start(f32[1,4096]{1,0:T(1,128)S(1)} %get-tuple-element.16.refs_0_), channel_id=1, source_target_pairs={{0,2},{1,3},{2,0},{3,1},{4,6},{5,7},{6,4},{7,5},{8,10},{9,11},{10,... | collective-permute-start | bytes 49160 | tf_op jit(solution)/shard_map/ppermute | solution.py:396
  10.3 0.0 collective-permute-start
  10.3 0.2 collective-permute-done.2.refs_3_
  10.5 2.3 %collective-permute-done.1.refs_2_ = f32[1,4096]{1,0:T(1,128)S(1)} collective-permute-done((f32[1,4096]{1,0:T(1,128)S(1)}, f32[1,4096]{1,0:T(1,128)S(1)}, u32[]{:S(2)}, u32[]{:S(2)}) %collective-permute-start.1) | collective-permute-done | bytes 16416 | tf_op jit(solution)/shard_map/ppermute | solution.py:396
  12.8 0.0 collective-permute-done.refs_1_
  12.8 3.3 %shard_map.112 = f32[8,1,4096]{2,1,0:T(1,128)S(1)} custom-call(f32[1,4096]{1,0:T(1,128)S(1)} %get-tuple-element.16.refs_0_, f32[1,4096]{1,0:T(1,128)S(1)} %collective-permute-done.refs_1_, f32[1,4096]{1,0:T(1,128)S(1)} %collective-permute-done.1.refs_2_, f32[1,4096]{1,0:T(1,128)S(1)} %collective-permute-done.2.refs_3_, ...), custom_call_target="tpu_custom_call" | custom-call | tf_op jit(solution)/shard_map/pallas_call | solution.py:379
  16.1 13.4 %all_to_all.15.parts = f32[8,1,4096]{2,1,0:T(1,128)S(1)} all-to-all(f32[8,1,4096]{2,1,0:T(1,128)S(1)} %shard_map.112), channel_id=1, replica_groups=mesh['src'=8,'tgt'=4] {'src'}, dimensions={0} | all-to-all | bytes 262144 | tf_op jit(solution)/shard_map/all_to_all | solution.py:444
  29.5 3.0 %shard_map.113.refs_0_ = f32[1,4096]{1,0:T(1,128)S(1)} custom-call(f32[8,1,4096]{2,1,0:T(1,128)S(1)} %all_to_all.15.parts, f32[9,4096]{1,0:T(8,128)S(1)} %concatenate.3.points.refs_4_, bf16[32,4096]{1,0:T(8,128)(2,1)S(1)} %get-tuple-element.17.refs_5_.xc, bf16[32,4096]{1,0:T(8,128)(2,1)S(1)} %get-tuple-element.18.refs_6_.yc, ...), custom_call_target="tpu_custom_call" | custom-call | tf_op jit(solution)/shard_map/pallas_call | solution.py:379
  32.5 0.1 collective-permute-start.5
  32.6 1.9 %collective-permute-start.4 = (f32[1,4096]{1,0:T(1,128)S(1)}, f32[1,4096]{1,0:T(1,128)S(1)}, u32[]{:S(2)}, u32[]{:S(2)}) collective-permute-start(f32[1,4096]{1,0:T(1,128)S(1)} %shard_map.113.refs_0_), channel_id=1, source_target_pairs={{0,2},{1,3},{2,0},{3,1},{4,6},{5,7},{6,4},{7,5},{8,10},{9,11},{10,... | collective-permute-start | bytes 49160 | tf_op jit(solution)/shard_map/ppermute | solution.py:396
  34.5 0.0 collective-permute-start.3
  34.5 1.2 %collective-permute-done.5.refs_3_ = f32[1,4096]{1,0:T(1,128)S(1)} collective-permute-done((f32[1,4096]{1,0:T(1,128)S(1)}, f32[1,4096]{1,0:T(1,128)S(1)}, u32[]{:S(2)}, u32[]{:S(2)}) %collective-permute-start.5) | collective-permute-done | bytes 16416 | tf_op jit(solution)/shard_map/ppermute | solution.py:396
  35.7 0.7 collective-permute-done.4.refs_2_
  36.4 0.0 collective-permute-done.3.refs_1_
  36.4 9.0 %shard_map.114 = (f32[1,4096]{1,0:T(1,128)}, f32[1,4096]{1,0:T(1,128)S(1)}, f32[8,4,512]{2,1,0:T(4,128)S(1)}) custom-call(f32[1,4096]{1,0:T(1,128)S(1)} %shard_map.113.refs_0_, f32[1,4096]{1,0:T(1,128)S(1)} %collective-permute-done.3.refs_1_, f32[1,4096]{1,0:T(1,128)S(1)} %collective-permute-done.4.refs_2_, f32[1,4096]{1,0:T(1,128)S(1)} %collective-permute-done.5.refs_3_, ...), custom_call_target="tpu_custom_call" | custom-call | tf_op jit(solution)/shard_map/pallas_call | solution.py:379
  45.4 10.6 %all_to_all.16.parts = f32[8,4,512]{2,1,0:T(4,128)S(1)} all-to-all(f32[8,4,512]{2,1,0:T(4,128)S(1)} %get-tuple-element.20), channel_id=1, replica_groups=mesh['src'=8,'tgt'=4] {'src'}, dimensions={0} | all-to-all | bytes 131072 | tf_op jit(solution)/shard_map/all_to_all | solution.py:462
  56.0 9.3 %all_to_all.17.parts = f32[8,4,512]{2,1,0:T(4,128)S(1)} all-to-all(f32[8,4,512]{2,1,0:T(4,128)S(1)} %shard_map.115), channel_id=1, replica_groups=mesh['src'=8,'tgt'=4] {'src'}, dimensions={0} | all-to-all | bytes 131072 | tf_op jit(solution)/shard_map/all_to_all | solution.py:465
  65.3 8.9 %shard_map.116 = (f32[1,4096]{1,0:T(1,128)}, f32[3,4096]{1,0:T(4,128)}, f32[3,1024]{1,0:T(4,128)S(1)}, f32[3,1024]{1,0:T(4,128)S(1)}, f32[3,1024]{1,0:T(4,128)S(1)}, /*index=5*/f32[3,1024]{1,0:T(4,128)S(1)}) custom-call(f32[8,4,512]{2,1,0:T(4,128)S(1)} %all_to_all.17.parts, f32[1,4096]{1,0:T(1,128)S(1)} %get-tuple-element.21.u, ...), custom_call_target="tpu_custom_call" | custom-call | tf_op jit(solution)/shard_map/pallas_call | solution.py:379
  74.2 0.1 collective-permute-start.6
  74.3 3.4 %collective-permute-start.7 = (f32[3,1024]{1,0:T(4,128)S(1)}, f32[3,1024]{1,0:T(4,128)S(1)}, u32[]{:S(2)}, u32[]{:S(2)}) collective-permute-start(f32[3,1024]{1,0:T(4,128)S(1)} %get-tuple-element.25), channel_id=1, source_target_pairs={{0,2},{1,3},{2,0},{3,1},{4,6},{5,7},{6,4},{7,5},{8,10},{9,11},{10,... | collective-permute-start | bytes 36872 | tf_op jit(solution)/shard_map/ppermute | solution.py:396
  77.7 0.1 collective-permute-start.8
  77.7 0.0 collective-permute-done.6
  77.7 1.6 %collective-permute-done.7 = f32[3,1024]{1,0:T(4,128)S(1)} collective-permute-done((f32[3,1024]{1,0:T(4,128)S(1)}, f32[3,1024]{1,0:T(4,128)S(1)}, u32[]{:S(2)}, u32[]{:S(2)}) %collective-permute-start.7) | collective-permute-done | bytes 12320 | tf_op jit(solution)/shard_map/ppermute | solution.py:396
  79.4 1.4 %collective-permute-done.8 = f32[3,1024]{1,0:T(4,128)S(1)} collective-permute-done((f32[3,1024]{1,0:T(4,128)S(1)}, f32[3,1024]{1,0:T(4,128)S(1)}, u32[]{:S(2)}, u32[]{:S(2)}) %collective-permute-start.8) | collective-permute-done | bytes 12320 | tf_op jit(solution)/shard_map/ppermute | solution.py:396
  80.8 0.6 add_add_fusion
  (2 shorter events, 0.0 us)
Async XLA Ops:
  1.3 0.7 copy-start
  1.3 0.7 copy-start.1
  6.6 3.9 %collective-permute-start.2 = (f32[1,4096]{1,0:T(1,128)S(1)}, f32[1,4096]{1,0:T(1,128)S(1)}, u32[]{:S(2)}, u32[]{:S(2)}) collective-permute-start(f32[1,4096]{1,0:T(1,128)S(1)} %get-tuple-element.16.refs_0_), channel_id=1, source_target_pairs={{0,3},{1,2},{2,1},{3,0},{4,7},{5,6},{6,5},{7,4},{8,11},{9,10},{10,... | collective-permute-start | bytes 49160 | tf_op jit(solution)/shard_map/ppermute | solution.py:396
  9.1 3.7 %collective-permute-start.1 = (f32[1,4096]{1,0:T(1,128)S(1)}, f32[1,4096]{1,0:T(1,128)S(1)}, u32[]{:S(2)}, u32[]{:S(2)}) collective-permute-start(f32[1,4096]{1,0:T(1,128)S(1)} %get-tuple-element.16.refs_0_), channel_id=1, source_target_pairs={{0,2},{1,3},{2,0},{3,1},{4,6},{5,7},{6,4},{7,5},{8,10},{9,11},{10,... | collective-permute-start | bytes 49160 | tf_op jit(solution)/shard_map/ppermute | solution.py:396
  10.3 2.5 %collective-permute-start = (f32[1,4096]{1,0:T(1,128)S(1)}, f32[1,4096]{1,0:T(1,128)S(1)}, u32[]{:S(2)}, u32[]{:S(2)}) collective-permute-start(f32[1,4096]{1,0:T(1,128)S(1)} %get-tuple-element.16.refs_0_), channel_id=1, source_target_pairs={{0,1},{1,0},{2,3},{3,2},{4,5},{5,4},{6,7},{7,6},{8,9},{9,8},{10,11... | collective-permute-start | bytes 49160 | tf_op jit(solution)/shard_map/ppermute | solution.py:396
  32.5 3.2 %collective-permute-start.5 = (f32[1,4096]{1,0:T(1,128)S(1)}, f32[1,4096]{1,0:T(1,128)S(1)}, u32[]{:S(2)}, u32[]{:S(2)}) collective-permute-start(f32[1,4096]{1,0:T(1,128)S(1)} %shard_map.113.refs_0_), channel_id=1, source_target_pairs={{0,3},{1,2},{2,1},{3,0},{4,7},{5,6},{6,5},{7,4},{8,11},{9,10},{10,... | collective-permute-start | bytes 49160 | tf_op jit(solution)/shard_map/ppermute | solution.py:396
  32.6 3.8 %collective-permute-start.4 = (f32[1,4096]{1,0:T(1,128)S(1)}, f32[1,4096]{1,0:T(1,128)S(1)}, u32[]{:S(2)}, u32[]{:S(2)}) collective-permute-start(f32[1,4096]{1,0:T(1,128)S(1)} %shard_map.113.refs_0_), channel_id=1, source_target_pairs={{0,2},{1,3},{2,0},{3,1},{4,6},{5,7},{6,4},{7,5},{8,10},{9,11},{10,... | collective-permute-start | bytes 49160 | tf_op jit(solution)/shard_map/ppermute | solution.py:396
  34.5 1.9 %collective-permute-start.3 = (f32[1,4096]{1,0:T(1,128)S(1)}, f32[1,4096]{1,0:T(1,128)S(1)}, u32[]{:S(2)}, u32[]{:S(2)}) collective-permute-start(f32[1,4096]{1,0:T(1,128)S(1)} %shard_map.113.refs_0_), channel_id=1, source_target_pairs={{0,1},{1,0},{2,3},{3,2},{4,5},{5,4},{6,7},{7,6},{8,9},{9,8},{10,11... | collective-permute-start | bytes 49160 | tf_op jit(solution)/shard_map/ppermute | solution.py:396
  74.2 3.6 %collective-permute-start.6 = (f32[3,1024]{1,0:T(4,128)S(1)}, f32[3,1024]{1,0:T(4,128)S(1)}, u32[]{:S(2)}, u32[]{:S(2)}) collective-permute-start(f32[3,1024]{1,0:T(4,128)S(1)} %get-tuple-element.24), channel_id=1, source_target_pairs={{0,1},{1,0},{2,3},{3,2},{4,5},{5,4},{6,7},{7,6},{8,9},{9,8},{10,11... | collective-permute-start | bytes 36872 | tf_op jit(solution)/shard_map/ppermute | solution.py:396
  74.3 5.1 %collective-permute-start.7 = (f32[3,1024]{1,0:T(4,128)S(1)}, f32[3,1024]{1,0:T(4,128)S(1)}, u32[]{:S(2)}, u32[]{:S(2)}) collective-permute-start(f32[3,1024]{1,0:T(4,128)S(1)} %get-tuple-element.25), channel_id=1, source_target_pairs={{0,2},{1,3},{2,0},{3,1},{4,6},{5,7},{6,4},{7,5},{8,10},{9,11},{10,... | collective-permute-start | bytes 36872 | tf_op jit(solution)/shard_map/ppermute | solution.py:396
  77.7 3.2 %collective-permute-start.8 = (f32[3,1024]{1,0:T(4,128)S(1)}, f32[3,1024]{1,0:T(4,128)S(1)}, u32[]{:S(2)}, u32[]{:S(2)}) collective-permute-start(f32[3,1024]{1,0:T(4,128)S(1)} %get-tuple-element.26), channel_id=1, source_target_pairs={{0,3},{1,2},{2,1},{3,0},{4,7},{5,6},{6,5},{7,4},{8,11},{9,10},{10,... | collective-permute-start | bytes 36872 | tf_op jit(solution)/shard_map/ppermute | solution.py:396

commit v4 on v3

v4 whole, which is shorter than its diff:
```python
import functools
import math

import jax
import jax.numpy as jnp
from jax import lax
from jax.experimental import pallas as pl
from jax.experimental.pallas import tpu as pltpu
from jax.sharding import PartitionSpec as P

CLUSTER = 512
EPSILON = 0.02
KAPPA = math.log2(math.e) / EPSILON
LOG2E = math.log2(math.e)
DEPTH = 32
FLOOR = -1e30
EXTRAS = 4
F32 = jnp.float32
BF16 = jnp.bfloat16


def log2(value):
    return jnp.log(value) * LOG2E


def split(value):
    high = value.astype(BF16).astype(F32)
    rest = value - high
    middle = rest.astype(BF16).astype(F32)
    return (high, middle, rest - middle)


def half_square(points):
    return 0.5 * (points[0:1] * points[0:1] + points[1:2] * points[1:2] + points[2:3] * points[2:3])


SOURCE_ORDER = (0, 1, 2, 0, 0, 1)
TARGET_ORDER = (0, 0, 0, 1, 2, 1)
ONE = 15


def place(scratch, parts, order):
    scratch[...] = jnp.zeros_like(scratch)
    for at, which in enumerate(order[:5]):
        scratch[3 * at : 3 * at + 3, :] = parts[which]
    scratch[ONE : ONE + 1, :] = jnp.ones_like(parts[0][0:1])
    scratch[16:19, :] = parts[order[5]]
    scratch[19:22, :] = jnp.ones_like(parts[0])


def with_rows(out, static, first, second=()):
    out[0:16, :] = static[0:16, :]
    low = static[16:32, :].astype(F32)
    row = lax.broadcasted_iota(jnp.int32, low.shape, 0)
    for at, part in enumerate(tuple(first) + tuple(second)):
        low = jnp.where(row == 3 + at, part, low)
    out[16:32, :] = low.astype(BF16)


def pieces(potential):
    return split(potential - 1.0)


ONES = (1.0, 1.0, 1.0)


def scores(left, right):
    return lax.dot_general(left, right, (((0,), (0,)), ((), ())), preferred_element_type=F32)


def start_of(index):
    return pl.multiple_of(index * CLUSTER, CLUSTER)


def grouped(value):
    return value.reshape(value.shape[0] // 8, 8, value.shape[1])


def each_tile(tiles, left, right, visit, first, more, unroll=8, ahead=1, chunk=128):
    once = right.shape[1] // CLUSTER

    def group_states(group, fresh):
        steps = []
        for which, slot in enumerate(group):
            r, k = tiles.starts(slot)
            for at in range(CLUSTER // chunk):
                steps.append((which, pl.ds(k, CLUSTER), pl.ds(pl.multiple_of(r + at * chunk, chunk), chunk)))
        states = [None] * len(group)
        scores = [None] * len(steps)

        def start(n):
            if n < len(steps):
                which, here, rows = steps[n]
                scores[n] = grouped(jnp.dot(left[rows, :], right[:, here], preferred_element_type=F32))

        for n in range(ahead):
            start(n)
        for n, (which, here, rows) in enumerate(steps):
            start(n + ahead)
            states[which] = visit(scores[n], states[which], rows, fresh)
        return [(steps[which * (CLUSTER // chunk)][1], state) for which, state in enumerate(states)]

    def several(at, carry):
        for here, state in group_states([at * unroll + k for k in range(unroll)], True):
            first(here, state)
        return carry

    def others(at, carry):
        slots = [once + at * EXTRAS + k for k in range(EXTRAS)]
        states = group_states([jnp.minimum(slot, tiles.slots - 1) for slot in slots], False)
        for slot, (here, state) in zip(slots, states):
            more(here, state, slot < tiles.count())
        return carry

    lax.fori_loop(0, once // unroll, several, 0)
    lax.fori_loop(0, lax.div(tiles.count() - once + EXTRAS - 1, EXTRAS), others, 0)


def lse_tiles(tiles, left, right, top, total, **how):
    def visit(s, state, rows, fresh):
        largest = jnp.max(s, axis=0)
        if state is None:
            return largest, jnp.sum(jnp.exp2(s - largest[None]), axis=0)
        new = jnp.maximum(state[0], largest)
        return new, state[1] * jnp.exp2(state[0] - new) + jnp.sum(jnp.exp2(s - new[None]), axis=0)

    def first(here, state):
        top[:, here], total[:, here] = state

    def more(here, state, live):
        old, m = top[:, here], jnp.where(live, state[0], FLOOR)
        new = jnp.maximum(old, m)
        top[:, here] = new
        total[:, here] = total[:, here] * jnp.exp2(old - new) + state[1] * jnp.exp2(m - new)

    each_tile(tiles, left, right, visit, first, more, **how)
    m = top[...]
    largest = jnp.max(m, axis=0, keepdims=True)
    return largest + log2(jnp.sum(total[...] * jnp.exp2(m - largest), axis=0, keepdims=True))


def weighed(p, columns, points, start, rows, fresh):
    block = points[0:8, rows].T if fresh else None
    for c in range(3):
        lanes = slice(128 * c, 128 * (c + 1))
        if fresh:
            col = jnp.broadcast_to(block[:, start + c : start + c + 1], (block.shape[0], 128))
            columns[rows, lanes] = col
        else:
            col = columns[rows, lanes]
        yield jnp.sum(p * jnp.concatenate([col] * (CLUSTER // 128), axis=1).reshape(p.shape), axis=0)


def mean_tiles(tiles, left, right, columns, points, start, top, sums, **how):
    def visit(s, state, rows, fresh):
        largest = jnp.max(s, axis=0)
        new = largest if state is None else jnp.maximum(state[0], largest)
        p = jnp.exp2(s - new[None])
        totals = [jnp.sum(p, axis=0)] + list(weighed(p, columns, points, start, rows, fresh))
        if state is not None:
            scale = jnp.exp2(state[0] - new)
            totals = [old * scale + total for old, total in zip(state[1:], totals)]
        return [new] + totals

    def first(here, state):
        top[:, here] = state[0]
        for c, total in enumerate(state[1:]):
            sums[c, :, here] = total

    def more(here, state, live):
        old, m = top[:, here], jnp.where(live, state[0], FLOOR)
        new = jnp.maximum(old, m)
        before, now = jnp.exp2(old - new), jnp.exp2(m - new)
        top[:, here] = new
        for c, total in enumerate(state[1:]):
            sums[c, :, here] = sums[c, :, here] * before + total * now

    each_tile(tiles, left, right, visit, first, more, **how)
    m = top[...]
    largest = jnp.max(m, axis=0, keepdims=True)
    scale = jnp.exp2(m - largest)
    mass, *others = [jnp.sum(sums[c] * scale, axis=0, keepdims=True) for c in range(4)]
    return [largest + log2(mass)] + [other / mass for other in others]


def plan_tiles(tiles, left, right, columns, points, start, sums, **how):
    def visit(s, state, rows, fresh):
        p = jnp.exp2(s)
        totals = [jnp.sum(p, axis=0)] + list(weighed(p, columns, points, start, rows, fresh))
        return totals if state is None else [old + new for old, new in zip(state, totals)]

    def first(here, state):
        for c, total in enumerate(state):
            sums[c, :, here] = total

    def more(here, state, live):
        for c, total in enumerate(state):
            sums[c, :, here] += jnp.where(live, total, 0.0)

    each_tile(tiles, left, right, visit, first, more, **how)
    return [jnp.sum(sums[c], axis=0, keepdims=True) for c in range(4)]


def combine(parts):
    largest = functools.reduce(jnp.maximum, parts)
    terms = [jnp.exp2(part - largest) for part in parts]
    whole = functools.reduce(jnp.add, terms)
    return largest + log2(whole), [term / whole for term in terms]


def rows_of(refs):
    return [refs[at] for at in range(refs.shape[0])]


class Tiles:
    def __init__(self, ref, points, kept_source):
        self.ref, self.slots, self.kept_source = ref, ref.shape[-1], kept_source
        self.sources, self.targets = points

    def count(self):
        return lax.div(self.ref[0, 0, 0], self.sources * self.targets)

    def starts(self, slot):
        packed = self.ref[0, 0, slot]
        source = start_of(lax.rem(packed, self.sources))
        target = start_of(lax.rem(lax.div(packed, self.sources), self.targets))
        return (target, source) if self.kept_source else (source, target)


def fetch(lists_in, lists, sem):
    copy = pltpu.make_async_copy(lists_in, lists, sem)
    copy.start()
    return copy


def turn(out, operand):
    out[...] = operand[...].T


def sides(xc, yc):
    return xc.shape[1] // CLUSTER, yc.shape[1] // CLUSTER


def first_row_kernel(points, lists_in, xc_out, yc_out, part_out, lists, sem, stack, red, turned, top, total):
    copy = fetch(lists_in, lists, sem)
    xs, ys = points[0:3, :], points[3:6, :]
    place(stack, split(ys * KAPPA), TARGET_ORDER)
    yc_out[...] = stack[...].astype(BF16)
    potential = log2(points[7:8, :]) + KAPPA * (points[8:9, :] - half_square(ys))
    with_rows(red, yc_out, pieces(potential))
    turn(turned, red)
    place(stack, split(xs), SOURCE_ORDER)
    xc_out[...] = stack[...].astype(BF16)
    copy.wait()
    part_out[...] = lse_tiles(Tiles(lists, sides(xc_out, yc_out), True), turned, xc_out, top, total)


def col_kernel(parts, points, xc, yc, lists_in, part_out, lists, sem, red, turned, top, total):
    copy = fetch(lists_in, lists, sem)
    potential = log2(points[6:7, :]) - combine([ref[...] for ref in parts])[0]
    with_rows(red, xc, pieces(potential))
    turn(turned, red)
    copy.wait()
    part_out[...] = lse_tiles(Tiles(lists, sides(xc, yc), False), turned, yc, top, total)


def row_kernel(parts, points, xc, yc, lists_in, part_out, lists, sem, red, turned, top, total):
    copy = fetch(lists_in, lists, sem)
    potential = log2(points[7:8, :]) - combine([ref[...] for ref in parts])[0]
    with_rows(red, yc, pieces(potential))
    turn(turned, red)
    copy.wait()
    part_out[...] = lse_tiles(Tiles(lists, sides(xc, yc), True), turned, xc, top, total)


def last_col_kernel(
    parts, points, xc, yc, lists_in, f_out, u_out, part_out, means_out, lists, sem, red, turned, top, sums, columns, f, sem_out
):
    copy = fetch(lists_in, lists, sem)
    u = -combine([ref[...] for ref in parts])[0]
    u_out[...] = u
    f[...] = u * (1.0 / KAPPA) + half_square(points[0:3, :])
    back = fetch(f, f_out, sem_out)
    with_rows(red, xc, pieces(log2(points[6:7, :]) + u))
    turn(turned, red)
    copy.wait()
    tiles = Tiles(lists, sides(xc, yc), False)
    part_out[...], *means = mean_tiles(tiles, turned, yc, columns, points, 0, top, sums, unroll=4)
    for c, row in enumerate(means):
        means_out[c : c + 1, :] = row
    back.wait()


def merge_kernel(parts, out):
    out[...] = combine([ref[...] for ref in parts])[0]


def merge_and_pass_kernel(parts, means, out, means_out):
    merge_kernel(parts, out)
    means_out[...] = means[...]


def mean_of(parts, means):
    shares = combine([ref[...] for ref in parts])[1]
    return functools.reduce(jnp.add, [share * ref[...] for share, ref in zip(shares, means)])


def merge_means_kernel(parts, means, after, out):
    out[...] = mean_of(parts, means)


def closing_kernel(parts, means, moved, points, target_out, source_out):
    target_out[...] = points[7:8, :] * (points[3:6, :] - mean_of(parts, means))
    source_out[...] = functools.reduce(jnp.add, [ref[...] for ref in moved])


def gradient_kernel(
    parts, u, points, xc, yc, lists_in, g_out, *rest, shares
):
    source_out, (lists, sem, red, turned, kept, sums, columns, g, whole, sem_out) = rest[:shares], rest[shares:]
    copy = fetch(lists_in, lists, sem)
    lse = combine([ref[...] for ref in parts])[0]
    xs, ys = points[0:3, :], points[3:6, :]
    g[...] = half_square(ys) - lse * (1.0 / KAPPA)
    back = fetch(g, g_out, sem_out)
    with_rows(red, yc, pieces(log2(points[7:8, :]) - lse), ONES)
    turn(turned, red)
    with_rows(kept, xc, ONES, split(log2(points[6:7, :]) + u[...]))
    copy.wait()
    tiles = Tiles(lists, sides(xc, yc), True)
    mass, *moved = plan_tiles(tiles, turned, kept, columns, points, 3, sums, unroll=4)
    for c in range(3):
        whole[c : c + 1, :] = xs[c : c + 1, :] * mass - moved[c]
    place_tgt = lax.axis_index("tgt")
    for k, out in enumerate(source_out):
        width = out.shape[1]
        at = pl.multiple_of(peer(place_tgt, k, shares) * width, width)
        out[...] = whole[:, pl.ds(at, width)]
    back.wait()


VMEM = pl.BlockSpec(memory_space=pltpu.VMEM)
HBM = pl.BlockSpec(memory_space=pltpu.HBM)


def call(kernel, ins, lists, outs, scratch, far=(), flops=0):
    return pl.pallas_call(
        kernel,
        out_shape=outs,
        in_specs=[VMEM] * len(ins) + [HBM] * len(lists),
        out_specs=[HBM if at in far else VMEM for at in range(len(outs))],
        scratch_shapes=scratch,
        compiler_params=pltpu.CompilerParams(vmem_limit_bytes=48 * 1024 * 1024),
        cost_estimate=pl.CostEstimate(flops=flops, bytes_accessed=0, transcendentals=0) if flops else None,
    )(*ins, *lists)


def peer(i, k, n):
    return i ^ k if n & (n - 1) == 0 else (i + k) % n


def exchange(values, axis):
    n = lax.axis_size(axis)
    return values[:1] + [
        lax.ppermute(values[k], axis, [(i, peer(i, k, n)) for i in range(n)]) for k in range(1, n)
    ]


def exchange_step(value, axis, step):
    n = lax.axis_size(axis)
    others = [k * step for k in range(1, min(4, n // step))]
    return [value] + [lax.ppermute(value, axis, [(i, i ^ k) for i in range(n)]) for k in others]


def bunch(kernel, *sizes):
    def run(*refs):
        lists = []
        for size in sizes:
            lists.append(refs[:size])
            refs = refs[size:]
        kernel(*lists, *refs)

    return run


def like(*values):
    return [jax.ShapeDtypeStruct(value.shape, value.dtype) for value in values]


def sum_up(axis, part):
    n, step = lax.axis_size(axis), 1
    while True:
        parts = exchange_step(part, axis, step)
        step *= 4
        if step >= n:
            return parts
        (part,) = call(bunch(merge_kernel, len(parts)), parts, (), like(part), [])


def body(source_points, target_points, source_weight, target_weight, target_start, tile_source, tile_target, tile_count):
    ns, nt = source_points.shape[1], target_points.shape[1]
    n_tgt = lax.axis_size("tgt")
    points = jnp.concatenate(
        [source_points, target_points] + [a.reshape(1, -1) for a in (source_weight, target_weight, target_start)]
    )
    lists = ((tile_count[:, :, None] * (nt // CLUSTER) + tile_target) * (ns // CLUSTER) + tile_source,)

    def rows(n, *k):
        return jax.ShapeDtypeStruct((*k, n), F32)

    def split_rows(n):
        return jax.ShapeDtypeStruct((DEPTH, n), BF16)

    def work(red):
        return [
            pltpu.SMEM(lists[0].shape, jnp.int32),
            pltpu.SemaphoreType.DMA,
            pltpu.VMEM((DEPTH, red), BF16),
            pltpu.VMEM((red, DEPTH), BF16),
        ]

    def state(kept):
        return [pltpu.VMEM((8, kept), F32), pltpu.VMEM((8, kept), F32)]

    first = work(nt)
    xc, yc, part = call(
        first_row_kernel,
        (points,),
        lists,
        [split_rows(ns), split_rows(nt), rows(ns, 1)],
        first[:2] + [pltpu.VMEM((DEPTH, ns), F32)] + first[2:] + state(ns),
    )
    known = (points, xc, yc)
    parts = exchange([part] * n_tgt, "tgt")
    (part,) = call(
        bunch(col_kernel, n_tgt),
        (*parts, *known),
        lists,
        [rows(nt, 1)],
        work(ns) + state(nt),
    )
    parts = sum_up("src", part)
    (part,) = call(
        bunch(row_kernel, len(parts)),
        (*parts, *known),
        lists,
        [rows(ns, 1)],
        work(nt) + state(ns),
    )
    parts = exchange([part] * n_tgt, "tgt")
    f, u, part, means = call(
        bunch(last_col_kernel, n_tgt),
        (*parts, *known),
        lists,
        [rows(ns, 1), rows(ns, 1), rows(nt, 1), rows(nt, 3)],
        work(ns)
        + [
            pltpu.VMEM((8, nt), F32),
            pltpu.VMEM((4, 8, nt), F32),
            pltpu.VMEM((ns, 384), F32),
            pltpu.VMEM((1, ns), F32),
            pltpu.SemaphoreType.DMA,
        ],
        far=(0,),
    )
    n_src, step, late = lax.axis_size("src"), 1, []
    while True:
        parts = exchange_step(part, "src", step)
        if 4 * step >= n_src:
            break
        part, means = call(
            bunch(merge_and_pass_kernel, len(parts)), (*parts, means), (), like(part, means), []
        )
        late.append((step, parts))
        step *= 4
    n = len(parts)
    g, *moved = call(
        bunch(functools.partial(gradient_kernel, shares=n_tgt), n),
        (*parts, u, *known),
        lists,
        [rows(nt, 1)] + [rows(ns // n_tgt, 3)] * n_tgt,
        work(nt)
        + [
            pltpu.VMEM((DEPTH, ns), BF16),
            pltpu.VMEM((4, 8, ns), F32),
            pltpu.VMEM((nt, 384), F32),
            pltpu.VMEM((1, nt), F32),
            pltpu.VMEM((3, ns), F32),
            pltpu.SemaphoreType.DMA,
        ],
        far=(0,),
        flops=40 * ns * CLUSTER,
    )
    for at, some in late:
        others = exchange_step(means, "src", at)
        (means,) = call(
            bunch(merge_means_kernel, len(some), len(some)), (*some, *others, moved[0]), (), like(means), []
        )
    means = exchange_step(means, "src", step)
    moved = exchange(moved, "tgt")
    target_grad, own_grad = call(
        bunch(closing_kernel, n, n, n_tgt),
        (*parts, *means, *moved, points),
        (),
        [rows(nt, 3), rows(ns // n_tgt, 3)],
        [],
    )
    return (f.reshape(-1), g.reshape(-1), own_grad, target_grad)


def solution(mesh):
    return jax.shard_map(
        body,
        mesh=mesh,
        in_specs=(
            P(None, "src"),
            P(None, "tgt"),
            P("src"),
            P("tgt"),
            P("tgt"),
            P("src", "tgt", None),
            P("src", "tgt", None),
            P("src", "tgt"),
        ),
        out_specs=(P("src"), P("tgt"), P(None, ("src", "tgt")), P(None, "tgt")),
        check_vma=False,
    )
```

time: 81.3 us -> 71.1 us (0.87); the launches traced: 81.4 us -> 70.1 us
  blocking collectives: 33.3 us -> 0 us
  starting transfers between devices: 9.22 us -> 23 us
  waiting for transfers between devices: 7.46 us -> 18.2 us
  Pallas kernels: 27.1 us -> 25.1 us
    all_to_all x3 -> x0, blocking collectives: 33.3 us -> none  [body(): lax.all_to_all(part, 'src', 0, 0)]
    ppermute x0 -> x12, starting transfers between devices: none -> 16.1 us  [exchange_step(): lax.ppermute(value, axis, [(i, i ^ k) for i in range(n)])]
    ppermute x0 -> x12, waiting for transfers between devices: none -> 10.2 us  [exchange_step(): lax.ppermute(value, axis, [(i, i ^ k) for i in range(n)])]
    ppermute x9, starting transfers between devices: 9.22 us -> 6.91 us  [exchange(): lax.ppermute(values[k], axis, [(i, peer(i, k, n)) for i in range(n)])]
    pallas_call x6 -> x9, Pallas kernels: 27.1 us -> 25.1 us  [call(): pl.pallas_call(kernel, out_shape=outs, in_specs=[VMEM] * len(ins) + [HBM]...]
  transfers between devices with their start and end apart: 9 -> 21, of which waited for: 6 -> 14; matrix products, arithmetic and copies ran while one was open for 0% -> 0% of each run, Pallas kernels for 0% -> 9%
where the time goes in v4:
time: 71.1 us; the launch traced here: 70.1 us
  Pallas kernels  25.1 us (35%)
  starting transfers between devices  23 us (32%)
  waiting for transfers between devices  18.2 us (26%)
  local copies, waits for them, and re-layouts  2.37 us (3%)
  between operations  1.4 us (2%)
    pallas_call x9, Pallas kernels, call(): pl.pallas_call(kernel, out_shape=outs, in_specs=[VMEM] * len(ins) + [HBM]...  25.1 us
    ppermute x12, starting transfers between devices, exchange_step(): lax.ppermute(value, axis, [(i, i ^ k) for i in range(n)])  16.1 us
    ppermute x12, waiting for transfers between devices, exchange_step(): lax.ppermute(value, axis, [(i, i ^ k) for i in range(n)])  10.2 us
    ppermute x9, waiting for transfers between devices, exchange(): lax.ppermute(values[k], axis, [(i, peer(i, k, n)) for i in range(n)])  7.95 us
    ppermute x9, starting transfers between devices, exchange(): lax.ppermute(values[k], axis, [(i, peer(i, k, n)) for i in range(n)])  6.91 us
    concatenate x1, local copies, waits for them, and re-layouts, body(): jnp.concatenate([source_points, target_points] + [a.reshape(1, -1) for a...  1.71 us
  transfers between devices with their start and end apart: 21, of which 14 were waited for; matrix products, arithmetic and copies ran while one was open for 0% of the time, Pallas kernels for 9%

profile of v4, /device:TPU:0, one launch (start us, length us, event | category | flops | bytes accessed | tf_op | source)
XLA Modules:
  0.0 70.1 jit_solution(16402292419250728700)
XLA Ops:
  1.3 0.0 copy-start
  1.3 0.0 copy-start.1
  1.3 0.6 copy-done
  1.9 0.0 copy-done.1
  2.0 1.7 %concatenate.3.points.refs_4_.refs_2_.refs_3_.refs_8_ = f32[9,4096]{1,0:T(8,128)S(1)} concatenate(f32[3,4096]{1,0:T(4,128)} %param.8, f32[3,4096]{1,0:T(4,128)} %param.9, f32[1,4096]{1,0:T(1,128)} %bitcast.6, f32[1,4096]{1,0:T(1,128)} %bitcast.7, f32[1,4096]{1,0:T(1,128)} %bitcast.8), dimensions={0} | concatenate | bytes 294912 | tf_op jit(solution)/shard_map/concatenate | solution.py:403
  3.7 3.6 %shard_map.111 = (bf16[32,4096]{1,0:T(8,128)(2,1)S(1)}, bf16[32,4096]{1,0:T(8,128)(2,1)S(1)}, f32[1,4096]{1,0:T(1,128)S(1)}) custom-call(f32[9,4096]{1,0:T(8,128)S(1)} %concatenate.3.points.refs_4_.refs_2_.refs_3_.refs_8_, s32[1,1,12]{2,1,0:T(1,128)S(1)} %multiply_add_fusion.lists_in.refs_7_.refs_5_.refs_6_), custom_call_target="tpu_custom_call" | custom-call | tf_op jit(solution)/shard_map/pallas_call | solution.py:347
  7.3 2.4 %collective-permute-start.2 = (f32[1,4096]{1,0:T(1,128)S(1)}, f32[1,4096]{1,0:T(1,128)S(1)}, u32[]{:S(2)}, u32[]{:S(2)}) collective-permute-start(f32[1,4096]{1,0:T(1,128)S(1)} %get-tuple-element.20.refs_0_), channel_id=1, source_target_pairs={{0,3},{1,2},{2,1},{3,0},{4,7},{5,6},{6,5},{7,4},{8,11},{9,10},{10,... | collective-permute-start | bytes 49160 | tf_op jit(solution)/shard_map/ppermute | solution.py:365
  9.7 0.7 collective-permute-start.1
  10.4 0.0 collective-permute-start
  10.4 0.8 %collective-permute-done.2.refs_3_ = f32[1,4096]{1,0:T(1,128)S(1)} collective-permute-done((f32[1,4096]{1,0:T(1,128)S(1)}, f32[1,4096]{1,0:T(1,128)S(1)}, u32[]{:S(2)}, u32[]{:S(2)}) %collective-permute-start.2) | collective-permute-done | bytes 16416 | tf_op jit(solution)/shard_map/ppermute | solution.py:365
  11.2 2.3 %collective-permute-done.1.refs_2_ = f32[1,4096]{1,0:T(1,128)S(1)} collective-permute-done((f32[1,4096]{1,0:T(1,128)S(1)}, f32[1,4096]{1,0:T(1,128)S(1)}, u32[]{:S(2)}, u32[]{:S(2)}) %collective-permute-start.1) | collective-permute-done | bytes 16416 | tf_op jit(solution)/shard_map/ppermute | solution.py:365
  13.5 0.0 collective-permute-done.refs_1_
  13.5 3.2 %shard_map.112.refs_0_ = f32[1,4096]{1,0:T(1,128)S(1)} custom-call(f32[1,4096]{1,0:T(1,128)S(1)} %get-tuple-element.20.refs_0_, f32[1,4096]{1,0:T(1,128)S(1)} %collective-permute-done.refs_1_, f32[1,4096]{1,0:T(1,128)S(1)} %collective-permute-done.1.refs_2_, f32[1,4096]{1,0:T(1,128)S(1)} %collective-permute-done.2.refs_3_, ...), custom_call_target="tpu_custom_call" | custom-call | tf_op jit(solution)/shard_map/pallas_call | solution.py:347
  16.7 1.7 %collective-permute-start.5 = (f32[1,4096]{1,0:T(1,128)S(1)}, f32[1,4096]{1,0:T(1,128)S(1)}, u32[]{:S(2)}, u32[]{:S(2)}) collective-permute-start(f32[1,4096]{1,0:T(1,128)S(1)} %shard_map.112.refs_0_), channel_id=1, source_target_pairs={{0,12},{4,8},{8,4},{12,0},{16,28},{20,24},{24,20},{28,16},{1,13},{... | collective-permute-start | bytes 49160 | tf_op jit(solution)/shard_map/ppermute | solution.py:372
  18.3 1.4 %collective-permute-start.4 = (f32[1,4096]{1,0:T(1,128)S(1)}, f32[1,4096]{1,0:T(1,128)S(1)}, u32[]{:S(2)}, u32[]{:S(2)}) collective-permute-start(f32[1,4096]{1,0:T(1,128)S(1)} %shard_map.112.refs_0_), channel_id=1, source_target_pairs={{0,8},{4,12},{8,0},{12,4},{16,24},{20,28},{24,16},{28,20},{1,9},{5... | collective-permute-start | bytes 49160 | tf_op jit(solution)/shard_map/ppermute | solution.py:372
  19.7 0.5 collective-permute-start.3
  20.2 1.1 %collective-permute-done.5.refs_3_ = f32[1,4096]{1,0:T(1,128)S(1)} collective-permute-done((f32[1,4096]{1,0:T(1,128)S(1)}, f32[1,4096]{1,0:T(1,128)S(1)}, u32[]{:S(2)}, u32[]{:S(2)}) %collective-permute-start.5) | collective-permute-done | bytes 16416 | tf_op jit(solution)/shard_map/ppermute | solution.py:372
  21.4 0.7 collective-permute-done.4.refs_2_
  22.1 1.4 %collective-permute-done.3.refs_1_ = f32[1,4096]{1,0:T(1,128)S(1)} collective-permute-done((f32[1,4096]{1,0:T(1,128)S(1)}, f32[1,4096]{1,0:T(1,128)S(1)}, u32[]{:S(2)}, u32[]{:S(2)}) %collective-permute-start.3) | collective-permute-done | bytes 16416 | tf_op jit(solution)/shard_map/ppermute | solution.py:372
  23.5 2.6 %collective-permute-start.6 = (f32[1,4096]{1,0:T(1,128)S(1)}, f32[1,4096]{1,0:T(1,128)S(1)}, u32[]{:S(2)}, u32[]{:S(2)}) collective-permute-start(f32[1,4096]{1,0:T(1,128)S(1)} %shard_map.113.refs_0_), channel_id=1, source_target_pairs={{0,16},{4,20},{8,24},{12,28},{16,0},{20,4},{24,8},{28,12},{1,17},{... | collective-permute-start | bytes 49160 | tf_op jit(solution)/shard_map/ppermute | solution.py:372
  26.2 2.2 %collective-permute-done.6.refs_1_ = f32[1,4096]{1,0:T(1,128)S(1)} collective-permute-done((f32[1,4096]{1,0:T(1,128)S(1)}, f32[1,4096]{1,0:T(1,128)S(1)}, u32[]{:S(2)}, u32[]{:S(2)}) %collective-permute-start.6) | collective-permute-done | bytes 16416 | tf_op jit(solution)/shard_map/ppermute | solution.py:372
  28.4 3.4 %shard_map.114.refs_0_ = f32[1,4096]{1,0:T(1,128)S(1)} custom-call(f32[1,4096]{1,0:T(1,128)S(1)} %shard_map.113.refs_0_, f32[1,4096]{1,0:T(1,128)S(1)} %collective-permute-done.6.refs_1_, f32[9,4096]{1,0:T(8,128)S(1)} %concatenate.3.points.refs_4_.refs_2_.refs_3_.refs_8_, bf16[32,4096]{1,0:T(8,128)(2,1)S(1)} %get-tuple-element.21.refs_5_.refs_3_.refs_4_, ...), custom_call_target="tpu_custom_call" | custom-call | tf_op jit(solution)/shard_map/pallas_call | solution.py:347
  31.8 0.1 collective-permute-start.9
  31.9 0.2 collective-permute-start.8
  32.1 1.7 %collective-permute-start.7 = (f32[1,4096]{1,0:T(1,128)S(1)}, f32[1,4096]{1,0:T(1,128)S(1)}, u32[]{:S(2)}, u32[]{:S(2)}) collective-permute-start(f32[1,4096]{1,0:T(1,128)S(1)} %shard_map.114.refs_0_), channel_id=1, source_target_pairs={{0,1},{1,0},{2,3},{3,2},{4,5},{5,4},{6,7},{7,6},{8,9},{9,8},{10,11... | collective-permute-start | bytes 49160 | tf_op jit(solution)/shard_map/ppermute | solution.py:365
  33.7 1.3 %collective-permute-done.9.refs_3_ = f32[1,4096]{1,0:T(1,128)S(1)} collective-permute-done((f32[1,4096]{1,0:T(1,128)S(1)}, f32[1,4096]{1,0:T(1,128)S(1)}, u32[]{:S(2)}, u32[]{:S(2)}) %collective-permute-start.9) | collective-permute-done | bytes 16416 | tf_op jit(solution)/shard_map/ppermute | solution.py:365
  35.0 0.7 collective-permute-done.8.refs_2_
  35.7 0.0 collective-permute-done.7.refs_1_
  35.7 7.7 %shard_map.115 = (f32[1,4096]{1,0:T(1,128)}, f32[1,4096]{1,0:T(1,128)S(1)}, f32[1,4096]{1,0:T(1,128)S(1)}, f32[3,4096]{1,0:T(4,128)S(1)}) custom-call(f32[1,4096]{1,0:T(1,128)S(1)} %shard_map.114.refs_0_, f32[1,4096]{1,0:T(1,128)S(1)} %collective-permute-done.7.refs_1_, f32[1,4096]{1,0:T(1,128)S(1)} %collective-permute-done.8.refs_2_, ...), custom_call_target="tpu_custom_call" | custom-call | tf_op jit(solution)/shard_map/pallas_call | solution.py:347
  43.4 0.1 collective-permute-start.12
  43.5 1.8 %collective-permute-start.11 = (f32[1,4096]{1,0:T(1,128)S(1)}, f32[1,4096]{1,0:T(1,128)S(1)}, u32[]{:S(2)}, u32[]{:S(2)}) collective-permute-start(f32[1,4096]{1,0:T(1,128)S(1)} %get-tuple-element.24.refs_0_), channel_id=1, source_target_pairs={{0,8},{4,12},{8,0},{12,4},{16,24},{20,28},{24,16},{28,20},{1,9},{5... | collective-permute-start | bytes 49160 | tf_op jit(solution)/shard_map/ppermute | solution.py:372
  45.2 1.7 %collective-permute-start.10 = (f32[1,4096]{1,0:T(1,128)S(1)}, f32[1,4096]{1,0:T(1,128)S(1)}, u32[]{:S(2)}, u32[]{:S(2)}) collective-permute-start(f32[1,4096]{1,0:T(1,128)S(1)} %get-tuple-element.24.refs_0_), channel_id=1, source_target_pairs={{0,4},{4,0},{8,12},{12,8},{16,20},{20,16},{24,28},{28,24},{1,5},{5... | collective-permute-start | bytes 49160 | tf_op jit(solution)/shard_map/ppermute | solution.py:372
  46.9 1.1 %collective-permute-done.12.refs_3_ = f32[1,4096]{1,0:T(1,128)S(1)} collective-permute-done((f32[1,4096]{1,0:T(1,128)S(1)}, f32[1,4096]{1,0:T(1,128)S(1)}, u32[]{:S(2)}, u32[]{:S(2)}) %collective-permute-start.12) | collective-permute-done | bytes 16416 | tf_op jit(solution)/shard_map/ppermute | solution.py:372
  48.1 0.0 collective-permute-done.11.refs_2_
  48.1 0.9 %collective-permute-done.10.refs_1_ = f32[1,4096]{1,0:T(1,128)S(1)} collective-permute-done((f32[1,4096]{1,0:T(1,128)S(1)}, f32[1,4096]{1,0:T(1,128)S(1)}, u32[]{:S(2)}, u32[]{:S(2)}) %collective-permute-start.10) | collective-permute-done | bytes 16416 | tf_op jit(solution)/shard_map/ppermute | solution.py:372
  49.0 1.8 %collective-permute-start.16 = (f32[3,4096]{1,0:T(4,128)S(1)}, f32[3,4096]{1,0:T(4,128)S(1)}, u32[]{:S(2)}, u32[]{:S(2)}) collective-permute-start(f32[3,4096]{1,0:T(4,128)S(1)} %get-tuple-element.29.refs_4_), channel_id=1, source_target_pairs={{0,12},{4,8},{8,4},{12,0},{16,28},{20,24},{24,20},{28,16},{1,13},{... | collective-permute-start | bytes 147464 | tf_op jit(solution)/shard_map/ppermute | solution.py:372
  50.8 1.5 %collective-permute-start.15 = (f32[3,4096]{1,0:T(4,128)S(1)}, f32[3,4096]{1,0:T(4,128)S(1)}, u32[]{:S(2)}, u32[]{:S(2)}) collective-permute-start(f32[3,4096]{1,0:T(4,128)S(1)} %get-tuple-element.29.refs_4_), channel_id=1, source_target_pairs={{0,8},{4,12},{8,0},{12,4},{16,24},{20,28},{24,16},{28,20},{1,9},{5... | collective-permute-start | bytes 147464 | tf_op jit(solution)/shard_map/ppermute | solution.py:372
  52.2 0.3 collective-permute-start.14
  52.6 2.2 %collective-permute-start.13 = (f32[1,4096]{1,0:T(1,128)S(1)}, f32[1,4096]{1,0:T(1,128)S(1)}, u32[]{:S(2)}, u32[]{:S(2)}) collective-permute-start(f32[1,4096]{1,0:T(1,128)S(1)} %get-tuple-element.26.refs_0_), channel_id=1, source_target_pairs={{0,16},{4,20},{8,24},{12,28},{16,0},{20,4},{24,8},{28,12},{1,17},{... | collective-permute-start | bytes 49160 | tf_op jit(solution)/shard_map/ppermute | solution.py:372
  54.7 2.5 %collective-permute-done.13.refs_1_ = f32[1,4096]{1,0:T(1,128)S(1)} collective-permute-done((f32[1,4096]{1,0:T(1,128)S(1)}, f32[1,4096]{1,0:T(1,128)S(1)}, u32[]{:S(2)}, u32[]{:S(2)}) %collective-permute-start.13) | collective-permute-done | bytes 16416 | tf_op jit(solution)/shard_map/ppermute | solution.py:372
  57.2 6.3 %shard_map.117 = (f32[1,4096]{1,0:T(1,128)}, f32[3,1024]{1,0:T(4,128)S(1)}, f32[3,1024]{1,0:T(4,128)S(1)}, f32[3,1024]{1,0:T(4,128)S(1)}, f32[3,1024]{1,0:T(4,128)S(1)}) custom-call(f32[1,4096]{1,0:T(1,128)S(1)} %get-tuple-element.26.refs_0_, f32[1,4096]{1,0:T(1,128)S(1)} %collective-permute-done.13.refs_1_, f32[1,4096]{1,0:T(1,128)S(1)} %get-tuple-element.27.refs_2_, ...), custom_call_target="tpu_custom_call" | custom-call | flops 83886080 | tf_op jit(solution)/shard_map/pallas_call | solution.py:347
  63.5 0.0 collective-permute-done.16.refs_7_
  63.5 0.0 collective-permute-done.15.refs_6_
  63.5 0.0 collective-permute-done.14.refs_5_
  63.5 0.1 shard_map.118.refs_2_
  63.6 0.6 collective-permute-start.17
  64.3 0.0 collective-permute-start.18
  64.3 1.6 %collective-permute-start.19 = (f32[3,1024]{1,0:T(4,128)S(1)}, f32[3,1024]{1,0:T(4,128)S(1)}, u32[]{:S(2)}, u32[]{:S(2)}) collective-permute-start(f32[3,1024]{1,0:T(4,128)S(1)} %get-tuple-element.32), channel_id=1, source_target_pairs={{0,2},{1,3},{2,0},{3,1},{4,6},{5,7},{6,4},{7,5},{8,10},{9,11},{10,... | collective-permute-start | bytes 36872 | tf_op jit(solution)/shard_map/ppermute | solution.py:365
  65.9 0.2 collective-permute-start.20
  66.1 0.0 collective-permute-done.18.refs_5_
  66.1 1.9 %collective-permute-done.19.refs_6_ = f32[3,1024]{1,0:T(4,128)S(1)} collective-permute-done((f32[3,1024]{1,0:T(4,128)S(1)}, f32[3,1024]{1,0:T(4,128)S(1)}, u32[]{:S(2)}, u32[]{:S(2)}) %collective-permute-start.19) | collective-permute-done | bytes 12320 | tf_op jit(solution)/shard_map/ppermute | solution.py:365
  68.0 1.1 %collective-permute-done.20.refs_7_ = f32[3,1024]{1,0:T(4,128)S(1)} collective-permute-done((f32[3,1024]{1,0:T(4,128)S(1)}, f32[3,1024]{1,0:T(4,128)S(1)}, u32[]{:S(2)}, u32[]{:S(2)}) %collective-permute-start.20) | collective-permute-done | bytes 12320 | tf_op jit(solution)/shard_map/ppermute | solution.py:365
  69.1 0.3 collective-permute-done.17.refs_3_
  69.3 0.7 %shard_map.119 = (f32[3,4096]{1,0:T(4,128)}, f32[3,1024]{1,0:T(4,128)}) custom-call(f32[1,4096]{1,0:T(1,128)S(1)} %get-tuple-element.26.refs_0_, f32[1,4096]{1,0:T(1,128)S(1)} %collective-permute-done.13.refs_1_, f32[3,4096]{1,0:T(4,128)S(1)} %shard_map.118.refs_2_, f32[3,4096]{1,0:T(4,128)S(1)} %collective-permute-done.17.refs_3_, ...), custom_call_target="tpu_custom_call" | custom-call | tf_op jit(solution)/shard_map/pallas_call | solution.py:347
  (3 shorter events, 0.1 us)
Async XLA Ops:
  1.3 0.7 copy-start
  1.3 0.7 copy-start.1
  7.3 3.9 %collective-permute-start.2 = (f32[1,4096]{1,0:T(1,128)S(1)}, f32[1,4096]{1,0:T(1,128)S(1)}, u32[]{:S(2)}, u32[]{:S(2)}) collective-permute-start(f32[1,4096]{1,0:T(1,128)S(1)} %get-tuple-element.20.refs_0_), channel_id=1, source_target_pairs={{0,3},{1,2},{2,1},{3,0},{4,7},{5,6},{6,5},{7,4},{8,11},{9,10},{10,... | collective-permute-start | bytes 49160 | tf_op jit(solution)/shard_map/ppermute | solution.py:365
  9.7 3.7 %collective-permute-start.1 = (f32[1,4096]{1,0:T(1,128)S(1)}, f32[1,4096]{1,0:T(1,128)S(1)}, u32[]{:S(2)}, u32[]{:S(2)}) collective-permute-start(f32[1,4096]{1,0:T(1,128)S(1)} %get-tuple-element.20.refs_0_), channel_id=1, source_target_pairs={{0,2},{1,3},{2,0},{3,1},{4,6},{5,7},{6,4},{7,5},{8,10},{9,11},{10,... | collective-permute-start | bytes 49160 | tf_op jit(solution)/shard_map/ppermute | solution.py:365
  10.4 3.1 %collective-permute-start = (f32[1,4096]{1,0:T(1,128)S(1)}, f32[1,4096]{1,0:T(1,128)S(1)}, u32[]{:S(2)}, u32[]{:S(2)}) collective-permute-start(f32[1,4096]{1,0:T(1,128)S(1)} %get-tuple-element.20.refs_0_), channel_id=1, source_target_pairs={{0,1},{1,0},{2,3},{3,2},{4,5},{5,4},{6,7},{7,6},{8,9},{9,8},{10,11... | collective-permute-start | bytes 49160 | tf_op jit(solution)/shard_map/ppermute | solution.py:365
  16.7 4.7 %collective-permute-start.5 = (f32[1,4096]{1,0:T(1,128)S(1)}, f32[1,4096]{1,0:T(1,128)S(1)}, u32[]{:S(2)}, u32[]{:S(2)}) collective-permute-start(f32[1,4096]{1,0:T(1,128)S(1)} %shard_map.112.refs_0_), channel_id=1, source_target_pairs={{0,12},{4,8},{8,4},{12,0},{16,28},{20,24},{24,20},{28,16},{1,13},{... | collective-permute-start | bytes 49160 | tf_op jit(solution)/shard_map/ppermute | solution.py:372
  18.3 3.7 %collective-permute-start.4 = (f32[1,4096]{1,0:T(1,128)S(1)}, f32[1,4096]{1,0:T(1,128)S(1)}, u32[]{:S(2)}, u32[]{:S(2)}) collective-permute-start(f32[1,4096]{1,0:T(1,128)S(1)} %shard_map.112.refs_0_), channel_id=1, source_target_pairs={{0,8},{4,12},{8,0},{12,4},{16,24},{20,28},{24,16},{28,20},{1,9},{5... | collective-permute-start | bytes 49160 | tf_op jit(solution)/shard_map/ppermute | solution.py:372
  19.7 3.7 %collective-permute-start.3 = (f32[1,4096]{1,0:T(1,128)S(1)}, f32[1,4096]{1,0:T(1,128)S(1)}, u32[]{:S(2)}, u32[]{:S(2)}) collective-permute-start(f32[1,4096]{1,0:T(1,128)S(1)} %shard_map.112.refs_0_), channel_id=1, source_target_pairs={{0,4},{4,0},{8,12},{12,8},{16,20},{20,16},{24,28},{28,24},{1,5},{5... | collective-permute-start | bytes 49160 | tf_op jit(solution)/shard_map/ppermute | solution.py:372
  23.5 4.9 %collective-permute-start.6 = (f32[1,4096]{1,0:T(1,128)S(1)}, f32[1,4096]{1,0:T(1,128)S(1)}, u32[]{:S(2)}, u32[]{:S(2)}) collective-permute-start(f32[1,4096]{1,0:T(1,128)S(1)} %shard_map.113.refs_0_), channel_id=1, source_target_pairs={{0,16},{4,20},{8,24},{12,28},{16,0},{20,4},{24,8},{28,12},{1,17},{... | collective-permute-start | bytes 49160 | tf_op jit(solution)/shard_map/ppermute | solution.py:372
  31.8 3.2 %collective-permute-start.9 = (f32[1,4096]{1,0:T(1,128)S(1)}, f32[1,4096]{1,0:T(1,128)S(1)}, u32[]{:S(2)}, u32[]{:S(2)}) collective-permute-start(f32[1,4096]{1,0:T(1,128)S(1)} %shard_map.114.refs_0_), channel_id=1, source_target_pairs={{0,3},{1,2},{2,1},{3,0},{4,7},{5,6},{6,5},{7,4},{8,11},{9,10},{10,... | collective-permute-start | bytes 49160 | tf_op jit(solution)/shard_map/ppermute | solution.py:365
  31.9 3.8 %collective-permute-start.8 = (f32[1,4096]{1,0:T(1,128)S(1)}, f32[1,4096]{1,0:T(1,128)S(1)}, u32[]{:S(2)}, u32[]{:S(2)}) collective-permute-start(f32[1,4096]{1,0:T(1,128)S(1)} %shard_map.114.refs_0_), channel_id=1, source_target_pairs={{0,2},{1,3},{2,0},{3,1},{4,6},{5,7},{6,4},{7,5},{8,10},{9,11},{10,... | collective-permute-start | bytes 49160 | tf_op jit(solution)/shard_map/ppermute | solution.py:365
  32.1 3.6 %collective-permute-start.7 = (f32[1,4096]{1,0:T(1,128)S(1)}, f32[1,4096]{1,0:T(1,128)S(1)}, u32[]{:S(2)}, u32[]{:S(2)}) collective-permute-start(f32[1,4096]{1,0:T(1,128)S(1)} %shard_map.114.refs_0_), channel_id=1, source_target_pairs={{0,1},{1,0},{2,3},{3,2},{4,5},{5,4},{6,7},{7,6},{8,9},{9,8},{10,11... | collective-permute-start | bytes 49160 | tf_op jit(solution)/shard_map/ppermute | solution.py:365
  43.4 4.7 %collective-permute-start.12 = (f32[1,4096]{1,0:T(1,128)S(1)}, f32[1,4096]{1,0:T(1,128)S(1)}, u32[]{:S(2)}, u32[]{:S(2)}) collective-permute-start(f32[1,4096]{1,0:T(1,128)S(1)} %get-tuple-element.24.refs_0_), channel_id=1, source_target_pairs={{0,12},{4,8},{8,4},{12,0},{16,28},{20,24},{24,20},{28,16},{1,13},{... | collective-permute-start | bytes 49160 | tf_op jit(solution)/shard_map/ppermute | solution.py:372
  43.5 4.6 %collective-permute-start.11 = (f32[1,4096]{1,0:T(1,128)S(1)}, f32[1,4096]{1,0:T(1,128)S(1)}, u32[]{:S(2)}, u32[]{:S(2)}) collective-permute-start(f32[1,4096]{1,0:T(1,128)S(1)} %get-tuple-element.24.refs_0_), channel_id=1, source_target_pairs={{0,8},{4,12},{8,0},{12,4},{16,24},{20,28},{24,16},{28,20},{1,9},{5... | collective-permute-start | bytes 49160 | tf_op jit(solution)/shard_map/ppermute | solution.py:372
  45.2 3.7 %collective-permute-start.10 = (f32[1,4096]{1,0:T(1,128)S(1)}, f32[1,4096]{1,0:T(1,128)S(1)}, u32[]{:S(2)}, u32[]{:S(2)}) collective-permute-start(f32[1,4096]{1,0:T(1,128)S(1)} %get-tuple-element.24.refs_0_), channel_id=1, source_target_pairs={{0,4},{4,0},{8,12},{12,8},{16,20},{20,16},{24,28},{28,24},{1,5},{5... | collective-permute-start | bytes 49160 | tf_op jit(solution)/shard_map/ppermute | solution.py:372
  49.0 14.5 %collective-permute-start.16 = (f32[3,4096]{1,0:T(4,128)S(1)}, f32[3,4096]{1,0:T(4,128)S(1)}, u32[]{:S(2)}, u32[]{:S(2)}) collective-permute-start(f32[3,4096]{1,0:T(4,128)S(1)} %get-tuple-element.29.refs_4_), channel_id=1, source_target_pairs={{0,12},{4,8},{8,4},{12,0},{16,28},{20,24},{24,20},{28,16},{1,13},{... | collective-permute-start | bytes 147464 | tf_op jit(solution)/shard_map/ppermute | solution.py:372
  50.8 12.8 %collective-permute-start.15 = (f32[3,4096]{1,0:T(4,128)S(1)}, f32[3,4096]{1,0:T(4,128)S(1)}, u32[]{:S(2)}, u32[]{:S(2)}) collective-permute-start(f32[3,4096]{1,0:T(4,128)S(1)} %get-tuple-element.29.refs_4_), channel_id=1, source_target_pairs={{0,8},{4,12},{8,0},{12,4},{16,24},{20,28},{24,16},{28,20},{1,9},{5... | collective-permute-start | bytes 147464 | tf_op jit(solution)/shard_map/ppermute | solution.py:372
  52.2 11.3 %collective-permute-start.14 = (f32[3,4096]{1,0:T(4,128)S(1)}, f32[3,4096]{1,0:T(4,128)S(1)}, u32[]{:S(2)}, u32[]{:S(2)}) collective-permute-start(f32[3,4096]{1,0:T(4,128)S(1)} %get-tuple-element.29.refs_4_), channel_id=1, source_target_pairs={{0,4},{4,0},{8,12},{12,8},{16,20},{20,16},{24,28},{28,24},{1,5},{5... | collective-permute-start | bytes 147464 | tf_op jit(solution)/shard_map/ppermute | solution.py:372
  52.6 4.6 %collective-permute-start.13 = (f32[1,4096]{1,0:T(1,128)S(1)}, f32[1,4096]{1,0:T(1,128)S(1)}, u32[]{:S(2)}, u32[]{:S(2)}) collective-permute-start(f32[1,4096]{1,0:T(1,128)S(1)} %get-tuple-element.26.refs_0_), channel_id=1, source_target_pairs={{0,16},{4,20},{8,24},{12,28},{16,0},{20,4},{24,8},{28,12},{1,17},{... | collective-permute-start | bytes 49160 | tf_op jit(solution)/shard_map/ppermute | solution.py:372
  63.6 5.7 %collective-permute-start.17 = (f32[3,4096]{1,0:T(4,128)S(1)}, f32[3,4096]{1,0:T(4,128)S(1)}, u32[]{:S(2)}, u32[]{:S(2)}) collective-permute-start(f32[3,4096]{1,0:T(4,128)S(1)} %shard_map.118.refs_2_), channel_id=1, source_target_pairs={{0,16},{4,20},{8,24},{12,28},{16,0},{20,4},{24,8},{28,12},{1,17},{... | collective-permute-start | bytes 147464 | tf_op jit(solution)/shard_map/ppermute | solution.py:372
  64.3 1.9 %collective-permute-start.18 = (f32[3,1024]{1,0:T(4,128)S(1)}, f32[3,1024]{1,0:T(4,128)S(1)}, u32[]{:S(2)}, u32[]{:S(2)}) collective-permute-start(f32[3,1024]{1,0:T(4,128)S(1)} %get-tuple-element.31), channel_id=1, source_target_pairs={{0,1},{1,0},{2,3},{3,2},{4,5},{5,4},{6,7},{7,6},{8,9},{9,8},{10,11... | collective-permute-start | bytes 36872 | tf_op jit(solution)/shard_map/ppermute | solution.py:365
  64.3 3.7 %collective-permute-start.19 = (f32[3,1024]{1,0:T(4,128)S(1)}, f32[3,1024]{1,0:T(4,128)S(1)}, u32[]{:S(2)}, u32[]{:S(2)}) collective-permute-start(f32[3,1024]{1,0:T(4,128)S(1)} %get-tuple-element.32), channel_id=1, source_target_pairs={{0,2},{1,3},{2,0},{3,1},{4,6},{5,7},{6,4},{7,5},{8,10},{9,11},{10,... | collective-permute-start | bytes 36872 | tf_op jit(solution)/shard_map/ppermute | solution.py:365
  65.9 3.2 %collective-permute-start.20 = (f32[3,1024]{1,0:T(4,128)S(1)}, f32[3,1024]{1,0:T(4,128)S(1)}, u32[]{:S(2)}, u32[]{:S(2)}) collective-permute-start(f32[3,1024]{1,0:T(4,128)S(1)} %get-tuple-element.33), channel_id=1, source_target_pairs={{0,3},{1,2},{2,1},{3,0},{4,7},{5,6},{6,5},{7,4},{8,11},{9,10},{10,... | collective-permute-start | bytes 36872 | tf_op jit(solution)/shard_map/ppermute | solution.py:365

commit v5 on v4

--- a/solution.py
+++ b/solution.py
@@ -241,8 +241,13 @@
     return xc.shape[1] // CLUSTER, yc.shape[1] // CLUSTER
 
 
-def first_row_kernel(points, lists_in, xc_out, yc_out, part_out, lists, sem, stack, red, turned, top, total):
-    copy = fetch(lists_in, lists, sem)
+def first_row_kernel(
+    points, sources, targets, xc_out, yc_out, part_out, lists_out, lists, sem, stack, red, turned, top, total
+):
+    cps, cpt = sides(xc_out, yc_out)
+    count = points[9:10, 0:1].astype(jnp.int32)
+    lists_out[...] = (count.reshape(1, 1, 1) * cpt + targets[...]) * cps + sources[...]
+    copy = fetch(lists_out, lists, sem)
     xs, ys = points[0:3, :], points[3:6, :]
     place(stack, split(ys * KAPPA), TARGET_ORDER)
     yc_out[...] = stack[...].astype(BF16)
@@ -274,7 +279,7 @@
 
 
 def last_col_kernel(
-    parts, points, xc, yc, lists_in, f_out, u_out, part_out, means_out, lists, sem, red, turned, top, sums, columns, f, sem_out
+    parts, points, xc, yc, lists_in, f_out, u_out, part_out, lists, sem, red, turned, top, sums, columns, f, sem_out
 ):
     copy = fetch(lists_in, lists, sem)
     u = -combine([ref[...] for ref in parts])[0]
@@ -285,44 +290,33 @@
     turn(turned, red)
     copy.wait()
     tiles = Tiles(lists, sides(xc, yc), False)
-    part_out[...], *means = mean_tiles(tiles, turned, yc, columns, points, 0, top, sums, unroll=4)
-    for c, row in enumerate(means):
-        means_out[c : c + 1, :] = row
+    for r, row in enumerate(mean_tiles(tiles, turned, yc, columns, points, 0, top, sums, unroll=4)):
+        part_out[r : r + 1, :] = row
     back.wait()
 
 
-def merge_kernel(parts, out):
-    out[...] = combine([ref[...] for ref in parts])[0]
-
-
-def merge_and_pass_kernel(parts, means, out, means_out):
-    merge_kernel(parts, out)
-    means_out[...] = means[...]
-
-
-def mean_of(parts, means):
-    shares = combine([ref[...] for ref in parts])[1]
-    return functools.reduce(jnp.add, [share * ref[...] for share, ref in zip(shares, means)])
-
-
-def merge_means_kernel(parts, means, after, out):
-    out[...] = mean_of(parts, means)
-
-
-def closing_kernel(parts, means, moved, points, target_out, source_out):
-    target_out[...] = points[7:8, :] * (points[3:6, :] - mean_of(parts, means))
-    source_out[...] = functools.reduce(jnp.add, [ref[...] for ref in moved])
+def merged(parts):
+    lse, shares = combine([ref[0:1, :] for ref in parts])
+    rows = range(1, parts[0].shape[0])
+    return [lse] + [functools.reduce(jnp.add, [w * ref[r : r + 1, :] for w, ref in zip(shares, parts)]) for r in rows]
+
+
+def merge_kernel(*refs):
+    for r, row in enumerate(merged(refs[:-1])):
+        refs[-1][r : r + 1, :] = row
 
 
 def gradient_kernel(
-    parts, u, points, xc, yc, lists_in, g_out, *rest, shares
+    parts, u, points, xc, yc, lists_in, g_out, target_out, *rest, shares
 ):
-    source_out, (lists, sem, red, turned, kept, sums, columns, g, whole, sem_out) = rest[:shares], rest[shares:]
+    source_out, (lists, sem, red, turned, kept, sums, columns, g, target, whole, sems) = rest[:shares], rest[shares:]
     copy = fetch(lists_in, lists, sem)
-    lse = combine([ref[...] for ref in parts])[0]
+    lse, *means = merged(parts)
     xs, ys = points[0:3, :], points[3:6, :]
     g[...] = half_square(ys) - lse * (1.0 / KAPPA)
-    back = fetch(g, g_out, sem_out)
+    for c in range(3):
+        target[c : c + 1, :] = points[7:8, :] * (ys[c : c + 1, :] - means[c])
+    back = [fetch(g, g_out, sems.at[0]), fetch(target, target_out, sems.at[1])]
     with_rows(red, yc, pieces(log2(points[7:8, :]) - lse), ONES)
     turn(turned, red)
     with_rows(kept, xc, ONES, split(log2(points[6:7, :]) + u[...]))
@@ -336,14 +330,15 @@
         width = out.shape[1]
         at = pl.multiple_of(peer(place_tgt, k, shares) * width, width)
         out[...] = whole[:, pl.ds(at, width)]
-    back.wait()
+    for one in back:
+        one.wait()
 
 
 VMEM = pl.BlockSpec(memory_space=pltpu.VMEM)
 HBM = pl.BlockSpec(memory_space=pltpu.HBM)
 
 
-def call(kernel, ins, lists, outs, scratch, far=(), flops=0):
+def call(kernel, ins, lists, outs, scratch, far=()):
     return pl.pallas_call(
         kernel,
         out_shape=outs,
@@ -351,7 +346,6 @@
         out_specs=[HBM if at in far else VMEM for at in range(len(outs))],
         scratch_shapes=scratch,
         compiler_params=pltpu.CompilerParams(vmem_limit_bytes=48 * 1024 * 1024),
-        cost_estimate=pl.CostEstimate(flops=flops, bytes_accessed=0, transcendentals=0) if flops else None,
     )(*ins, *lists)
 
 
@@ -366,44 +360,39 @@
     ]
 
 
-def exchange_step(value, axis, step):
+def sum_up(value, axis):
     n = lax.axis_size(axis)
-    others = [k * step for k in range(1, min(4, n // step))]
-    return [value] + [lax.ppermute(value, axis, [(i, i ^ k) for i in range(n)]) for k in others]
-
-
-def bunch(kernel, *sizes):
-    def run(*refs):
-        lists = []
-        for size in sizes:
-            lists.append(refs[:size])
-            refs = refs[size:]
-        kernel(*lists, *refs)
-
-    return run
-
-
-def like(*values):
-    return [jax.ShapeDtypeStruct(value.shape, value.dtype) for value in values]
-
-
-def sum_up(axis, part):
-    n, step = lax.axis_size(axis), 1
+    step = 1
     while True:
-        parts = exchange_step(part, axis, step)
+        others = [k * step for k in range(1, min(4, n // step))]
+        values = [value] + [lax.ppermute(value, axis, [(i, i ^ k) for i in range(n)]) for k in others]
         step *= 4
         if step >= n:
-            return parts
-        (part,) = call(bunch(merge_kernel, len(parts)), parts, (), like(part), [])
+            return values
+        (value,) = call(merge_kernel, values, (), [jax.ShapeDtypeStruct(value.shape, F32)], [])
+
+
+def bunch(kernel, size):
+    return lambda *refs: kernel(refs[:size], *refs[size:])
+
+
+def stacked(values, width):
+    whole = sum(value.shape[0] for value in values)
+    total, first = None, 0
+    for value in values:
+        after = whole - first - value.shape[0]
+        padded = lax.pad(value, jnp.zeros((), value.dtype), [(first, after, 0), (0, width - value.shape[1], 0)]).astype(F32)
+        total = padded if total is None else total + padded
+        first += value.shape[0]
+    return total
 
 
 def body(source_points, target_points, source_weight, target_weight, target_start, tile_source, tile_target, tile_count):
     ns, nt = source_points.shape[1], target_points.shape[1]
     n_tgt = lax.axis_size("tgt")
-    points = jnp.concatenate(
-        [source_points, target_points] + [a.reshape(1, -1) for a in (source_weight, target_weight, target_start)]
-    )
-    lists = ((tile_count[:, :, None] * (nt // CLUSTER) + tile_target) * (ns // CLUSTER) + tile_source,)
+    given = (source_points, target_points) + tuple(a.reshape(1, -1) for a in (source_weight, target_weight, target_start))
+    points = stacked(given + (tile_count,), ns)
+    given = (tile_source, tile_target)
 
     def rows(n, *k):
         return jax.ShapeDtypeStruct((*k, n), F32)
@@ -413,7 +402,7 @@
 
     def work(red):
         return [
-            pltpu.SMEM(lists[0].shape, jnp.int32),
+            pltpu.SMEM(tile_source.shape, jnp.int32),
             pltpu.SemaphoreType.DMA,
             pltpu.VMEM((DEPTH, red), BF16),
             pltpu.VMEM((red, DEPTH), BF16),
@@ -423,11 +412,11 @@
         return [pltpu.VMEM((8, kept), F32), pltpu.VMEM((8, kept), F32)]
 
     first = work(nt)
-    xc, yc, part = call(
+    xc, yc, part, *lists = call(
         first_row_kernel,
-        (points,),
-        lists,
-        [split_rows(ns), split_rows(nt), rows(ns, 1)],
+        (points, *given),
+        (),
+        [split_rows(ns), split_rows(nt), rows(ns, 1), jax.ShapeDtypeStruct(tile_source.shape, jnp.int32)],
         first[:2] + [pltpu.VMEM((DEPTH, ns), F32)] + first[2:] + state(ns),
     )
     known = (points, xc, yc)
@@ -439,7 +428,7 @@
         [rows(nt, 1)],
         work(ns) + state(nt),
     )
-    parts = sum_up("src", part)
+    parts = sum_up(part, "src")
     (part,) = call(
         bunch(row_kernel, len(parts)),
         (*parts, *known),
@@ -448,11 +437,11 @@
         work(nt) + state(ns),
     )
     parts = exchange([part] * n_tgt, "tgt")
-    f, u, part, means = call(
+    f, u, part = call(
         bunch(last_col_kernel, n_tgt),
         (*parts, *known),
         lists,
-        [rows(ns, 1), rows(ns, 1), rows(nt, 1), rows(nt, 3)],
+        [rows(ns, 1), rows(ns, 1), rows(nt, 4)],
         work(ns)
         + [
             pltpu.VMEM((8, nt), F32),
@@ -463,48 +452,25 @@
         ],
         far=(0,),
     )
-    n_src, step, late = lax.axis_size("src"), 1, []
-    while True:
-        parts = exchange_step(part, "src", step)
-        if 4 * step >= n_src:
-            break
-        part, means = call(
-            bunch(merge_and_pass_kernel, len(parts)), (*parts, means), (), like(part, means), []
-        )
-        late.append((step, parts))
-        step *= 4
-    n = len(parts)
-    g, *moved = call(
-        bunch(functools.partial(gradient_kernel, shares=n_tgt), n),
+    parts = sum_up(part, "src")
+    g, target_grad, *parts = call(
+        bunch(functools.partial(gradient_kernel, shares=n_tgt), len(parts)),
         (*parts, u, *known),
         lists,
-        [rows(nt, 1)] + [rows(ns // n_tgt, 3)] * n_tgt,
+        [rows(nt, 1), rows(nt, 3)] + [rows(ns // n_tgt, 3)] * n_tgt,
         work(nt)
         + [
             pltpu.VMEM((DEPTH, ns), BF16),
             pltpu.VMEM((4, 8, ns), F32),
             pltpu.VMEM((nt, 384), F32),
             pltpu.VMEM((1, nt), F32),
+            pltpu.VMEM((3, nt), F32),
             pltpu.VMEM((3, ns), F32),
-            pltpu.SemaphoreType.DMA,
+            pltpu.SemaphoreType.DMA((2,)),
         ],
-        far=(0,),
-        flops=40 * ns * CLUSTER,
-    )
-    for at, some in late:
-        others = exchange_step(means, "src", at)
-        (means,) = call(
-            bunch(merge_means_kernel, len(some), len(some)), (*some, *others, moved[0]), (), like(means), []
-        )
-    means = exchange_step(means, "src", step)
-    moved = exchange(moved, "tgt")
-    target_grad, own_grad = call(
-        bunch(closing_kernel, n, n, n_tgt),
-        (*parts, *means, *moved, points),
-        (),
-        [rows(nt, 3), rows(ns // n_tgt, 3)],
-        [],
-    )
+        far=(0, 1),
+    )
+    own_grad = functools.reduce(jnp.add, exchange(parts, "tgt"))
     return (f.reshape(-1), g.reshape(-1), own_grad, target_grad)
 
 

time: 71.1 us -> 65.2 us (0.917); the launches traced: 70.1 us -> 65.4 us
  starting transfers between devices: 23 us -> 19.5 us
  local copies, waits for them, and re-layouts: 2.37 us -> 0.01 us
  other arithmetic: 0.01 us -> 1.65 us
  Pallas kernels: 25.1 us -> 24.3 us
    ppermute x12 -> x8, starting transfers between devices: 16.1 us -> 12.5 us  [sum_up(): lax.ppermute(value, axis, [(i, i ^ k) for i in range(n)])]
    concatenate x1 -> x0, local copies, waits for them, and re-layouts: 1.71 us -> none  [body(): jnp.concatenate([source_points, target_points] + [a.reshape(1, -1) for a...]
    add x1 -> x2, other arithmetic: 0.01 us -> 1.65 us  [the longest x1 1.03 us: stacked(): total = padded if total is None else total + padded]
    ppermute x12 -> x8, waiting for transfers between devices: 10.2 us -> 11.6 us  [sum_up(): lax.ppermute(value, axis, [(i, i ^ k) for i in range(n)])]
    ppermute x9, waiting for transfers between devices: 7.95 us -> 6.96 us  [exchange(): lax.ppermute(values[k], axis, [(i, peer(i, k, n)) for i in range(n)])]
    pallas_call x9 -> x7, Pallas kernels: 25.1 us -> 24.3 us  [call(): pl.pallas_call(kernel, out_shape=outs, in_specs=[VMEM] * len(ins) + [HBM]...]
  transfers between devices with their start and end apart: 21 -> 17, of which waited for: 14 -> 12; matrix products, arithmetic and copies ran while one was open for 0% -> 0% of each run, Pallas kernels for 9% -> 0%
where the time goes in v5:
time: 65.2 us; the launch traced here: 65.4 us
  Pallas kernels  24.3 us (37%)
  starting transfers between devices  19.5 us (30%)
  waiting for transfers between devices  18.6 us (29%)
  other arithmetic  1.65 us (3%)
  between operations  1.4 us (2%)
    pallas_call x7, Pallas kernels, call(): pl.pallas_call(kernel, out_shape=outs, in_specs=[VMEM] * len(ins) + [HBM]...  24.3 us
    ppermute x8, starting transfers between devices, sum_up(): lax.ppermute(value, axis, [(i, i ^ k) for i in range(n)])  12.5 us
    ppermute x8, waiting for transfers between devices, sum_up(): lax.ppermute(value, axis, [(i, i ^ k) for i in range(n)])  11.6 us
    ppermute x9, starting transfers between devices, exchange(): lax.ppermute(values[k], axis, [(i, peer(i, k, n)) for i in range(n)])  6.97 us
    ppermute x9, waiting for transfers between devices, exchange(): lax.ppermute(values[k], axis, [(i, peer(i, k, n)) for i in range(n)])  6.96 us
  transfers between devices with their start and end apart: 17, of which 12 were waited for; matrix products, arithmetic and copies ran while one was open for 0% of the time, Pallas kernels for 0%

profile of v5, /device:TPU:0, one launch (start us, length us, event | category | flops | bytes accessed | tf_op | source)
XLA Modules:
  0.0 65.4 jit_solution(6091508947637424981)
XLA Ops:
  1.3 0.0 copy-start
  1.3 0.0 copy-start.1
  1.3 1.0 %convert_add_fusion.points.refs_4_.refs_2_.refs_3_ = f32[10,4096]{1,0:T(8,128)S(1)} fusion(s32[1,1]{1,0:T(1,128)S(6)} %copy.12, f32[1,4096]{1,0:T(1,128)} %bitcast.5, f32[1,4096]{1,0:T(1,128)} %bitcast.6, f32[1,4096]{1,0:T(1,128)} %bitcast.7, f32[3,4096]{1,0:T(4,128)} %param.9, f32[3,4096]{1,0:T(4,128)} %param.8), kind=kLoop, calls=%fused_computation | loop fusion | flops 245760 | bytes 311300 | tf_op jit(solution)/shard_map/add | solution.py:385
  2.3 0.0 copy-done
  2.3 0.0 copy-done.1
  2.4 3.6 %shard_map.111 = (bf16[32,4096]{1,0:T(8,128)(2,1)S(1)}, bf16[32,4096]{1,0:T(8,128)(2,1)S(1)}, f32[1,4096]{1,0:T(1,128)S(1)}, s32[1,1,12]{2,1,0:T(1,128)S(1)}) custom-call(f32[10,4096]{1,0:T(8,128)S(1)} %convert_add_fusion.points.refs_4_.refs_2_.refs_3_, s32[1,1,12]{2,1,0:T(1,128)S(1)} %copy-done, s32[1,1,12]{2,1,0:T(1,128)S(1)} %copy-done.1), custom_call_target="tpu_custom_call" | custom-call | tf_op jit(solution)/shard_map/pallas_call | solution.py:342
  6.0 2.4 %collective-permute-start.2 = (f32[1,4096]{1,0:T(1,128)S(1)}, f32[1,4096]{1,0:T(1,128)S(1)}, u32[]{:S(2)}, u32[]{:S(2)}) collective-permute-start(f32[1,4096]{1,0:T(1,128)S(1)} %get-tuple-element.17.refs_0_), channel_id=1, source_target_pairs={{0,3},{1,2},{2,1},{3,0},{4,7},{5,6},{6,5},{7,4},{8,11},{9,10},{10,... | collective-permute-start | bytes 49160 | tf_op jit(solution)/shard_map/ppermute | solution.py:359
  8.4 0.6 collective-permute-start.1
  9.1 0.0 collective-permute-start
  9.1 0.8 %collective-permute-done.2.refs_3_ = f32[1,4096]{1,0:T(1,128)S(1)} collective-permute-done((f32[1,4096]{1,0:T(1,128)S(1)}, f32[1,4096]{1,0:T(1,128)S(1)}, u32[]{:S(2)}, u32[]{:S(2)}) %collective-permute-start.2) | collective-permute-done | bytes 16416 | tf_op jit(solution)/shard_map/ppermute | solution.py:359
  9.9 2.3 %collective-permute-done.1.refs_2_ = f32[1,4096]{1,0:T(1,128)S(1)} collective-permute-done((f32[1,4096]{1,0:T(1,128)S(1)}, f32[1,4096]{1,0:T(1,128)S(1)}, u32[]{:S(2)}, u32[]{:S(2)}) %collective-permute-start.1) | collective-permute-done | bytes 16416 | tf_op jit(solution)/shard_map/ppermute | solution.py:359
  12.2 0.0 collective-permute-done.refs_1_
  12.2 3.2 %shard_map.112.refs_0_ = f32[1,4096]{1,0:T(1,128)S(1)} custom-call(f32[1,4096]{1,0:T(1,128)S(1)} %get-tuple-element.17.refs_0_, f32[1,4096]{1,0:T(1,128)S(1)} %collective-permute-done.refs_1_, f32[1,4096]{1,0:T(1,128)S(1)} %collective-permute-done.1.refs_2_, f32[1,4096]{1,0:T(1,128)S(1)} %collective-permute-done.2.refs_3_, ...), custom_call_target="tpu_custom_call" | custom-call | tf_op jit(solution)/shard_map/pallas_call | solution.py:342
  15.4 1.7 %collective-permute-start.5 = (f32[1,4096]{1,0:T(1,128)S(1)}, f32[1,4096]{1,0:T(1,128)S(1)}, u32[]{:S(2)}, u32[]{:S(2)}) collective-permute-start(f32[1,4096]{1,0:T(1,128)S(1)} %shard_map.112.refs_0_), channel_id=1, source_target_pairs={{0,12},{4,8},{8,4},{12,0},{16,28},{20,24},{24,20},{28,16},{1,13},{... | collective-permute-start | bytes 49160 | tf_op jit(solution)/shard_map/ppermute | solution.py:368
  17.0 1.4 %collective-permute-start.4 = (f32[1,4096]{1,0:T(1,128)S(1)}, f32[1,4096]{1,0:T(1,128)S(1)}, u32[]{:S(2)}, u32[]{:S(2)}) collective-permute-start(f32[1,4096]{1,0:T(1,128)S(1)} %shard_map.112.refs_0_), channel_id=1, source_target_pairs={{0,8},{4,12},{8,0},{12,4},{16,24},{20,28},{24,16},{28,20},{1,9},{5... | collective-permute-start | bytes 49160 | tf_op jit(solution)/shard_map/ppermute | solution.py:368
  18.4 0.5 collective-permute-start.3
  18.9 1.3 %collective-permute-done.5.refs_3_ = f32[1,4096]{1,0:T(1,128)S(1)} collective-permute-done((f32[1,4096]{1,0:T(1,128)S(1)}, f32[1,4096]{1,0:T(1,128)S(1)}, u32[]{:S(2)}, u32[]{:S(2)}) %collective-permute-start.5) | collective-permute-done | bytes 16416 | tf_op jit(solution)/shard_map/ppermute | solution.py:368
  20.2 0.6 collective-permute-done.4.refs_2_
  20.8 1.4 %collective-permute-done.3.refs_1_ = f32[1,4096]{1,0:T(1,128)S(1)} collective-permute-done((f32[1,4096]{1,0:T(1,128)S(1)}, f32[1,4096]{1,0:T(1,128)S(1)}, u32[]{:S(2)}, u32[]{:S(2)}) %collective-permute-start.3) | collective-permute-done | bytes 16416 | tf_op jit(solution)/shard_map/ppermute | solution.py:368
  22.2 2.6 %collective-permute-start.6 = (f32[1,4096]{1,0:T(1,128)S(1)}, f32[1,4096]{1,0:T(1,128)S(1)}, u32[]{:S(2)}, u32[]{:S(2)}) collective-permute-start(f32[1,4096]{1,0:T(1,128)S(1)} %shard_map.113.refs_0_), channel_id=1, source_target_pairs={{0,16},{4,20},{8,24},{12,28},{16,0},{20,4},{24,8},{28,12},{1,17},{... | collective-permute-start | bytes 49160 | tf_op jit(solution)/shard_map/ppermute | solution.py:368
  24.8 2.1 %collective-permute-done.6.refs_1_ = f32[1,4096]{1,0:T(1,128)S(1)} collective-permute-done((f32[1,4096]{1,0:T(1,128)S(1)}, f32[1,4096]{1,0:T(1,128)S(1)}, u32[]{:S(2)}, u32[]{:S(2)}) %collective-permute-start.6) | collective-permute-done | bytes 16416 | tf_op jit(solution)/shard_map/ppermute | solution.py:368
  26.9 3.4 %shard_map.114.refs_0_ = f32[1,4096]{1,0:T(1,128)S(1)} custom-call(f32[1,4096]{1,0:T(1,128)S(1)} %shard_map.113.refs_0_, f32[1,4096]{1,0:T(1,128)S(1)} %collective-permute-done.6.refs_1_, f32[10,4096]{1,0:T(8,128)S(1)} %convert_add_fusion.points.refs_4_.refs_2_.refs_3_, bf16[32,4096]{1,0:T(8,128)(2,1)S(1)} %get-tuple-element.18.refs_5_.refs_3_.refs_4_, ...), custom_call_target="tpu_custom_call" | custom-call | tf_op jit(solution)/shard_map/pallas_call | solution.py:342
  30.3 0.1 collective-permute-start.9
  30.4 0.7 %collective-permute-start.8 = (f32[1,4096]{1,0:T(1,128)S(1)}, f32[1,4096]{1,0:T(1,128)S(1)}, u32[]{:S(2)}, u32[]{:S(2)}) collective-permute-start(f32[1,4096]{1,0:T(1,128)S(1)} %shard_map.114.refs_0_), channel_id=1, source_target_pairs={{0,2},{1,3},{2,0},{3,1},{4,6},{5,7},{6,4},{7,5},{8,10},{9,11},{10,... | collective-permute-start | bytes 49160 | tf_op jit(solution)/shard_map/ppermute | solution.py:359
  31.1 1.2 %collective-permute-start.7 = (f32[1,4096]{1,0:T(1,128)S(1)}, f32[1,4096]{1,0:T(1,128)S(1)}, u32[]{:S(2)}, u32[]{:S(2)}) collective-permute-start(f32[1,4096]{1,0:T(1,128)S(1)} %shard_map.114.refs_0_), channel_id=1, source_target_pairs={{0,1},{1,0},{2,3},{3,2},{4,5},{5,4},{6,7},{7,6},{8,9},{9,8},{10,11... | collective-permute-start | bytes 49160 | tf_op jit(solution)/shard_map/ppermute | solution.py:359
  32.2 1.3 %collective-permute-done.9.refs_3_ = f32[1,4096]{1,0:T(1,128)S(1)} collective-permute-done((f32[1,4096]{1,0:T(1,128)S(1)}, f32[1,4096]{1,0:T(1,128)S(1)}, u32[]{:S(2)}, u32[]{:S(2)}) %collective-permute-start.9) | collective-permute-done | bytes 16416 | tf_op jit(solution)/shard_map/ppermute | solution.py:359
  33.5 0.7 collective-permute-done.8.refs_2_
  34.2 0.0 collective-permute-done.7.refs_1_
  34.2 7.4 %shard_map.115 = (f32[1,4096]{1,0:T(1,128)}, f32[1,4096]{1,0:T(1,128)S(1)}, f32[4,4096]{1,0:T(4,128)S(1)}) custom-call(f32[1,4096]{1,0:T(1,128)S(1)} %shard_map.114.refs_0_, f32[1,4096]{1,0:T(1,128)S(1)} %collective-permute-done.7.refs_1_, f32[1,4096]{1,0:T(1,128)S(1)} %collective-permute-done.8.refs_2_, f32[1,4096]{1,0:T(1,128)S(1)} %collective-permute-done.9.refs_3_, ...), custom_call_target="tpu_custom_call" | custom-call | tf_op jit(solution)/shard_map/pallas_call | solution.py:342
  41.6 0.1 collective-permute-start.12
  41.7 1.9 %collective-permute-start.11 = (f32[4,4096]{1,0:T(4,128)S(1)}, f32[4,4096]{1,0:T(4,128)S(1)}, u32[]{:S(2)}, u32[]{:S(2)}) collective-permute-start(f32[4,4096]{1,0:T(4,128)S(1)} %get-tuple-element.22.refs_0_), channel_id=1, source_target_pairs={{0,8},{4,12},{8,0},{12,4},{16,24},{20,28},{24,16},{28,20},{1,9},{5... | collective-permute-start | bytes 196616 | tf_op jit(solution)/shard_map/ppermute | solution.py:368
  43.6 1.5 %collective-permute-start.10 = (f32[4,4096]{1,0:T(4,128)S(1)}, f32[4,4096]{1,0:T(4,128)S(1)}, u32[]{:S(2)}, u32[]{:S(2)}) collective-permute-start(f32[4,4096]{1,0:T(4,128)S(1)} %get-tuple-element.22.refs_0_), channel_id=1, source_target_pairs={{0,4},{4,0},{8,12},{12,8},{16,20},{20,16},{24,28},{28,24},{1,5},{5... | collective-permute-start | bytes 196616 | tf_op jit(solution)/shard_map/ppermute | solution.py:368
  45.2 2.1 %collective-permute-done.12.refs_3_ = f32[4,4096]{1,0:T(4,128)S(1)} collective-permute-done((f32[4,4096]{1,0:T(4,128)S(1)}, f32[4,4096]{1,0:T(4,128)S(1)}, u32[]{:S(2)}, u32[]{:S(2)}) %collective-permute-start.12) | collective-permute-done | bytes 65568 | tf_op jit(solution)/shard_map/ppermute | solution.py:368
  47.3 0.0 collective-permute-done.11.refs_2_
  47.3 0.6 collective-permute-done.10.refs_1_
  48.0 2.8 %collective-permute-start.13 = (f32[4,4096]{1,0:T(4,128)S(1)}, f32[4,4096]{1,0:T(4,128)S(1)}, u32[]{:S(2)}, u32[]{:S(2)}) collective-permute-start(f32[4,4096]{1,0:T(4,128)S(1)} %shard_map.116.refs_0_), channel_id=1, source_target_pairs={{0,16},{4,20},{8,24},{12,28},{16,0},{20,4},{24,8},{28,12},{1,17},{... | collective-permute-start | bytes 196616 | tf_op jit(solution)/shard_map/ppermute | solution.py:368
  50.8 3.5 %collective-permute-done.13.refs_1_ = f32[4,4096]{1,0:T(4,128)S(1)} collective-permute-done((f32[4,4096]{1,0:T(4,128)S(1)}, f32[4,4096]{1,0:T(4,128)S(1)}, u32[]{:S(2)}, u32[]{:S(2)}) %collective-permute-start.13) | collective-permute-done | bytes 65568 | tf_op jit(solution)/shard_map/ppermute | solution.py:368
  54.3 6.6 %shard_map.117 = (f32[1,4096]{1,0:T(1,128)}, f32[3,4096]{1,0:T(4,128)}, f32[3,1024]{1,0:T(4,128)S(1)}, f32[3,1024]{1,0:T(4,128)S(1)}, f32[3,1024]{1,0:T(4,128)S(1)}, /*index=5*/f32[3,1024]{1,0:T(4,128)S(1)}) custom-call(f32[4,4096]{1,0:T(4,128)S(1)} %shard_map.116.refs_0_, f32[4,4096]{1,0:T(4,128)S(1)} %collective-permute-done.13.refs_1_, ...), custom_call_target="tpu_custom_call" | custom-call | tf_op jit(solution)/shard_map/pallas_call | solution.py:342
  60.9 0.1 collective-permute-start.14
  61.0 0.1 collective-permute-start.15
  61.1 1.8 %collective-permute-start.16 = (f32[3,1024]{1,0:T(4,128)S(1)}, f32[3,1024]{1,0:T(4,128)S(1)}, u32[]{:S(2)}, u32[]{:S(2)}) collective-permute-start(f32[3,1024]{1,0:T(4,128)S(1)} %get-tuple-element.28), channel_id=1, source_target_pairs={{0,3},{1,2},{2,1},{3,0},{4,7},{5,6},{6,5},{7,4},{8,11},{9,10},{10,... | collective-permute-start | bytes 36872 | tf_op jit(solution)/shard_map/ppermute | solution.py:359
  62.9 0.0 collective-permute-done.14
  62.9 1.9 %collective-permute-done.15 = f32[3,1024]{1,0:T(4,128)S(1)} collective-permute-done((f32[3,1024]{1,0:T(4,128)S(1)}, f32[3,1024]{1,0:T(4,128)S(1)}, u32[]{:S(2)}, u32[]{:S(2)}) %collective-permute-start.15) | collective-permute-done | bytes 12320 | tf_op jit(solution)/shard_map/ppermute | solution.py:359
  64.8 0.0 collective-permute-done.16
  64.8 0.6 add_add_fusion
  (2 shorter events, 0.1 us)
Async XLA Ops:
  1.3 1.1 %copy-start = (s32[1,1,12]{2,1,0:T(1,128)S(1)}, s32[1,1,12]{2,1,0:T(1,128)}, u32[]{:S(2)}) copy-start(s32[1,1,12]{2,1,0:T(1,128)} %sources.1) | copy-start | bytes 148
  1.3 1.1 %copy-start.1 = (s32[1,1,12]{2,1,0:T(1,128)S(1)}, s32[1,1,12]{2,1,0:T(1,128)}, u32[]{:S(2)}) copy-start(s32[1,1,12]{2,1,0:T(1,128)} %targets.1) | copy-start | bytes 148
  6.0 3.9 %collective-permute-start.2 = (f32[1,4096]{1,0:T(1,128)S(1)}, f32[1,4096]{1,0:T(1,128)S(1)}, u32[]{:S(2)}, u32[]{:S(2)}) collective-permute-start(f32[1,4096]{1,0:T(1,128)S(1)} %get-tuple-element.17.refs_0_), channel_id=1, source_target_pairs={{0,3},{1,2},{2,1},{3,0},{4,7},{5,6},{6,5},{7,4},{8,11},{9,10},{10,... | collective-permute-start | bytes 49160 | tf_op jit(solution)/shard_map/ppermute | solution.py:359
  8.4 3.7 %collective-permute-start.1 = (f32[1,4096]{1,0:T(1,128)S(1)}, f32[1,4096]{1,0:T(1,128)S(1)}, u32[]{:S(2)}, u32[]{:S(2)}) collective-permute-start(f32[1,4096]{1,0:T(1,128)S(1)} %get-tuple-element.17.refs_0_), channel_id=1, source_target_pairs={{0,2},{1,3},{2,0},{3,1},{4,6},{5,7},{6,4},{7,5},{8,10},{9,11},{10,... | collective-permute-start | bytes 49160 | tf_op jit(solution)/shard_map/ppermute | solution.py:359
  9.1 3.1 %collective-permute-start = (f32[1,4096]{1,0:T(1,128)S(1)}, f32[1,4096]{1,0:T(1,128)S(1)}, u32[]{:S(2)}, u32[]{:S(2)}) collective-permute-start(f32[1,4096]{1,0:T(1,128)S(1)} %get-tuple-element.17.refs_0_), channel_id=1, source_target_pairs={{0,1},{1,0},{2,3},{3,2},{4,5},{5,4},{6,7},{7,6},{8,9},{9,8},{10,11... | collective-permute-start | bytes 49160 | tf_op jit(solution)/shard_map/ppermute | solution.py:359
  15.4 4.9 %collective-permute-start.5 = (f32[1,4096]{1,0:T(1,128)S(1)}, f32[1,4096]{1,0:T(1,128)S(1)}, u32[]{:S(2)}, u32[]{:S(2)}) collective-permute-start(f32[1,4096]{1,0:T(1,128)S(1)} %shard_map.112.refs_0_), channel_id=1, source_target_pairs={{0,12},{4,8},{8,4},{12,0},{16,28},{20,24},{24,20},{28,16},{1,13},{... | collective-permute-start | bytes 49160 | tf_op jit(solution)/shard_map/ppermute | solution.py:368
  17.0 3.7 %collective-permute-start.4 = (f32[1,4096]{1,0:T(1,128)S(1)}, f32[1,4096]{1,0:T(1,128)S(1)}, u32[]{:S(2)}, u32[]{:S(2)}) collective-permute-start(f32[1,4096]{1,0:T(1,128)S(1)} %shard_map.112.refs_0_), channel_id=1, source_target_pairs={{0,8},{4,12},{8,0},{12,4},{16,24},{20,28},{24,16},{28,20},{1,9},{5... | collective-permute-start | bytes 49160 | tf_op jit(solution)/shard_map/ppermute | solution.py:368
  18.4 3.7 %collective-permute-start.3 = (f32[1,4096]{1,0:T(1,128)S(1)}, f32[1,4096]{1,0:T(1,128)S(1)}, u32[]{:S(2)}, u32[]{:S(2)}) collective-permute-start(f32[1,4096]{1,0:T(1,128)S(1)} %shard_map.112.refs_0_), channel_id=1, source_target_pairs={{0,4},{4,0},{8,12},{12,8},{16,20},{20,16},{24,28},{28,24},{1,5},{5... | collective-permute-start | bytes 49160 | tf_op jit(solution)/shard_map/ppermute | solution.py:368
  22.2 4.7 %collective-permute-start.6 = (f32[1,4096]{1,0:T(1,128)S(1)}, f32[1,4096]{1,0:T(1,128)S(1)}, u32[]{:S(2)}, u32[]{:S(2)}) collective-permute-start(f32[1,4096]{1,0:T(1,128)S(1)} %shard_map.113.refs_0_), channel_id=1, source_target_pairs={{0,16},{4,20},{8,24},{12,28},{16,0},{20,4},{24,8},{28,12},{1,17},{... | collective-permute-start | bytes 49160 | tf_op jit(solution)/shard_map/ppermute | solution.py:368
  30.3 3.2 %collective-permute-start.9 = (f32[1,4096]{1,0:T(1,128)S(1)}, f32[1,4096]{1,0:T(1,128)S(1)}, u32[]{:S(2)}, u32[]{:S(2)}) collective-permute-start(f32[1,4096]{1,0:T(1,128)S(1)} %shard_map.114.refs_0_), channel_id=1, source_target_pairs={{0,3},{1,2},{2,1},{3,0},{4,7},{5,6},{6,5},{7,4},{8,11},{9,10},{10,... | collective-permute-start | bytes 49160 | tf_op jit(solution)/shard_map/ppermute | solution.py:359
  30.4 3.8 %collective-permute-start.8 = (f32[1,4096]{1,0:T(1,128)S(1)}, f32[1,4096]{1,0:T(1,128)S(1)}, u32[]{:S(2)}, u32[]{:S(2)}) collective-permute-start(f32[1,4096]{1,0:T(1,128)S(1)} %shard_map.114.refs_0_), channel_id=1, source_target_pairs={{0,2},{1,3},{2,0},{3,1},{4,6},{5,7},{6,4},{7,5},{8,10},{9,11},{10,... | collective-permute-start | bytes 49160 | tf_op jit(solution)/shard_map/ppermute | solution.py:359
  31.1 3.1 %collective-permute-start.7 = (f32[1,4096]{1,0:T(1,128)S(1)}, f32[1,4096]{1,0:T(1,128)S(1)}, u32[]{:S(2)}, u32[]{:S(2)}) collective-permute-start(f32[1,4096]{1,0:T(1,128)S(1)} %shard_map.114.refs_0_), channel_id=1, source_target_pairs={{0,1},{1,0},{2,3},{3,2},{4,5},{5,4},{6,7},{7,6},{8,9},{9,8},{10,11... | collective-permute-start | bytes 49160 | tf_op jit(solution)/shard_map/ppermute | solution.py:359
  41.6 5.7 %collective-permute-start.12 = (f32[4,4096]{1,0:T(4,128)S(1)}, f32[4,4096]{1,0:T(4,128)S(1)}, u32[]{:S(2)}, u32[]{:S(2)}) collective-permute-start(f32[4,4096]{1,0:T(4,128)S(1)} %get-tuple-element.22.refs_0_), channel_id=1, source_target_pairs={{0,12},{4,8},{8,4},{12,0},{16,28},{20,24},{24,20},{28,16},{1,13},{... | collective-permute-start | bytes 196616 | tf_op jit(solution)/shard_map/ppermute | solution.py:368
  41.7 5.6 %collective-permute-start.11 = (f32[4,4096]{1,0:T(4,128)S(1)}, f32[4,4096]{1,0:T(4,128)S(1)}, u32[]{:S(2)}, u32[]{:S(2)}) collective-permute-start(f32[4,4096]{1,0:T(4,128)S(1)} %get-tuple-element.22.refs_0_), channel_id=1, source_target_pairs={{0,8},{4,12},{8,0},{12,4},{16,24},{20,28},{24,16},{28,20},{1,9},{5... | collective-permute-start | bytes 196616 | tf_op jit(solution)/shard_map/ppermute | solution.py:368
  43.6 4.3 %collective-permute-start.10 = (f32[4,4096]{1,0:T(4,128)S(1)}, f32[4,4096]{1,0:T(4,128)S(1)}, u32[]{:S(2)}, u32[]{:S(2)}) collective-permute-start(f32[4,4096]{1,0:T(4,128)S(1)} %get-tuple-element.22.refs_0_), channel_id=1, source_target_pairs={{0,4},{4,0},{8,12},{12,8},{16,20},{20,16},{24,28},{28,24},{1,5},{5... | collective-permute-start | bytes 196616 | tf_op jit(solution)/shard_map/ppermute | solution.py:368
  48.0 6.3 %collective-permute-start.13 = (f32[4,4096]{1,0:T(4,128)S(1)}, f32[4,4096]{1,0:T(4,128)S(1)}, u32[]{:S(2)}, u32[]{:S(2)}) collective-permute-start(f32[4,4096]{1,0:T(4,128)S(1)} %shard_map.116.refs_0_), channel_id=1, source_target_pairs={{0,16},{4,20},{8,24},{12,28},{16,0},{20,4},{24,8},{28,12},{1,17},{... | collective-permute-start | bytes 196616 | tf_op jit(solution)/shard_map/ppermute | solution.py:368
  60.9 1.9 %collective-permute-start.14 = (f32[3,1024]{1,0:T(4,128)S(1)}, f32[3,1024]{1,0:T(4,128)S(1)}, u32[]{:S(2)}, u32[]{:S(2)}) collective-permute-start(f32[3,1024]{1,0:T(4,128)S(1)} %get-tuple-element.26), channel_id=1, source_target_pairs={{0,1},{1,0},{2,3},{3,2},{4,5},{5,4},{6,7},{7,6},{8,9},{9,8},{10,11... | collective-permute-start | bytes 36872 | tf_op jit(solution)/shard_map/ppermute | solution.py:359
  61.0 3.8 %collective-permute-start.15 = (f32[3,1024]{1,0:T(4,128)S(1)}, f32[3,1024]{1,0:T(4,128)S(1)}, u32[]{:S(2)}, u32[]{:S(2)}) collective-permute-start(f32[3,1024]{1,0:T(4,128)S(1)} %get-tuple-element.27), channel_id=1, source_target_pairs={{0,2},{1,3},{2,0},{3,1},{4,6},{5,7},{6,4},{7,5},{8,10},{9,11},{10,... | collective-permute-start | bytes 36872 | tf_op jit(solution)/shard_map/ppermute | solution.py:359
  61.1 3.7 %collective-permute-start.16 = (f32[3,1024]{1,0:T(4,128)S(1)}, f32[3,1024]{1,0:T(4,128)S(1)}, u32[]{:S(2)}, u32[]{:S(2)}) collective-permute-start(f32[3,1024]{1,0:T(4,128)S(1)} %get-tuple-element.28), channel_id=1, source_target_pairs={{0,3},{1,2},{2,1},{3,0},{4,7},{5,6},{6,5},{7,4},{8,11},{9,10},{10,... | collective-permute-start | bytes 36872 | tf_op jit(solution)/shard_map/ppermute | solution.py:359

commit v6 on v5

--- a/solution.py
+++ b/solution.py
@@ -36,36 +36,26 @@
 
 SOURCE_ORDER = (0, 1, 2, 0, 0, 1)
 TARGET_ORDER = (0, 0, 0, 1, 2, 1)
-ONE = 15
 
 
 def place(scratch, parts, order):
     scratch[...] = jnp.zeros_like(scratch)
     for at, which in enumerate(order[:5]):
         scratch[3 * at : 3 * at + 3, :] = parts[which]
-    scratch[ONE : ONE + 1, :] = jnp.ones_like(parts[0][0:1])
     scratch[16:19, :] = parts[order[5]]
     scratch[19:22, :] = jnp.ones_like(parts[0])
 
 
-def with_rows(out, static, first, second=()):
-    out[0:16, :] = static[0:16, :]
-    low = static[16:32, :].astype(F32)
-    row = lax.broadcasted_iota(jnp.int32, low.shape, 0)
-    for at, part in enumerate(tuple(first) + tuple(second)):
-        low = jnp.where(row == 3 + at, part, low)
-    out[16:32, :] = low.astype(BF16)
-
-
-def pieces(potential):
-    return split(potential - 1.0)
-
-
-ONES = (1.0, 1.0, 1.0)
-
-
-def scores(left, right):
-    return lax.dot_general(left, right, (((0,), (0,)), ((), ())), preferred_element_type=F32)
+def lower_half(low, static, first=None, second=None):
+    low[...] = static[16:32, :].astype(F32)
+    for start, parts in ((3, first), (6, second)):
+        for at, part in enumerate(parts or ()):
+            low[start + at : start + at + 1, :] = part
+    return low[...].astype(BF16)
+
+
+def turn(turned, low, static, first, second=None):
+    turned[...] = jnp.concatenate([static[0:16, :], lower_half(low, static, first, second)], axis=0).T
 
 
 def start_of(index):
@@ -233,64 +223,57 @@
     return copy
 
 
-def turn(out, operand):
-    out[...] = operand[...].T
-
-
 def sides(xc, yc):
     return xc.shape[1] // CLUSTER, yc.shape[1] // CLUSTER
 
 
 def first_row_kernel(
-    points, sources, targets, xc_out, yc_out, part_out, lists_out, lists, sem, stack, red, turned, top, total
+    points, sources, targets, xc_out, yc_out, part_out, lists_out, log_source, log_target,
+    lists, sem, stack, low, turned, top, total,
 ):
     cps, cpt = sides(xc_out, yc_out)
     count = points[9:10, 0:1].astype(jnp.int32)
     lists_out[...] = (count.reshape(1, 1, 1) * cpt + targets[...]) * cps + sources[...]
     copy = fetch(lists_out, lists, sem)
+    log_source[...] = log2(points[6:7, :])
+    log_target[...] = log2(points[7:8, :])
     xs, ys = points[0:3, :], points[3:6, :]
     place(stack, split(ys * KAPPA), TARGET_ORDER)
     yc_out[...] = stack[...].astype(BF16)
-    potential = log2(points[7:8, :]) + KAPPA * (points[8:9, :] - half_square(ys))
-    with_rows(red, yc_out, pieces(potential))
-    turn(turned, red)
+    turn(turned, low, yc_out, split(log_target[...] + KAPPA * (points[8:9, :] - half_square(ys))))
     place(stack, split(xs), SOURCE_ORDER)
     xc_out[...] = stack[...].astype(BF16)
     copy.wait()
     part_out[...] = lse_tiles(Tiles(lists, sides(xc_out, yc_out), True), turned, xc_out, top, total)
 
 
-def col_kernel(parts, points, xc, yc, lists_in, part_out, lists, sem, red, turned, top, total):
+def col_kernel(parts, log_source, xc, yc, lists_in, part_out, lists, sem, low, turned, top, total):
     copy = fetch(lists_in, lists, sem)
-    potential = log2(points[6:7, :]) - combine([ref[...] for ref in parts])[0]
-    with_rows(red, xc, pieces(potential))
-    turn(turned, red)
+    turn(turned, low, xc, split(log_source[...] - combine([ref[...] for ref in parts])[0]))
     copy.wait()
-    part_out[...] = lse_tiles(Tiles(lists, sides(xc, yc), False), turned, yc, top, total)
-
-
-def row_kernel(parts, points, xc, yc, lists_in, part_out, lists, sem, red, turned, top, total):
+    part_out[...] = lse_tiles(Tiles(lists, sides(xc, yc), False), turned, yc, top, total, chunk=256)
+
+
+def row_kernel(parts, log_target, xc, yc, lists_in, part_out, lists, sem, low, turned, top, total):
     copy = fetch(lists_in, lists, sem)
-    potential = log2(points[7:8, :]) - combine([ref[...] for ref in parts])[0]
-    with_rows(red, yc, pieces(potential))
-    turn(turned, red)
+    turn(turned, low, yc, split(log_target[...] - combine([ref[...] for ref in parts])[0]))
     copy.wait()
     part_out[...] = lse_tiles(Tiles(lists, sides(xc, yc), True), turned, xc, top, total)
 
 
 def last_col_kernel(
-    parts, points, xc, yc, lists_in, f_out, u_out, part_out, lists, sem, red, turned, top, sums, columns, f, sem_out
+    parts, log_source, points, xc, yc, lists_in, f_out, u_out, part_out,
+    lists, sem, low, turned, top, sums, columns, f, sem_out,
 ):
     copy = fetch(lists_in, lists, sem)
     u = -combine([ref[...] for ref in parts])[0]
-    u_out[...] = u
+    u_out[...] = log_source[...] + u
     f[...] = u * (1.0 / KAPPA) + half_square(points[0:3, :])
     back = fetch(f, f_out, sem_out)
-    with_rows(red, xc, pieces(log2(points[6:7, :]) + u))
-    turn(turned, red)
+    turn(turned, low, xc, split(u_out[...]))
     copy.wait()
     tiles = Tiles(lists, sides(xc, yc), False)
-    for r, row in enumerate(mean_tiles(tiles, turned, yc, columns, points, 0, top, sums, unroll=4)):
+    for r, row in enumerate(mean_tiles(tiles, turned, yc, columns, points, 0, top, sums)):
         part_out[r : r + 1, :] = row
     back.wait()
 
@@ -307,9 +290,9 @@
 
 
 def gradient_kernel(
-    parts, u, points, xc, yc, lists_in, g_out, target_out, *rest, shares
+    parts, u, log_target, points, xc, yc, lists_in, g_out, target_out, *rest, shares
 ):
-    source_out, (lists, sem, red, turned, kept, sums, columns, g, target, whole, sems) = rest[:shares], rest[shares:]
+    source_out, (lists, sem, low, turned, kept, sums, columns, g, target, whole, sems) = rest[:shares], rest[shares:]
     copy = fetch(lists_in, lists, sem)
     lse, *means = merged(parts)
     xs, ys = points[0:3, :], points[3:6, :]
@@ -317,12 +300,12 @@
     for c in range(3):
         target[c : c + 1, :] = points[7:8, :] * (ys[c : c + 1, :] - means[c])
     back = [fetch(g, g_out, sems.at[0]), fetch(target, target_out, sems.at[1])]
-    with_rows(red, yc, pieces(log2(points[7:8, :]) - lse), ONES)
-    turn(turned, red)
-    with_rows(kept, xc, ONES, split(log2(points[6:7, :]) + u[...]))
+    turn(turned, low, yc, split(log_target[...] - lse), [jnp.ones_like(lse)] * 3)
+    kept[0:16, :] = xc[0:16, :]
+    kept[16:32, :] = lower_half(low, xc, None, split(u[...]))
     copy.wait()
     tiles = Tiles(lists, sides(xc, yc), True)
-    mass, *moved = plan_tiles(tiles, turned, kept, columns, points, 3, sums, unroll=4)
+    mass, *moved = plan_tiles(tiles, turned, kept, columns, points, 3, sums)
     for c in range(3):
         whole[c : c + 1, :] = xs[c : c + 1, :] * mass - moved[c]
     place_tgt = lax.axis_index("tgt")
@@ -404,7 +387,7 @@
         return [
             pltpu.SMEM(tile_source.shape, jnp.int32),
             pltpu.SemaphoreType.DMA,
-            pltpu.VMEM((DEPTH, red), BF16),
+            pltpu.VMEM((DEPTH // 2, red), F32),
             pltpu.VMEM((red, DEPTH), BF16),
         ]
 
@@ -412,18 +395,18 @@
         return [pltpu.VMEM((8, kept), F32), pltpu.VMEM((8, kept), F32)]
 
     first = work(nt)
-    xc, yc, part, *lists = call(
+    xc, yc, part, lists, log_source, log_target = call(
         first_row_kernel,
         (points, *given),
         (),
-        [split_rows(ns), split_rows(nt), rows(ns, 1), jax.ShapeDtypeStruct(tile_source.shape, jnp.int32)],
+        [split_rows(ns), split_rows(nt), rows(ns, 1), jax.ShapeDtypeStruct(tile_source.shape, jnp.int32), rows(ns, 1), rows(nt, 1)],
         first[:2] + [pltpu.VMEM((DEPTH, ns), F32)] + first[2:] + state(ns),
     )
-    known = (points, xc, yc)
+    known, lists = (xc, yc), (lists,)
     parts = exchange([part] * n_tgt, "tgt")
     (part,) = call(
         bunch(col_kernel, n_tgt),
-        (*parts, *known),
+        (*parts, log_source, *known),
         lists,
         [rows(nt, 1)],
         work(ns) + state(nt),
@@ -431,7 +414,7 @@
     parts = sum_up(part, "src")
     (part,) = call(
         bunch(row_kernel, len(parts)),
-        (*parts, *known),
+        (*parts, log_target, *known),
         lists,
         [rows(ns, 1)],
         work(nt) + state(ns),
@@ -439,7 +422,7 @@
     parts = exchange([part] * n_tgt, "tgt")
     f, u, part = call(
         bunch(last_col_kernel, n_tgt),
-        (*parts, *known),
+        (*parts, log_source, points, *known),
         lists,
         [rows(ns, 1), rows(ns, 1), rows(nt, 4)],
         work(ns)
@@ -455,7 +438,7 @@
     parts = sum_up(part, "src")
     g, target_grad, *parts = call(
         bunch(functools.partial(gradient_kernel, shares=n_tgt), len(parts)),
-        (*parts, u, *known),
+        (*parts, u, log_target, points, *known),
         lists,
         [rows(nt, 1), rows(nt, 3)] + [rows(ns // n_tgt, 3)] * n_tgt,
         work(nt)

time: 65.2 us -> 64.9 us (level); the launches traced: 65.4 us -> 64 us
  Pallas kernels: 24.3 us -> 23.6 us
  starting transfers between devices: 19.5 us -> 18.8 us
    pallas_call x7, Pallas kernels: 24.3 us -> 23.6 us  [call(): pl.pallas_call(kernel, out_shape=outs, in_specs=[VMEM] * len(ins) + [HBM]...]
    ppermute x8, starting transfers between devices: 12.5 us -> 11.8 us  [sum_up(): lax.ppermute(value, axis, [(i, i ^ k) for i in range(n)])]
  transfers between devices with their start and end apart: 17 -> 17, of which waited for: 12 -> 13; matrix products, arithmetic and copies ran while one was open for 0% -> 0% of each run, Pallas kernels for 0% -> 0%
where the time goes in v6:
time: 64.9 us; the launch traced here: 64 us
  Pallas kernels  23.6 us (36%)
  starting transfers between devices  18.8 us (29%)
  waiting for transfers between devices  18.6 us (29%)
  other arithmetic  1.65 us (3%)
  between operations  1.39 us (2%)
    pallas_call x7, Pallas kernels, call(): pl.pallas_call(kernel, out_shape=outs, in_specs=[VMEM] * len(ins) + [HBM]...  23.6 us
    ppermute x8, starting transfers between devices, sum_up(): lax.ppermute(value, axis, [(i, i ^ k) for i in range(n)])  11.8 us
    ppermute x8, waiting for transfers between devices, sum_up(): lax.ppermute(value, axis, [(i, i ^ k) for i in range(n)])  11.4 us
    ppermute x9, waiting for transfers between devices, exchange(): lax.ppermute(values[k], axis, [(i, peer(i, k, n)) for i in range(n)])  7.22 us
    ppermute x9, starting transfers between devices, exchange(): lax.ppermute(values[k], axis, [(i, peer(i, k, n)) for i in range(n)])  6.98 us
  transfers between devices with their start and end apart: 17, of which 13 were waited for; matrix products, arithmetic and copies ran while one was open for 0% of the time, Pallas kernels for 0%

profile of v6, /device:TPU:0, one launch (start us, length us, event | category | flops | bytes accessed | tf_op | source)
XLA Modules:
  0.0 64.0 jit_solution(833502336748184211)
XLA Ops:
  1.3 0.0 copy-start
  1.3 0.0 copy-start.1
  1.3 1.0 %convert_add_fusion.points.refs_5_.refs_4_ = f32[10,4096]{1,0:T(8,128)S(1)} fusion(s32[1,1]{1,0:T(1,128)S(6)} %copy.12, f32[1,4096]{1,0:T(1,128)} %bitcast.5, f32[1,4096]{1,0:T(1,128)} %bitcast.6, f32[1,4096]{1,0:T(1,128)} %bitcast.7, f32[3,4096]{1,0:T(4,128)} %param.9, f32[3,4096]{1,0:T(4,128)} %param.8), kind=kLoop, calls=%fused_computation | loop fusion | flops 245760 | bytes 311300 | tf_op jit(solution)/shard_map/add | solution.py:368
  2.3 0.0 copy-done
  2.3 0.0 copy-done.1
  2.4 3.4 %shard_map.111 = (bf16[32,4096]{1,0:T(8,128)(2,1)S(1)}, bf16[32,4096]{1,0:T(8,128)(2,1)S(1)}, f32[1,4096]{1,0:T(1,128)S(1)}, s32[1,1,12]{2,1,0:T(1,128)S(1)}, f3...) custom-call(f32[10,4096]{1,0:T(8,128)S(1)} %convert_add_fusion.points.refs_5_.refs_4_, s32[1,1,12]{2,1,0:T(1,128)S(1)} %copy-done, ...), custom_call_target="tpu_custom_call" | custom-call | tf_op jit(solution)/shard_map/pallas_call | solution.py:325
  5.8 2.4 %collective-permute-start.2 = (f32[1,4096]{1,0:T(1,128)S(1)}, f32[1,4096]{1,0:T(1,128)S(1)}, u32[]{:S(2)}, u32[]{:S(2)}) collective-permute-start(f32[1,4096]{1,0:T(1,128)S(1)} %get-tuple-element.19.refs_0_), channel_id=1, source_target_pairs={{0,3},{1,2},{2,1},{3,0},{4,7},{5,6},{6,5},{7,4},{8,11},{9,10},{10,... | collective-permute-start | bytes 49160 | tf_op jit(solution)/shard_map/ppermute | solution.py:342
  8.2 0.7 %collective-permute-start.1 = (f32[1,4096]{1,0:T(1,128)S(1)}, f32[1,4096]{1,0:T(1,128)S(1)}, u32[]{:S(2)}, u32[]{:S(2)}) collective-permute-start(f32[1,4096]{1,0:T(1,128)S(1)} %get-tuple-element.19.refs_0_), channel_id=1, source_target_pairs={{0,2},{1,3},{2,0},{3,1},{4,6},{5,7},{6,4},{7,5},{8,10},{9,11},{10,... | collective-permute-start | bytes 49160 | tf_op jit(solution)/shard_map/ppermute | solution.py:342
  8.8 0.0 collective-permute-start
  8.9 0.8 %collective-permute-done.2.refs_3_ = f32[1,4096]{1,0:T(1,128)S(1)} collective-permute-done((f32[1,4096]{1,0:T(1,128)S(1)}, f32[1,4096]{1,0:T(1,128)S(1)}, u32[]{:S(2)}, u32[]{:S(2)}) %collective-permute-start.2) | collective-permute-done | bytes 16416 | tf_op jit(solution)/shard_map/ppermute | solution.py:342
  9.6 2.3 %collective-permute-done.1.refs_2_ = f32[1,4096]{1,0:T(1,128)S(1)} collective-permute-done((f32[1,4096]{1,0:T(1,128)S(1)}, f32[1,4096]{1,0:T(1,128)S(1)}, u32[]{:S(2)}, u32[]{:S(2)}) %collective-permute-start.1) | collective-permute-done | bytes 16416 | tf_op jit(solution)/shard_map/ppermute | solution.py:342
  11.9 0.0 collective-permute-done.refs_1_
  11.9 3.4 %shard_map.112.refs_0_ = f32[1,4096]{1,0:T(1,128)S(1)} custom-call(f32[1,4096]{1,0:T(1,128)S(1)} %get-tuple-element.19.refs_0_, f32[1,4096]{1,0:T(1,128)S(1)} %collective-permute-done.refs_1_, f32[1,4096]{1,0:T(1,128)S(1)} %collective-permute-done.1.refs_2_, f32[1,4096]{1,0:T(1,128)S(1)} %collective-permute-done.2.refs_3_, ...), custom_call_target="tpu_custom_call" | custom-call | tf_op jit(solution)/shard_map/pallas_call | solution.py:325
  15.3 1.7 %collective-permute-start.5 = (f32[1,4096]{1,0:T(1,128)S(1)}, f32[1,4096]{1,0:T(1,128)S(1)}, u32[]{:S(2)}, u32[]{:S(2)}) collective-permute-start(f32[1,4096]{1,0:T(1,128)S(1)} %shard_map.112.refs_0_), channel_id=1, source_target_pairs={{0,12},{4,8},{8,4},{12,0},{16,28},{20,24},{24,20},{28,16},{1,13},{... | collective-permute-start | bytes 49160 | tf_op jit(solution)/shard_map/ppermute | solution.py:351
  17.1 1.3 %collective-permute-start.4 = (f32[1,4096]{1,0:T(1,128)S(1)}, f32[1,4096]{1,0:T(1,128)S(1)}, u32[]{:S(2)}, u32[]{:S(2)}) collective-permute-start(f32[1,4096]{1,0:T(1,128)S(1)} %shard_map.112.refs_0_), channel_id=1, source_target_pairs={{0,8},{4,12},{8,0},{12,4},{16,24},{20,28},{24,16},{28,20},{1,9},{5... | collective-permute-start | bytes 49160 | tf_op jit(solution)/shard_map/ppermute | solution.py:351
  18.4 0.5 collective-permute-start.3
  18.9 1.2 %collective-permute-done.5.refs_3_ = f32[1,4096]{1,0:T(1,128)S(1)} collective-permute-done((f32[1,4096]{1,0:T(1,128)S(1)}, f32[1,4096]{1,0:T(1,128)S(1)}, u32[]{:S(2)}, u32[]{:S(2)}) %collective-permute-start.5) | collective-permute-done | bytes 16416 | tf_op jit(solution)/shard_map/ppermute | solution.py:351
  20.1 0.7 %collective-permute-done.4.refs_2_ = f32[1,4096]{1,0:T(1,128)S(1)} collective-permute-done((f32[1,4096]{1,0:T(1,128)S(1)}, f32[1,4096]{1,0:T(1,128)S(1)}, u32[]{:S(2)}, u32[]{:S(2)}) %collective-permute-start.4) | collective-permute-done | bytes 16416 | tf_op jit(solution)/shard_map/ppermute | solution.py:351
  20.8 1.3 %collective-permute-done.3.refs_1_ = f32[1,4096]{1,0:T(1,128)S(1)} collective-permute-done((f32[1,4096]{1,0:T(1,128)S(1)}, f32[1,4096]{1,0:T(1,128)S(1)}, u32[]{:S(2)}, u32[]{:S(2)}) %collective-permute-start.3) | collective-permute-done | bytes 16416 | tf_op jit(solution)/shard_map/ppermute | solution.py:351
  22.2 2.6 %collective-permute-start.6 = (f32[1,4096]{1,0:T(1,128)S(1)}, f32[1,4096]{1,0:T(1,128)S(1)}, u32[]{:S(2)}, u32[]{:S(2)}) collective-permute-start(f32[1,4096]{1,0:T(1,128)S(1)} %shard_map.113.refs_0_), channel_id=1, source_target_pairs={{0,16},{4,20},{8,24},{12,28},{16,0},{20,4},{24,8},{28,12},{1,17},{... | collective-permute-start | bytes 49160 | tf_op jit(solution)/shard_map/ppermute | solution.py:351
  24.8 2.1 %collective-permute-done.6.refs_1_ = f32[1,4096]{1,0:T(1,128)S(1)} collective-permute-done((f32[1,4096]{1,0:T(1,128)S(1)}, f32[1,4096]{1,0:T(1,128)S(1)}, u32[]{:S(2)}, u32[]{:S(2)}) %collective-permute-start.6) | collective-permute-done | bytes 16416 | tf_op jit(solution)/shard_map/ppermute | solution.py:351
  26.9 3.4 %shard_map.114.refs_0_ = f32[1,4096]{1,0:T(1,128)S(1)} custom-call(f32[1,4096]{1,0:T(1,128)S(1)} %shard_map.113.refs_0_, f32[1,4096]{1,0:T(1,128)S(1)} %collective-permute-done.6.refs_1_, f32[1,4096]{1,0:T(1,128)S(1)} %get-tuple-element.24.refs_2_.refs_3_, bf16[32,4096]{1,0:T(8,128)(2,1)S(1)} %get-tuple-element.21.refs_5_.refs_3_.refs_6_, ...), custom_call_target="tpu_custom_call" | custom-call | tf_op jit(solution)/shard_map/pallas_call | solution.py:325
  30.3 0.1 collective-permute-start.9
  30.3 0.7 %collective-permute-start.8 = (f32[1,4096]{1,0:T(1,128)S(1)}, f32[1,4096]{1,0:T(1,128)S(1)}, u32[]{:S(2)}, u32[]{:S(2)}) collective-permute-start(f32[1,4096]{1,0:T(1,128)S(1)} %shard_map.114.refs_0_), channel_id=1, source_target_pairs={{0,2},{1,3},{2,0},{3,1},{4,6},{5,7},{6,4},{7,5},{8,10},{9,11},{10,... | collective-permute-start | bytes 49160 | tf_op jit(solution)/shard_map/ppermute | solution.py:342
  31.0 1.2 %collective-permute-start.7 = (f32[1,4096]{1,0:T(1,128)S(1)}, f32[1,4096]{1,0:T(1,128)S(1)}, u32[]{:S(2)}, u32[]{:S(2)}) collective-permute-start(f32[1,4096]{1,0:T(1,128)S(1)} %shard_map.114.refs_0_), channel_id=1, source_target_pairs={{0,1},{1,0},{2,3},{3,2},{4,5},{5,4},{6,7},{7,6},{8,9},{9,8},{10,11... | collective-permute-start | bytes 49160 | tf_op jit(solution)/shard_map/ppermute | solution.py:342
  32.2 1.3 %collective-permute-done.9.refs_3_ = f32[1,4096]{1,0:T(1,128)S(1)} collective-permute-done((f32[1,4096]{1,0:T(1,128)S(1)}, f32[1,4096]{1,0:T(1,128)S(1)}, u32[]{:S(2)}, u32[]{:S(2)}) %collective-permute-start.9) | collective-permute-done | bytes 16416 | tf_op jit(solution)/shard_map/ppermute | solution.py:342
  33.5 0.7 %collective-permute-done.8.refs_2_ = f32[1,4096]{1,0:T(1,128)S(1)} collective-permute-done((f32[1,4096]{1,0:T(1,128)S(1)}, f32[1,4096]{1,0:T(1,128)S(1)}, u32[]{:S(2)}, u32[]{:S(2)}) %collective-permute-start.8) | collective-permute-done | bytes 16416 | tf_op jit(solution)/shard_map/ppermute | solution.py:342
  34.1 0.0 collective-permute-done.7.refs_1_
  34.1 7.2 %shard_map.115 = (f32[1,4096]{1,0:T(1,128)}, f32[1,4096]{1,0:T(1,128)S(1)}, f32[4,4096]{1,0:T(4,128)S(1)}) custom-call(f32[1,4096]{1,0:T(1,128)S(1)} %shard_map.114.refs_0_, f32[1,4096]{1,0:T(1,128)S(1)} %collective-permute-done.7.refs_1_, f32[1,4096]{1,0:T(1,128)S(1)} %collective-permute-done.8.refs_2_, f32[1,4096]{1,0:T(1,128)S(1)} %collective-permute-done.9.refs_3_, ...), custom_call_target="tpu_custom_call" | custom-call | tf_op jit(solution)/shard_map/pallas_call | solution.py:325
  41.3 1.6 %collective-permute-start.12 = (f32[4,4096]{1,0:T(4,128)S(1)}, f32[4,4096]{1,0:T(4,128)S(1)}, u32[]{:S(2)}, u32[]{:S(2)}) collective-permute-start(f32[4,4096]{1,0:T(4,128)S(1)} %get-tuple-element.26.refs_0_), channel_id=1, source_target_pairs={{0,12},{4,8},{8,4},{12,0},{16,28},{20,24},{24,20},{28,16},{1,13},{... | collective-permute-start | bytes 196616 | tf_op jit(solution)/shard_map/ppermute | solution.py:351
  42.9 0.4 collective-permute-start.11
  43.3 1.6 %collective-permute-start.10 = (f32[4,4096]{1,0:T(4,128)S(1)}, f32[4,4096]{1,0:T(4,128)S(1)}, u32[]{:S(2)}, u32[]{:S(2)}) collective-permute-start(f32[4,4096]{1,0:T(4,128)S(1)} %get-tuple-element.26.refs_0_), channel_id=1, source_target_pairs={{0,4},{4,0},{8,12},{12,8},{16,20},{20,16},{24,28},{28,24},{1,5},{5... | collective-permute-start | bytes 196616 | tf_op jit(solution)/shard_map/ppermute | solution.py:351
  44.9 2.3 %collective-permute-done.12.refs_3_ = f32[4,4096]{1,0:T(4,128)S(1)} collective-permute-done((f32[4,4096]{1,0:T(4,128)S(1)}, f32[4,4096]{1,0:T(4,128)S(1)}, u32[]{:S(2)}, u32[]{:S(2)}) %collective-permute-start.12) | collective-permute-done | bytes 65568 | tf_op jit(solution)/shard_map/ppermute | solution.py:351
  47.2 0.0 collective-permute-done.11.refs_2_
  47.2 0.6 collective-permute-done.10.refs_1_
  47.8 2.1 %collective-permute-start.13 = (f32[4,4096]{1,0:T(4,128)S(1)}, f32[4,4096]{1,0:T(4,128)S(1)}, u32[]{:S(2)}, u32[]{:S(2)}) collective-permute-start(f32[4,4096]{1,0:T(4,128)S(1)} %shard_map.116.refs_0_), channel_id=1, source_target_pairs={{0,16},{4,20},{8,24},{12,28},{16,0},{20,4},{24,8},{28,12},{1,17},{... | collective-permute-start | bytes 196616 | tf_op jit(solution)/shard_map/ppermute | solution.py:351
  49.9 3.2 %collective-permute-done.13.refs_1_ = f32[4,4096]{1,0:T(4,128)S(1)} collective-permute-done((f32[4,4096]{1,0:T(4,128)S(1)}, f32[4,4096]{1,0:T(4,128)S(1)}, u32[]{:S(2)}, u32[]{:S(2)}) %collective-permute-start.13) | collective-permute-done | bytes 65568 | tf_op jit(solution)/shard_map/ppermute | solution.py:351
  53.0 6.2 %shard_map.117 = (f32[1,4096]{1,0:T(1,128)}, f32[3,4096]{1,0:T(4,128)}, f32[3,1024]{1,0:T(4,128)S(1)}, f32[3,1024]{1,0:T(4,128)S(1)}, f32[3,1024]{1,0:T(4,128)S(1)}, /*index=5*/f32[3,1024]{1,0:T(4,128)S(1)}) custom-call(f32[4,4096]{1,0:T(4,128)S(1)} %shard_map.116.refs_0_, f32[4,4096]{1,0:T(4,128)S(1)} %collective-permute-done.13.refs_1_, ...), custom_call_target="tpu_custom_call" | custom-call | tf_op jit(solution)/shard_map/pallas_call | solution.py:325
  59.2 0.1 collective-permute-start.14
  59.3 0.9 %collective-permute-start.15 = (f32[3,1024]{1,0:T(4,128)S(1)}, f32[3,1024]{1,0:T(4,128)S(1)}, u32[]{:S(2)}, u32[]{:S(2)}) collective-permute-start(f32[3,1024]{1,0:T(4,128)S(1)} %get-tuple-element.31), channel_id=1, source_target_pairs={{0,2},{1,3},{2,0},{3,1},{4,6},{5,7},{6,4},{7,5},{8,10},{9,11},{10,... | collective-permute-start | bytes 36872 | tf_op jit(solution)/shard_map/ppermute | solution.py:342
  60.2 1.0 %collective-permute-start.16 = (f32[3,1024]{1,0:T(4,128)S(1)}, f32[3,1024]{1,0:T(4,128)S(1)}, u32[]{:S(2)}, u32[]{:S(2)}) collective-permute-start(f32[3,1024]{1,0:T(4,128)S(1)} %get-tuple-element.32), channel_id=1, source_target_pairs={{0,3},{1,2},{2,1},{3,0},{4,7},{5,6},{6,5},{7,4},{8,11},{9,10},{10,... | collective-permute-start | bytes 36872 | tf_op jit(solution)/shard_map/ppermute | solution.py:342
  61.2 0.0 collective-permute-done.14
  61.2 1.9 %collective-permute-done.15 = f32[3,1024]{1,0:T(4,128)S(1)} collective-permute-done((f32[3,1024]{1,0:T(4,128)S(1)}, f32[3,1024]{1,0:T(4,128)S(1)}, u32[]{:S(2)}, u32[]{:S(2)}) %collective-permute-start.15) | collective-permute-done | bytes 12320 | tf_op jit(solution)/shard_map/ppermute | solution.py:342
  63.1 0.3 collective-permute-done.16
  63.4 0.6 add_add_fusion
  (2 shorter events, 0.1 us)
Async XLA Ops:
  1.3 1.1 %copy-start = (s32[1,1,12]{2,1,0:T(1,128)S(1)}, s32[1,1,12]{2,1,0:T(1,128)}, u32[]{:S(2)}) copy-start(s32[1,1,12]{2,1,0:T(1,128)} %sources.1) | copy-start | bytes 148
  1.3 1.1 %copy-start.1 = (s32[1,1,12]{2,1,0:T(1,128)S(1)}, s32[1,1,12]{2,1,0:T(1,128)}, u32[]{:S(2)}) copy-start(s32[1,1,12]{2,1,0:T(1,128)} %targets.1) | copy-start | bytes 148
  5.8 3.9 %collective-permute-start.2 = (f32[1,4096]{1,0:T(1,128)S(1)}, f32[1,4096]{1,0:T(1,128)S(1)}, u32[]{:S(2)}, u32[]{:S(2)}) collective-permute-start(f32[1,4096]{1,0:T(1,128)S(1)} %get-tuple-element.19.refs_0_), channel_id=1, source_target_pairs={{0,3},{1,2},{2,1},{3,0},{4,7},{5,6},{6,5},{7,4},{8,11},{9,10},{10,... | collective-permute-start | bytes 49160 | tf_op jit(solution)/shard_map/ppermute | solution.py:342
  8.2 3.7 %collective-permute-start.1 = (f32[1,4096]{1,0:T(1,128)S(1)}, f32[1,4096]{1,0:T(1,128)S(1)}, u32[]{:S(2)}, u32[]{:S(2)}) collective-permute-start(f32[1,4096]{1,0:T(1,128)S(1)} %get-tuple-element.19.refs_0_), channel_id=1, source_target_pairs={{0,2},{1,3},{2,0},{3,1},{4,6},{5,7},{6,4},{7,5},{8,10},{9,11},{10,... | collective-permute-start | bytes 49160 | tf_op jit(solution)/shard_map/ppermute | solution.py:342
  8.8 3.1 %collective-permute-start = (f32[1,4096]{1,0:T(1,128)S(1)}, f32[1,4096]{1,0:T(1,128)S(1)}, u32[]{:S(2)}, u32[]{:S(2)}) collective-permute-start(f32[1,4096]{1,0:T(1,128)S(1)} %get-tuple-element.19.refs_0_), channel_id=1, source_target_pairs={{0,1},{1,0},{2,3},{3,2},{4,5},{5,4},{6,7},{7,6},{8,9},{9,8},{10,11... | collective-permute-start | bytes 49160 | tf_op jit(solution)/shard_map/ppermute | solution.py:342
  15.3 4.8 %collective-permute-start.5 = (f32[1,4096]{1,0:T(1,128)S(1)}, f32[1,4096]{1,0:T(1,128)S(1)}, u32[]{:S(2)}, u32[]{:S(2)}) collective-permute-start(f32[1,4096]{1,0:T(1,128)S(1)} %shard_map.112.refs_0_), channel_id=1, source_target_pairs={{0,12},{4,8},{8,4},{12,0},{16,28},{20,24},{24,20},{28,16},{1,13},{... | collective-permute-start | bytes 49160 | tf_op jit(solution)/shard_map/ppermute | solution.py:351
  17.1 3.7 %collective-permute-start.4 = (f32[1,4096]{1,0:T(1,128)S(1)}, f32[1,4096]{1,0:T(1,128)S(1)}, u32[]{:S(2)}, u32[]{:S(2)}) collective-permute-start(f32[1,4096]{1,0:T(1,128)S(1)} %shard_map.112.refs_0_), channel_id=1, source_target_pairs={{0,8},{4,12},{8,0},{12,4},{16,24},{20,28},{24,16},{28,20},{1,9},{5... | collective-permute-start | bytes 49160 | tf_op jit(solution)/shard_map/ppermute | solution.py:351
  18.4 3.7 %collective-permute-start.3 = (f32[1,4096]{1,0:T(1,128)S(1)}, f32[1,4096]{1,0:T(1,128)S(1)}, u32[]{:S(2)}, u32[]{:S(2)}) collective-permute-start(f32[1,4096]{1,0:T(1,128)S(1)} %shard_map.112.refs_0_), channel_id=1, source_target_pairs={{0,4},{4,0},{8,12},{12,8},{16,20},{20,16},{24,28},{28,24},{1,5},{5... | collective-permute-start | bytes 49160 | tf_op jit(solution)/shard_map/ppermute | solution.py:351
  22.2 4.7 %collective-permute-start.6 = (f32[1,4096]{1,0:T(1,128)S(1)}, f32[1,4096]{1,0:T(1,128)S(1)}, u32[]{:S(2)}, u32[]{:S(2)}) collective-permute-start(f32[1,4096]{1,0:T(1,128)S(1)} %shard_map.113.refs_0_), channel_id=1, source_target_pairs={{0,16},{4,20},{8,24},{12,28},{16,0},{20,4},{24,8},{28,12},{1,17},{... | collective-permute-start | bytes 49160 | tf_op jit(solution)/shard_map/ppermute | solution.py:351
  30.3 3.2 %collective-permute-start.9 = (f32[1,4096]{1,0:T(1,128)S(1)}, f32[1,4096]{1,0:T(1,128)S(1)}, u32[]{:S(2)}, u32[]{:S(2)}) collective-permute-start(f32[1,4096]{1,0:T(1,128)S(1)} %shard_map.114.refs_0_), channel_id=1, source_target_pairs={{0,3},{1,2},{2,1},{3,0},{4,7},{5,6},{6,5},{7,4},{8,11},{9,10},{10,... | collective-permute-start | bytes 49160 | tf_op jit(solution)/shard_map/ppermute | solution.py:342
  30.3 3.8 %collective-permute-start.8 = (f32[1,4096]{1,0:T(1,128)S(1)}, f32[1,4096]{1,0:T(1,128)S(1)}, u32[]{:S(2)}, u32[]{:S(2)}) collective-permute-start(f32[1,4096]{1,0:T(1,128)S(1)} %shard_map.114.refs_0_), channel_id=1, source_target_pairs={{0,2},{1,3},{2,0},{3,1},{4,6},{5,7},{6,4},{7,5},{8,10},{9,11},{10,... | collective-permute-start | bytes 49160 | tf_op jit(solution)/shard_map/ppermute | solution.py:342
  31.0 3.1 %collective-permute-start.7 = (f32[1,4096]{1,0:T(1,128)S(1)}, f32[1,4096]{1,0:T(1,128)S(1)}, u32[]{:S(2)}, u32[]{:S(2)}) collective-permute-start(f32[1,4096]{1,0:T(1,128)S(1)} %shard_map.114.refs_0_), channel_id=1, source_target_pairs={{0,1},{1,0},{2,3},{3,2},{4,5},{5,4},{6,7},{7,6},{8,9},{9,8},{10,11... | collective-permute-start | bytes 49160 | tf_op jit(solution)/shard_map/ppermute | solution.py:342
  41.3 5.9 %collective-permute-start.12 = (f32[4,4096]{1,0:T(4,128)S(1)}, f32[4,4096]{1,0:T(4,128)S(1)}, u32[]{:S(2)}, u32[]{:S(2)}) collective-permute-start(f32[4,4096]{1,0:T(4,128)S(1)} %get-tuple-element.26.refs_0_), channel_id=1, source_target_pairs={{0,12},{4,8},{8,4},{12,0},{16,28},{20,24},{24,20},{28,16},{1,13},{... | collective-permute-start | bytes 196616 | tf_op jit(solution)/shard_map/ppermute | solution.py:351
  42.9 4.3 %collective-permute-start.11 = (f32[4,4096]{1,0:T(4,128)S(1)}, f32[4,4096]{1,0:T(4,128)S(1)}, u32[]{:S(2)}, u32[]{:S(2)}) collective-permute-start(f32[4,4096]{1,0:T(4,128)S(1)} %get-tuple-element.26.refs_0_), channel_id=1, source_target_pairs={{0,8},{4,12},{8,0},{12,4},{16,24},{20,28},{24,16},{28,20},{1,9},{5... | collective-permute-start | bytes 196616 | tf_op jit(solution)/shard_map/ppermute | solution.py:351
  43.3 4.5 %collective-permute-start.10 = (f32[4,4096]{1,0:T(4,128)S(1)}, f32[4,4096]{1,0:T(4,128)S(1)}, u32[]{:S(2)}, u32[]{:S(2)}) collective-permute-start(f32[4,4096]{1,0:T(4,128)S(1)} %get-tuple-element.26.refs_0_), channel_id=1, source_target_pairs={{0,4},{4,0},{8,12},{12,8},{16,20},{20,16},{24,28},{28,24},{1,5},{5... | collective-permute-start | bytes 196616 | tf_op jit(solution)/shard_map/ppermute | solution.py:351
  47.8 5.2 %collective-permute-start.13 = (f32[4,4096]{1,0:T(4,128)S(1)}, f32[4,4096]{1,0:T(4,128)S(1)}, u32[]{:S(2)}, u32[]{:S(2)}) collective-permute-start(f32[4,4096]{1,0:T(4,128)S(1)} %shard_map.116.refs_0_), channel_id=1, source_target_pairs={{0,16},{4,20},{8,24},{12,28},{16,0},{20,4},{24,8},{28,12},{1,17},{... | collective-permute-start | bytes 196616 | tf_op jit(solution)/shard_map/ppermute | solution.py:351
  59.2 1.9 %collective-permute-start.14 = (f32[3,1024]{1,0:T(4,128)S(1)}, f32[3,1024]{1,0:T(4,128)S(1)}, u32[]{:S(2)}, u32[]{:S(2)}) collective-permute-start(f32[3,1024]{1,0:T(4,128)S(1)} %get-tuple-element.30), channel_id=1, source_target_pairs={{0,1},{1,0},{2,3},{3,2},{4,5},{5,4},{6,7},{7,6},{8,9},{9,8},{10,11... | collective-permute-start | bytes 36872 | tf_op jit(solution)/shard_map/ppermute | solution.py:342
  59.3 3.8 %collective-permute-start.15 = (f32[3,1024]{1,0:T(4,128)S(1)}, f32[3,1024]{1,0:T(4,128)S(1)}, u32[]{:S(2)}, u32[]{:S(2)}) collective-permute-start(f32[3,1024]{1,0:T(4,128)S(1)} %get-tuple-element.31), channel_id=1, source_target_pairs={{0,2},{1,3},{2,0},{3,1},{4,6},{5,7},{6,4},{7,5},{8,10},{9,11},{10,... | collective-permute-start | bytes 36872 | tf_op jit(solution)/shard_map/ppermute | solution.py:342
  60.2 3.2 %collective-permute-start.16 = (f32[3,1024]{1,0:T(4,128)S(1)}, f32[3,1024]{1,0:T(4,128)S(1)}, u32[]{:S(2)}, u32[]{:S(2)}) collective-permute-start(f32[3,1024]{1,0:T(4,128)S(1)} %get-tuple-element.32), channel_id=1, source_target_pairs={{0,3},{1,2},{2,1},{3,0},{4,7},{5,6},{6,5},{7,4},{8,11},{9,10},{10,... | collective-permute-start | bytes 36872 | tf_op jit(solution)/shard_map/ppermute | solution.py:342

commit v7 on v6

--- a/solution.py
+++ b/solution.py
@@ -14,7 +14,6 @@
 LOG2E = math.log2(math.e)
 DEPTH = 32
 FLOOR = -1e30
-EXTRAS = 4
 F32 = jnp.float32
 BF16 = jnp.bfloat16
 
@@ -66,7 +65,7 @@
     return value.reshape(value.shape[0] // 8, 8, value.shape[1])
 
 
-def each_tile(tiles, left, right, visit, first, more, unroll=8, ahead=1, chunk=128):
+def each_tile(tiles, left, right, visit, first, more, ahead=1, chunk=128):
     once = right.shape[1] // CLUSTER
 
     def group_states(group, fresh):
@@ -90,20 +89,12 @@
             states[which] = visit(scores[n], states[which], rows, fresh)
         return [(steps[which * (CLUSTER // chunk)][1], state) for which, state in enumerate(states)]
 
-    def several(at, carry):
-        for here, state in group_states([at * unroll + k for k in range(unroll)], True):
-            first(here, state)
-        return carry
-
-    def others(at, carry):
-        slots = [once + at * EXTRAS + k for k in range(EXTRAS)]
-        states = group_states([jnp.minimum(slot, tiles.slots - 1) for slot in slots], False)
-        for slot, (here, state) in zip(slots, states):
-            more(here, state, slot < tiles.count())
-        return carry
-
-    lax.fori_loop(0, once // unroll, several, 0)
-    lax.fori_loop(0, lax.div(tiles.count() - once + EXTRAS - 1, EXTRAS), others, 0)
+    slots = list(range(tiles.slots))
+    count = tiles.count()
+    for here, state in group_states(slots[:once], True):
+        first(here, state)
+    for slot, (here, state) in zip(slots[once:], group_states(slots[once:], False)):
+        more(here, state, slot < count)
 
 
 def lse_tiles(tiles, left, right, top, total, **how):
@@ -251,7 +242,7 @@
     copy = fetch(lists_in, lists, sem)
     turn(turned, low, xc, split(log_source[...] - combine([ref[...] for ref in parts])[0]))
     copy.wait()
-    part_out[...] = lse_tiles(Tiles(lists, sides(xc, yc), False), turned, yc, top, total, chunk=256)
+    part_out[...] = lse_tiles(Tiles(lists, sides(xc, yc), False), turned, yc, top, total)
 
 
 def row_kernel(parts, log_target, xc, yc, lists_in, part_out, lists, sem, low, turned, top, total):
@@ -289,20 +280,25 @@
         refs[-1][r : r + 1, :] = row
 
 
-def gradient_kernel(
-    parts, u, log_target, points, xc, yc, lists_in, g_out, target_out, *rest, shares
-):
-    source_out, (lists, sem, low, turned, kept, sums, columns, g, target, whole, sems) = rest[:shares], rest[shares:]
+def kept_kernel(u, xc, out, low):
+    out[0:16, :] = xc[0:16, :]
+    out[16:32, :] = lower_half(low, xc, None, split(u[...]))
+
+
+def target_kernel(parts, points, after, out):
+    means = merged(parts)[1:]
+    for c in range(3):
+        out[c : c + 1, :] = points[7:8, :] * (points[3 + c : 4 + c, :] - means[c])
+
+
+def gradient_kernel(parts, kept, log_target, points, xc, yc, lists_in, g_out, *rest, shares):
+    source_out, (lists, sem, low, turned, sums, columns, g, whole, sem_out) = rest[:shares], rest[shares:]
     copy = fetch(lists_in, lists, sem)
-    lse, *means = merged(parts)
-    xs, ys = points[0:3, :], points[3:6, :]
-    g[...] = half_square(ys) - lse * (1.0 / KAPPA)
-    for c in range(3):
-        target[c : c + 1, :] = points[7:8, :] * (ys[c : c + 1, :] - means[c])
-    back = [fetch(g, g_out, sems.at[0]), fetch(target, target_out, sems.at[1])]
+    lse = combine([ref[0:1, :] for ref in parts])[0]
+    xs = points[0:3, :]
+    g[...] = half_square(points[3:6, :]) - lse * (1.0 / KAPPA)
+    back = fetch(g, g_out, sem_out)
     turn(turned, low, yc, split(log_target[...] - lse), [jnp.ones_like(lse)] * 3)
-    kept[0:16, :] = xc[0:16, :]
-    kept[16:32, :] = lower_half(low, xc, None, split(u[...]))
     copy.wait()
     tiles = Tiles(lists, sides(xc, yc), True)
     mass, *moved = plan_tiles(tiles, turned, kept, columns, points, 3, sums)
@@ -313,8 +309,7 @@
         width = out.shape[1]
         at = pl.multiple_of(peer(place_tgt, k, shares) * width, width)
         out[...] = whole[:, pl.ds(at, width)]
-    for one in back:
-        one.wait()
+    back.wait()
 
 
 VMEM = pl.BlockSpec(memory_space=pltpu.VMEM)
@@ -435,25 +430,25 @@
         ],
         far=(0,),
     )
+    (kept,) = call(kept_kernel, (u, xc), (), [split_rows(ns)], [pltpu.VMEM((DEPTH // 2, ns), F32)])
     parts = sum_up(part, "src")
-    g, target_grad, *parts = call(
+    g, *moved = call(
         bunch(functools.partial(gradient_kernel, shares=n_tgt), len(parts)),
-        (*parts, u, log_target, points, *known),
+        (*parts, kept, log_target, points, *known),
         lists,
-        [rows(nt, 1), rows(nt, 3)] + [rows(ns // n_tgt, 3)] * n_tgt,
+        [rows(nt, 1)] + [rows(ns // n_tgt, 3)] * n_tgt,
         work(nt)
         + [
-            pltpu.VMEM((DEPTH, ns), BF16),
             pltpu.VMEM((4, 8, ns), F32),
             pltpu.VMEM((nt, 384), F32),
             pltpu.VMEM((1, nt), F32),
-            pltpu.VMEM((3, nt), F32),
             pltpu.VMEM((3, ns), F32),
-            pltpu.SemaphoreType.DMA((2,)),
+            pltpu.SemaphoreType.DMA,
         ],
-        far=(0, 1),
-    )
-    own_grad = functools.reduce(jnp.add, exchange(parts, "tgt"))
+        far=(0,),
+    )
+    (target_grad,) = call(bunch(target_kernel, len(parts)), (*parts, points, moved[0]), (), [rows(nt, 3)], [])
+    own_grad = functools.reduce(jnp.add, exchange(moved, "tgt"))
     return (f.reshape(-1), g.reshape(-1), own_grad, target_grad)
 
 

time: 64.9 us -> 63.8 us (0.983); the launches traced: 64 us -> 63.6 us
  waiting for transfers between devices: 18.6 us -> 17.6 us
    ppermute x8, waiting for transfers between devices: 11.4 us -> 10.7 us  [sum_up(): lax.ppermute(value, axis, [(i, i ^ k) for i in range(n)])]
    pallas_call x7 -> x9, Pallas kernels: 23.6 us -> 23.6 us  [call(): pl.pallas_call(kernel, out_shape=outs, in_specs=[VMEM] * len(ins) + [HBM]...]
  transfers between devices with their start and end apart: 17 -> 17, of which waited for: 13 -> 13; matrix products, arithmetic and copies ran while one was open for 0% -> 0% of each run, Pallas kernels for 0% -> 1%
where the time goes in v7:
time: 63.8 us; the launch traced here: 63.6 us
  Pallas kernels  23.6 us (37%)
  starting transfers between devices  19.4 us (30%)
  waiting for transfers between devices  17.6 us (28%)
  other arithmetic  1.65 us (3%)
  between operations  1.39 us (2%)
    pallas_call x9, Pallas kernels, call(): pl.pallas_call(kernel, out_shape=outs, in_specs=[VMEM] * len(ins) + [HBM]...  23.6 us
    ppermute x8, starting transfers between devices, sum_up(): lax.ppermute(value, axis, [(i, i ^ k) for i in range(n)])  12.4 us
    ppermute x8, waiting for transfers between devices, sum_up(): lax.ppermute(value, axis, [(i, i ^ k) for i in range(n)])  10.7 us
    ppermute x9, starting transfers between devices, exchange(): lax.ppermute(values[k], axis, [(i, peer(i, k, n)) for i in range(n)])  6.98 us
    ppermute x9, waiting for transfers between devices, exchange(): lax.ppermute(values[k], axis, [(i, peer(i, k, n)) for i in range(n)])  6.85 us
  transfers between devices with their start and end apart: 17, of which 13 were waited for; matrix products, arithmetic and copies ran while one was open for 0% of the time, Pallas kernels for 1%

profile of v7, /device:TPU:0, one launch (start us, length us, event | category | flops | bytes accessed | tf_op | source)
XLA Modules:
  0.0 63.6 jit_solution(7394412185680740801)
XLA Ops:
  1.3 0.0 copy-start
  1.3 0.0 copy-start.1
  1.3 1.0 %convert_add_fusion.points.refs_5_.refs_4_.refs_2_ = f32[10,4096]{1,0:T(8,128)S(1)} fusion(s32[1,1]{1,0:T(1,128)S(6)} %copy.12, f32[1,4096]{1,0:T(1,128)} %bitcast.5, f32[1,4096]{1,0:T(1,128)} %bitcast.6, f32[1,4096]{1,0:T(1,128)} %bitcast.7, f32[3,4096]{1,0:T(4,128)} %param.9, f32[3,4096]{1,0:T(4,128)} %param.8), kind=kLoop, calls=%fused_computation | loop fusion | flops 245760 | bytes 311300 | tf_op jit(solution)/shard_map/add | solution.py:363
  2.3 0.0 copy-done
  2.3 0.0 copy-done.1
  2.4 3.3 %shard_map.111 = (bf16[32,4096]{1,0:T(8,128)(2,1)S(1)}, bf16[32,4096]{1,0:T(8,128)(2,1)S(1)}, f32[1,4096]{1,0:T(1,128)S(1)}, s32[1,1,12]{2,1,0:T(1,128)S(1)}, f3...) custom-call(f32[10,4096]{1,0:T(8,128)S(1)} %convert_add_fusion.points.refs_5_.refs_4_.refs_2_, s32[1,1,12]{2,1,0:T(1,128)S(1)} %copy-done, ...), custom_call_target="tpu_custom_call" | custom-call | tf_op jit(solution)/shard_map/pallas_call | solution.py:320
  5.6 2.4 %collective-permute-start.2 = (f32[1,4096]{1,0:T(1,128)S(1)}, f32[1,4096]{1,0:T(1,128)S(1)}, u32[]{:S(2)}, u32[]{:S(2)}) collective-permute-start(f32[1,4096]{1,0:T(1,128)S(1)} %get-tuple-element.18.refs_0_), channel_id=1, source_target_pairs={{0,3},{1,2},{2,1},{3,0},{4,7},{5,6},{6,5},{7,4},{8,11},{9,10},{10,... | collective-permute-start | bytes 49160 | tf_op jit(solution)/shard_map/ppermute | solution.py:337
  8.1 0.7 %collective-permute-start.1 = (f32[1,4096]{1,0:T(1,128)S(1)}, f32[1,4096]{1,0:T(1,128)S(1)}, u32[]{:S(2)}, u32[]{:S(2)}) collective-permute-start(f32[1,4096]{1,0:T(1,128)S(1)} %get-tuple-element.18.refs_0_), channel_id=1, source_target_pairs={{0,2},{1,3},{2,0},{3,1},{4,6},{5,7},{6,4},{7,5},{8,10},{9,11},{10,... | collective-permute-start | bytes 49160 | tf_op jit(solution)/shard_map/ppermute | solution.py:337
  8.7 0.0 collective-permute-start
  8.8 0.7 %collective-permute-done.2.refs_3_ = f32[1,4096]{1,0:T(1,128)S(1)} collective-permute-done((f32[1,4096]{1,0:T(1,128)S(1)}, f32[1,4096]{1,0:T(1,128)S(1)}, u32[]{:S(2)}, u32[]{:S(2)}) %collective-permute-start.2) | collective-permute-done | bytes 16416 | tf_op jit(solution)/shard_map/ppermute | solution.py:337
  9.5 2.3 %collective-permute-done.1.refs_2_ = f32[1,4096]{1,0:T(1,128)S(1)} collective-permute-done((f32[1,4096]{1,0:T(1,128)S(1)}, f32[1,4096]{1,0:T(1,128)S(1)}, u32[]{:S(2)}, u32[]{:S(2)}) %collective-permute-start.1) | collective-permute-done | bytes 16416 | tf_op jit(solution)/shard_map/ppermute | solution.py:337
  11.8 0.0 collective-permute-done.refs_1_
  11.8 3.1 %shard_map.112.refs_0_ = f32[1,4096]{1,0:T(1,128)S(1)} custom-call(f32[1,4096]{1,0:T(1,128)S(1)} %get-tuple-element.18.refs_0_, f32[1,4096]{1,0:T(1,128)S(1)} %collective-permute-done.refs_1_, f32[1,4096]{1,0:T(1,128)S(1)} %collective-permute-done.1.refs_2_, f32[1,4096]{1,0:T(1,128)S(1)} %collective-permute-done.2.refs_3_, ...), custom_call_target="tpu_custom_call" | custom-call | tf_op jit(solution)/shard_map/pallas_call | solution.py:320
  14.9 2.6 %collective-permute-start.5 = (f32[1,4096]{1,0:T(1,128)S(1)}, f32[1,4096]{1,0:T(1,128)S(1)}, u32[]{:S(2)}, u32[]{:S(2)}) collective-permute-start(f32[1,4096]{1,0:T(1,128)S(1)} %shard_map.112.refs_0_), channel_id=1, source_target_pairs={{0,12},{4,8},{8,4},{12,0},{16,28},{20,24},{24,20},{28,16},{1,13},{... | collective-permute-start | bytes 49160 | tf_op jit(solution)/shard_map/ppermute | solution.py:346
  17.5 0.5 collective-permute-start.4
  17.9 0.5 collective-permute-start.3
  18.4 1.2 %collective-permute-done.5.refs_3_ = f32[1,4096]{1,0:T(1,128)S(1)} collective-permute-done((f32[1,4096]{1,0:T(1,128)S(1)}, f32[1,4096]{1,0:T(1,128)S(1)}, u32[]{:S(2)}, u32[]{:S(2)}) %collective-permute-start.5) | collective-permute-done | bytes 16416 | tf_op jit(solution)/shard_map/ppermute | solution.py:346
  19.6 1.6 %collective-permute-done.4.refs_2_ = f32[1,4096]{1,0:T(1,128)S(1)} collective-permute-done((f32[1,4096]{1,0:T(1,128)S(1)}, f32[1,4096]{1,0:T(1,128)S(1)}, u32[]{:S(2)}, u32[]{:S(2)}) %collective-permute-start.4) | collective-permute-done | bytes 16416 | tf_op jit(solution)/shard_map/ppermute | solution.py:346
  21.2 0.5 collective-permute-done.3.refs_1_
  21.7 2.6 %collective-permute-start.6 = (f32[1,4096]{1,0:T(1,128)S(1)}, f32[1,4096]{1,0:T(1,128)S(1)}, u32[]{:S(2)}, u32[]{:S(2)}) collective-permute-start(f32[1,4096]{1,0:T(1,128)S(1)} %shard_map.113.refs_0_), channel_id=1, source_target_pairs={{0,16},{4,20},{8,24},{12,28},{16,0},{20,4},{24,8},{28,12},{1,17},{... | collective-permute-start | bytes 49160 | tf_op jit(solution)/shard_map/ppermute | solution.py:346
  24.3 2.1 %collective-permute-done.6.refs_1_ = f32[1,4096]{1,0:T(1,128)S(1)} collective-permute-done((f32[1,4096]{1,0:T(1,128)S(1)}, f32[1,4096]{1,0:T(1,128)S(1)}, u32[]{:S(2)}, u32[]{:S(2)}) %collective-permute-start.6) | collective-permute-done | bytes 16416 | tf_op jit(solution)/shard_map/ppermute | solution.py:346
  26.4 3.1 %shard_map.114.refs_0_ = f32[1,4096]{1,0:T(1,128)S(1)} custom-call(f32[1,4096]{1,0:T(1,128)S(1)} %shard_map.113.refs_0_, f32[1,4096]{1,0:T(1,128)S(1)} %collective-permute-done.6.refs_1_, f32[1,4096]{1,0:T(1,128)S(1)} %get-tuple-element.23.refs_2_.refs_3_, bf16[32,4096]{1,0:T(8,128)(2,1)S(1)} %get-tuple-element.20.refs_5_.refs_3_.refs_6_.xc, ...), custom_call_target="tpu_custom_call" | custom-call | tf_op jit(solution)/shard_map/pallas_call | solution.py:320
  29.5 0.1 collective-permute-start.9
  29.6 0.7 %collective-permute-start.8 = (f32[1,4096]{1,0:T(1,128)S(1)}, f32[1,4096]{1,0:T(1,128)S(1)}, u32[]{:S(2)}, u32[]{:S(2)}) collective-permute-start(f32[1,4096]{1,0:T(1,128)S(1)} %shard_map.114.refs_0_), channel_id=1, source_target_pairs={{0,2},{1,3},{2,0},{3,1},{4,6},{5,7},{6,4},{7,5},{8,10},{9,11},{10,... | collective-permute-start | bytes 49160 | tf_op jit(solution)/shard_map/ppermute | solution.py:337
  30.2 1.2 %collective-permute-start.7 = (f32[1,4096]{1,0:T(1,128)S(1)}, f32[1,4096]{1,0:T(1,128)S(1)}, u32[]{:S(2)}, u32[]{:S(2)}) collective-permute-start(f32[1,4096]{1,0:T(1,128)S(1)} %shard_map.114.refs_0_), channel_id=1, source_target_pairs={{0,1},{1,0},{2,3},{3,2},{4,5},{5,4},{6,7},{7,6},{8,9},{9,8},{10,11... | collective-permute-start | bytes 49160 | tf_op jit(solution)/shard_map/ppermute | solution.py:337
  31.4 1.3 %collective-permute-done.9.refs_3_ = f32[1,4096]{1,0:T(1,128)S(1)} collective-permute-done((f32[1,4096]{1,0:T(1,128)S(1)}, f32[1,4096]{1,0:T(1,128)S(1)}, u32[]{:S(2)}, u32[]{:S(2)}) %collective-permute-start.9) | collective-permute-done | bytes 16416 | tf_op jit(solution)/shard_map/ppermute | solution.py:337
  32.7 0.7 %collective-permute-done.8.refs_2_ = f32[1,4096]{1,0:T(1,128)S(1)} collective-permute-done((f32[1,4096]{1,0:T(1,128)S(1)}, f32[1,4096]{1,0:T(1,128)S(1)}, u32[]{:S(2)}, u32[]{:S(2)}) %collective-permute-start.8) | collective-permute-done | bytes 16416 | tf_op jit(solution)/shard_map/ppermute | solution.py:337
  33.4 0.0 collective-permute-done.7.refs_1_
  33.4 7.3 %shard_map.115 = (f32[1,4096]{1,0:T(1,128)}, f32[1,4096]{1,0:T(1,128)S(1)}, f32[4,4096]{1,0:T(4,128)S(1)}) custom-call(f32[1,4096]{1,0:T(1,128)S(1)} %shard_map.114.refs_0_, f32[1,4096]{1,0:T(1,128)S(1)} %collective-permute-done.7.refs_1_, f32[1,4096]{1,0:T(1,128)S(1)} %collective-permute-done.8.refs_2_, f32[1,4096]{1,0:T(1,128)S(1)} %collective-permute-done.9.refs_3_, ...), custom_call_target="tpu_custom_call" | custom-call | tf_op jit(solution)/shard_map/pallas_call | solution.py:320
  40.7 1.6 %collective-permute-start.12 = (f32[4,4096]{1,0:T(4,128)S(1)}, f32[4,4096]{1,0:T(4,128)S(1)}, u32[]{:S(2)}, u32[]{:S(2)}) collective-permute-start(f32[4,4096]{1,0:T(4,128)S(1)} %get-tuple-element.25.refs_0_), channel_id=1, source_target_pairs={{0,12},{4,8},{8,4},{12,0},{16,28},{20,24},{24,20},{28,16},{1,13},{... | collective-permute-start | bytes 196616 | tf_op jit(solution)/shard_map/ppermute | solution.py:346
  42.3 0.4 collective-permute-start.11
  42.7 1.5 %collective-permute-start.10 = (f32[4,4096]{1,0:T(4,128)S(1)}, f32[4,4096]{1,0:T(4,128)S(1)}, u32[]{:S(2)}, u32[]{:S(2)}) collective-permute-start(f32[4,4096]{1,0:T(4,128)S(1)} %get-tuple-element.25.refs_0_), channel_id=1, source_target_pairs={{0,4},{4,0},{8,12},{12,8},{16,20},{20,16},{24,28},{28,24},{1,5},{5... | collective-permute-start | bytes 196616 | tf_op jit(solution)/shard_map/ppermute | solution.py:346
  44.2 2.3 %collective-permute-done.12.refs_3_ = f32[4,4096]{1,0:T(4,128)S(1)} collective-permute-done((f32[4,4096]{1,0:T(4,128)S(1)}, f32[4,4096]{1,0:T(4,128)S(1)}, u32[]{:S(2)}, u32[]{:S(2)}) %collective-permute-start.12) | collective-permute-done | bytes 65568 | tf_op jit(solution)/shard_map/ppermute | solution.py:346
  46.6 0.0 collective-permute-done.11.refs_2_
  46.6 0.6 collective-permute-done.10.refs_1_
  47.2 2.7 %collective-permute-start.13 = (f32[4,4096]{1,0:T(4,128)S(1)}, f32[4,4096]{1,0:T(4,128)S(1)}, u32[]{:S(2)}, u32[]{:S(2)}) collective-permute-start(f32[4,4096]{1,0:T(4,128)S(1)} %shard_map.116.refs_0_), channel_id=1, source_target_pairs={{0,16},{4,20},{8,24},{12,28},{16,0},{20,4},{24,8},{28,12},{1,17},{... | collective-permute-start | bytes 196616 | tf_op jit(solution)/shard_map/ppermute | solution.py:346
  49.8 0.1 shard_map.117.refs_2_
  49.9 2.5 %collective-permute-done.13.refs_1_ = f32[4,4096]{1,0:T(4,128)S(1)} collective-permute-done((f32[4,4096]{1,0:T(4,128)S(1)}, f32[4,4096]{1,0:T(4,128)S(1)}, u32[]{:S(2)}, u32[]{:S(2)}) %collective-permute-start.13) | collective-permute-done | bytes 65568 | tf_op jit(solution)/shard_map/ppermute | solution.py:346
  52.4 6.1 %shard_map.118 = (f32[1,4096]{1,0:T(1,128)}, f32[3,1024]{1,0:T(4,128)S(1)}, f32[3,1024]{1,0:T(4,128)S(1)}, f32[3,1024]{1,0:T(4,128)S(1)}, f32[3,1024]{1,0:T(4,128)S(1)}) custom-call(f32[4,4096]{1,0:T(4,128)S(1)} %shard_map.116.refs_0_, f32[4,4096]{1,0:T(4,128)S(1)} %collective-permute-done.13.refs_1_, bf16[32,4096]{1,0:T(8,128)(2,1)S(1)} %shard_map.117.refs_2_, ...), custom_call_target="tpu_custom_call" | custom-call | tf_op jit(solution)/shard_map/pallas_call | solution.py:320
  58.6 0.1 collective-permute-start.14
  58.6 1.2 %collective-permute-start.15 = (f32[3,1024]{1,0:T(4,128)S(1)}, f32[3,1024]{1,0:T(4,128)S(1)}, u32[]{:S(2)}, u32[]{:S(2)}) collective-permute-start(f32[3,1024]{1,0:T(4,128)S(1)} %get-tuple-element.30), channel_id=1, source_target_pairs={{0,2},{1,3},{2,0},{3,1},{4,6},{5,7},{6,4},{7,5},{8,10},{9,11},{10,... | collective-permute-start | bytes 36872 | tf_op jit(solution)/shard_map/ppermute | solution.py:337
  59.8 0.7 %collective-permute-start.16 = (f32[3,1024]{1,0:T(4,128)S(1)}, f32[3,1024]{1,0:T(4,128)S(1)}, u32[]{:S(2)}, u32[]{:S(2)}) collective-permute-start(f32[3,1024]{1,0:T(4,128)S(1)} %get-tuple-element.31), channel_id=1, source_target_pairs={{0,3},{1,2},{2,1},{3,0},{4,7},{5,6},{6,5},{7,4},{8,11},{9,10},{10,... | collective-permute-start | bytes 36872 | tf_op jit(solution)/shard_map/ppermute | solution.py:337
  60.5 0.7 %shard_map.119 = f32[3,4096]{1,0:T(4,128)} custom-call(f32[4,4096]{1,0:T(4,128)S(1)} %shard_map.116.refs_0_, f32[4,4096]{1,0:T(4,128)S(1)} %collective-permute-done.13.refs_1_, f32[10,4096]{1,0:T(8,128)S(1)} %convert_add_fusion.points.refs_5_.refs_4_.refs_2_, f32[3,1024]{1,0:T(4,128)S(1)} %get-tuple-element.28.refs_3_), custom_call_target="tpu_custom_call" | custom-call | tf_op jit(solution)/shard_map/pallas_call | solution.py:320
  61.2 0.0 collective-permute-done.14
  61.2 1.3 %collective-permute-done.15 = f32[3,1024]{1,0:T(4,128)S(1)} collective-permute-done((f32[3,1024]{1,0:T(4,128)S(1)}, f32[3,1024]{1,0:T(4,128)S(1)}, u32[]{:S(2)}, u32[]{:S(2)}) %collective-permute-start.15) | collective-permute-done | bytes 12320 | tf_op jit(solution)/shard_map/ppermute | solution.py:337
  62.4 0.6 collective-permute-done.16
  63.0 0.6 add_add_fusion
  (2 shorter events, 0.1 us)
Async XLA Ops:
  1.3 1.1 %copy-start = (s32[1,1,12]{2,1,0:T(1,128)S(1)}, s32[1,1,12]{2,1,0:T(1,128)}, u32[]{:S(2)}) copy-start(s32[1,1,12]{2,1,0:T(1,128)} %sources.1) | copy-start | bytes 148
  1.3 1.1 %copy-start.1 = (s32[1,1,12]{2,1,0:T(1,128)S(1)}, s32[1,1,12]{2,1,0:T(1,128)}, u32[]{:S(2)}) copy-start(s32[1,1,12]{2,1,0:T(1,128)} %targets.1) | copy-start | bytes 148
  5.6 3.9 %collective-permute-start.2 = (f32[1,4096]{1,0:T(1,128)S(1)}, f32[1,4096]{1,0:T(1,128)S(1)}, u32[]{:S(2)}, u32[]{:S(2)}) collective-permute-start(f32[1,4096]{1,0:T(1,128)S(1)} %get-tuple-element.18.refs_0_), channel_id=1, source_target_pairs={{0,3},{1,2},{2,1},{3,0},{4,7},{5,6},{6,5},{7,4},{8,11},{9,10},{10,... | collective-permute-start | bytes 49160 | tf_op jit(solution)/shard_map/ppermute | solution.py:337
  8.1 3.7 %collective-permute-start.1 = (f32[1,4096]{1,0:T(1,128)S(1)}, f32[1,4096]{1,0:T(1,128)S(1)}, u32[]{:S(2)}, u32[]{:S(2)}) collective-permute-start(f32[1,4096]{1,0:T(1,128)S(1)} %get-tuple-element.18.refs_0_), channel_id=1, source_target_pairs={{0,2},{1,3},{2,0},{3,1},{4,6},{5,7},{6,4},{7,5},{8,10},{9,11},{10,... | collective-permute-start | bytes 49160 | tf_op jit(solution)/shard_map/ppermute | solution.py:337
  8.7 3.1 %collective-permute-start = (f32[1,4096]{1,0:T(1,128)S(1)}, f32[1,4096]{1,0:T(1,128)S(1)}, u32[]{:S(2)}, u32[]{:S(2)}) collective-permute-start(f32[1,4096]{1,0:T(1,128)S(1)} %get-tuple-element.18.refs_0_), channel_id=1, source_target_pairs={{0,1},{1,0},{2,3},{3,2},{4,5},{5,4},{6,7},{7,6},{8,9},{9,8},{10,11... | collective-permute-start | bytes 49160 | tf_op jit(solution)/shard_map/ppermute | solution.py:337
  14.9 4.7 %collective-permute-start.5 = (f32[1,4096]{1,0:T(1,128)S(1)}, f32[1,4096]{1,0:T(1,128)S(1)}, u32[]{:S(2)}, u32[]{:S(2)}) collective-permute-start(f32[1,4096]{1,0:T(1,128)S(1)} %shard_map.112.refs_0_), channel_id=1, source_target_pairs={{0,12},{4,8},{8,4},{12,0},{16,28},{20,24},{24,20},{28,16},{1,13},{... | collective-permute-start | bytes 49160 | tf_op jit(solution)/shard_map/ppermute | solution.py:346
  17.5 3.7 %collective-permute-start.4 = (f32[1,4096]{1,0:T(1,128)S(1)}, f32[1,4096]{1,0:T(1,128)S(1)}, u32[]{:S(2)}, u32[]{:S(2)}) collective-permute-start(f32[1,4096]{1,0:T(1,128)S(1)} %shard_map.112.refs_0_), channel_id=1, source_target_pairs={{0,8},{4,12},{8,0},{12,4},{16,24},{20,28},{24,16},{28,20},{1,9},{5... | collective-permute-start | bytes 49160 | tf_op jit(solution)/shard_map/ppermute | solution.py:346
  17.9 3.7 %collective-permute-start.3 = (f32[1,4096]{1,0:T(1,128)S(1)}, f32[1,4096]{1,0:T(1,128)S(1)}, u32[]{:S(2)}, u32[]{:S(2)}) collective-permute-start(f32[1,4096]{1,0:T(1,128)S(1)} %shard_map.112.refs_0_), channel_id=1, source_target_pairs={{0,4},{4,0},{8,12},{12,8},{16,20},{20,16},{24,28},{28,24},{1,5},{5... | collective-permute-start | bytes 49160 | tf_op jit(solution)/shard_map/ppermute | solution.py:346
  21.7 4.7 %collective-permute-start.6 = (f32[1,4096]{1,0:T(1,128)S(1)}, f32[1,4096]{1,0:T(1,128)S(1)}, u32[]{:S(2)}, u32[]{:S(2)}) collective-permute-start(f32[1,4096]{1,0:T(1,128)S(1)} %shard_map.113.refs_0_), channel_id=1, source_target_pairs={{0,16},{4,20},{8,24},{12,28},{16,0},{20,4},{24,8},{28,12},{1,17},{... | collective-permute-start | bytes 49160 | tf_op jit(solution)/shard_map/ppermute | solution.py:346
  29.5 3.2 %collective-permute-start.9 = (f32[1,4096]{1,0:T(1,128)S(1)}, f32[1,4096]{1,0:T(1,128)S(1)}, u32[]{:S(2)}, u32[]{:S(2)}) collective-permute-start(f32[1,4096]{1,0:T(1,128)S(1)} %shard_map.114.refs_0_), channel_id=1, source_target_pairs={{0,3},{1,2},{2,1},{3,0},{4,7},{5,6},{6,5},{7,4},{8,11},{9,10},{10,... | collective-permute-start | bytes 49160 | tf_op jit(solution)/shard_map/ppermute | solution.py:337
  29.6 3.8 %collective-permute-start.8 = (f32[1,4096]{1,0:T(1,128)S(1)}, f32[1,4096]{1,0:T(1,128)S(1)}, u32[]{:S(2)}, u32[]{:S(2)}) collective-permute-start(f32[1,4096]{1,0:T(1,128)S(1)} %shard_map.114.refs_0_), channel_id=1, source_target_pairs={{0,2},{1,3},{2,0},{3,1},{4,6},{5,7},{6,4},{7,5},{8,10},{9,11},{10,... | collective-permute-start | bytes 49160 | tf_op jit(solution)/shard_map/ppermute | solution.py:337
  30.2 3.1 %collective-permute-start.7 = (f32[1,4096]{1,0:T(1,128)S(1)}, f32[1,4096]{1,0:T(1,128)S(1)}, u32[]{:S(2)}, u32[]{:S(2)}) collective-permute-start(f32[1,4096]{1,0:T(1,128)S(1)} %shard_map.114.refs_0_), channel_id=1, source_target_pairs={{0,1},{1,0},{2,3},{3,2},{4,5},{5,4},{6,7},{7,6},{8,9},{9,8},{10,11... | collective-permute-start | bytes 49160 | tf_op jit(solution)/shard_map/ppermute | solution.py:337
  40.7 5.9 %collective-permute-start.12 = (f32[4,4096]{1,0:T(4,128)S(1)}, f32[4,4096]{1,0:T(4,128)S(1)}, u32[]{:S(2)}, u32[]{:S(2)}) collective-permute-start(f32[4,4096]{1,0:T(4,128)S(1)} %get-tuple-element.25.refs_0_), channel_id=1, source_target_pairs={{0,12},{4,8},{8,4},{12,0},{16,28},{20,24},{24,20},{28,16},{1,13},{... | collective-permute-start | bytes 196616 | tf_op jit(solution)/shard_map/ppermute | solution.py:346
  42.3 4.3 %collective-permute-start.11 = (f32[4,4096]{1,0:T(4,128)S(1)}, f32[4,4096]{1,0:T(4,128)S(1)}, u32[]{:S(2)}, u32[]{:S(2)}) collective-permute-start(f32[4,4096]{1,0:T(4,128)S(1)} %get-tuple-element.25.refs_0_), channel_id=1, source_target_pairs={{0,8},{4,12},{8,0},{12,4},{16,24},{20,28},{24,16},{28,20},{1,9},{5... | collective-permute-start | bytes 196616 | tf_op jit(solution)/shard_map/ppermute | solution.py:346
  42.7 4.4 %collective-permute-start.10 = (f32[4,4096]{1,0:T(4,128)S(1)}, f32[4,4096]{1,0:T(4,128)S(1)}, u32[]{:S(2)}, u32[]{:S(2)}) collective-permute-start(f32[4,4096]{1,0:T(4,128)S(1)} %get-tuple-element.25.refs_0_), channel_id=1, source_target_pairs={{0,4},{4,0},{8,12},{12,8},{16,20},{20,16},{24,28},{28,24},{1,5},{5... | collective-permute-start | bytes 196616 | tf_op jit(solution)/shard_map/ppermute | solution.py:346
  47.2 5.2 %collective-permute-start.13 = (f32[4,4096]{1,0:T(4,128)S(1)}, f32[4,4096]{1,0:T(4,128)S(1)}, u32[]{:S(2)}, u32[]{:S(2)}) collective-permute-start(f32[4,4096]{1,0:T(4,128)S(1)} %shard_map.116.refs_0_), channel_id=1, source_target_pairs={{0,16},{4,20},{8,24},{12,28},{16,0},{20,4},{24,8},{28,12},{1,17},{... | collective-permute-start | bytes 196616 | tf_op jit(solution)/shard_map/ppermute | solution.py:346
  58.6 2.6 %collective-permute-start.14 = (f32[3,1024]{1,0:T(4,128)S(1)}, f32[3,1024]{1,0:T(4,128)S(1)}, u32[]{:S(2)}, u32[]{:S(2)}) collective-permute-start(f32[3,1024]{1,0:T(4,128)S(1)} %get-tuple-element.29), channel_id=1, source_target_pairs={{0,1},{1,0},{2,3},{3,2},{4,5},{5,4},{6,7},{7,6},{8,9},{9,8},{10,11... | collective-permute-start | bytes 36872 | tf_op jit(solution)/shard_map/ppermute | solution.py:337
  58.6 3.8 %collective-permute-start.15 = (f32[3,1024]{1,0:T(4,128)S(1)}, f32[3,1024]{1,0:T(4,128)S(1)}, u32[]{:S(2)}, u32[]{:S(2)}) collective-permute-start(f32[3,1024]{1,0:T(4,128)S(1)} %get-tuple-element.30), channel_id=1, source_target_pairs={{0,2},{1,3},{2,0},{3,1},{4,6},{5,7},{6,4},{7,5},{8,10},{9,11},{10,... | collective-permute-start | bytes 36872 | tf_op jit(solution)/shard_map/ppermute | solution.py:337
  59.8 3.2 %collective-permute-start.16 = (f32[3,1024]{1,0:T(4,128)S(1)}, f32[3,1024]{1,0:T(4,128)S(1)}, u32[]{:S(2)}, u32[]{:S(2)}) collective-permute-start(f32[3,1024]{1,0:T(4,128)S(1)} %get-tuple-element.31), channel_id=1, source_target_pairs={{0,3},{1,2},{2,1},{3,0},{4,7},{5,6},{6,5},{7,4},{8,11},{9,10},{10,... | collective-permute-start | bytes 36872 | tf_op jit(solution)/shard_map/ppermute | solution.py:337

commit v8 on v7

--- a/solution.py
+++ b/solution.py
@@ -14,6 +14,7 @@
 LOG2E = math.log2(math.e)
 DEPTH = 32
 FLOOR = -1e30
+RANGE = 90.0
 F32 = jnp.float32
 BF16 = jnp.bfloat16
 
@@ -34,7 +35,9 @@
 
 
 SOURCE_ORDER = (0, 1, 2, 0, 0, 1)
+SOURCE_PARTS = (0, 3, 6)
 TARGET_ORDER = (0, 0, 0, 1, 2, 1)
+TARGET_PARTS = (0, 9, 12)
 
 
 def place(scratch, parts, order):
@@ -65,32 +68,48 @@
     return value.reshape(value.shape[0] // 8, 8, value.shape[1])
 
 
-def each_tile(tiles, left, right, visit, first, more, ahead=1, chunk=128):
+def each_tile(tiles, left, right, visit, first, more, ahead=1, chunk=128, loop=False):
     once = right.shape[1] // CLUSTER
+    chunks = CLUSTER // chunk
 
     def group_states(group, fresh):
         steps = []
         for which, slot in enumerate(group):
             r, k = tiles.starts(slot)
-            for at in range(CLUSTER // chunk):
-                steps.append((which, pl.ds(k, CLUSTER), pl.ds(pl.multiple_of(r + at * chunk, chunk), chunk)))
+            for at in range(chunks):
+                steps.append((which, at, pl.ds(k, CLUSTER), pl.ds(pl.multiple_of(r + at * chunk, chunk), chunk)))
         states = [None] * len(group)
         scores = [None] * len(steps)
 
         def start(n):
             if n < len(steps):
-                which, here, rows = steps[n]
+                _, _, here, rows = steps[n]
                 scores[n] = grouped(jnp.dot(left[rows, :], right[:, here], preferred_element_type=F32))
 
         for n in range(ahead):
             start(n)
-        for n, (which, here, rows) in enumerate(steps):
+        for n, (which, at, here, rows) in enumerate(steps):
             start(n + ahead)
-            states[which] = visit(scores[n], states[which], rows, fresh)
-        return [(steps[which * (CLUSTER // chunk)][1], state) for which, state in enumerate(states)]
-
+            states[which] = visit(scores[n], states[which], rows, fresh, at)
+        return [(steps[which * chunks][2], state) for which, state in enumerate(states)]
+
+    count = tiles.count()
+    if loop:
+
+        def one(slot, carry):
+            ((here, state),) = group_states([slot], True)
+            first(here, state)
+            return carry
+
+        def another(slot, carry):
+            ((here, state),) = group_states([slot], False)
+            more(here, state, slot < count)
+            return carry
+
+        lax.fori_loop(0, once, one, 0)
+        lax.fori_loop(once, count, another, 0)
+        return
     slots = list(range(tiles.slots))
-    count = tiles.count()
     for here, state in group_states(slots[:once], True):
         first(here, state)
     for slot, (here, state) in zip(slots[once:], group_states(slots[once:], False)):
@@ -98,7 +117,7 @@
 
 
 def lse_tiles(tiles, left, right, top, total, **how):
-    def visit(s, state, rows, fresh):
+    def visit(s, state, rows, fresh, at):
         largest = jnp.max(s, axis=0)
         if state is None:
             return largest, jnp.sum(jnp.exp2(s - largest[None]), axis=0)
@@ -117,7 +136,7 @@
     each_tile(tiles, left, right, visit, first, more, **how)
     m = top[...]
     largest = jnp.max(m, axis=0, keepdims=True)
-    return largest + log2(jnp.sum(total[...] * jnp.exp2(m - largest), axis=0, keepdims=True))
+    return largest, largest + log2(jnp.sum(total[...] * jnp.exp2(m - largest), axis=0, keepdims=True))
 
 
 def weighed(p, columns, points, start, rows, fresh):
@@ -133,7 +152,7 @@
 
 
 def mean_tiles(tiles, left, right, columns, points, start, top, sums, **how):
-    def visit(s, state, rows, fresh):
+    def visit(s, state, rows, fresh, at):
         largest = jnp.max(s, axis=0)
         new = largest if state is None else jnp.maximum(state[0], largest)
         p = jnp.exp2(s - new[None])
@@ -164,22 +183,48 @@
     return [largest + log2(mass)] + [other / mass for other in others]
 
 
-def plan_tiles(tiles, left, right, columns, points, start, sums, **how):
-    def visit(s, state, rows, fresh):
+def moments(p, static, rows):
+    p = p.reshape(p.shape[0] * 8, p.shape[2])
+    high = p.astype(BF16)
+    low = (p - high.astype(F32)).astype(BF16)
+    weights = static[:, rows]
+    return jnp.dot(
+        jnp.concatenate([weights, weights], axis=1), jnp.concatenate([high, low], axis=0), preferred_element_type=F32
+    )
+
+
+def added(state, totals):
+    return totals if state is None else [old + new for old, new in zip(state, totals)]
+
+
+def plan_tiles(tiles, left, right, columns, points, start, sums, product=None):
+    def visit(s, state, rows, fresh, at):
         p = jnp.exp2(s)
-        totals = [jnp.sum(p, axis=0)] + list(weighed(p, columns, points, start, rows, fresh))
-        return totals if state is None else [old + new for old, new in zip(state, totals)]
+        plain, other = state or (None, None)
+        if product is not None and at == CLUSTER // 128 - 1:
+            return plain, moments(p, product[0], rows)
+        return added(plain, [jnp.sum(p, axis=0)] + list(weighed(p, columns, points, start, rows, fresh))), other
 
     def first(here, state):
-        for c, total in enumerate(state):
+        for c, total in enumerate(state[0]):
             sums[c, :, here] = total
+        if product is not None:
+            product[3][:, here] = state[1]
 
     def more(here, state, live):
-        for c, total in enumerate(state):
+        for c, total in enumerate(state[0]):
             sums[c, :, here] += jnp.where(live, total, 0.0)
-
-    each_tile(tiles, left, right, visit, first, more, **how)
-    return [jnp.sum(sums[c], axis=0, keepdims=True) for c in range(4)]
+        if product is not None:
+            product[3][:, here] += jnp.where(live, state[1], 0.0)
+
+    each_tile(tiles, left, right, visit, first, more)
+    out = [jnp.sum(sums[c], axis=0, keepdims=True) for c in range(4)]
+    if product is not None:
+        _, starts, scale, other = product
+        out[0] += other[19:20, :]
+        for c in range(3):
+            out[c + 1] += scale * functools.reduce(jnp.add, [other[at + c : at + c + 1, :] for at in starts])
+    return out
 
 
 def combine(parts):
@@ -235,25 +280,29 @@
     place(stack, split(xs), SOURCE_ORDER)
     xc_out[...] = stack[...].astype(BF16)
     copy.wait()
-    part_out[...] = lse_tiles(Tiles(lists, sides(xc_out, yc_out), True), turned, xc_out, top, total)
-
-
-def col_kernel(parts, log_source, xc, yc, lists_in, part_out, lists, sem, low, turned, top, total):
+    part_out[...] = lse_tiles(Tiles(lists, sides(xc_out, yc_out), True), turned, xc_out, top, total)[1]
+
+
+def col_kernel(
+    parts, log_source, xc, yc, lists_in, part_out, top_out, u_out, lists, sem, low, turned, top, total
+):
     copy = fetch(lists_in, lists, sem)
-    turn(turned, low, xc, split(log_source[...] - combine([ref[...] for ref in parts])[0]))
+    u = -combine([ref[...] for ref in parts])[0]
+    u_out[...] = u
+    turn(turned, low, xc, split(log_source[...] + u))
     copy.wait()
-    part_out[...] = lse_tiles(Tiles(lists, sides(xc, yc), False), turned, yc, top, total)
+    top_out[...], part_out[...] = lse_tiles(Tiles(lists, sides(xc, yc), False), turned, yc, top, total)
 
 
 def row_kernel(parts, log_target, xc, yc, lists_in, part_out, lists, sem, low, turned, top, total):
     copy = fetch(lists_in, lists, sem)
     turn(turned, low, yc, split(log_target[...] - combine([ref[...] for ref in parts])[0]))
     copy.wait()
-    part_out[...] = lse_tiles(Tiles(lists, sides(xc, yc), True), turned, xc, top, total)
+    part_out[...] = lse_tiles(Tiles(lists, sides(xc, yc), True), turned, xc, top, total)[1]
 
 
 def last_col_kernel(
-    parts, log_source, points, xc, yc, lists_in, f_out, u_out, part_out,
+    parts, u_before, top_before, kept, log_source, points, xc, yc, lists_in, f_out, u_out, part_out,
     lists, sem, low, turned, top, sums, columns, f, sem_out,
 ):
     copy = fetch(lists_in, lists, sem)
@@ -261,11 +310,28 @@
     u_out[...] = log_source[...] + u
     f[...] = u * (1.0 / KAPPA) + half_square(points[0:3, :])
     back = fetch(f, f_out, sem_out)
-    turn(turned, low, xc, split(u_out[...]))
+    change = u - u_before[...]
+    highest = jnp.max(change)
+    shift = top_before[...] + highest
+    turn(turned, low, xc, split(u_out[...] - highest), [jnp.ones_like(u)] * 3)
     copy.wait()
     tiles = Tiles(lists, sides(xc, yc), False)
-    for r, row in enumerate(mean_tiles(tiles, turned, yc, columns, points, 0, top, sums)):
-        part_out[r : r + 1, :] = row
+    near = highest - jnp.min(change) < RANGE
+
+    @pl.when(near)
+    def _():
+        mass, *moved = plan_tiles(tiles, turned, kept, columns, points, 0, sums)
+        part_out[0:1, :] = shift + log2(mass)
+        for c, total in enumerate(moved):
+            part_out[c + 1 : c + 2, :] = total / mass
+
+    @pl.when(jnp.logical_not(near))
+    def _():
+        part, *means = mean_tiles(tiles, turned, kept, columns, points, 0, top, sums, loop=True)
+        part_out[0:1, :] = shift + part
+        for c, mean in enumerate(means):
+            part_out[c + 1 : c + 2, :] = mean
+
     back.wait()
 
 
@@ -280,9 +346,9 @@
         refs[-1][r : r + 1, :] = row
 
 
-def kept_kernel(u, xc, out, low):
-    out[0:16, :] = xc[0:16, :]
-    out[16:32, :] = lower_half(low, xc, None, split(u[...]))
+def kept_kernel(potential, static, out, low, sign):
+    out[0:16, :] = static[0:16, :]
+    out[16:32, :] = lower_half(low, static, None, split(sign * potential[...]))
 
 
 def target_kernel(parts, points, after, out):
@@ -292,7 +358,7 @@
 
 
 def gradient_kernel(parts, kept, log_target, points, xc, yc, lists_in, g_out, *rest, shares):
-    source_out, (lists, sem, low, turned, sums, columns, g, whole, sem_out) = rest[:shares], rest[shares:]
+    source_out, (lists, sem, low, turned, sums, other, columns, g, whole, sem_out) = rest[:shares], rest[shares:]
     copy = fetch(lists_in, lists, sem)
     lse = combine([ref[0:1, :] for ref in parts])[0]
     xs = points[0:3, :]
@@ -301,7 +367,9 @@
     turn(turned, low, yc, split(log_target[...] - lse), [jnp.ones_like(lse)] * 3)
     copy.wait()
     tiles = Tiles(lists, sides(xc, yc), True)
-    mass, *moved = plan_tiles(tiles, turned, kept, columns, points, 3, sums)
+    mass, *moved = plan_tiles(
+        tiles, turned, kept, columns, points, 3, sums, (yc, TARGET_PARTS, 1.0 / KAPPA, other)
+    )
     for c in range(3):
         whole[c : c + 1, :] = xs[c : c + 1, :] * mass - moved[c]
     place_tgt = lax.axis_index("tgt")
@@ -389,6 +457,11 @@
     def state(kept):
         return [pltpu.VMEM((8, kept), F32), pltpu.VMEM((8, kept), F32)]
 
+    def kept_operand(potential, static, sign):
+        n = static.shape[1]
+        kernel = functools.partial(kept_kernel, sign=sign)
+        return call(kernel, (potential, static), (), [split_rows(n)], [pltpu.VMEM((DEPTH // 2, n), F32)])[0]
+
     first = work(nt)
     xc, yc, part, lists, log_source, log_target = call(
         first_row_kernel,
@@ -399,13 +472,14 @@
     )
     known, lists = (xc, yc), (lists,)
     parts = exchange([part] * n_tgt, "tgt")
-    (part,) = call(
+    part, top, u = call(
         bunch(col_kernel, n_tgt),
         (*parts, log_source, *known),
         lists,
-        [rows(nt, 1)],
+        [rows(nt, 1), rows(nt, 1), rows(ns, 1)],
         work(ns) + state(nt),
     )
+    kept = kept_operand(top, yc, -1.0)
     parts = sum_up(part, "src")
     (part,) = call(
         bunch(row_kernel, len(parts)),
@@ -417,7 +491,7 @@
     parts = exchange([part] * n_tgt, "tgt")
     f, u, part = call(
         bunch(last_col_kernel, n_tgt),
-        (*parts, log_source, points, *known),
+        (*parts, u, top, kept, log_source, points, *known),
         lists,
         [rows(ns, 1), rows(ns, 1), rows(nt, 4)],
         work(ns)
@@ -430,7 +504,7 @@
         ],
         far=(0,),
     )
-    (kept,) = call(kept_kernel, (u, xc), (), [split_rows(ns)], [pltpu.VMEM((DEPTH // 2, ns), F32)])
+    kept = kept_operand(u, xc, 1.0)
     parts = sum_up(part, "src")
     g, *moved = call(
         bunch(functools.partial(gradient_kernel, shares=n_tgt), len(parts)),
@@ -440,6 +514,7 @@
         work(nt)
         + [
             pltpu.VMEM((4, 8, ns), F32),
+            pltpu.VMEM((DEPTH, ns), F32),
             pltpu.VMEM((nt, 384), F32),
             pltpu.VMEM((1, nt), F32),
             pltpu.VMEM((3, ns), F32),

time: 63.8 us -> 63.3 us (level)
    pallas_call x9 -> x10, Pallas kernels: 23.6 us -> 23.3 us  [call(): pl.pallas_call(kernel, out_shape=outs, in_specs=[VMEM] * len(ins) + [HBM]...]
where the time goes in v8:
time: 63.3 us; the launch traced here: 63.2 us
  Pallas kernels  23.3 us (37%)
  starting transfers between devices  19.4 us (31%)
  waiting for transfers between devices  17.5 us (28%)
  other arithmetic  1.65 us (3%)
  between operations  1.4 us (2%)
    pallas_call x10, Pallas kernels, call(): pl.pallas_call(kernel, out_shape=outs, in_specs=[VMEM] * len(ins) + [HBM]...  23.3 us
    ppermute x8, starting transfers between devices, sum_up(): lax.ppermute(value, axis, [(i, i ^ k) for i in range(n)])  12.4 us
    ppermute x8, waiting for transfers between devices, sum_up(): lax.ppermute(value, axis, [(i, i ^ k) for i in range(n)])  10.7 us
    ppermute x9, starting transfers between devices, exchange(): lax.ppermute(values[k], axis, [(i, peer(i, k, n)) for i in range(n)])  6.98 us
    ppermute x9, waiting for transfers between devices, exchange(): lax.ppermute(values[k], axis, [(i, peer(i, k, n)) for i in range(n)])  6.79 us
  transfers between devices with their start and end apart: 17, of which 13 were waited for; matrix products, arithmetic and copies ran while one was open for 0% of the time, Pallas kernels for 1%

profile of v8, /device:TPU:0, one launch (start us, length us, event | category | flops | bytes accessed | tf_op | source)
XLA Modules:
  0.0 63.2 jit_solution(8649876235118073155)
XLA Ops:
  1.3 0.0 copy-start
  1.3 0.0 copy-start.1
  1.3 1.0 %convert_add_fusion.points.refs_8_.refs_4_.refs_2_ = f32[10,4096]{1,0:T(8,128)S(1)} fusion(s32[1,1]{1,0:T(1,128)S(6)} %copy.12, f32[1,4096]{1,0:T(1,128)} %bitcast.5, f32[1,4096]{1,0:T(1,128)} %bitcast.6, f32[1,4096]{1,0:T(1,128)} %bitcast.7, f32[3,4096]{1,0:T(4,128)} %param.9, f32[3,4096]{1,0:T(4,128)} %param.8), kind=kLoop, calls=%fused_computation | loop fusion | flops 245760 | bytes 311300 | tf_op jit(solution)/shard_map/add | solution.py:431
  2.3 0.0 copy-done
  2.3 0.0 copy-done.1
  2.4 3.3 %shard_map.111 = (bf16[32,4096]{1,0:T(8,128)(2,1)S(1)}, bf16[32,4096]{1,0:T(8,128)(2,1)S(1)}, f32[1,4096]{1,0:T(1,128)S(1)}, s32[1,1,12]{2,1,0:T(1,128)S(1)}, f3...) custom-call(f32[10,4096]{1,0:T(8,128)S(1)} %convert_add_fusion.points.refs_8_.refs_4_.refs_2_, s32[1,1,12]{2,1,0:T(1,128)S(1)} %copy-done, ...), custom_call_target="tpu_custom_call" | custom-call | tf_op jit(solution)/shard_map/pallas_call | solution.py:388
  5.6 2.4 %collective-permute-start.2 = (f32[1,4096]{1,0:T(1,128)S(1)}, f32[1,4096]{1,0:T(1,128)S(1)}, u32[]{:S(2)}, u32[]{:S(2)}) collective-permute-start(f32[1,4096]{1,0:T(1,128)S(1)} %get-tuple-element.21.refs_0_), channel_id=1, source_target_pairs={{0,3},{1,2},{2,1},{3,0},{4,7},{5,6},{6,5},{7,4},{8,11},{9,10},{10,... | collective-permute-start | bytes 49160 | tf_op jit(solution)/shard_map/ppermute | solution.py:405
  8.1 0.7 %collective-permute-start.1 = (f32[1,4096]{1,0:T(1,128)S(1)}, f32[1,4096]{1,0:T(1,128)S(1)}, u32[]{:S(2)}, u32[]{:S(2)}) collective-permute-start(f32[1,4096]{1,0:T(1,128)S(1)} %get-tuple-element.21.refs_0_), channel_id=1, source_target_pairs={{0,2},{1,3},{2,0},{3,1},{4,6},{5,7},{6,4},{7,5},{8,10},{9,11},{10,... | collective-permute-start | bytes 49160 | tf_op jit(solution)/shard_map/ppermute | solution.py:405
  8.7 0.0 collective-permute-start
  8.8 0.8 %collective-permute-done.2.refs_3_ = f32[1,4096]{1,0:T(1,128)S(1)} collective-permute-done((f32[1,4096]{1,0:T(1,128)S(1)}, f32[1,4096]{1,0:T(1,128)S(1)}, u32[]{:S(2)}, u32[]{:S(2)}) %collective-permute-start.2) | collective-permute-done | bytes 16416 | tf_op jit(solution)/shard_map/ppermute | solution.py:405
  9.5 2.3 %collective-permute-done.1.refs_2_ = f32[1,4096]{1,0:T(1,128)S(1)} collective-permute-done((f32[1,4096]{1,0:T(1,128)S(1)}, f32[1,4096]{1,0:T(1,128)S(1)}, u32[]{:S(2)}, u32[]{:S(2)}) %collective-permute-start.1) | collective-permute-done | bytes 16416 | tf_op jit(solution)/shard_map/ppermute | solution.py:405
  11.8 0.0 collective-permute-done.refs_1_
  11.8 3.2 %shard_map.112 = (f32[1,4096]{1,0:T(1,128)S(1)}, f32[1,4096]{1,0:T(1,128)S(1)}, f32[1,4096]{1,0:T(1,128)S(1)}) custom-call(f32[1,4096]{1,0:T(1,128)S(1)} %get-tuple-element.21.refs_0_, f32[1,4096]{1,0:T(1,128)S(1)} %collective-permute-done.refs_1_, f32[1,4096]{1,0:T(1,128)S(1)} %collective-permute-done.1.refs_2_, ...), custom_call_target="tpu_custom_call" | custom-call | tf_op jit(solution)/shard_map/pallas_call | solution.py:388
  15.0 2.6 %collective-permute-start.5 = (f32[1,4096]{1,0:T(1,128)S(1)}, f32[1,4096]{1,0:T(1,128)S(1)}, u32[]{:S(2)}, u32[]{:S(2)}) collective-permute-start(f32[1,4096]{1,0:T(1,128)S(1)} %get-tuple-element.26.refs_0_), channel_id=1, source_target_pairs={{0,12},{4,8},{8,4},{12,0},{16,28},{20,24},{24,20},{28,16},{1,13},{... | collective-permute-start | bytes 49160 | tf_op jit(solution)/shard_map/ppermute | solution.py:414
  17.6 0.5 collective-permute-start.4
  18.1 0.5 collective-permute-start.3
  18.6 1.2 %collective-permute-done.5.refs_3_ = f32[1,4096]{1,0:T(1,128)S(1)} collective-permute-done((f32[1,4096]{1,0:T(1,128)S(1)}, f32[1,4096]{1,0:T(1,128)S(1)}, u32[]{:S(2)}, u32[]{:S(2)}) %collective-permute-start.5) | collective-permute-done | bytes 16416 | tf_op jit(solution)/shard_map/ppermute | solution.py:414
  19.8 1.6 %collective-permute-done.4.refs_2_ = f32[1,4096]{1,0:T(1,128)S(1)} collective-permute-done((f32[1,4096]{1,0:T(1,128)S(1)}, f32[1,4096]{1,0:T(1,128)S(1)}, u32[]{:S(2)}, u32[]{:S(2)}) %collective-permute-start.4) | collective-permute-done | bytes 16416 | tf_op jit(solution)/shard_map/ppermute | solution.py:414
  21.4 0.5 collective-permute-done.3.refs_1_
  21.9 2.6 %collective-permute-start.6 = (f32[1,4096]{1,0:T(1,128)S(1)}, f32[1,4096]{1,0:T(1,128)S(1)}, u32[]{:S(2)}, u32[]{:S(2)}) collective-permute-start(f32[1,4096]{1,0:T(1,128)S(1)} %shard_map.113.refs_0_), channel_id=1, source_target_pairs={{0,16},{4,20},{8,24},{12,28},{16,0},{20,4},{24,8},{28,12},{1,17},{... | collective-permute-start | bytes 49160 | tf_op jit(solution)/shard_map/ppermute | solution.py:414
  24.5 2.1 %collective-permute-done.6.refs_1_ = f32[1,4096]{1,0:T(1,128)S(1)} collective-permute-done((f32[1,4096]{1,0:T(1,128)S(1)}, f32[1,4096]{1,0:T(1,128)S(1)}, u32[]{:S(2)}, u32[]{:S(2)}) %collective-permute-start.6) | collective-permute-done | bytes 16416 | tf_op jit(solution)/shard_map/ppermute | solution.py:414
  26.6 3.1 %shard_map.114.refs_0_ = f32[1,4096]{1,0:T(1,128)S(1)} custom-call(f32[1,4096]{1,0:T(1,128)S(1)} %shard_map.113.refs_0_, f32[1,4096]{1,0:T(1,128)S(1)} %collective-permute-done.6.refs_1_, f32[1,4096]{1,0:T(1,128)S(1)} %get-tuple-element.27.refs_2_.refs_3_, bf16[32,4096]{1,0:T(8,128)(2,1)S(1)} %get-tuple-element.23.refs_5_.refs_3_.refs_9_.static, ...), custom_call_target="tpu_custom_call" | custom-call | tf_op jit(solution)/shard_map/pallas_call | solution.py:388
  29.6 0.1 collective-permute-start.9
  29.7 0.7 %collective-permute-start.8 = (f32[1,4096]{1,0:T(1,128)S(1)}, f32[1,4096]{1,0:T(1,128)S(1)}, u32[]{:S(2)}, u32[]{:S(2)}) collective-permute-start(f32[1,4096]{1,0:T(1,128)S(1)} %shard_map.114.refs_0_), channel_id=1, source_target_pairs={{0,2},{1,3},{2,0},{3,1},{4,6},{5,7},{6,4},{7,5},{8,10},{9,11},{10,... | collective-permute-start | bytes 49160 | tf_op jit(solution)/shard_map/ppermute | solution.py:405
  30.4 1.2 %collective-permute-start.7 = (f32[1,4096]{1,0:T(1,128)S(1)}, f32[1,4096]{1,0:T(1,128)S(1)}, u32[]{:S(2)}, u32[]{:S(2)}) collective-permute-start(f32[1,4096]{1,0:T(1,128)S(1)} %shard_map.114.refs_0_), channel_id=1, source_target_pairs={{0,1},{1,0},{2,3},{3,2},{4,5},{5,4},{6,7},{7,6},{8,9},{9,8},{10,11... | collective-permute-start | bytes 49160 | tf_op jit(solution)/shard_map/ppermute | solution.py:405
  31.6 0.1 shard_map.115.refs_6_
  31.7 1.2 %collective-permute-done.9.refs_3_ = f32[1,4096]{1,0:T(1,128)S(1)} collective-permute-done((f32[1,4096]{1,0:T(1,128)S(1)}, f32[1,4096]{1,0:T(1,128)S(1)}, u32[]{:S(2)}, u32[]{:S(2)}) %collective-permute-start.9) | collective-permute-done | bytes 16416 | tf_op jit(solution)/shard_map/ppermute | solution.py:405
  32.9 0.7 %collective-permute-done.8.refs_2_ = f32[1,4096]{1,0:T(1,128)S(1)} collective-permute-done((f32[1,4096]{1,0:T(1,128)S(1)}, f32[1,4096]{1,0:T(1,128)S(1)}, u32[]{:S(2)}, u32[]{:S(2)}) %collective-permute-start.8) | collective-permute-done | bytes 16416 | tf_op jit(solution)/shard_map/ppermute | solution.py:405
  33.5 0.0 collective-permute-done.7.refs_1_
  33.5 6.8 %shard_map.116 = (f32[1,4096]{1,0:T(1,128)}, f32[1,4096]{1,0:T(1,128)S(1)}, f32[4,4096]{1,0:T(4,128)S(1)}) custom-call(f32[1,4096]{1,0:T(1,128)S(1)} %shard_map.114.refs_0_, f32[1,4096]{1,0:T(1,128)S(1)} %collective-permute-done.7.refs_1_, f32[1,4096]{1,0:T(1,128)S(1)} %collective-permute-done.8.refs_2_, f32[1,4096]{1,0:T(1,128)S(1)} %collective-permute-done.9.refs_3_, ...), custom_call_target="tpu_custom_call" | custom-call | tf_op jit(solution)/shard_map/pallas_call | solution.py:388
  40.3 1.6 %collective-permute-start.12 = (f32[4,4096]{1,0:T(4,128)S(1)}, f32[4,4096]{1,0:T(4,128)S(1)}, u32[]{:S(2)}, u32[]{:S(2)}) collective-permute-start(f32[4,4096]{1,0:T(4,128)S(1)} %get-tuple-element.31.refs_0_), channel_id=1, source_target_pairs={{0,12},{4,8},{8,4},{12,0},{16,28},{20,24},{24,20},{28,16},{1,13},{... | collective-permute-start | bytes 196616 | tf_op jit(solution)/shard_map/ppermute | solution.py:414
  41.9 0.5 collective-permute-start.11
  42.3 1.5 %collective-permute-start.10 = (f32[4,4096]{1,0:T(4,128)S(1)}, f32[4,4096]{1,0:T(4,128)S(1)}, u32[]{:S(2)}, u32[]{:S(2)}) collective-permute-start(f32[4,4096]{1,0:T(4,128)S(1)} %get-tuple-element.31.refs_0_), channel_id=1, source_target_pairs={{0,4},{4,0},{8,12},{12,8},{16,20},{20,16},{24,28},{28,24},{1,5},{5... | collective-permute-start | bytes 196616 | tf_op jit(solution)/shard_map/ppermute | solution.py:414
  43.9 2.3 %collective-permute-done.12.refs_3_ = f32[4,4096]{1,0:T(4,128)S(1)} collective-permute-done((f32[4,4096]{1,0:T(4,128)S(1)}, f32[4,4096]{1,0:T(4,128)S(1)}, u32[]{:S(2)}, u32[]{:S(2)}) %collective-permute-start.12) | collective-permute-done | bytes 65568 | tf_op jit(solution)/shard_map/ppermute | solution.py:414
  46.2 0.0 collective-permute-done.11.refs_2_
  46.2 0.6 collective-permute-done.10.refs_1_
  46.8 2.7 %collective-permute-start.13 = (f32[4,4096]{1,0:T(4,128)S(1)}, f32[4,4096]{1,0:T(4,128)S(1)}, u32[]{:S(2)}, u32[]{:S(2)}) collective-permute-start(f32[4,4096]{1,0:T(4,128)S(1)} %shard_map.117.refs_0_), channel_id=1, source_target_pairs={{0,16},{4,20},{8,24},{12,28},{16,0},{20,4},{24,8},{28,12},{1,17},{... | collective-permute-start | bytes 196616 | tf_op jit(solution)/shard_map/ppermute | solution.py:414
  49.5 0.1 shard_map.118.refs_2_
  49.6 2.5 %collective-permute-done.13.refs_1_ = f32[4,4096]{1,0:T(4,128)S(1)} collective-permute-done((f32[4,4096]{1,0:T(4,128)S(1)}, f32[4,4096]{1,0:T(4,128)S(1)}, u32[]{:S(2)}, u32[]{:S(2)}) %collective-permute-start.13) | collective-permute-done | bytes 65568 | tf_op jit(solution)/shard_map/ppermute | solution.py:414
  52.0 6.0 %shard_map.119 = (f32[1,4096]{1,0:T(1,128)}, f32[3,1024]{1,0:T(4,128)S(1)}, f32[3,1024]{1,0:T(4,128)S(1)}, f32[3,1024]{1,0:T(4,128)S(1)}, f32[3,1024]{1,0:T(4,128)S(1)}) custom-call(f32[4,4096]{1,0:T(4,128)S(1)} %shard_map.117.refs_0_, f32[4,4096]{1,0:T(4,128)S(1)} %collective-permute-done.13.refs_1_, bf16[32,4096]{1,0:T(8,128)(2,1)S(1)} %shard_map.118.refs_2_, ...), custom_call_target="tpu_custom_call" | custom-call | tf_op jit(solution)/shard_map/pallas_call | solution.py:388
  58.1 0.1 collective-permute-start.14
  58.2 1.2 %collective-permute-start.15 = (f32[3,1024]{1,0:T(4,128)S(1)}, f32[3,1024]{1,0:T(4,128)S(1)}, u32[]{:S(2)}, u32[]{:S(2)}) collective-permute-start(f32[3,1024]{1,0:T(4,128)S(1)} %get-tuple-element.36), channel_id=1, source_target_pairs={{0,2},{1,3},{2,0},{3,1},{4,6},{5,7},{6,4},{7,5},{8,10},{9,11},{10,... | collective-permute-start | bytes 36872 | tf_op jit(solution)/shard_map/ppermute | solution.py:405
  59.4 0.6 %collective-permute-start.16 = (f32[3,1024]{1,0:T(4,128)S(1)}, f32[3,1024]{1,0:T(4,128)S(1)}, u32[]{:S(2)}, u32[]{:S(2)}) collective-permute-start(f32[3,1024]{1,0:T(4,128)S(1)} %get-tuple-element.37), channel_id=1, source_target_pairs={{0,3},{1,2},{2,1},{3,0},{4,7},{5,6},{6,5},{7,4},{8,11},{9,10},{10,... | collective-permute-start | bytes 36872 | tf_op jit(solution)/shard_map/ppermute | solution.py:405
  60.0 0.7 %shard_map.120 = f32[3,4096]{1,0:T(4,128)} custom-call(f32[4,4096]{1,0:T(4,128)S(1)} %shard_map.117.refs_0_, f32[4,4096]{1,0:T(4,128)S(1)} %collective-permute-done.13.refs_1_, f32[10,4096]{1,0:T(8,128)S(1)} %convert_add_fusion.points.refs_8_.refs_4_.refs_2_, f32[3,1024]{1,0:T(4,128)S(1)} %get-tuple-element.34.refs_3_), custom_call_target="tpu_custom_call" | custom-call | tf_op jit(solution)/shard_map/pallas_call | solution.py:388
  60.7 0.0 collective-permute-done.14
  60.7 1.3 %collective-permute-done.15 = f32[3,1024]{1,0:T(4,128)S(1)} collective-permute-done((f32[3,1024]{1,0:T(4,128)S(1)}, f32[3,1024]{1,0:T(4,128)S(1)}, u32[]{:S(2)}, u32[]{:S(2)}) %collective-permute-start.15) | collective-permute-done | bytes 12320 | tf_op jit(solution)/shard_map/ppermute | solution.py:405
  62.0 0.6 collective-permute-done.16
  62.6 0.6 add_add_fusion
  (2 shorter events, 0.1 us)
Async XLA Ops:
  1.3 1.1 %copy-start = (s32[1,1,12]{2,1,0:T(1,128)S(1)}, s32[1,1,12]{2,1,0:T(1,128)}, u32[]{:S(2)}) copy-start(s32[1,1,12]{2,1,0:T(1,128)} %sources.1) | copy-start | bytes 148
  1.3 1.1 %copy-start.1 = (s32[1,1,12]{2,1,0:T(1,128)S(1)}, s32[1,1,12]{2,1,0:T(1,128)}, u32[]{:S(2)}) copy-start(s32[1,1,12]{2,1,0:T(1,128)} %targets.1) | copy-start | bytes 148
  5.6 3.9 %collective-permute-start.2 = (f32[1,4096]{1,0:T(1,128)S(1)}, f32[1,4096]{1,0:T(1,128)S(1)}, u32[]{:S(2)}, u32[]{:S(2)}) collective-permute-start(f32[1,4096]{1,0:T(1,128)S(1)} %get-tuple-element.21.refs_0_), channel_id=1, source_target_pairs={{0,3},{1,2},{2,1},{3,0},{4,7},{5,6},{6,5},{7,4},{8,11},{9,10},{10,... | collective-permute-start | bytes 49160 | tf_op jit(solution)/shard_map/ppermute | solution.py:405
  8.1 3.7 %collective-permute-start.1 = (f32[1,4096]{1,0:T(1,128)S(1)}, f32[1,4096]{1,0:T(1,128)S(1)}, u32[]{:S(2)}, u32[]{:S(2)}) collective-permute-start(f32[1,4096]{1,0:T(1,128)S(1)} %get-tuple-element.21.refs_0_), channel_id=1, source_target_pairs={{0,2},{1,3},{2,0},{3,1},{4,6},{5,7},{6,4},{7,5},{8,10},{9,11},{10,... | collective-permute-start | bytes 49160 | tf_op jit(solution)/shard_map/ppermute | solution.py:405
  8.7 3.1 %collective-permute-start = (f32[1,4096]{1,0:T(1,128)S(1)}, f32[1,4096]{1,0:T(1,128)S(1)}, u32[]{:S(2)}, u32[]{:S(2)}) collective-permute-start(f32[1,4096]{1,0:T(1,128)S(1)} %get-tuple-element.21.refs_0_), channel_id=1, source_target_pairs={{0,1},{1,0},{2,3},{3,2},{4,5},{5,4},{6,7},{7,6},{8,9},{9,8},{10,11... | collective-permute-start | bytes 49160 | tf_op jit(solution)/shard_map/ppermute | solution.py:405
  15.0 4.8 %collective-permute-start.5 = (f32[1,4096]{1,0:T(1,128)S(1)}, f32[1,4096]{1,0:T(1,128)S(1)}, u32[]{:S(2)}, u32[]{:S(2)}) collective-permute-start(f32[1,4096]{1,0:T(1,128)S(1)} %get-tuple-element.26.refs_0_), channel_id=1, source_target_pairs={{0,12},{4,8},{8,4},{12,0},{16,28},{20,24},{24,20},{28,16},{1,13},{... | collective-permute-start | bytes 49160 | tf_op jit(solution)/shard_map/ppermute | solution.py:414
  17.6 3.7 %collective-permute-start.4 = (f32[1,4096]{1,0:T(1,128)S(1)}, f32[1,4096]{1,0:T(1,128)S(1)}, u32[]{:S(2)}, u32[]{:S(2)}) collective-permute-start(f32[1,4096]{1,0:T(1,128)S(1)} %get-tuple-element.26.refs_0_), channel_id=1, source_target_pairs={{0,8},{4,12},{8,0},{12,4},{16,24},{20,28},{24,16},{28,20},{1,9},{5... | collective-permute-start | bytes 49160 | tf_op jit(solution)/shard_map/ppermute | solution.py:414
  18.1 3.7 %collective-permute-start.3 = (f32[1,4096]{1,0:T(1,128)S(1)}, f32[1,4096]{1,0:T(1,128)S(1)}, u32[]{:S(2)}, u32[]{:S(2)}) collective-permute-start(f32[1,4096]{1,0:T(1,128)S(1)} %get-tuple-element.26.refs_0_), channel_id=1, source_target_pairs={{0,4},{4,0},{8,12},{12,8},{16,20},{20,16},{24,28},{28,24},{1,5},{5... | collective-permute-start | bytes 49160 | tf_op jit(solution)/shard_map/ppermute | solution.py:414
  21.9 4.7 %collective-permute-start.6 = (f32[1,4096]{1,0:T(1,128)S(1)}, f32[1,4096]{1,0:T(1,128)S(1)}, u32[]{:S(2)}, u32[]{:S(2)}) collective-permute-start(f32[1,4096]{1,0:T(1,128)S(1)} %shard_map.113.refs_0_), channel_id=1, source_target_pairs={{0,16},{4,20},{8,24},{12,28},{16,0},{20,4},{24,8},{28,12},{1,17},{... | collective-permute-start | bytes 49160 | tf_op jit(solution)/shard_map/ppermute | solution.py:414
  29.6 3.2 %collective-permute-start.9 = (f32[1,4096]{1,0:T(1,128)S(1)}, f32[1,4096]{1,0:T(1,128)S(1)}, u32[]{:S(2)}, u32[]{:S(2)}) collective-permute-start(f32[1,4096]{1,0:T(1,128)S(1)} %shard_map.114.refs_0_), channel_id=1, source_target_pairs={{0,3},{1,2},{2,1},{3,0},{4,7},{5,6},{6,5},{7,4},{8,11},{9,10},{10,... | collective-permute-start | bytes 49160 | tf_op jit(solution)/shard_map/ppermute | solution.py:405
  29.7 3.8 %collective-permute-start.8 = (f32[1,4096]{1,0:T(1,128)S(1)}, f32[1,4096]{1,0:T(1,128)S(1)}, u32[]{:S(2)}, u32[]{:S(2)}) collective-permute-start(f32[1,4096]{1,0:T(1,128)S(1)} %shard_map.114.refs_0_), channel_id=1, source_target_pairs={{0,2},{1,3},{2,0},{3,1},{4,6},{5,7},{6,4},{7,5},{8,10},{9,11},{10,... | collective-permute-start | bytes 49160 | tf_op jit(solution)/shard_map/ppermute | solution.py:405
  30.4 3.1 %collective-permute-start.7 = (f32[1,4096]{1,0:T(1,128)S(1)}, f32[1,4096]{1,0:T(1,128)S(1)}, u32[]{:S(2)}, u32[]{:S(2)}) collective-permute-start(f32[1,4096]{1,0:T(1,128)S(1)} %shard_map.114.refs_0_), channel_id=1, source_target_pairs={{0,1},{1,0},{2,3},{3,2},{4,5},{5,4},{6,7},{7,6},{8,9},{9,8},{10,11... | collective-permute-start | bytes 49160 | tf_op jit(solution)/shard_map/ppermute | solution.py:405
  40.3 5.9 %collective-permute-start.12 = (f32[4,4096]{1,0:T(4,128)S(1)}, f32[4,4096]{1,0:T(4,128)S(1)}, u32[]{:S(2)}, u32[]{:S(2)}) collective-permute-start(f32[4,4096]{1,0:T(4,128)S(1)} %get-tuple-element.31.refs_0_), channel_id=1, source_target_pairs={{0,12},{4,8},{8,4},{12,0},{16,28},{20,24},{24,20},{28,16},{1,13},{... | collective-permute-start | bytes 196616 | tf_op jit(solution)/shard_map/ppermute | solution.py:414
  41.9 4.3 %collective-permute-start.11 = (f32[4,4096]{1,0:T(4,128)S(1)}, f32[4,4096]{1,0:T(4,128)S(1)}, u32[]{:S(2)}, u32[]{:S(2)}) collective-permute-start(f32[4,4096]{1,0:T(4,128)S(1)} %get-tuple-element.31.refs_0_), channel_id=1, source_target_pairs={{0,8},{4,12},{8,0},{12,4},{16,24},{20,28},{24,16},{28,20},{1,9},{5... | collective-permute-start | bytes 196616 | tf_op jit(solution)/shard_map/ppermute | solution.py:414
  42.3 4.4 %collective-permute-start.10 = (f32[4,4096]{1,0:T(4,128)S(1)}, f32[4,4096]{1,0:T(4,128)S(1)}, u32[]{:S(2)}, u32[]{:S(2)}) collective-permute-start(f32[4,4096]{1,0:T(4,128)S(1)} %get-tuple-element.31.refs_0_), channel_id=1, source_target_pairs={{0,4},{4,0},{8,12},{12,8},{16,20},{20,16},{24,28},{28,24},{1,5},{5... | collective-permute-start | bytes 196616 | tf_op jit(solution)/shard_map/ppermute | solution.py:414
  46.8 5.2 %collective-permute-start.13 = (f32[4,4096]{1,0:T(4,128)S(1)}, f32[4,4096]{1,0:T(4,128)S(1)}, u32[]{:S(2)}, u32[]{:S(2)}) collective-permute-start(f32[4,4096]{1,0:T(4,128)S(1)} %shard_map.117.refs_0_), channel_id=1, source_target_pairs={{0,16},{4,20},{8,24},{12,28},{16,0},{20,4},{24,8},{28,12},{1,17},{... | collective-permute-start | bytes 196616 | tf_op jit(solution)/shard_map/ppermute | solution.py:414
  58.1 2.6 %collective-permute-start.14 = (f32[3,1024]{1,0:T(4,128)S(1)}, f32[3,1024]{1,0:T(4,128)S(1)}, u32[]{:S(2)}, u32[]{:S(2)}) collective-permute-start(f32[3,1024]{1,0:T(4,128)S(1)} %get-tuple-element.35), channel_id=1, source_target_pairs={{0,1},{1,0},{2,3},{3,2},{4,5},{5,4},{6,7},{7,6},{8,9},{9,8},{10,11... | collective-permute-start | bytes 36872 | tf_op jit(solution)/shard_map/ppermute | solution.py:405
  58.2 3.8 %collective-permute-start.15 = (f32[3,1024]{1,0:T(4,128)S(1)}, f32[3,1024]{1,0:T(4,128)S(1)}, u32[]{:S(2)}, u32[]{:S(2)}) collective-permute-start(f32[3,1024]{1,0:T(4,128)S(1)} %get-tuple-element.36), channel_id=1, source_target_pairs={{0,2},{1,3},{2,0},{3,1},{4,6},{5,7},{6,4},{7,5},{8,10},{9,11},{10,... | collective-permute-start | bytes 36872 | tf_op jit(solution)/shard_map/ppermute | solution.py:405
  59.4 3.2 %collective-permute-start.16 = (f32[3,1024]{1,0:T(4,128)S(1)}, f32[3,1024]{1,0:T(4,128)S(1)}, u32[]{:S(2)}, u32[]{:S(2)}) collective-permute-start(f32[3,1024]{1,0:T(4,128)S(1)} %get-tuple-element.37), channel_id=1, source_target_pairs={{0,3},{1,2},{2,1},{3,0},{4,7},{5,6},{6,5},{7,4},{8,11},{9,10},{10,... | collective-permute-start | bytes 36872 | tf_op jit(solution)/shard_map/ppermute | solution.py:405

commit v9 on v8

--- a/solution.py
+++ b/solution.py
@@ -14,7 +14,7 @@
 LOG2E = math.log2(math.e)
 DEPTH = 32
 FLOOR = -1e30
-RANGE = 90.0
+LIMIT = 60.0
 F32 = jnp.float32
 BF16 = jnp.bfloat16
 
@@ -35,9 +35,7 @@
 
 
 SOURCE_ORDER = (0, 1, 2, 0, 0, 1)
-SOURCE_PARTS = (0, 3, 6)
 TARGET_ORDER = (0, 0, 0, 1, 2, 1)
-TARGET_PARTS = (0, 9, 12)
 
 
 def place(scratch, parts, order):
@@ -68,17 +66,22 @@
     return value.reshape(value.shape[0] // 8, 8, value.shape[1])
 
 
-def each_tile(tiles, left, right, visit, first, more, ahead=1, chunk=128, loop=False):
+def each_tile(tiles, left, right, visit, first, more, points=None, ahead=1, chunk=128, lanes=CLUSTER, loop=False):
     once = right.shape[1] // CLUSTER
-    chunks = CLUSTER // chunk
+    chunks, blocks = CLUSTER // chunk, CLUSTER // lanes
 
     def group_states(group, fresh):
         steps = []
         for which, slot in enumerate(group):
             r, k = tiles.starts(slot)
-            for at in range(chunks):
-                steps.append((which, at, pl.ds(k, CLUSTER), pl.ds(pl.multiple_of(r + at * chunk, chunk), chunk)))
-        states = [None] * len(group)
+            given = points[0:8, pl.ds(r, CLUSTER)].T if fresh and points is not None else None
+            for block in range(blocks):
+                here = pl.ds(pl.multiple_of(k + block * lanes, lanes), lanes)
+                for at in range(chunks):
+                    rows = pl.ds(pl.multiple_of(r + at * chunk, chunk), chunk)
+                    some = None if given is None or block else given[at * chunk : (at + 1) * chunk, :]
+                    steps.append((which * blocks + block, some, here, rows))
+        states = [None] * (len(group) * blocks)
         scores = [None] * len(steps)
 
         def start(n):
@@ -88,41 +91,42 @@
 
         for n in range(ahead):
             start(n)
-        for n, (which, at, here, rows) in enumerate(steps):
+        for n, (which, some, here, rows) in enumerate(steps):
             start(n + ahead)
-            states[which] = visit(scores[n], states[which], rows, fresh, at)
+            states[which] = visit(scores[n], states[which], rows, some)
         return [(steps[which * chunks][2], state) for which, state in enumerate(states)]
 
     count = tiles.count()
     if loop:
 
         def one(slot, carry):
-            ((here, state),) = group_states([slot], True)
-            first(here, state)
+            for here, state in group_states([slot], True):
+                first(here, state)
             return carry
 
         def another(slot, carry):
-            ((here, state),) = group_states([slot], False)
-            more(here, state, slot < count)
+            for here, state in group_states([slot], False):
+                more(here, state, slot < count)
             return carry
 
         lax.fori_loop(0, once, one, 0)
         lax.fori_loop(once, count, another, 0)
         return
-    slots = list(range(tiles.slots))
-    for here, state in group_states(slots[:once], True):
+    for here, state in group_states(range(once), True):
         first(here, state)
-    for slot, (here, state) in zip(slots[once:], group_states(slots[once:], False)):
-        more(here, state, slot < count)
+    for n, (here, state) in enumerate(group_states(range(once, tiles.slots), False)):
+        more(here, state, once + n // blocks < count)
 
 
 def lse_tiles(tiles, left, right, top, total, **how):
-    def visit(s, state, rows, fresh, at):
-        largest = jnp.max(s, axis=0)
-        if state is None:
-            return largest, jnp.sum(jnp.exp2(s - largest[None]), axis=0)
-        new = jnp.maximum(state[0], largest)
-        return new, state[1] * jnp.exp2(state[0] - new) + jnp.sum(jnp.exp2(s - new[None]), axis=0)
+    def visit(s, state, rows, some):
+        groups = [s[g] for g in range(s.shape[0])]
+        new = functools.reduce(jnp.maximum, groups if state is None else [state[0]] + groups)
+        total = None if state is None else state[1] * jnp.exp2(state[0] - new)
+        for group in groups:
+            p = jnp.exp2(group - new)
+            total = p if total is None else total + p
+        return new, total
 
     def first(here, state):
         top[:, here], total[:, here] = state
@@ -139,28 +143,32 @@
     return largest, largest + log2(jnp.sum(total[...] * jnp.exp2(m - largest), axis=0, keepdims=True))
 
 
-def weighed(p, columns, points, start, rows, fresh):
-    block = points[0:8, rows].T if fresh else None
-    for c in range(3):
-        lanes = slice(128 * c, 128 * (c + 1))
-        if fresh:
-            col = jnp.broadcast_to(block[:, start + c : start + c + 1], (block.shape[0], 128))
-            columns[rows, lanes] = col
-        else:
-            col = columns[rows, lanes]
-        yield jnp.sum(p * jnp.concatenate([col] * (CLUSTER // 128), axis=1).reshape(p.shape), axis=0)
+def weighed(groups, totals, columns, start, rows, some):
+    for g, p in enumerate(groups):
+        here = pl.ds(pl.multiple_of(rows.start + 8 * g, 8), 8)
+        terms = [p]
+        for c in range(3):
+            lanes = slice(128 * c, 128 * (c + 1))
+            if some is not None:
+                col = jnp.broadcast_to(some[8 * g : 8 * (g + 1), start + c : start + c + 1], (8, 128))
+                columns[here, lanes] = col
+            else:
+                col = columns[here, lanes]
+            terms.append(p * jnp.concatenate([col] * (p.shape[1] // 128), axis=1))
+        totals = terms if totals is None else [total + term for total, term in zip(totals, terms)]
+    return totals
 
 
 def mean_tiles(tiles, left, right, columns, points, start, top, sums, **how):
-    def visit(s, state, rows, fresh, at):
+    def visit(s, state, rows, some):
         largest = jnp.max(s, axis=0)
         new = largest if state is None else jnp.maximum(state[0], largest)
-        p = jnp.exp2(s - new[None])
-        totals = [jnp.sum(p, axis=0)] + list(weighed(p, columns, points, start, rows, fresh))
+        totals = None
         if state is not None:
             scale = jnp.exp2(state[0] - new)
-            totals = [old * scale + total for old, total in zip(state[1:], totals)]
-        return [new] + totals
+            totals = [old * scale for old in state[1:]]
+        groups = [jnp.exp2(s[g] - new) for g in range(s.shape[0])]
+        return [new] + weighed(groups, totals, columns, start, rows, some)
 
     def first(here, state):
         top[:, here] = state[0]
@@ -175,7 +183,7 @@
         for c, total in enumerate(state[1:]):
             sums[c, :, here] = sums[c, :, here] * before + total * now
 
-    each_tile(tiles, left, right, visit, first, more, **how)
+    each_tile(tiles, left, right, visit, first, more, points, **how)
     m = top[...]
     largest = jnp.max(m, axis=0, keepdims=True)
     scale = jnp.exp2(m - largest)
@@ -183,48 +191,21 @@
     return [largest + log2(mass)] + [other / mass for other in others]
 
 
-def moments(p, static, rows):
-    p = p.reshape(p.shape[0] * 8, p.shape[2])
-    high = p.astype(BF16)
-    low = (p - high.astype(F32)).astype(BF16)
-    weights = static[:, rows]
-    return jnp.dot(
-        jnp.concatenate([weights, weights], axis=1), jnp.concatenate([high, low], axis=0), preferred_element_type=F32
-    )
-
-
-def added(state, totals):
-    return totals if state is None else [old + new for old, new in zip(state, totals)]
-
-
-def plan_tiles(tiles, left, right, columns, points, start, sums, product=None):
-    def visit(s, state, rows, fresh, at):
-        p = jnp.exp2(s)
-        plain, other = state or (None, None)
-        if product is not None and at == CLUSTER // 128 - 1:
-            return plain, moments(p, product[0], rows)
-        return added(plain, [jnp.sum(p, axis=0)] + list(weighed(p, columns, points, start, rows, fresh))), other
+def plan_tiles(tiles, left, right, columns, points, start, sums, **how):
+    def visit(s, state, rows, some):
+        groups = (jnp.exp2(s[g]) for g in range(s.shape[0]))
+        return weighed(groups, state, columns, start, rows, some)
 
     def first(here, state):
-        for c, total in enumerate(state[0]):
+        for c, total in enumerate(state):
             sums[c, :, here] = total
-        if product is not None:
-            product[3][:, here] = state[1]
 
     def more(here, state, live):
-        for c, total in enumerate(state[0]):
+        for c, total in enumerate(state):
             sums[c, :, here] += jnp.where(live, total, 0.0)
-        if product is not None:
-            product[3][:, here] += jnp.where(live, state[1], 0.0)
-
-    each_tile(tiles, left, right, visit, first, more)
-    out = [jnp.sum(sums[c], axis=0, keepdims=True) for c in range(4)]
-    if product is not None:
-        _, starts, scale, other = product
-        out[0] += other[19:20, :]
-        for c in range(3):
-            out[c + 1] += scale * functools.reduce(jnp.add, [other[at + c : at + c + 1, :] for at in starts])
-    return out
+
+    each_tile(tiles, left, right, visit, first, more, points, **how)
+    return [jnp.sum(sums[c], axis=0, keepdims=True) for c in range(4)]
 
 
 def combine(parts):
@@ -280,7 +261,7 @@
     place(stack, split(xs), SOURCE_ORDER)
     xc_out[...] = stack[...].astype(BF16)
     copy.wait()
-    part_out[...] = lse_tiles(Tiles(lists, sides(xc_out, yc_out), True), turned, xc_out, top, total)[1]
+    part_out[...] = lse_tiles(Tiles(lists, sides(xc_out, yc_out), True), turned, xc_out, top, total, lanes=256)[1]
 
 
 def col_kernel(
@@ -291,14 +272,14 @@
     u_out[...] = u
     turn(turned, low, xc, split(log_source[...] + u))
     copy.wait()
-    top_out[...], part_out[...] = lse_tiles(Tiles(lists, sides(xc, yc), False), turned, yc, top, total)
+    top_out[...], part_out[...] = lse_tiles(Tiles(lists, sides(xc, yc), False), turned, yc, top, total, lanes=256)
 
 
 def row_kernel(parts, log_target, xc, yc, lists_in, part_out, lists, sem, low, turned, top, total):
     copy = fetch(lists_in, lists, sem)
     turn(turned, low, yc, split(log_target[...] - combine([ref[...] for ref in parts])[0]))
     copy.wait()
-    part_out[...] = lse_tiles(Tiles(lists, sides(xc, yc), True), turned, xc, top, total)[1]
+    part_out[...] = lse_tiles(Tiles(lists, sides(xc, yc), True), turned, xc, top, total, chunk=64)[1]
 
 
 def last_col_kernel(
@@ -310,25 +291,23 @@
     u_out[...] = log_source[...] + u
     f[...] = u * (1.0 / KAPPA) + half_square(points[0:3, :])
     back = fetch(f, f_out, sem_out)
-    change = u - u_before[...]
-    highest = jnp.max(change)
-    shift = top_before[...] + highest
-    turn(turned, low, xc, split(u_out[...] - highest), [jnp.ones_like(u)] * 3)
+    near = jnp.max(jnp.abs(u - u_before[...])) < LIMIT
+    turn(turned, low, xc, split(u_out[...]), [jnp.ones_like(u)] * 3)
     copy.wait()
     tiles = Tiles(lists, sides(xc, yc), False)
-    near = highest - jnp.min(change) < RANGE
 
     @pl.when(near)
     def _():
-        mass, *moved = plan_tiles(tiles, turned, kept, columns, points, 0, sums)
-        part_out[0:1, :] = shift + log2(mass)
+        mass, *moved = plan_tiles(tiles, turned, kept, columns, points, 0, sums, chunk=32, ahead=2)
+        part_out[0:1, :] = top_before[...] + log2(mass)
+        inverse = 1.0 / mass
         for c, total in enumerate(moved):
-            part_out[c + 1 : c + 2, :] = total / mass
+            part_out[c + 1 : c + 2, :] = total * inverse
 
     @pl.when(jnp.logical_not(near))
     def _():
         part, *means = mean_tiles(tiles, turned, kept, columns, points, 0, top, sums, loop=True)
-        part_out[0:1, :] = shift + part
+        part_out[0:1, :] = top_before[...] + part
         for c, mean in enumerate(means):
             part_out[c + 1 : c + 2, :] = mean
 
@@ -358,7 +337,7 @@
 
 
 def gradient_kernel(parts, kept, log_target, points, xc, yc, lists_in, g_out, *rest, shares):
-    source_out, (lists, sem, low, turned, sums, other, columns, g, whole, sem_out) = rest[:shares], rest[shares:]
+    source_out, (lists, sem, low, turned, sums, columns, g, whole, sem_out) = rest[:shares], rest[shares:]
     copy = fetch(lists_in, lists, sem)
     lse = combine([ref[0:1, :] for ref in parts])[0]
     xs = points[0:3, :]
@@ -367,9 +346,7 @@
     turn(turned, low, yc, split(log_target[...] - lse), [jnp.ones_like(lse)] * 3)
     copy.wait()
     tiles = Tiles(lists, sides(xc, yc), True)
-    mass, *moved = plan_tiles(
-        tiles, turned, kept, columns, points, 3, sums, (yc, TARGET_PARTS, 1.0 / KAPPA, other)
-    )
+    mass, *moved = plan_tiles(tiles, turned, kept, columns, points, 3, sums, chunk=32, ahead=2)
     for c in range(3):
         whole[c : c + 1, :] = xs[c : c + 1, :] * mass - moved[c]
     place_tgt = lax.axis_index("tgt")
@@ -514,7 +491,6 @@
         work(nt)
         + [
             pltpu.VMEM((4, 8, ns), F32),
-            pltpu.VMEM((DEPTH, ns), F32),
             pltpu.VMEM((nt, 384), F32),
             pltpu.VMEM((1, nt), F32),
             pltpu.VMEM((3, ns), F32),

time: 63.3 us -> 62.8 us (level)
  no operation moved by 1% of the time
where the time goes in v9:
time: 62.8 us; the launch traced here: 62.6 us
  Pallas kernels  22.7 us (36%)
  starting transfers between devices  19.4 us (31%)
  waiting for transfers between devices  17.5 us (28%)
  other arithmetic  1.65 us (3%)
  between operations  1.4 us (2%)
    pallas_call x10, Pallas kernels, call(): pl.pallas_call(kernel, out_shape=outs, in_specs=[VMEM] * len(ins) + [HBM]...  22.7 us
    ppermute x8, starting transfers between devices, sum_up(): lax.ppermute(value, axis, [(i, i ^ k) for i in range(n)])  12.4 us
    ppermute x8, waiting for transfers between devices, sum_up(): lax.ppermute(value, axis, [(i, i ^ k) for i in range(n)])  10.7 us
    ppermute x9, starting transfers between devices, exchange(): lax.ppermute(values[k], axis, [(i, peer(i, k, n)) for i in range(n)])  6.97 us
    ppermute x9, waiting for transfers between devices, exchange(): lax.ppermute(values[k], axis, [(i, peer(i, k, n)) for i in range(n)])  6.8 us
  transfers between devices with their start and end apart: 17, of which 13 were waited for; matrix products, arithmetic and copies ran while one was open for 0% of the time, Pallas kernels for 1%

profile of v9, /device:TPU:0, one launch (start us, length us, event | category | flops | bytes accessed | tf_op | source)
XLA Modules:
  0.0 62.6 jit_solution(4779055353781415495)
XLA Ops:
  1.3 0.0 copy-start
  1.3 0.0 copy-start.1
  1.3 1.0 %convert_add_fusion.points.refs_8_.refs_4_.refs_2_ = f32[10,4096]{1,0:T(8,128)S(1)} fusion(s32[1,1]{1,0:T(1,128)S(6)} %copy.12, f32[1,4096]{1,0:T(1,128)} %bitcast.5, f32[1,4096]{1,0:T(1,128)} %bitcast.6, f32[1,4096]{1,0:T(1,128)} %bitcast.7, f32[3,4096]{1,0:T(4,128)} %param.9, f32[3,4096]{1,0:T(4,128)} %param.8), kind=kLoop, calls=%fused_computation | loop fusion | flops 245760 | bytes 311300 | tf_op jit(solution)/shard_map/add | solution.py:408
  2.3 0.0 copy-done
  2.3 0.0 copy-done.1
  2.4 3.0 %shard_map.111 = (bf16[32,4096]{1,0:T(8,128)(2,1)S(1)}, bf16[32,4096]{1,0:T(8,128)(2,1)S(1)}, f32[1,4096]{1,0:T(1,128)S(1)}, s32[1,1,12]{2,1,0:T(1,128)S(1)}, f3...) custom-call(f32[10,4096]{1,0:T(8,128)S(1)} %convert_add_fusion.points.refs_8_.refs_4_.refs_2_, s32[1,1,12]{2,1,0:T(1,128)S(1)} %copy-done, ...), custom_call_target="tpu_custom_call" | custom-call | tf_op jit(solution)/shard_map/pallas_call | solution.py:365
  5.4 2.4 %collective-permute-start.2 = (f32[1,4096]{1,0:T(1,128)S(1)}, f32[1,4096]{1,0:T(1,128)S(1)}, u32[]{:S(2)}, u32[]{:S(2)}) collective-permute-start(f32[1,4096]{1,0:T(1,128)S(1)} %get-tuple-element.21.refs_0_), channel_id=1, source_target_pairs={{0,3},{1,2},{2,1},{3,0},{4,7},{5,6},{6,5},{7,4},{8,11},{9,10},{10,... | collective-permute-start | bytes 49160 | tf_op jit(solution)/shard_map/ppermute | solution.py:382
  7.8 0.6 %collective-permute-start.1 = (f32[1,4096]{1,0:T(1,128)S(1)}, f32[1,4096]{1,0:T(1,128)S(1)}, u32[]{:S(2)}, u32[]{:S(2)}) collective-permute-start(f32[1,4096]{1,0:T(1,128)S(1)} %get-tuple-element.21.refs_0_), channel_id=1, source_target_pairs={{0,2},{1,3},{2,0},{3,1},{4,6},{5,7},{6,4},{7,5},{8,10},{9,11},{10,... | collective-permute-start | bytes 49160 | tf_op jit(solution)/shard_map/ppermute | solution.py:382
  8.5 0.0 collective-permute-start
  8.5 0.8 %collective-permute-done.2.refs_3_ = f32[1,4096]{1,0:T(1,128)S(1)} collective-permute-done((f32[1,4096]{1,0:T(1,128)S(1)}, f32[1,4096]{1,0:T(1,128)S(1)}, u32[]{:S(2)}, u32[]{:S(2)}) %collective-permute-start.2) | collective-permute-done | bytes 16416 | tf_op jit(solution)/shard_map/ppermute | solution.py:382
  9.3 2.3 %collective-permute-done.1.refs_2_ = f32[1,4096]{1,0:T(1,128)S(1)} collective-permute-done((f32[1,4096]{1,0:T(1,128)S(1)}, f32[1,4096]{1,0:T(1,128)S(1)}, u32[]{:S(2)}, u32[]{:S(2)}) %collective-permute-start.1) | collective-permute-done | bytes 16416 | tf_op jit(solution)/shard_map/ppermute | solution.py:382
  11.6 0.0 collective-permute-done.refs_1_
  11.6 3.0 %shard_map.112 = (f32[1,4096]{1,0:T(1,128)S(1)}, f32[1,4096]{1,0:T(1,128)S(1)}, f32[1,4096]{1,0:T(1,128)S(1)}) custom-call(f32[1,4096]{1,0:T(1,128)S(1)} %get-tuple-element.21.refs_0_, f32[1,4096]{1,0:T(1,128)S(1)} %collective-permute-done.refs_1_, f32[1,4096]{1,0:T(1,128)S(1)} %collective-permute-done.1.refs_2_, ...), custom_call_target="tpu_custom_call" | custom-call | tf_op jit(solution)/shard_map/pallas_call | solution.py:365
  14.6 2.6 %collective-permute-start.5 = (f32[1,4096]{1,0:T(1,128)S(1)}, f32[1,4096]{1,0:T(1,128)S(1)}, u32[]{:S(2)}, u32[]{:S(2)}) collective-permute-start(f32[1,4096]{1,0:T(1,128)S(1)} %get-tuple-element.26.refs_0_), channel_id=1, source_target_pairs={{0,12},{4,8},{8,4},{12,0},{16,28},{20,24},{24,20},{28,16},{1,13},{... | collective-permute-start | bytes 49160 | tf_op jit(solution)/shard_map/ppermute | solution.py:391
  17.2 0.4 collective-permute-start.4
  17.6 0.5 collective-permute-start.3
  18.1 1.2 %collective-permute-done.5.refs_3_ = f32[1,4096]{1,0:T(1,128)S(1)} collective-permute-done((f32[1,4096]{1,0:T(1,128)S(1)}, f32[1,4096]{1,0:T(1,128)S(1)}, u32[]{:S(2)}, u32[]{:S(2)}) %collective-permute-start.5) | collective-permute-done | bytes 16416 | tf_op jit(solution)/shard_map/ppermute | solution.py:391
  19.3 1.6 %collective-permute-done.4.refs_2_ = f32[1,4096]{1,0:T(1,128)S(1)} collective-permute-done((f32[1,4096]{1,0:T(1,128)S(1)}, f32[1,4096]{1,0:T(1,128)S(1)}, u32[]{:S(2)}, u32[]{:S(2)}) %collective-permute-start.4) | collective-permute-done | bytes 16416 | tf_op jit(solution)/shard_map/ppermute | solution.py:391
  20.9 0.4 collective-permute-done.3.refs_1_
  21.4 2.6 %collective-permute-start.6 = (f32[1,4096]{1,0:T(1,128)S(1)}, f32[1,4096]{1,0:T(1,128)S(1)}, u32[]{:S(2)}, u32[]{:S(2)}) collective-permute-start(f32[1,4096]{1,0:T(1,128)S(1)} %shard_map.113.refs_0_), channel_id=1, source_target_pairs={{0,16},{4,20},{8,24},{12,28},{16,0},{20,4},{24,8},{28,12},{1,17},{... | collective-permute-start | bytes 49160 | tf_op jit(solution)/shard_map/ppermute | solution.py:391
  24.0 2.1 %collective-permute-done.6.refs_1_ = f32[1,4096]{1,0:T(1,128)S(1)} collective-permute-done((f32[1,4096]{1,0:T(1,128)S(1)}, f32[1,4096]{1,0:T(1,128)S(1)}, u32[]{:S(2)}, u32[]{:S(2)}) %collective-permute-start.6) | collective-permute-done | bytes 16416 | tf_op jit(solution)/shard_map/ppermute | solution.py:391
  26.1 3.1 %shard_map.114.refs_0_ = f32[1,4096]{1,0:T(1,128)S(1)} custom-call(f32[1,4096]{1,0:T(1,128)S(1)} %shard_map.113.refs_0_, f32[1,4096]{1,0:T(1,128)S(1)} %collective-permute-done.6.refs_1_, f32[1,4096]{1,0:T(1,128)S(1)} %get-tuple-element.27.refs_2_.refs_3_, bf16[32,4096]{1,0:T(8,128)(2,1)S(1)} %get-tuple-element.23.refs_5_.refs_3_.refs_9_.static, ...), custom_call_target="tpu_custom_call" | custom-call | tf_op jit(solution)/shard_map/pallas_call | solution.py:365
  29.2 0.1 collective-permute-start.9
  29.3 0.7 %collective-permute-start.8 = (f32[1,4096]{1,0:T(1,128)S(1)}, f32[1,4096]{1,0:T(1,128)S(1)}, u32[]{:S(2)}, u32[]{:S(2)}) collective-permute-start(f32[1,4096]{1,0:T(1,128)S(1)} %shard_map.114.refs_0_), channel_id=1, source_target_pairs={{0,2},{1,3},{2,0},{3,1},{4,6},{5,7},{6,4},{7,5},{8,10},{9,11},{10,... | collective-permute-start | bytes 49160 | tf_op jit(solution)/shard_map/ppermute | solution.py:382
  30.0 1.2 %collective-permute-start.7 = (f32[1,4096]{1,0:T(1,128)S(1)}, f32[1,4096]{1,0:T(1,128)S(1)}, u32[]{:S(2)}, u32[]{:S(2)}) collective-permute-start(f32[1,4096]{1,0:T(1,128)S(1)} %shard_map.114.refs_0_), channel_id=1, source_target_pairs={{0,1},{1,0},{2,3},{3,2},{4,5},{5,4},{6,7},{7,6},{8,9},{9,8},{10,11... | collective-permute-start | bytes 49160 | tf_op jit(solution)/shard_map/ppermute | solution.py:382
  31.1 0.1 shard_map.115.refs_6_
  31.2 1.2 %collective-permute-done.9.refs_3_ = f32[1,4096]{1,0:T(1,128)S(1)} collective-permute-done((f32[1,4096]{1,0:T(1,128)S(1)}, f32[1,4096]{1,0:T(1,128)S(1)}, u32[]{:S(2)}, u32[]{:S(2)}) %collective-permute-start.9) | collective-permute-done | bytes 16416 | tf_op jit(solution)/shard_map/ppermute | solution.py:382
  32.4 0.7 %collective-permute-done.8.refs_2_ = f32[1,4096]{1,0:T(1,128)S(1)} collective-permute-done((f32[1,4096]{1,0:T(1,128)S(1)}, f32[1,4096]{1,0:T(1,128)S(1)}, u32[]{:S(2)}, u32[]{:S(2)}) %collective-permute-start.8) | collective-permute-done | bytes 16416 | tf_op jit(solution)/shard_map/ppermute | solution.py:382
  33.1 0.0 collective-permute-done.7.refs_1_
  33.1 6.5 %shard_map.116 = (f32[1,4096]{1,0:T(1,128)}, f32[1,4096]{1,0:T(1,128)S(1)}, f32[4,4096]{1,0:T(4,128)S(1)}) custom-call(f32[1,4096]{1,0:T(1,128)S(1)} %shard_map.114.refs_0_, f32[1,4096]{1,0:T(1,128)S(1)} %collective-permute-done.7.refs_1_, f32[1,4096]{1,0:T(1,128)S(1)} %collective-permute-done.8.refs_2_, f32[1,4096]{1,0:T(1,128)S(1)} %collective-permute-done.9.refs_3_, ...), custom_call_target="tpu_custom_call" | custom-call | tf_op jit(solution)/shard_map/pallas_call | solution.py:365
  39.6 1.6 %collective-permute-start.12 = (f32[4,4096]{1,0:T(4,128)S(1)}, f32[4,4096]{1,0:T(4,128)S(1)}, u32[]{:S(2)}, u32[]{:S(2)}) collective-permute-start(f32[4,4096]{1,0:T(4,128)S(1)} %get-tuple-element.31.refs_0_), channel_id=1, source_target_pairs={{0,12},{4,8},{8,4},{12,0},{16,28},{20,24},{24,20},{28,16},{1,13},{... | collective-permute-start | bytes 196616 | tf_op jit(solution)/shard_map/ppermute | solution.py:391
  41.2 0.4 collective-permute-start.11
  41.7 1.5 %collective-permute-start.10 = (f32[4,4096]{1,0:T(4,128)S(1)}, f32[4,4096]{1,0:T(4,128)S(1)}, u32[]{:S(2)}, u32[]{:S(2)}) collective-permute-start(f32[4,4096]{1,0:T(4,128)S(1)} %get-tuple-element.31.refs_0_), channel_id=1, source_target_pairs={{0,4},{4,0},{8,12},{12,8},{16,20},{20,16},{24,28},{28,24},{1,5},{5... | collective-permute-start | bytes 196616 | tf_op jit(solution)/shard_map/ppermute | solution.py:391
  43.2 2.3 %collective-permute-done.12.refs_3_ = f32[4,4096]{1,0:T(4,128)S(1)} collective-permute-done((f32[4,4096]{1,0:T(4,128)S(1)}, f32[4,4096]{1,0:T(4,128)S(1)}, u32[]{:S(2)}, u32[]{:S(2)}) %collective-permute-start.12) | collective-permute-done | bytes 65568 | tf_op jit(solution)/shard_map/ppermute | solution.py:391
  45.5 0.0 collective-permute-done.11.refs_2_
  45.5 0.6 collective-permute-done.10.refs_1_
  46.1 2.7 %collective-permute-start.13 = (f32[4,4096]{1,0:T(4,128)S(1)}, f32[4,4096]{1,0:T(4,128)S(1)}, u32[]{:S(2)}, u32[]{:S(2)}) collective-permute-start(f32[4,4096]{1,0:T(4,128)S(1)} %shard_map.117.refs_0_), channel_id=1, source_target_pairs={{0,16},{4,20},{8,24},{12,28},{16,0},{20,4},{24,8},{28,12},{1,17},{... | collective-permute-start | bytes 196616 | tf_op jit(solution)/shard_map/ppermute | solution.py:391
  48.8 0.1 shard_map.118.refs_2_
  48.9 2.5 %collective-permute-done.13.refs_1_ = f32[4,4096]{1,0:T(4,128)S(1)} collective-permute-done((f32[4,4096]{1,0:T(4,128)S(1)}, f32[4,4096]{1,0:T(4,128)S(1)}, u32[]{:S(2)}, u32[]{:S(2)}) %collective-permute-start.13) | collective-permute-done | bytes 65568 | tf_op jit(solution)/shard_map/ppermute | solution.py:391
  51.4 6.1 %shard_map.119 = (f32[1,4096]{1,0:T(1,128)}, f32[3,1024]{1,0:T(4,128)S(1)}, f32[3,1024]{1,0:T(4,128)S(1)}, f32[3,1024]{1,0:T(4,128)S(1)}, f32[3,1024]{1,0:T(4,128)S(1)}) custom-call(f32[4,4096]{1,0:T(4,128)S(1)} %shard_map.117.refs_0_, f32[4,4096]{1,0:T(4,128)S(1)} %collective-permute-done.13.refs_1_, bf16[32,4096]{1,0:T(8,128)(2,1)S(1)} %shard_map.118.refs_2_, ...), custom_call_target="tpu_custom_call" | custom-call | tf_op jit(solution)/shard_map/pallas_call | solution.py:365
  57.5 0.1 collective-permute-start.14
  57.6 1.2 %collective-permute-start.15 = (f32[3,1024]{1,0:T(4,128)S(1)}, f32[3,1024]{1,0:T(4,128)S(1)}, u32[]{:S(2)}, u32[]{:S(2)}) collective-permute-start(f32[3,1024]{1,0:T(4,128)S(1)} %get-tuple-element.36), channel_id=1, source_target_pairs={{0,2},{1,3},{2,0},{3,1},{4,6},{5,7},{6,4},{7,5},{8,10},{9,11},{10,... | collective-permute-start | bytes 36872 | tf_op jit(solution)/shard_map/ppermute | solution.py:382
  58.8 0.6 collective-permute-start.16
  59.4 0.7 %shard_map.120 = f32[3,4096]{1,0:T(4,128)} custom-call(f32[4,4096]{1,0:T(4,128)S(1)} %shard_map.117.refs_0_, f32[4,4096]{1,0:T(4,128)S(1)} %collective-permute-done.13.refs_1_, f32[10,4096]{1,0:T(8,128)S(1)} %convert_add_fusion.points.refs_8_.refs_4_.refs_2_, f32[3,1024]{1,0:T(4,128)S(1)} %get-tuple-element.34.refs_3_), custom_call_target="tpu_custom_call" | custom-call | tf_op jit(solution)/shard_map/pallas_call | solution.py:365
  60.1 0.0 collective-permute-done.14
  60.1 1.3 %collective-permute-done.15 = f32[3,1024]{1,0:T(4,128)S(1)} collective-permute-done((f32[3,1024]{1,0:T(4,128)S(1)}, f32[3,1024]{1,0:T(4,128)S(1)}, u32[]{:S(2)}, u32[]{:S(2)}) %collective-permute-start.15) | collective-permute-done | bytes 12320 | tf_op jit(solution)/shard_map/ppermute | solution.py:382
  61.4 0.6 collective-permute-done.16
  62.0 0.6 add_add_fusion
  (2 shorter events, 0.1 us)
Async XLA Ops:
  1.3 1.1 %copy-start = (s32[1,1,12]{2,1,0:T(1,128)S(1)}, s32[1,1,12]{2,1,0:T(1,128)}, u32[]{:S(2)}) copy-start(s32[1,1,12]{2,1,0:T(1,128)} %sources.1) | copy-start | bytes 148
  1.3 1.1 %copy-start.1 = (s32[1,1,12]{2,1,0:T(1,128)S(1)}, s32[1,1,12]{2,1,0:T(1,128)}, u32[]{:S(2)}) copy-start(s32[1,1,12]{2,1,0:T(1,128)} %targets.1) | copy-start | bytes 148
  5.4 3.9 %collective-permute-start.2 = (f32[1,4096]{1,0:T(1,128)S(1)}, f32[1,4096]{1,0:T(1,128)S(1)}, u32[]{:S(2)}, u32[]{:S(2)}) collective-permute-start(f32[1,4096]{1,0:T(1,128)S(1)} %get-tuple-element.21.refs_0_), channel_id=1, source_target_pairs={{0,3},{1,2},{2,1},{3,0},{4,7},{5,6},{6,5},{7,4},{8,11},{9,10},{10,... | collective-permute-start | bytes 49160 | tf_op jit(solution)/shard_map/ppermute | solution.py:382
  7.8 3.7 %collective-permute-start.1 = (f32[1,4096]{1,0:T(1,128)S(1)}, f32[1,4096]{1,0:T(1,128)S(1)}, u32[]{:S(2)}, u32[]{:S(2)}) collective-permute-start(f32[1,4096]{1,0:T(1,128)S(1)} %get-tuple-element.21.refs_0_), channel_id=1, source_target_pairs={{0,2},{1,3},{2,0},{3,1},{4,6},{5,7},{6,4},{7,5},{8,10},{9,11},{10,... | collective-permute-start | bytes 49160 | tf_op jit(solution)/shard_map/ppermute | solution.py:382
  8.5 3.1 %collective-permute-start = (f32[1,4096]{1,0:T(1,128)S(1)}, f32[1,4096]{1,0:T(1,128)S(1)}, u32[]{:S(2)}, u32[]{:S(2)}) collective-permute-start(f32[1,4096]{1,0:T(1,128)S(1)} %get-tuple-element.21.refs_0_), channel_id=1, source_target_pairs={{0,1},{1,0},{2,3},{3,2},{4,5},{5,4},{6,7},{7,6},{8,9},{9,8},{10,11... | collective-permute-start | bytes 49160 | tf_op jit(solution)/shard_map/ppermute | solution.py:382
  14.6 4.8 %collective-permute-start.5 = (f32[1,4096]{1,0:T(1,128)S(1)}, f32[1,4096]{1,0:T(1,128)S(1)}, u32[]{:S(2)}, u32[]{:S(2)}) collective-permute-start(f32[1,4096]{1,0:T(1,128)S(1)} %get-tuple-element.26.refs_0_), channel_id=1, source_target_pairs={{0,12},{4,8},{8,4},{12,0},{16,28},{20,24},{24,20},{28,16},{1,13},{... | collective-permute-start | bytes 49160 | tf_op jit(solution)/shard_map/ppermute | solution.py:391
  17.2 3.7 %collective-permute-start.4 = (f32[1,4096]{1,0:T(1,128)S(1)}, f32[1,4096]{1,0:T(1,128)S(1)}, u32[]{:S(2)}, u32[]{:S(2)}) collective-permute-start(f32[1,4096]{1,0:T(1,128)S(1)} %get-tuple-element.26.refs_0_), channel_id=1, source_target_pairs={{0,8},{4,12},{8,0},{12,4},{16,24},{20,28},{24,16},{28,20},{1,9},{5... | collective-permute-start | bytes 49160 | tf_op jit(solution)/shard_map/ppermute | solution.py:391
  17.6 3.7 %collective-permute-start.3 = (f32[1,4096]{1,0:T(1,128)S(1)}, f32[1,4096]{1,0:T(1,128)S(1)}, u32[]{:S(2)}, u32[]{:S(2)}) collective-permute-start(f32[1,4096]{1,0:T(1,128)S(1)} %get-tuple-element.26.refs_0_), channel_id=1, source_target_pairs={{0,4},{4,0},{8,12},{12,8},{16,20},{20,16},{24,28},{28,24},{1,5},{5... | collective-permute-start | bytes 49160 | tf_op jit(solution)/shard_map/ppermute | solution.py:391
  21.4 4.7 %collective-permute-start.6 = (f32[1,4096]{1,0:T(1,128)S(1)}, f32[1,4096]{1,0:T(1,128)S(1)}, u32[]{:S(2)}, u32[]{:S(2)}) collective-permute-start(f32[1,4096]{1,0:T(1,128)S(1)} %shard_map.113.refs_0_), channel_id=1, source_target_pairs={{0,16},{4,20},{8,24},{12,28},{16,0},{20,4},{24,8},{28,12},{1,17},{... | collective-permute-start | bytes 49160 | tf_op jit(solution)/shard_map/ppermute | solution.py:391
  29.2 3.2 %collective-permute-start.9 = (f32[1,4096]{1,0:T(1,128)S(1)}, f32[1,4096]{1,0:T(1,128)S(1)}, u32[]{:S(2)}, u32[]{:S(2)}) collective-permute-start(f32[1,4096]{1,0:T(1,128)S(1)} %shard_map.114.refs_0_), channel_id=1, source_target_pairs={{0,3},{1,2},{2,1},{3,0},{4,7},{5,6},{6,5},{7,4},{8,11},{9,10},{10,... | collective-permute-start | bytes 49160 | tf_op jit(solution)/shard_map/ppermute | solution.py:382
  29.3 3.8 %collective-permute-start.8 = (f32[1,4096]{1,0:T(1,128)S(1)}, f32[1,4096]{1,0:T(1,128)S(1)}, u32[]{:S(2)}, u32[]{:S(2)}) collective-permute-start(f32[1,4096]{1,0:T(1,128)S(1)} %shard_map.114.refs_0_), channel_id=1, source_target_pairs={{0,2},{1,3},{2,0},{3,1},{4,6},{5,7},{6,4},{7,5},{8,10},{9,11},{10,... | collective-permute-start | bytes 49160 | tf_op jit(solution)/shard_map/ppermute | solution.py:382
  30.0 3.1 %collective-permute-start.7 = (f32[1,4096]{1,0:T(1,128)S(1)}, f32[1,4096]{1,0:T(1,128)S(1)}, u32[]{:S(2)}, u32[]{:S(2)}) collective-permute-start(f32[1,4096]{1,0:T(1,128)S(1)} %shard_map.114.refs_0_), channel_id=1, source_target_pairs={{0,1},{1,0},{2,3},{3,2},{4,5},{5,4},{6,7},{7,6},{8,9},{9,8},{10,11... | collective-permute-start | bytes 49160 | tf_op jit(solution)/shard_map/ppermute | solution.py:382
  39.6 5.9 %collective-permute-start.12 = (f32[4,4096]{1,0:T(4,128)S(1)}, f32[4,4096]{1,0:T(4,128)S(1)}, u32[]{:S(2)}, u32[]{:S(2)}) collective-permute-start(f32[4,4096]{1,0:T(4,128)S(1)} %get-tuple-element.31.refs_0_), channel_id=1, source_target_pairs={{0,12},{4,8},{8,4},{12,0},{16,28},{20,24},{24,20},{28,16},{1,13},{... | collective-permute-start | bytes 196616 | tf_op jit(solution)/shard_map/ppermute | solution.py:391
  41.2 4.3 %collective-permute-start.11 = (f32[4,4096]{1,0:T(4,128)S(1)}, f32[4,4096]{1,0:T(4,128)S(1)}, u32[]{:S(2)}, u32[]{:S(2)}) collective-permute-start(f32[4,4096]{1,0:T(4,128)S(1)} %get-tuple-element.31.refs_0_), channel_id=1, source_target_pairs={{0,8},{4,12},{8,0},{12,4},{16,24},{20,28},{24,16},{28,20},{1,9},{5... | collective-permute-start | bytes 196616 | tf_op jit(solution)/shard_map/ppermute | solution.py:391
  41.7 4.4 %collective-permute-start.10 = (f32[4,4096]{1,0:T(4,128)S(1)}, f32[4,4096]{1,0:T(4,128)S(1)}, u32[]{:S(2)}, u32[]{:S(2)}) collective-permute-start(f32[4,4096]{1,0:T(4,128)S(1)} %get-tuple-element.31.refs_0_), channel_id=1, source_target_pairs={{0,4},{4,0},{8,12},{12,8},{16,20},{20,16},{24,28},{28,24},{1,5},{5... | collective-permute-start | bytes 196616 | tf_op jit(solution)/shard_map/ppermute | solution.py:391
  46.1 5.2 %collective-permute-start.13 = (f32[4,4096]{1,0:T(4,128)S(1)}, f32[4,4096]{1,0:T(4,128)S(1)}, u32[]{:S(2)}, u32[]{:S(2)}) collective-permute-start(f32[4,4096]{1,0:T(4,128)S(1)} %shard_map.117.refs_0_), channel_id=1, source_target_pairs={{0,16},{4,20},{8,24},{12,28},{16,0},{20,4},{24,8},{28,12},{1,17},{... | collective-permute-start | bytes 196616 | tf_op jit(solution)/shard_map/ppermute | solution.py:391
  57.5 2.6 %collective-permute-start.14 = (f32[3,1024]{1,0:T(4,128)S(1)}, f32[3,1024]{1,0:T(4,128)S(1)}, u32[]{:S(2)}, u32[]{:S(2)}) collective-permute-start(f32[3,1024]{1,0:T(4,128)S(1)} %get-tuple-element.35), channel_id=1, source_target_pairs={{0,1},{1,0},{2,3},{3,2},{4,5},{5,4},{6,7},{7,6},{8,9},{9,8},{10,11... | collective-permute-start | bytes 36872 | tf_op jit(solution)/shard_map/ppermute | solution.py:382
  57.6 3.8 %collective-permute-start.15 = (f32[3,1024]{1,0:T(4,128)S(1)}, f32[3,1024]{1,0:T(4,128)S(1)}, u32[]{:S(2)}, u32[]{:S(2)}) collective-permute-start(f32[3,1024]{1,0:T(4,128)S(1)} %get-tuple-element.36), channel_id=1, source_target_pairs={{0,2},{1,3},{2,0},{3,1},{4,6},{5,7},{6,4},{7,5},{8,10},{9,11},{10,... | collective-permute-start | bytes 36872 | tf_op jit(solution)/shard_map/ppermute | solution.py:382
  58.8 3.2 %collective-permute-start.16 = (f32[3,1024]{1,0:T(4,128)S(1)}, f32[3,1024]{1,0:T(4,128)S(1)}, u32[]{:S(2)}, u32[]{:S(2)}) collective-permute-start(f32[3,1024]{1,0:T(4,128)S(1)} %get-tuple-element.37), channel_id=1, source_target_pairs={{0,3},{1,2},{2,1},{3,0},{4,7},{5,6},{6,5},{7,4},{8,11},{9,10},{10,... | collective-permute-start | bytes 36872 | tf_op jit(solution)/shard_map/ppermute | solution.py:382

commit v10 on v9

--- a/solution.py
+++ b/solution.py
@@ -261,7 +261,7 @@
     place(stack, split(xs), SOURCE_ORDER)
     xc_out[...] = stack[...].astype(BF16)
     copy.wait()
-    part_out[...] = lse_tiles(Tiles(lists, sides(xc_out, yc_out), True), turned, xc_out, top, total, lanes=256)[1]
+    part_out[...] = lse_tiles(Tiles(lists, sides(xc_out, yc_out), True), turned, xc_out, top, total, lanes=256, ahead=2)[1]
 
 
 def col_kernel(
@@ -279,7 +279,7 @@
     copy = fetch(lists_in, lists, sem)
     turn(turned, low, yc, split(log_target[...] - combine([ref[...] for ref in parts])[0]))
     copy.wait()
-    part_out[...] = lse_tiles(Tiles(lists, sides(xc, yc), True), turned, xc, top, total, chunk=64)[1]
+    part_out[...] = lse_tiles(Tiles(lists, sides(xc, yc), True), turned, xc, top, total, lanes=256)[1]
 
 
 def last_col_kernel(
@@ -298,7 +298,7 @@
 
     @pl.when(near)
     def _():
-        mass, *moved = plan_tiles(tiles, turned, kept, columns, points, 0, sums, chunk=32, ahead=2)
+        mass, *moved = plan_tiles(tiles, turned, kept, columns, points, 0, sums, chunk=64, lanes=256, ahead=2)
         part_out[0:1, :] = top_before[...] + log2(mass)
         inverse = 1.0 / mass
         for c, total in enumerate(moved):
@@ -346,7 +346,7 @@
     turn(turned, low, yc, split(log_target[...] - lse), [jnp.ones_like(lse)] * 3)
     copy.wait()
     tiles = Tiles(lists, sides(xc, yc), True)
-    mass, *moved = plan_tiles(tiles, turned, kept, columns, points, 3, sums, chunk=32, ahead=2)
+    mass, *moved = plan_tiles(tiles, turned, kept, columns, points, 3, sums, lanes=256)
     for c in range(3):
         whole[c : c + 1, :] = xs[c : c + 1, :] * mass - moved[c]
     place_tgt = lax.axis_index("tgt")

time: 62.8 us -> 62.9 us (level)
  no operation moved by 1% of the time
where the time goes in v10:
time: 62.9 us; the launch traced here: 62.7 us
  Pallas kernels  22.8 us (36%)
  starting transfers between devices  19.4 us (31%)
  waiting for transfers between devices  17.5 us (28%)
  other arithmetic  1.65 us (3%)
  between operations  1.4 us (2%)
    pallas_call x10, Pallas kernels, call(): pl.pallas_call(kernel, out_shape=outs, in_specs=[VMEM] * len(ins) + [HBM]...  22.8 us
    ppermute x8, starting transfers between devices, sum_up(): lax.ppermute(value, axis, [(i, i ^ k) for i in range(n)])  12.4 us
    ppermute x8, waiting for transfers between devices, sum_up(): lax.ppermute(value, axis, [(i, i ^ k) for i in range(n)])  10.7 us
    ppermute x9, starting transfers between devices, exchange(): lax.ppermute(values[k], axis, [(i, peer(i, k, n)) for i in range(n)])  6.97 us
    ppermute x9, waiting for transfers between devices, exchange(): lax.ppermute(values[k], axis, [(i, peer(i, k, n)) for i in range(n)])  6.79 us
  transfers between devices with their start and end apart: 17, of which 13 were waited for; matrix products, arithmetic and copies ran while one was open for 0% of the time, Pallas kernels for 1%

profile of v10, /device:TPU:0, one launch (start us, length us, event | category | flops | bytes accessed | tf_op | source)
XLA Modules:
  0.0 62.7 jit_solution(14272638672164230602)
XLA Ops:
  1.3 0.0 copy-start
  1.3 0.0 copy-start.1
  1.3 1.0 %convert_add_fusion.points.refs_8_.refs_4_.refs_2_ = f32[10,4096]{1,0:T(8,128)S(1)} fusion(s32[1,1]{1,0:T(1,128)S(6)} %copy.12, f32[1,4096]{1,0:T(1,128)} %bitcast.5, f32[1,4096]{1,0:T(1,128)} %bitcast.6, f32[1,4096]{1,0:T(1,128)} %bitcast.7, f32[3,4096]{1,0:T(4,128)} %param.9, f32[3,4096]{1,0:T(4,128)} %param.8), kind=kLoop, calls=%fused_computation | loop fusion | flops 245760 | bytes 311300 | tf_op jit(solution)/shard_map/add | solution.py:408
  2.3 0.0 copy-done
  2.3 0.0 copy-done.1
  2.4 3.0 %shard_map.111 = (bf16[32,4096]{1,0:T(8,128)(2,1)S(1)}, bf16[32,4096]{1,0:T(8,128)(2,1)S(1)}, f32[1,4096]{1,0:T(1,128)S(1)}, s32[1,1,12]{2,1,0:T(1,128)S(1)}, f3...) custom-call(f32[10,4096]{1,0:T(8,128)S(1)} %convert_add_fusion.points.refs_8_.refs_4_.refs_2_, s32[1,1,12]{2,1,0:T(1,128)S(1)} %copy-done, ...), custom_call_target="tpu_custom_call" | custom-call | tf_op jit(solution)/shard_map/pallas_call | solution.py:365
  5.4 2.4 %collective-permute-start.2 = (f32[1,4096]{1,0:T(1,128)S(1)}, f32[1,4096]{1,0:T(1,128)S(1)}, u32[]{:S(2)}, u32[]{:S(2)}) collective-permute-start(f32[1,4096]{1,0:T(1,128)S(1)} %get-tuple-element.21.refs_0_), channel_id=1, source_target_pairs={{0,3},{1,2},{2,1},{3,0},{4,7},{5,6},{6,5},{7,4},{8,11},{9,10},{10,... | collective-permute-start | bytes 49160 | tf_op jit(solution)/shard_map/ppermute | solution.py:382
  7.8 0.6 %collective-permute-start.1 = (f32[1,4096]{1,0:T(1,128)S(1)}, f32[1,4096]{1,0:T(1,128)S(1)}, u32[]{:S(2)}, u32[]{:S(2)}) collective-permute-start(f32[1,4096]{1,0:T(1,128)S(1)} %get-tuple-element.21.refs_0_), channel_id=1, source_target_pairs={{0,2},{1,3},{2,0},{3,1},{4,6},{5,7},{6,4},{7,5},{8,10},{9,11},{10,... | collective-permute-start | bytes 49160 | tf_op jit(solution)/shard_map/ppermute | solution.py:382
  8.5 0.0 collective-permute-start
  8.5 0.8 %collective-permute-done.2.refs_3_ = f32[1,4096]{1,0:T(1,128)S(1)} collective-permute-done((f32[1,4096]{1,0:T(1,128)S(1)}, f32[1,4096]{1,0:T(1,128)S(1)}, u32[]{:S(2)}, u32[]{:S(2)}) %collective-permute-start.2) | collective-permute-done | bytes 16416 | tf_op jit(solution)/shard_map/ppermute | solution.py:382
  9.3 2.3 %collective-permute-done.1.refs_2_ = f32[1,4096]{1,0:T(1,128)S(1)} collective-permute-done((f32[1,4096]{1,0:T(1,128)S(1)}, f32[1,4096]{1,0:T(1,128)S(1)}, u32[]{:S(2)}, u32[]{:S(2)}) %collective-permute-start.1) | collective-permute-done | bytes 16416 | tf_op jit(solution)/shard_map/ppermute | solution.py:382
  11.6 0.0 collective-permute-done.refs_1_
  11.6 3.0 %shard_map.112 = (f32[1,4096]{1,0:T(1,128)S(1)}, f32[1,4096]{1,0:T(1,128)S(1)}, f32[1,4096]{1,0:T(1,128)S(1)}) custom-call(f32[1,4096]{1,0:T(1,128)S(1)} %get-tuple-element.21.refs_0_, f32[1,4096]{1,0:T(1,128)S(1)} %collective-permute-done.refs_1_, f32[1,4096]{1,0:T(1,128)S(1)} %collective-permute-done.1.refs_2_, ...), custom_call_target="tpu_custom_call" | custom-call | tf_op jit(solution)/shard_map/pallas_call | solution.py:365
  14.6 2.6 %collective-permute-start.5 = (f32[1,4096]{1,0:T(1,128)S(1)}, f32[1,4096]{1,0:T(1,128)S(1)}, u32[]{:S(2)}, u32[]{:S(2)}) collective-permute-start(f32[1,4096]{1,0:T(1,128)S(1)} %get-tuple-element.26.refs_0_), channel_id=1, source_target_pairs={{0,12},{4,8},{8,4},{12,0},{16,28},{20,24},{24,20},{28,16},{1,13},{... | collective-permute-start | bytes 49160 | tf_op jit(solution)/shard_map/ppermute | solution.py:391
  17.2 0.4 collective-permute-start.4
  17.6 0.5 collective-permute-start.3
  18.1 1.2 %collective-permute-done.5.refs_3_ = f32[1,4096]{1,0:T(1,128)S(1)} collective-permute-done((f32[1,4096]{1,0:T(1,128)S(1)}, f32[1,4096]{1,0:T(1,128)S(1)}, u32[]{:S(2)}, u32[]{:S(2)}) %collective-permute-start.5) | collective-permute-done | bytes 16416 | tf_op jit(solution)/shard_map/ppermute | solution.py:391
  19.3 1.6 %collective-permute-done.4.refs_2_ = f32[1,4096]{1,0:T(1,128)S(1)} collective-permute-done((f32[1,4096]{1,0:T(1,128)S(1)}, f32[1,4096]{1,0:T(1,128)S(1)}, u32[]{:S(2)}, u32[]{:S(2)}) %collective-permute-start.4) | collective-permute-done | bytes 16416 | tf_op jit(solution)/shard_map/ppermute | solution.py:391
  20.9 0.4 collective-permute-done.3.refs_1_
  21.4 2.6 %collective-permute-start.6 = (f32[1,4096]{1,0:T(1,128)S(1)}, f32[1,4096]{1,0:T(1,128)S(1)}, u32[]{:S(2)}, u32[]{:S(2)}) collective-permute-start(f32[1,4096]{1,0:T(1,128)S(1)} %shard_map.113.refs_0_), channel_id=1, source_target_pairs={{0,16},{4,20},{8,24},{12,28},{16,0},{20,4},{24,8},{28,12},{1,17},{... | collective-permute-start | bytes 49160 | tf_op jit(solution)/shard_map/ppermute | solution.py:391
  24.0 2.1 %collective-permute-done.6.refs_1_ = f32[1,4096]{1,0:T(1,128)S(1)} collective-permute-done((f32[1,4096]{1,0:T(1,128)S(1)}, f32[1,4096]{1,0:T(1,128)S(1)}, u32[]{:S(2)}, u32[]{:S(2)}) %collective-permute-start.6) | collective-permute-done | bytes 16416 | tf_op jit(solution)/shard_map/ppermute | solution.py:391
  26.1 2.8 %shard_map.114.refs_0_ = f32[1,4096]{1,0:T(1,128)S(1)} custom-call(f32[1,4096]{1,0:T(1,128)S(1)} %shard_map.113.refs_0_, f32[1,4096]{1,0:T(1,128)S(1)} %collective-permute-done.6.refs_1_, f32[1,4096]{1,0:T(1,128)S(1)} %get-tuple-element.27.refs_2_.refs_3_, bf16[32,4096]{1,0:T(8,128)(2,1)S(1)} %get-tuple-element.23.refs_5_.refs_3_.refs_9_.static, ...), custom_call_target="tpu_custom_call" | custom-call | tf_op jit(solution)/shard_map/pallas_call | solution.py:365
  28.9 0.1 collective-permute-start.9
  29.0 0.7 %collective-permute-start.8 = (f32[1,4096]{1,0:T(1,128)S(1)}, f32[1,4096]{1,0:T(1,128)S(1)}, u32[]{:S(2)}, u32[]{:S(2)}) collective-permute-start(f32[1,4096]{1,0:T(1,128)S(1)} %shard_map.114.refs_0_), channel_id=1, source_target_pairs={{0,2},{1,3},{2,0},{3,1},{4,6},{5,7},{6,4},{7,5},{8,10},{9,11},{10,... | collective-permute-start | bytes 49160 | tf_op jit(solution)/shard_map/ppermute | solution.py:382
  29.7 1.1 %collective-permute-start.7 = (f32[1,4096]{1,0:T(1,128)S(1)}, f32[1,4096]{1,0:T(1,128)S(1)}, u32[]{:S(2)}, u32[]{:S(2)}) collective-permute-start(f32[1,4096]{1,0:T(1,128)S(1)} %shard_map.114.refs_0_), channel_id=1, source_target_pairs={{0,1},{1,0},{2,3},{3,2},{4,5},{5,4},{6,7},{7,6},{8,9},{9,8},{10,11... | collective-permute-start | bytes 49160 | tf_op jit(solution)/shard_map/ppermute | solution.py:382
  30.8 0.1 shard_map.115.refs_6_
  30.9 1.2 %collective-permute-done.9.refs_3_ = f32[1,4096]{1,0:T(1,128)S(1)} collective-permute-done((f32[1,4096]{1,0:T(1,128)S(1)}, f32[1,4096]{1,0:T(1,128)S(1)}, u32[]{:S(2)}, u32[]{:S(2)}) %collective-permute-start.9) | collective-permute-done | bytes 16416 | tf_op jit(solution)/shard_map/ppermute | solution.py:382
  32.2 0.7 %collective-permute-done.8.refs_2_ = f32[1,4096]{1,0:T(1,128)S(1)} collective-permute-done((f32[1,4096]{1,0:T(1,128)S(1)}, f32[1,4096]{1,0:T(1,128)S(1)}, u32[]{:S(2)}, u32[]{:S(2)}) %collective-permute-start.8) | collective-permute-done | bytes 16416 | tf_op jit(solution)/shard_map/ppermute | solution.py:382
  32.8 0.0 collective-permute-done.7.refs_1_
  32.8 6.8 %shard_map.116 = (f32[1,4096]{1,0:T(1,128)}, f32[1,4096]{1,0:T(1,128)S(1)}, f32[4,4096]{1,0:T(4,128)S(1)}) custom-call(f32[1,4096]{1,0:T(1,128)S(1)} %shard_map.114.refs_0_, f32[1,4096]{1,0:T(1,128)S(1)} %collective-permute-done.7.refs_1_, f32[1,4096]{1,0:T(1,128)S(1)} %collective-permute-done.8.refs_2_, f32[1,4096]{1,0:T(1,128)S(1)} %collective-permute-done.9.refs_3_, ...), custom_call_target="tpu_custom_call" | custom-call | tf_op jit(solution)/shard_map/pallas_call | solution.py:365
  39.6 1.6 %collective-permute-start.12 = (f32[4,4096]{1,0:T(4,128)S(1)}, f32[4,4096]{1,0:T(4,128)S(1)}, u32[]{:S(2)}, u32[]{:S(2)}) collective-permute-start(f32[4,4096]{1,0:T(4,128)S(1)} %get-tuple-element.31.refs_0_), channel_id=1, source_target_pairs={{0,12},{4,8},{8,4},{12,0},{16,28},{20,24},{24,20},{28,16},{1,13},{... | collective-permute-start | bytes 196616 | tf_op jit(solution)/shard_map/ppermute | solution.py:391
  41.2 0.5 collective-permute-start.11
  41.6 1.5 %collective-permute-start.10 = (f32[4,4096]{1,0:T(4,128)S(1)}, f32[4,4096]{1,0:T(4,128)S(1)}, u32[]{:S(2)}, u32[]{:S(2)}) collective-permute-start(f32[4,4096]{1,0:T(4,128)S(1)} %get-tuple-element.31.refs_0_), channel_id=1, source_target_pairs={{0,4},{4,0},{8,12},{12,8},{16,20},{20,16},{24,28},{28,24},{1,5},{5... | collective-permute-start | bytes 196616 | tf_op jit(solution)/shard_map/ppermute | solution.py:391
  43.1 2.3 %collective-permute-done.12.refs_3_ = f32[4,4096]{1,0:T(4,128)S(1)} collective-permute-done((f32[4,4096]{1,0:T(4,128)S(1)}, f32[4,4096]{1,0:T(4,128)S(1)}, u32[]{:S(2)}, u32[]{:S(2)}) %collective-permute-start.12) | collective-permute-done | bytes 65568 | tf_op jit(solution)/shard_map/ppermute | solution.py:391
  45.5 0.0 collective-permute-done.11.refs_2_
  45.5 0.6 collective-permute-done.10.refs_1_
  46.1 2.7 %collective-permute-start.13 = (f32[4,4096]{1,0:T(4,128)S(1)}, f32[4,4096]{1,0:T(4,128)S(1)}, u32[]{:S(2)}, u32[]{:S(2)}) collective-permute-start(f32[4,4096]{1,0:T(4,128)S(1)} %shard_map.117.refs_0_), channel_id=1, source_target_pairs={{0,16},{4,20},{8,24},{12,28},{16,0},{20,4},{24,8},{28,12},{1,17},{... | collective-permute-start | bytes 196616 | tf_op jit(solution)/shard_map/ppermute | solution.py:391
  48.8 0.1 shard_map.118.refs_2_
  48.9 2.5 %collective-permute-done.13.refs_1_ = f32[4,4096]{1,0:T(4,128)S(1)} collective-permute-done((f32[4,4096]{1,0:T(4,128)S(1)}, f32[4,4096]{1,0:T(4,128)S(1)}, u32[]{:S(2)}, u32[]{:S(2)}) %collective-permute-start.13) | collective-permute-done | bytes 65568 | tf_op jit(solution)/shard_map/ppermute | solution.py:391
  51.3 6.2 %shard_map.119 = (f32[1,4096]{1,0:T(1,128)}, f32[3,1024]{1,0:T(4,128)S(1)}, f32[3,1024]{1,0:T(4,128)S(1)}, f32[3,1024]{1,0:T(4,128)S(1)}, f32[3,1024]{1,0:T(4,128)S(1)}) custom-call(f32[4,4096]{1,0:T(4,128)S(1)} %shard_map.117.refs_0_, f32[4,4096]{1,0:T(4,128)S(1)} %collective-permute-done.13.refs_1_, bf16[32,4096]{1,0:T(8,128)(2,1)S(1)} %shard_map.118.refs_2_, ...), custom_call_target="tpu_custom_call" | custom-call | tf_op jit(solution)/shard_map/pallas_call | solution.py:365
  57.6 0.1 collective-permute-start.14
  57.7 1.2 %collective-permute-start.15 = (f32[3,1024]{1,0:T(4,128)S(1)}, f32[3,1024]{1,0:T(4,128)S(1)}, u32[]{:S(2)}, u32[]{:S(2)}) collective-permute-start(f32[3,1024]{1,0:T(4,128)S(1)} %get-tuple-element.36), channel_id=1, source_target_pairs={{0,2},{1,3},{2,0},{3,1},{4,6},{5,7},{6,4},{7,5},{8,10},{9,11},{10,... | collective-permute-start | bytes 36872 | tf_op jit(solution)/shard_map/ppermute | solution.py:382
  58.9 0.6 %collective-permute-start.16 = (f32[3,1024]{1,0:T(4,128)S(1)}, f32[3,1024]{1,0:T(4,128)S(1)}, u32[]{:S(2)}, u32[]{:S(2)}) collective-permute-start(f32[3,1024]{1,0:T(4,128)S(1)} %get-tuple-element.37), channel_id=1, source_target_pairs={{0,3},{1,2},{2,1},{3,0},{4,7},{5,6},{6,5},{7,4},{8,11},{9,10},{10,... | collective-permute-start | bytes 36872 | tf_op jit(solution)/shard_map/ppermute | solution.py:382
  59.5 0.7 %shard_map.120 = f32[3,4096]{1,0:T(4,128)} custom-call(f32[4,4096]{1,0:T(4,128)S(1)} %shard_map.117.refs_0_, f32[4,4096]{1,0:T(4,128)S(1)} %collective-permute-done.13.refs_1_, f32[10,4096]{1,0:T(8,128)S(1)} %convert_add_fusion.points.refs_8_.refs_4_.refs_2_, f32[3,1024]{1,0:T(4,128)S(1)} %get-tuple-element.34.refs_3_), custom_call_target="tpu_custom_call" | custom-call | tf_op jit(solution)/shard_map/pallas_call | solution.py:365
  60.2 0.0 collective-permute-done.14
  60.2 1.3 %collective-permute-done.15 = f32[3,1024]{1,0:T(4,128)S(1)} collective-permute-done((f32[3,1024]{1,0:T(4,128)S(1)}, f32[3,1024]{1,0:T(4,128)S(1)}, u32[]{:S(2)}, u32[]{:S(2)}) %collective-permute-start.15) | collective-permute-done | bytes 12320 | tf_op jit(solution)/shard_map/ppermute | solution.py:382
  61.5 0.6 collective-permute-done.16
  62.1 0.6 add_add_fusion
  (2 shorter events, 0.1 us)
Async XLA Ops:
  1.3 1.1 %copy-start = (s32[1,1,12]{2,1,0:T(1,128)S(1)}, s32[1,1,12]{2,1,0:T(1,128)}, u32[]{:S(2)}) copy-start(s32[1,1,12]{2,1,0:T(1,128)} %sources.1) | copy-start | bytes 148
  1.3 1.1 %copy-start.1 = (s32[1,1,12]{2,1,0:T(1,128)S(1)}, s32[1,1,12]{2,1,0:T(1,128)}, u32[]{:S(2)}) copy-start(s32[1,1,12]{2,1,0:T(1,128)} %targets.1) | copy-start | bytes 148
  5.4 3.9 %collective-permute-start.2 = (f32[1,4096]{1,0:T(1,128)S(1)}, f32[1,4096]{1,0:T(1,128)S(1)}, u32[]{:S(2)}, u32[]{:S(2)}) collective-permute-start(f32[1,4096]{1,0:T(1,128)S(1)} %get-tuple-element.21.refs_0_), channel_id=1, source_target_pairs={{0,3},{1,2},{2,1},{3,0},{4,7},{5,6},{6,5},{7,4},{8,11},{9,10},{10,... | collective-permute-start | bytes 49160 | tf_op jit(solution)/shard_map/ppermute | solution.py:382
  7.8 3.7 %collective-permute-start.1 = (f32[1,4096]{1,0:T(1,128)S(1)}, f32[1,4096]{1,0:T(1,128)S(1)}, u32[]{:S(2)}, u32[]{:S(2)}) collective-permute-start(f32[1,4096]{1,0:T(1,128)S(1)} %get-tuple-element.21.refs_0_), channel_id=1, source_target_pairs={{0,2},{1,3},{2,0},{3,1},{4,6},{5,7},{6,4},{7,5},{8,10},{9,11},{10,... | collective-permute-start | bytes 49160 | tf_op jit(solution)/shard_map/ppermute | solution.py:382
  8.5 3.1 %collective-permute-start = (f32[1,4096]{1,0:T(1,128)S(1)}, f32[1,4096]{1,0:T(1,128)S(1)}, u32[]{:S(2)}, u32[]{:S(2)}) collective-permute-start(f32[1,4096]{1,0:T(1,128)S(1)} %get-tuple-element.21.refs_0_), channel_id=1, source_target_pairs={{0,1},{1,0},{2,3},{3,2},{4,5},{5,4},{6,7},{7,6},{8,9},{9,8},{10,11... | collective-permute-start | bytes 49160 | tf_op jit(solution)/shard_map/ppermute | solution.py:382
  14.6 4.7 %collective-permute-start.5 = (f32[1,4096]{1,0:T(1,128)S(1)}, f32[1,4096]{1,0:T(1,128)S(1)}, u32[]{:S(2)}, u32[]{:S(2)}) collective-permute-start(f32[1,4096]{1,0:T(1,128)S(1)} %get-tuple-element.26.refs_0_), channel_id=1, source_target_pairs={{0,12},{4,8},{8,4},{12,0},{16,28},{20,24},{24,20},{28,16},{1,13},{... | collective-permute-start | bytes 49160 | tf_op jit(solution)/shard_map/ppermute | solution.py:391
  17.2 3.7 %collective-permute-start.4 = (f32[1,4096]{1,0:T(1,128)S(1)}, f32[1,4096]{1,0:T(1,128)S(1)}, u32[]{:S(2)}, u32[]{:S(2)}) collective-permute-start(f32[1,4096]{1,0:T(1,128)S(1)} %get-tuple-element.26.refs_0_), channel_id=1, source_target_pairs={{0,8},{4,12},{8,0},{12,4},{16,24},{20,28},{24,16},{28,20},{1,9},{5... | collective-permute-start | bytes 49160 | tf_op jit(solution)/shard_map/ppermute | solution.py:391
  17.6 3.7 %collective-permute-start.3 = (f32[1,4096]{1,0:T(1,128)S(1)}, f32[1,4096]{1,0:T(1,128)S(1)}, u32[]{:S(2)}, u32[]{:S(2)}) collective-permute-start(f32[1,4096]{1,0:T(1,128)S(1)} %get-tuple-element.26.refs_0_), channel_id=1, source_target_pairs={{0,4},{4,0},{8,12},{12,8},{16,20},{20,16},{24,28},{28,24},{1,5},{5... | collective-permute-start | bytes 49160 | tf_op jit(solution)/shard_map/ppermute | solution.py:391
  21.4 4.7 %collective-permute-start.6 = (f32[1,4096]{1,0:T(1,128)S(1)}, f32[1,4096]{1,0:T(1,128)S(1)}, u32[]{:S(2)}, u32[]{:S(2)}) collective-permute-start(f32[1,4096]{1,0:T(1,128)S(1)} %shard_map.113.refs_0_), channel_id=1, source_target_pairs={{0,16},{4,20},{8,24},{12,28},{16,0},{20,4},{24,8},{28,12},{1,17},{... | collective-permute-start | bytes 49160 | tf_op jit(solution)/shard_map/ppermute | solution.py:391
  28.9 3.2 %collective-permute-start.9 = (f32[1,4096]{1,0:T(1,128)S(1)}, f32[1,4096]{1,0:T(1,128)S(1)}, u32[]{:S(2)}, u32[]{:S(2)}) collective-permute-start(f32[1,4096]{1,0:T(1,128)S(1)} %shard_map.114.refs_0_), channel_id=1, source_target_pairs={{0,3},{1,2},{2,1},{3,0},{4,7},{5,6},{6,5},{7,4},{8,11},{9,10},{10,... | collective-permute-start | bytes 49160 | tf_op jit(solution)/shard_map/ppermute | solution.py:382
  29.0 3.8 %collective-permute-start.8 = (f32[1,4096]{1,0:T(1,128)S(1)}, f32[1,4096]{1,0:T(1,128)S(1)}, u32[]{:S(2)}, u32[]{:S(2)}) collective-permute-start(f32[1,4096]{1,0:T(1,128)S(1)} %shard_map.114.refs_0_), channel_id=1, source_target_pairs={{0,2},{1,3},{2,0},{3,1},{4,6},{5,7},{6,4},{7,5},{8,10},{9,11},{10,... | collective-permute-start | bytes 49160 | tf_op jit(solution)/shard_map/ppermute | solution.py:382
  29.7 3.1 %collective-permute-start.7 = (f32[1,4096]{1,0:T(1,128)S(1)}, f32[1,4096]{1,0:T(1,128)S(1)}, u32[]{:S(2)}, u32[]{:S(2)}) collective-permute-start(f32[1,4096]{1,0:T(1,128)S(1)} %shard_map.114.refs_0_), channel_id=1, source_target_pairs={{0,1},{1,0},{2,3},{3,2},{4,5},{5,4},{6,7},{7,6},{8,9},{9,8},{10,11... | collective-permute-start | bytes 49160 | tf_op jit(solution)/shard_map/ppermute | solution.py:382
  39.6 5.9 %collective-permute-start.12 = (f32[4,4096]{1,0:T(4,128)S(1)}, f32[4,4096]{1,0:T(4,128)S(1)}, u32[]{:S(2)}, u32[]{:S(2)}) collective-permute-start(f32[4,4096]{1,0:T(4,128)S(1)} %get-tuple-element.31.refs_0_), channel_id=1, source_target_pairs={{0,12},{4,8},{8,4},{12,0},{16,28},{20,24},{24,20},{28,16},{1,13},{... | collective-permute-start | bytes 196616 | tf_op jit(solution)/shard_map/ppermute | solution.py:391
  41.2 4.3 %collective-permute-start.11 = (f32[4,4096]{1,0:T(4,128)S(1)}, f32[4,4096]{1,0:T(4,128)S(1)}, u32[]{:S(2)}, u32[]{:S(2)}) collective-permute-start(f32[4,4096]{1,0:T(4,128)S(1)} %get-tuple-element.31.refs_0_), channel_id=1, source_target_pairs={{0,8},{4,12},{8,0},{12,4},{16,24},{20,28},{24,16},{28,20},{1,9},{5... | collective-permute-start | bytes 196616 | tf_op jit(solution)/shard_map/ppermute | solution.py:391
  41.6 4.4 %collective-permute-start.10 = (f32[4,4096]{1,0:T(4,128)S(1)}, f32[4,4096]{1,0:T(4,128)S(1)}, u32[]{:S(2)}, u32[]{:S(2)}) collective-permute-start(f32[4,4096]{1,0:T(4,128)S(1)} %get-tuple-element.31.refs_0_), channel_id=1, source_target_pairs={{0,4},{4,0},{8,12},{12,8},{16,20},{20,16},{24,28},{28,24},{1,5},{5... | collective-permute-start | bytes 196616 | tf_op jit(solution)/shard_map/ppermute | solution.py:391
  46.1 5.2 %collective-permute-start.13 = (f32[4,4096]{1,0:T(4,128)S(1)}, f32[4,4096]{1,0:T(4,128)S(1)}, u32[]{:S(2)}, u32[]{:S(2)}) collective-permute-start(f32[4,4096]{1,0:T(4,128)S(1)} %shard_map.117.refs_0_), channel_id=1, source_target_pairs={{0,16},{4,20},{8,24},{12,28},{16,0},{20,4},{24,8},{28,12},{1,17},{... | collective-permute-start | bytes 196616 | tf_op jit(solution)/shard_map/ppermute | solution.py:391
  57.6 2.6 %collective-permute-start.14 = (f32[3,1024]{1,0:T(4,128)S(1)}, f32[3,1024]{1,0:T(4,128)S(1)}, u32[]{:S(2)}, u32[]{:S(2)}) collective-permute-start(f32[3,1024]{1,0:T(4,128)S(1)} %get-tuple-element.35), channel_id=1, source_target_pairs={{0,1},{1,0},{2,3},{3,2},{4,5},{5,4},{6,7},{7,6},{8,9},{9,8},{10,11... | collective-permute-start | bytes 36872 | tf_op jit(solution)/shard_map/ppermute | solution.py:382
  57.7 3.8 %collective-permute-start.15 = (f32[3,1024]{1,0:T(4,128)S(1)}, f32[3,1024]{1,0:T(4,128)S(1)}, u32[]{:S(2)}, u32[]{:S(2)}) collective-permute-start(f32[3,1024]{1,0:T(4,128)S(1)} %get-tuple-element.36), channel_id=1, source_target_pairs={{0,2},{1,3},{2,0},{3,1},{4,6},{5,7},{6,4},{7,5},{8,10},{9,11},{10,... | collective-permute-start | bytes 36872 | tf_op jit(solution)/shard_map/ppermute | solution.py:382
  58.9 3.2 %collective-permute-start.16 = (f32[3,1024]{1,0:T(4,128)S(1)}, f32[3,1024]{1,0:T(4,128)S(1)}, u32[]{:S(2)}, u32[]{:S(2)}) collective-permute-start(f32[3,1024]{1,0:T(4,128)S(1)} %get-tuple-element.37), channel_id=1, source_target_pairs={{0,3},{1,2},{2,1},{3,0},{4,7},{5,6},{6,5},{7,4},{8,11},{9,10},{10,... | collective-permute-start | bytes 36872 | tf_op jit(solution)/shard_map/ppermute | solution.py:382

commit v11 on v9

--- a/solution.py
+++ b/solution.py
@@ -279,7 +279,7 @@
     copy = fetch(lists_in, lists, sem)
     turn(turned, low, yc, split(log_target[...] - combine([ref[...] for ref in parts])[0]))
     copy.wait()
-    part_out[...] = lse_tiles(Tiles(lists, sides(xc, yc), True), turned, xc, top, total, chunk=64)[1]
+    part_out[...] = lse_tiles(Tiles(lists, sides(xc, yc), True), turned, xc, top, total, lanes=256)[1]
 
 
 def last_col_kernel(
@@ -350,7 +350,7 @@
     for c in range(3):
         whole[c : c + 1, :] = xs[c : c + 1, :] * mass - moved[c]
     place_tgt = lax.axis_index("tgt")
-    for k, out in enumerate(source_out):
+    for k, out in enumerate(reversed(source_out)):
         width = out.shape[1]
         at = pl.multiple_of(peer(place_tgt, k, shares) * width, width)
         out[...] = whole[:, pl.ds(at, width)]
@@ -378,9 +378,8 @@
 
 def exchange(values, axis):
     n = lax.axis_size(axis)
-    return values[:1] + [
-        lax.ppermute(values[k], axis, [(i, peer(i, k, n)) for i in range(n)]) for k in range(1, n)
-    ]
+    far_first = [lax.ppermute(values[k], axis, [(i, peer(i, k, n)) for i in range(n)]) for k in range(n - 1, 0, -1)]
+    return values[:1] + far_first[::-1]
 
 
 def sum_up(value, axis):
@@ -498,8 +497,9 @@
         ],
         far=(0,),
     )
-    (target_grad,) = call(bunch(target_kernel, len(parts)), (*parts, points, moved[0]), (), [rows(nt, 3)], [])
-    own_grad = functools.reduce(jnp.add, exchange(moved, "tgt"))
+    (target_grad,) = call(bunch(target_kernel, len(parts)), (*parts, points, moved[-1]), (), [rows(nt, 3)], [])
+    own, *others = exchange(moved[::-1], "tgt")
+    own_grad = functools.reduce(jnp.add, others[::-1], own)
     return (f.reshape(-1), g.reshape(-1), own_grad, target_grad)
 
 

time: 62.8 us -> 61.9 us (0.986)
  no operation moved by 1% of the time
where the time goes in v11:
time: 61.9 us; the launch traced here: 61.7 us
  Pallas kernels  22.4 us (36%)
  starting transfers between devices  19.4 us (31%)
  waiting for transfers between devices  16.9 us (27%)
  other arithmetic  1.65 us (3%)
  between operations  1.4 us (2%)
    pallas_call x10, Pallas kernels, call(): pl.pallas_call(kernel, out_shape=outs, in_specs=[VMEM] * len(ins) + [HBM]...  22.4 us
    ppermute x8, starting transfers between devices, sum_up(): lax.ppermute(value, axis, [(i, i ^ k) for i in range(n)])  12.4 us
    ppermute x8, waiting for transfers between devices, sum_up(): lax.ppermute(value, axis, [(i, i ^ k) for i in range(n)])  10.7 us
    ppermute x9, starting transfers between devices, exchange(): lax.ppermute(values[k], axis, [(i, peer(i, k, n)) for i in range(n)])  6.96 us
    ppermute x9, waiting for transfers between devices, exchange(): lax.ppermute(values[k], axis, [(i, peer(i, k, n)) for i in range(n)])  6.23 us
  transfers between devices with their start and end apart: 17, of which 13 were waited for; matrix products, arithmetic and copies ran while one was open for 0% of the time, Pallas kernels for 1%

profile of v11, /device:TPU:0, one launch (start us, length us, event | category | flops | bytes accessed | tf_op | source)
XLA Modules:
  0.0 61.7 jit_solution(6244336007655180390)
XLA Ops:
  1.3 0.0 copy-start
  1.3 0.0 copy-start.1
  1.3 1.0 %convert_add_fusion.points.refs_8_.refs_4_.refs_2_ = f32[10,4096]{1,0:T(8,128)S(1)} fusion(s32[1,1]{1,0:T(1,128)S(6)} %copy.12, f32[1,4096]{1,0:T(1,128)} %bitcast.5, f32[1,4096]{1,0:T(1,128)} %bitcast.6, f32[1,4096]{1,0:T(1,128)} %bitcast.7, f32[3,4096]{1,0:T(4,128)} %param.9, f32[3,4096]{1,0:T(4,128)} %param.8), kind=kLoop, calls=%fused_computation | loop fusion | flops 245760 | bytes 311300 | tf_op jit(solution)/shard_map/add | solution.py:407
  2.3 0.0 copy-done
  2.3 0.0 copy-done.1
  2.4 3.0 %shard_map.111 = (bf16[32,4096]{1,0:T(8,128)(2,1)S(1)}, bf16[32,4096]{1,0:T(8,128)(2,1)S(1)}, f32[1,4096]{1,0:T(1,128)S(1)}, s32[1,1,12]{2,1,0:T(1,128)S(1)}, f3...) custom-call(f32[10,4096]{1,0:T(8,128)S(1)} %convert_add_fusion.points.refs_8_.refs_4_.refs_2_, s32[1,1,12]{2,1,0:T(1,128)S(1)} %copy-done, ...), custom_call_target="tpu_custom_call" | custom-call | tf_op jit(solution)/shard_map/pallas_call | solution.py:365
  5.4 2.4 %collective-permute-start.2 = (f32[1,4096]{1,0:T(1,128)S(1)}, f32[1,4096]{1,0:T(1,128)S(1)}, u32[]{:S(2)}, u32[]{:S(2)}) collective-permute-start(f32[1,4096]{1,0:T(1,128)S(1)} %get-tuple-element.21.refs_0_), channel_id=1, source_target_pairs={{0,3},{1,2},{2,1},{3,0},{4,7},{5,6},{6,5},{7,4},{8,11},{9,10},{10,... | collective-permute-start | bytes 49160 | tf_op jit(solution)/shard_map/ppermute | solution.py:381
  7.8 0.6 %collective-permute-start.1 = (f32[1,4096]{1,0:T(1,128)S(1)}, f32[1,4096]{1,0:T(1,128)S(1)}, u32[]{:S(2)}, u32[]{:S(2)}) collective-permute-start(f32[1,4096]{1,0:T(1,128)S(1)} %get-tuple-element.21.refs_0_), channel_id=1, source_target_pairs={{0,2},{1,3},{2,0},{3,1},{4,6},{5,7},{6,4},{7,5},{8,10},{9,11},{10,... | collective-permute-start | bytes 49160 | tf_op jit(solution)/shard_map/ppermute | solution.py:381
  8.5 0.0 collective-permute-start
  8.5 0.8 %collective-permute-done.2.refs_3_ = f32[1,4096]{1,0:T(1,128)S(1)} collective-permute-done((f32[1,4096]{1,0:T(1,128)S(1)}, f32[1,4096]{1,0:T(1,128)S(1)}, u32[]{:S(2)}, u32[]{:S(2)}) %collective-permute-start.2) | collective-permute-done | bytes 16416 | tf_op jit(solution)/shard_map/ppermute | solution.py:381
  9.3 2.3 %collective-permute-done.1.refs_2_ = f32[1,4096]{1,0:T(1,128)S(1)} collective-permute-done((f32[1,4096]{1,0:T(1,128)S(1)}, f32[1,4096]{1,0:T(1,128)S(1)}, u32[]{:S(2)}, u32[]{:S(2)}) %collective-permute-start.1) | collective-permute-done | bytes 16416 | tf_op jit(solution)/shard_map/ppermute | solution.py:381
  11.6 0.0 collective-permute-done.refs_1_
  11.6 3.0 %shard_map.112 = (f32[1,4096]{1,0:T(1,128)S(1)}, f32[1,4096]{1,0:T(1,128)S(1)}, f32[1,4096]{1,0:T(1,128)S(1)}) custom-call(f32[1,4096]{1,0:T(1,128)S(1)} %get-tuple-element.21.refs_0_, f32[1,4096]{1,0:T(1,128)S(1)} %collective-permute-done.refs_1_, f32[1,4096]{1,0:T(1,128)S(1)} %collective-permute-done.1.refs_2_, ...), custom_call_target="tpu_custom_call" | custom-call | tf_op jit(solution)/shard_map/pallas_call | solution.py:365
  14.6 2.6 %collective-permute-start.5 = (f32[1,4096]{1,0:T(1,128)S(1)}, f32[1,4096]{1,0:T(1,128)S(1)}, u32[]{:S(2)}, u32[]{:S(2)}) collective-permute-start(f32[1,4096]{1,0:T(1,128)S(1)} %get-tuple-element.26.refs_0_), channel_id=1, source_target_pairs={{0,12},{4,8},{8,4},{12,0},{16,28},{20,24},{24,20},{28,16},{1,13},{... | collective-permute-start | bytes 49160 | tf_op jit(solution)/shard_map/ppermute | solution.py:390
  17.2 0.4 collective-permute-start.4
  17.6 0.5 collective-permute-start.3
  18.1 1.2 %collective-permute-done.5.refs_3_ = f32[1,4096]{1,0:T(1,128)S(1)} collective-permute-done((f32[1,4096]{1,0:T(1,128)S(1)}, f32[1,4096]{1,0:T(1,128)S(1)}, u32[]{:S(2)}, u32[]{:S(2)}) %collective-permute-start.5) | collective-permute-done | bytes 16416 | tf_op jit(solution)/shard_map/ppermute | solution.py:390
  19.3 1.6 %collective-permute-done.4.refs_2_ = f32[1,4096]{1,0:T(1,128)S(1)} collective-permute-done((f32[1,4096]{1,0:T(1,128)S(1)}, f32[1,4096]{1,0:T(1,128)S(1)}, u32[]{:S(2)}, u32[]{:S(2)}) %collective-permute-start.4) | collective-permute-done | bytes 16416 | tf_op jit(solution)/shard_map/ppermute | solution.py:390
  20.9 0.4 collective-permute-done.3.refs_1_
  21.4 2.6 %collective-permute-start.6 = (f32[1,4096]{1,0:T(1,128)S(1)}, f32[1,4096]{1,0:T(1,128)S(1)}, u32[]{:S(2)}, u32[]{:S(2)}) collective-permute-start(f32[1,4096]{1,0:T(1,128)S(1)} %shard_map.113.refs_0_), channel_id=1, source_target_pairs={{0,16},{4,20},{8,24},{12,28},{16,0},{20,4},{24,8},{28,12},{1,17},{... | collective-permute-start | bytes 49160 | tf_op jit(solution)/shard_map/ppermute | solution.py:390
  24.0 2.1 %collective-permute-done.6.refs_1_ = f32[1,4096]{1,0:T(1,128)S(1)} collective-permute-done((f32[1,4096]{1,0:T(1,128)S(1)}, f32[1,4096]{1,0:T(1,128)S(1)}, u32[]{:S(2)}, u32[]{:S(2)}) %collective-permute-start.6) | collective-permute-done | bytes 16416 | tf_op jit(solution)/shard_map/ppermute | solution.py:390
  26.1 2.8 %shard_map.114.refs_0_ = f32[1,4096]{1,0:T(1,128)S(1)} custom-call(f32[1,4096]{1,0:T(1,128)S(1)} %shard_map.113.refs_0_, f32[1,4096]{1,0:T(1,128)S(1)} %collective-permute-done.6.refs_1_, f32[1,4096]{1,0:T(1,128)S(1)} %get-tuple-element.27.refs_2_.refs_3_, bf16[32,4096]{1,0:T(8,128)(2,1)S(1)} %get-tuple-element.23.refs_5_.refs_3_.refs_9_.static, ...), custom_call_target="tpu_custom_call" | custom-call | tf_op jit(solution)/shard_map/pallas_call | solution.py:365
  28.9 0.1 collective-permute-start.9
  29.0 0.7 %collective-permute-start.8 = (f32[1,4096]{1,0:T(1,128)S(1)}, f32[1,4096]{1,0:T(1,128)S(1)}, u32[]{:S(2)}, u32[]{:S(2)}) collective-permute-start(f32[1,4096]{1,0:T(1,128)S(1)} %shard_map.114.refs_0_), channel_id=1, source_target_pairs={{0,2},{1,3},{2,0},{3,1},{4,6},{5,7},{6,4},{7,5},{8,10},{9,11},{10,... | collective-permute-start | bytes 49160 | tf_op jit(solution)/shard_map/ppermute | solution.py:381
  29.7 1.1 %collective-permute-start.7 = (f32[1,4096]{1,0:T(1,128)S(1)}, f32[1,4096]{1,0:T(1,128)S(1)}, u32[]{:S(2)}, u32[]{:S(2)}) collective-permute-start(f32[1,4096]{1,0:T(1,128)S(1)} %shard_map.114.refs_0_), channel_id=1, source_target_pairs={{0,1},{1,0},{2,3},{3,2},{4,5},{5,4},{6,7},{7,6},{8,9},{9,8},{10,11... | collective-permute-start | bytes 49160 | tf_op jit(solution)/shard_map/ppermute | solution.py:381
  30.9 0.1 shard_map.115.refs_6_
  30.9 1.2 %collective-permute-done.9.refs_3_ = f32[1,4096]{1,0:T(1,128)S(1)} collective-permute-done((f32[1,4096]{1,0:T(1,128)S(1)}, f32[1,4096]{1,0:T(1,128)S(1)}, u32[]{:S(2)}, u32[]{:S(2)}) %collective-permute-start.9) | collective-permute-done | bytes 16416 | tf_op jit(solution)/shard_map/ppermute | solution.py:381
  32.2 0.7 %collective-permute-done.8.refs_2_ = f32[1,4096]{1,0:T(1,128)S(1)} collective-permute-done((f32[1,4096]{1,0:T(1,128)S(1)}, f32[1,4096]{1,0:T(1,128)S(1)}, u32[]{:S(2)}, u32[]{:S(2)}) %collective-permute-start.8) | collective-permute-done | bytes 16416 | tf_op jit(solution)/shard_map/ppermute | solution.py:381
  32.8 0.0 collective-permute-done.7.refs_1_
  32.8 6.5 %shard_map.116 = (f32[1,4096]{1,0:T(1,128)}, f32[1,4096]{1,0:T(1,128)S(1)}, f32[4,4096]{1,0:T(4,128)S(1)}) custom-call(f32[1,4096]{1,0:T(1,128)S(1)} %shard_map.114.refs_0_, f32[1,4096]{1,0:T(1,128)S(1)} %collective-permute-done.7.refs_1_, f32[1,4096]{1,0:T(1,128)S(1)} %collective-permute-done.8.refs_2_, f32[1,4096]{1,0:T(1,128)S(1)} %collective-permute-done.9.refs_3_, ...), custom_call_target="tpu_custom_call" | custom-call | tf_op jit(solution)/shard_map/pallas_call | solution.py:365
  39.4 1.6 %collective-permute-start.12 = (f32[4,4096]{1,0:T(4,128)S(1)}, f32[4,4096]{1,0:T(4,128)S(1)}, u32[]{:S(2)}, u32[]{:S(2)}) collective-permute-start(f32[4,4096]{1,0:T(4,128)S(1)} %get-tuple-element.31.refs_0_), channel_id=1, source_target_pairs={{0,12},{4,8},{8,4},{12,0},{16,28},{20,24},{24,20},{28,16},{1,13},{... | collective-permute-start | bytes 196616 | tf_op jit(solution)/shard_map/ppermute | solution.py:390
  40.9 0.5 collective-permute-start.11
  41.4 1.5 %collective-permute-start.10 = (f32[4,4096]{1,0:T(4,128)S(1)}, f32[4,4096]{1,0:T(4,128)S(1)}, u32[]{:S(2)}, u32[]{:S(2)}) collective-permute-start(f32[4,4096]{1,0:T(4,128)S(1)} %get-tuple-element.31.refs_0_), channel_id=1, source_target_pairs={{0,4},{4,0},{8,12},{12,8},{16,20},{20,16},{24,28},{28,24},{1,5},{5... | collective-permute-start | bytes 196616 | tf_op jit(solution)/shard_map/ppermute | solution.py:390
  42.9 2.3 %collective-permute-done.12.refs_3_ = f32[4,4096]{1,0:T(4,128)S(1)} collective-permute-done((f32[4,4096]{1,0:T(4,128)S(1)}, f32[4,4096]{1,0:T(4,128)S(1)}, u32[]{:S(2)}, u32[]{:S(2)}) %collective-permute-start.12) | collective-permute-done | bytes 65568 | tf_op jit(solution)/shard_map/ppermute | solution.py:390
  45.2 0.0 collective-permute-done.11.refs_2_
  45.2 0.6 collective-permute-done.10.refs_1_
  45.9 2.6 %collective-permute-start.13 = (f32[4,4096]{1,0:T(4,128)S(1)}, f32[4,4096]{1,0:T(4,128)S(1)}, u32[]{:S(2)}, u32[]{:S(2)}) collective-permute-start(f32[4,4096]{1,0:T(4,128)S(1)} %shard_map.117.refs_0_), channel_id=1, source_target_pairs={{0,16},{4,20},{8,24},{12,28},{16,0},{20,4},{24,8},{28,12},{1,17},{... | collective-permute-start | bytes 196616 | tf_op jit(solution)/shard_map/ppermute | solution.py:390
  48.5 0.1 shard_map.118.refs_2_
  48.6 2.5 %collective-permute-done.13.refs_1_ = f32[4,4096]{1,0:T(4,128)S(1)} collective-permute-done((f32[4,4096]{1,0:T(4,128)S(1)}, f32[4,4096]{1,0:T(4,128)S(1)}, u32[]{:S(2)}, u32[]{:S(2)}) %collective-permute-start.13) | collective-permute-done | bytes 65568 | tf_op jit(solution)/shard_map/ppermute | solution.py:390
  51.1 6.1 %shard_map.119 = (f32[1,4096]{1,0:T(1,128)}, f32[3,1024]{1,0:T(4,128)S(1)}, f32[3,1024]{1,0:T(4,128)S(1)}, f32[3,1024]{1,0:T(4,128)S(1)}, f32[3,1024]{1,0:T(4,128)S(1)}) custom-call(f32[4,4096]{1,0:T(4,128)S(1)} %shard_map.117.refs_0_, f32[4,4096]{1,0:T(4,128)S(1)} %collective-permute-done.13.refs_1_, bf16[32,4096]{1,0:T(8,128)(2,1)S(1)} %shard_map.118.refs_2_, ...), custom_call_target="tpu_custom_call" | custom-call | tf_op jit(solution)/shard_map/pallas_call | solution.py:365
  57.2 0.1 collective-permute-start.14
  57.3 1.2 %collective-permute-start.15 = (f32[3,1024]{1,0:T(4,128)S(1)}, f32[3,1024]{1,0:T(4,128)S(1)}, u32[]{:S(2)}, u32[]{:S(2)}) collective-permute-start(f32[3,1024]{1,0:T(4,128)S(1)} %get-tuple-element.36), channel_id=1, source_target_pairs={{0,2},{1,3},{2,0},{3,1},{4,6},{5,7},{6,4},{7,5},{8,10},{9,11},{10,... | collective-permute-start | bytes 36872 | tf_op jit(solution)/shard_map/ppermute | solution.py:381
  58.5 0.6 collective-permute-start.16
  59.1 0.7 %shard_map.120 = f32[3,4096]{1,0:T(4,128)} custom-call(f32[4,4096]{1,0:T(4,128)S(1)} %shard_map.117.refs_0_, f32[4,4096]{1,0:T(4,128)S(1)} %collective-permute-done.13.refs_1_, f32[10,4096]{1,0:T(8,128)S(1)} %convert_add_fusion.points.refs_8_.refs_4_.refs_2_, f32[3,1024]{1,0:T(4,128)S(1)} %get-tuple-element.34.refs_3_), custom_call_target="tpu_custom_call" | custom-call | tf_op jit(solution)/shard_map/pallas_call | solution.py:365
  59.8 0.6 %collective-permute-done.14 = f32[3,1024]{1,0:T(4,128)S(1)} collective-permute-done((f32[3,1024]{1,0:T(4,128)S(1)}, f32[3,1024]{1,0:T(4,128)S(1)}, u32[]{:S(2)}, u32[]{:S(2)}) %collective-permute-start.14) | collective-permute-done | bytes 12320 | tf_op jit(solution)/shard_map/ppermute | solution.py:381
  60.4 0.7 %collective-permute-done.15 = f32[3,1024]{1,0:T(4,128)S(1)} collective-permute-done((f32[3,1024]{1,0:T(4,128)S(1)}, f32[3,1024]{1,0:T(4,128)S(1)}, u32[]{:S(2)}, u32[]{:S(2)}) %collective-permute-start.15) | collective-permute-done | bytes 12320 | tf_op jit(solution)/shard_map/ppermute | solution.py:381
  61.1 0.0 collective-permute-done.16
  61.1 0.6 add_add_fusion
  (2 shorter events, 0.1 us)
Async XLA Ops:
  1.3 1.1 %copy-start = (s32[1,1,12]{2,1,0:T(1,128)S(1)}, s32[1,1,12]{2,1,0:T(1,128)}, u32[]{:S(2)}) copy-start(s32[1,1,12]{2,1,0:T(1,128)} %sources.1) | copy-start | bytes 148
  1.3 1.1 %copy-start.1 = (s32[1,1,12]{2,1,0:T(1,128)S(1)}, s32[1,1,12]{2,1,0:T(1,128)}, u32[]{:S(2)}) copy-start(s32[1,1,12]{2,1,0:T(1,128)} %targets.1) | copy-start | bytes 148
  5.4 3.9 %collective-permute-start.2 = (f32[1,4096]{1,0:T(1,128)S(1)}, f32[1,4096]{1,0:T(1,128)S(1)}, u32[]{:S(2)}, u32[]{:S(2)}) collective-permute-start(f32[1,4096]{1,0:T(1,128)S(1)} %get-tuple-element.21.refs_0_), channel_id=1, source_target_pairs={{0,3},{1,2},{2,1},{3,0},{4,7},{5,6},{6,5},{7,4},{8,11},{9,10},{10,... | collective-permute-start | bytes 49160 | tf_op jit(solution)/shard_map/ppermute | solution.py:381
  7.8 3.7 %collective-permute-start.1 = (f32[1,4096]{1,0:T(1,128)S(1)}, f32[1,4096]{1,0:T(1,128)S(1)}, u32[]{:S(2)}, u32[]{:S(2)}) collective-permute-start(f32[1,4096]{1,0:T(1,128)S(1)} %get-tuple-element.21.refs_0_), channel_id=1, source_target_pairs={{0,2},{1,3},{2,0},{3,1},{4,6},{5,7},{6,4},{7,5},{8,10},{9,11},{10,... | collective-permute-start | bytes 49160 | tf_op jit(solution)/shard_map/ppermute | solution.py:381
  8.5 3.1 %collective-permute-start = (f32[1,4096]{1,0:T(1,128)S(1)}, f32[1,4096]{1,0:T(1,128)S(1)}, u32[]{:S(2)}, u32[]{:S(2)}) collective-permute-start(f32[1,4096]{1,0:T(1,128)S(1)} %get-tuple-element.21.refs_0_), channel_id=1, source_target_pairs={{0,1},{1,0},{2,3},{3,2},{4,5},{5,4},{6,7},{7,6},{8,9},{9,8},{10,11... | collective-permute-start | bytes 49160 | tf_op jit(solution)/shard_map/ppermute | solution.py:381
  14.6 4.7 %collective-permute-start.5 = (f32[1,4096]{1,0:T(1,128)S(1)}, f32[1,4096]{1,0:T(1,128)S(1)}, u32[]{:S(2)}, u32[]{:S(2)}) collective-permute-start(f32[1,4096]{1,0:T(1,128)S(1)} %get-tuple-element.26.refs_0_), channel_id=1, source_target_pairs={{0,12},{4,8},{8,4},{12,0},{16,28},{20,24},{24,20},{28,16},{1,13},{... | collective-permute-start | bytes 49160 | tf_op jit(solution)/shard_map/ppermute | solution.py:390
  17.2 3.7 %collective-permute-start.4 = (f32[1,4096]{1,0:T(1,128)S(1)}, f32[1,4096]{1,0:T(1,128)S(1)}, u32[]{:S(2)}, u32[]{:S(2)}) collective-permute-start(f32[1,4096]{1,0:T(1,128)S(1)} %get-tuple-element.26.refs_0_), channel_id=1, source_target_pairs={{0,8},{4,12},{8,0},{12,4},{16,24},{20,28},{24,16},{28,20},{1,9},{5... | collective-permute-start | bytes 49160 | tf_op jit(solution)/shard_map/ppermute | solution.py:390
  17.6 3.7 %collective-permute-start.3 = (f32[1,4096]{1,0:T(1,128)S(1)}, f32[1,4096]{1,0:T(1,128)S(1)}, u32[]{:S(2)}, u32[]{:S(2)}) collective-permute-start(f32[1,4096]{1,0:T(1,128)S(1)} %get-tuple-element.26.refs_0_), channel_id=1, source_target_pairs={{0,4},{4,0},{8,12},{12,8},{16,20},{20,16},{24,28},{28,24},{1,5},{5... | collective-permute-start | bytes 49160 | tf_op jit(solution)/shard_map/ppermute | solution.py:390
  21.4 4.7 %collective-permute-start.6 = (f32[1,4096]{1,0:T(1,128)S(1)}, f32[1,4096]{1,0:T(1,128)S(1)}, u32[]{:S(2)}, u32[]{:S(2)}) collective-permute-start(f32[1,4096]{1,0:T(1,128)S(1)} %shard_map.113.refs_0_), channel_id=1, source_target_pairs={{0,16},{4,20},{8,24},{12,28},{16,0},{20,4},{24,8},{28,12},{1,17},{... | collective-permute-start | bytes 49160 | tf_op jit(solution)/shard_map/ppermute | solution.py:390
  28.9 3.2 %collective-permute-start.9 = (f32[1,4096]{1,0:T(1,128)S(1)}, f32[1,4096]{1,0:T(1,128)S(1)}, u32[]{:S(2)}, u32[]{:S(2)}) collective-permute-start(f32[1,4096]{1,0:T(1,128)S(1)} %shard_map.114.refs_0_), channel_id=1, source_target_pairs={{0,3},{1,2},{2,1},{3,0},{4,7},{5,6},{6,5},{7,4},{8,11},{9,10},{10,... | collective-permute-start | bytes 49160 | tf_op jit(solution)/shard_map/ppermute | solution.py:381
  29.0 3.8 %collective-permute-start.8 = (f32[1,4096]{1,0:T(1,128)S(1)}, f32[1,4096]{1,0:T(1,128)S(1)}, u32[]{:S(2)}, u32[]{:S(2)}) collective-permute-start(f32[1,4096]{1,0:T(1,128)S(1)} %shard_map.114.refs_0_), channel_id=1, source_target_pairs={{0,2},{1,3},{2,0},{3,1},{4,6},{5,7},{6,4},{7,5},{8,10},{9,11},{10,... | collective-permute-start | bytes 49160 | tf_op jit(solution)/shard_map/ppermute | solution.py:381
  29.7 3.1 %collective-permute-start.7 = (f32[1,4096]{1,0:T(1,128)S(1)}, f32[1,4096]{1,0:T(1,128)S(1)}, u32[]{:S(2)}, u32[]{:S(2)}) collective-permute-start(f32[1,4096]{1,0:T(1,128)S(1)} %shard_map.114.refs_0_), channel_id=1, source_target_pairs={{0,1},{1,0},{2,3},{3,2},{4,5},{5,4},{6,7},{7,6},{8,9},{9,8},{10,11... | collective-permute-start | bytes 49160 | tf_op jit(solution)/shard_map/ppermute | solution.py:381
  39.4 5.9 %collective-permute-start.12 = (f32[4,4096]{1,0:T(4,128)S(1)}, f32[4,4096]{1,0:T(4,128)S(1)}, u32[]{:S(2)}, u32[]{:S(2)}) collective-permute-start(f32[4,4096]{1,0:T(4,128)S(1)} %get-tuple-element.31.refs_0_), channel_id=1, source_target_pairs={{0,12},{4,8},{8,4},{12,0},{16,28},{20,24},{24,20},{28,16},{1,13},{... | collective-permute-start | bytes 196616 | tf_op jit(solution)/shard_map/ppermute | solution.py:390
  40.9 4.3 %collective-permute-start.11 = (f32[4,4096]{1,0:T(4,128)S(1)}, f32[4,4096]{1,0:T(4,128)S(1)}, u32[]{:S(2)}, u32[]{:S(2)}) collective-permute-start(f32[4,4096]{1,0:T(4,128)S(1)} %get-tuple-element.31.refs_0_), channel_id=1, source_target_pairs={{0,8},{4,12},{8,0},{12,4},{16,24},{20,28},{24,16},{28,20},{1,9},{5... | collective-permute-start | bytes 196616 | tf_op jit(solution)/shard_map/ppermute | solution.py:390
  41.4 4.4 %collective-permute-start.10 = (f32[4,4096]{1,0:T(4,128)S(1)}, f32[4,4096]{1,0:T(4,128)S(1)}, u32[]{:S(2)}, u32[]{:S(2)}) collective-permute-start(f32[4,4096]{1,0:T(4,128)S(1)} %get-tuple-element.31.refs_0_), channel_id=1, source_target_pairs={{0,4},{4,0},{8,12},{12,8},{16,20},{20,16},{24,28},{28,24},{1,5},{5... | collective-permute-start | bytes 196616 | tf_op jit(solution)/shard_map/ppermute | solution.py:390
  45.9 5.2 %collective-permute-start.13 = (f32[4,4096]{1,0:T(4,128)S(1)}, f32[4,4096]{1,0:T(4,128)S(1)}, u32[]{:S(2)}, u32[]{:S(2)}) collective-permute-start(f32[4,4096]{1,0:T(4,128)S(1)} %shard_map.117.refs_0_), channel_id=1, source_target_pairs={{0,16},{4,20},{8,24},{12,28},{16,0},{20,4},{24,8},{28,12},{1,17},{... | collective-permute-start | bytes 196616 | tf_op jit(solution)/shard_map/ppermute | solution.py:390
  57.2 3.2 %collective-permute-start.14 = (f32[3,1024]{1,0:T(4,128)S(1)}, f32[3,1024]{1,0:T(4,128)S(1)}, u32[]{:S(2)}, u32[]{:S(2)}) collective-permute-start(f32[3,1024]{1,0:T(4,128)S(1)} %get-tuple-element.35), channel_id=1, source_target_pairs={{0,3},{1,2},{2,1},{3,0},{4,7},{5,6},{6,5},{7,4},{8,11},{9,10},{10,... | collective-permute-start | bytes 36872 | tf_op jit(solution)/shard_map/ppermute | solution.py:381
  57.3 3.8 %collective-permute-start.15 = (f32[3,1024]{1,0:T(4,128)S(1)}, f32[3,1024]{1,0:T(4,128)S(1)}, u32[]{:S(2)}, u32[]{:S(2)}) collective-permute-start(f32[3,1024]{1,0:T(4,128)S(1)} %get-tuple-element.36), channel_id=1, source_target_pairs={{0,2},{1,3},{2,0},{3,1},{4,6},{5,7},{6,4},{7,5},{8,10},{9,11},{10,... | collective-permute-start | bytes 36872 | tf_op jit(solution)/shard_map/ppermute | solution.py:381
  58.5 2.6 %collective-permute-start.16 = (f32[3,1024]{1,0:T(4,128)S(1)}, f32[3,1024]{1,0:T(4,128)S(1)}, u32[]{:S(2)}, u32[]{:S(2)}) collective-permute-start(f32[3,1024]{1,0:T(4,128)S(1)} %get-tuple-element.37), channel_id=1, source_target_pairs={{0,1},{1,0},{2,3},{3,2},{4,5},{5,4},{6,7},{7,6},{8,9},{9,8},{10,11... | collective-permute-start | bytes 36872 | tf_op jit(solution)/shard_map/ppermute | solution.py:381

commit v12 on v11

--- a/solution.py
+++ b/solution.py
@@ -39,7 +39,8 @@
 
 
 def place(scratch, parts, order):
-    scratch[...] = jnp.zeros_like(scratch)
+    scratch[15:16, :] = jnp.zeros((1, scratch.shape[1]), F32)
+    scratch[22:DEPTH, :] = jnp.zeros((DEPTH - 22, scratch.shape[1]), F32)
     for at, which in enumerate(order[:5]):
         scratch[3 * at : 3 * at + 3, :] = parts[which]
     scratch[16:19, :] = parts[order[5]]
@@ -298,7 +299,7 @@
 
     @pl.when(near)
     def _():
-        mass, *moved = plan_tiles(tiles, turned, kept, columns, points, 0, sums, chunk=32, ahead=2)
+        mass, *moved = plan_tiles(tiles, turned, kept, columns, points, 0, sums, chunk=32, ahead=4)
         part_out[0:1, :] = top_before[...] + log2(mass)
         inverse = 1.0 / mass
         for c, total in enumerate(moved):
@@ -346,7 +347,7 @@
     turn(turned, low, yc, split(log_target[...] - lse), [jnp.ones_like(lse)] * 3)
     copy.wait()
     tiles = Tiles(lists, sides(xc, yc), True)
-    mass, *moved = plan_tiles(tiles, turned, kept, columns, points, 3, sums, chunk=32, ahead=2)
+    mass, *moved = plan_tiles(tiles, turned, kept, columns, points, 3, sums, chunk=64, ahead=2)
     for c in range(3):
         whole[c : c + 1, :] = xs[c : c + 1, :] * mass - moved[c]
     place_tgt = lax.axis_index("tgt")

time: 61.9 us -> 62.1 us (level)
  no operation moved by 1% of the time
where the time goes in v12:
time: 62.1 us; the launch traced here: 62 us
  Pallas kernels  22.6 us (36%)
  starting transfers between devices  19.4 us (31%)
  waiting for transfers between devices  16.9 us (27%)
  other arithmetic  1.65 us (3%)
  between operations  1.4 us (2%)
    pallas_call x10, Pallas kernels, call(): pl.pallas_call(kernel, out_shape=outs, in_specs=[VMEM] * len(ins) + [HBM]...  22.6 us
    ppermute x8, starting transfers between devices, sum_up(): lax.ppermute(value, axis, [(i, i ^ k) for i in range(n)])  12.4 us
    ppermute x8, waiting for transfers between devices, sum_up(): lax.ppermute(value, axis, [(i, i ^ k) for i in range(n)])  10.7 us
    ppermute x9, starting transfers between devices, exchange(): lax.ppermute(values[k], axis, [(i, peer(i, k, n)) for i in range(n)])  6.96 us
    ppermute x9, waiting for transfers between devices, exchange(): lax.ppermute(values[k], axis, [(i, peer(i, k, n)) for i in range(n)])  6.23 us
  transfers between devices with their start and end apart: 17, of which 13 were waited for; matrix products, arithmetic and copies ran while one was open for 0% of the time, Pallas kernels for 1%

profile of v12, /device:TPU:0, one launch (start us, length us, event | category | flops | bytes accessed | tf_op | source)
XLA Modules:
  0.0 62.0 jit_solution(1203888657692978824)
XLA Ops:
  1.3 0.0 copy-start
  1.3 0.0 copy-start.1
  1.3 1.0 %convert_add_fusion.points.refs_8_.refs_4_.refs_2_ = f32[10,4096]{1,0:T(8,128)S(1)} fusion(s32[1,1]{1,0:T(1,128)S(6)} %copy.12, f32[1,4096]{1,0:T(1,128)} %bitcast.5, f32[1,4096]{1,0:T(1,128)} %bitcast.6, f32[1,4096]{1,0:T(1,128)} %bitcast.7, f32[3,4096]{1,0:T(4,128)} %param.9, f32[3,4096]{1,0:T(4,128)} %param.8), kind=kLoop, calls=%fused_computation | loop fusion | flops 245760 | bytes 311300 | tf_op jit(solution)/shard_map/add | solution.py:408
  2.3 0.0 copy-done
  2.3 0.0 copy-done.1
  2.4 3.2 %shard_map.111 = (bf16[32,4096]{1,0:T(8,128)(2,1)S(1)}, bf16[32,4096]{1,0:T(8,128)(2,1)S(1)}, f32[1,4096]{1,0:T(1,128)S(1)}, s32[1,1,12]{2,1,0:T(1,128)S(1)}, f3...) custom-call(f32[10,4096]{1,0:T(8,128)S(1)} %convert_add_fusion.points.refs_8_.refs_4_.refs_2_, s32[1,1,12]{2,1,0:T(1,128)S(1)} %copy-done, ...), custom_call_target="tpu_custom_call" | custom-call | tf_op jit(solution)/shard_map/pallas_call | solution.py:366
  5.6 2.4 %collective-permute-start.2 = (f32[1,4096]{1,0:T(1,128)S(1)}, f32[1,4096]{1,0:T(1,128)S(1)}, u32[]{:S(2)}, u32[]{:S(2)}) collective-permute-start(f32[1,4096]{1,0:T(1,128)S(1)} %get-tuple-element.21.refs_0_), channel_id=1, source_target_pairs={{0,3},{1,2},{2,1},{3,0},{4,7},{5,6},{6,5},{7,4},{8,11},{9,10},{10,... | collective-permute-start | bytes 49160 | tf_op jit(solution)/shard_map/ppermute | solution.py:382
  8.0 0.6 %collective-permute-start.1 = (f32[1,4096]{1,0:T(1,128)S(1)}, f32[1,4096]{1,0:T(1,128)S(1)}, u32[]{:S(2)}, u32[]{:S(2)}) collective-permute-start(f32[1,4096]{1,0:T(1,128)S(1)} %get-tuple-element.21.refs_0_), channel_id=1, source_target_pairs={{0,2},{1,3},{2,0},{3,1},{4,6},{5,7},{6,4},{7,5},{8,10},{9,11},{10,... | collective-permute-start | bytes 49160 | tf_op jit(solution)/shard_map/ppermute | solution.py:382
  8.7 0.0 collective-permute-start
  8.7 0.8 %collective-permute-done.2.refs_3_ = f32[1,4096]{1,0:T(1,128)S(1)} collective-permute-done((f32[1,4096]{1,0:T(1,128)S(1)}, f32[1,4096]{1,0:T(1,128)S(1)}, u32[]{:S(2)}, u32[]{:S(2)}) %collective-permute-start.2) | collective-permute-done | bytes 16416 | tf_op jit(solution)/shard_map/ppermute | solution.py:382
  9.5 2.3 %collective-permute-done.1.refs_2_ = f32[1,4096]{1,0:T(1,128)S(1)} collective-permute-done((f32[1,4096]{1,0:T(1,128)S(1)}, f32[1,4096]{1,0:T(1,128)S(1)}, u32[]{:S(2)}, u32[]{:S(2)}) %collective-permute-start.1) | collective-permute-done | bytes 16416 | tf_op jit(solution)/shard_map/ppermute | solution.py:382
  11.8 0.0 collective-permute-done.refs_1_
  11.8 3.0 %shard_map.112 = (f32[1,4096]{1,0:T(1,128)S(1)}, f32[1,4096]{1,0:T(1,128)S(1)}, f32[1,4096]{1,0:T(1,128)S(1)}) custom-call(f32[1,4096]{1,0:T(1,128)S(1)} %get-tuple-element.21.refs_0_, f32[1,4096]{1,0:T(1,128)S(1)} %collective-permute-done.refs_1_, f32[1,4096]{1,0:T(1,128)S(1)} %collective-permute-done.1.refs_2_, ...), custom_call_target="tpu_custom_call" | custom-call | tf_op jit(solution)/shard_map/pallas_call | solution.py:366
  14.7 2.6 %collective-permute-start.5 = (f32[1,4096]{1,0:T(1,128)S(1)}, f32[1,4096]{1,0:T(1,128)S(1)}, u32[]{:S(2)}, u32[]{:S(2)}) collective-permute-start(f32[1,4096]{1,0:T(1,128)S(1)} %get-tuple-element.26.refs_0_), channel_id=1, source_target_pairs={{0,12},{4,8},{8,4},{12,0},{16,28},{20,24},{24,20},{28,16},{1,13},{... | collective-permute-start | bytes 49160 | tf_op jit(solution)/shard_map/ppermute | solution.py:391
  17.3 0.4 collective-permute-start.4
  17.8 0.5 collective-permute-start.3
  18.3 1.2 %collective-permute-done.5.refs_3_ = f32[1,4096]{1,0:T(1,128)S(1)} collective-permute-done((f32[1,4096]{1,0:T(1,128)S(1)}, f32[1,4096]{1,0:T(1,128)S(1)}, u32[]{:S(2)}, u32[]{:S(2)}) %collective-permute-start.5) | collective-permute-done | bytes 16416 | tf_op jit(solution)/shard_map/ppermute | solution.py:391
  19.5 1.6 %collective-permute-done.4.refs_2_ = f32[1,4096]{1,0:T(1,128)S(1)} collective-permute-done((f32[1,4096]{1,0:T(1,128)S(1)}, f32[1,4096]{1,0:T(1,128)S(1)}, u32[]{:S(2)}, u32[]{:S(2)}) %collective-permute-start.4) | collective-permute-done | bytes 16416 | tf_op jit(solution)/shard_map/ppermute | solution.py:391
  21.1 0.4 collective-permute-done.3.refs_1_
  21.6 2.7 %collective-permute-start.6 = (f32[1,4096]{1,0:T(1,128)S(1)}, f32[1,4096]{1,0:T(1,128)S(1)}, u32[]{:S(2)}, u32[]{:S(2)}) collective-permute-start(f32[1,4096]{1,0:T(1,128)S(1)} %shard_map.113.refs_0_), channel_id=1, source_target_pairs={{0,16},{4,20},{8,24},{12,28},{16,0},{20,4},{24,8},{28,12},{1,17},{... | collective-permute-start | bytes 49160 | tf_op jit(solution)/shard_map/ppermute | solution.py:391
  24.2 2.0 %collective-permute-done.6.refs_1_ = f32[1,4096]{1,0:T(1,128)S(1)} collective-permute-done((f32[1,4096]{1,0:T(1,128)S(1)}, f32[1,4096]{1,0:T(1,128)S(1)}, u32[]{:S(2)}, u32[]{:S(2)}) %collective-permute-start.6) | collective-permute-done | bytes 16416 | tf_op jit(solution)/shard_map/ppermute | solution.py:391
  26.3 2.8 %shard_map.114.refs_0_ = f32[1,4096]{1,0:T(1,128)S(1)} custom-call(f32[1,4096]{1,0:T(1,128)S(1)} %shard_map.113.refs_0_, f32[1,4096]{1,0:T(1,128)S(1)} %collective-permute-done.6.refs_1_, f32[1,4096]{1,0:T(1,128)S(1)} %get-tuple-element.27.refs_2_.refs_3_, bf16[32,4096]{1,0:T(8,128)(2,1)S(1)} %get-tuple-element.23.refs_5_.refs_3_.refs_9_.static, ...), custom_call_target="tpu_custom_call" | custom-call | tf_op jit(solution)/shard_map/pallas_call | solution.py:366
  29.1 0.1 collective-permute-start.9
  29.2 0.7 %collective-permute-start.8 = (f32[1,4096]{1,0:T(1,128)S(1)}, f32[1,4096]{1,0:T(1,128)S(1)}, u32[]{:S(2)}, u32[]{:S(2)}) collective-permute-start(f32[1,4096]{1,0:T(1,128)S(1)} %shard_map.114.refs_0_), channel_id=1, source_target_pairs={{0,2},{1,3},{2,0},{3,1},{4,6},{5,7},{6,4},{7,5},{8,10},{9,11},{10,... | collective-permute-start | bytes 49160 | tf_op jit(solution)/shard_map/ppermute | solution.py:382
  29.9 1.1 %collective-permute-start.7 = (f32[1,4096]{1,0:T(1,128)S(1)}, f32[1,4096]{1,0:T(1,128)S(1)}, u32[]{:S(2)}, u32[]{:S(2)}) collective-permute-start(f32[1,4096]{1,0:T(1,128)S(1)} %shard_map.114.refs_0_), channel_id=1, source_target_pairs={{0,1},{1,0},{2,3},{3,2},{4,5},{5,4},{6,7},{7,6},{8,9},{9,8},{10,11... | collective-permute-start | bytes 49160 | tf_op jit(solution)/shard_map/ppermute | solution.py:382
  31.0 0.1 shard_map.115.refs_6_
  31.1 1.2 %collective-permute-done.9.refs_3_ = f32[1,4096]{1,0:T(1,128)S(1)} collective-permute-done((f32[1,4096]{1,0:T(1,128)S(1)}, f32[1,4096]{1,0:T(1,128)S(1)}, u32[]{:S(2)}, u32[]{:S(2)}) %collective-permute-start.9) | collective-permute-done | bytes 16416 | tf_op jit(solution)/shard_map/ppermute | solution.py:382
  32.3 0.7 %collective-permute-done.8.refs_2_ = f32[1,4096]{1,0:T(1,128)S(1)} collective-permute-done((f32[1,4096]{1,0:T(1,128)S(1)}, f32[1,4096]{1,0:T(1,128)S(1)}, u32[]{:S(2)}, u32[]{:S(2)}) %collective-permute-start.8) | collective-permute-done | bytes 16416 | tf_op jit(solution)/shard_map/ppermute | solution.py:382
  33.0 0.0 collective-permute-done.7.refs_1_
  33.0 6.5 %shard_map.116 = (f32[1,4096]{1,0:T(1,128)}, f32[1,4096]{1,0:T(1,128)S(1)}, f32[4,4096]{1,0:T(4,128)S(1)}) custom-call(f32[1,4096]{1,0:T(1,128)S(1)} %shard_map.114.refs_0_, f32[1,4096]{1,0:T(1,128)S(1)} %collective-permute-done.7.refs_1_, f32[1,4096]{1,0:T(1,128)S(1)} %collective-permute-done.8.refs_2_, f32[1,4096]{1,0:T(1,128)S(1)} %collective-permute-done.9.refs_3_, ...), custom_call_target="tpu_custom_call" | custom-call | tf_op jit(solution)/shard_map/pallas_call | solution.py:366
  39.5 1.6 %collective-permute-start.12 = (f32[4,4096]{1,0:T(4,128)S(1)}, f32[4,4096]{1,0:T(4,128)S(1)}, u32[]{:S(2)}, u32[]{:S(2)}) collective-permute-start(f32[4,4096]{1,0:T(4,128)S(1)} %get-tuple-element.31.refs_0_), channel_id=1, source_target_pairs={{0,12},{4,8},{8,4},{12,0},{16,28},{20,24},{24,20},{28,16},{1,13},{... | collective-permute-start | bytes 196616 | tf_op jit(solution)/shard_map/ppermute | solution.py:391
  41.1 0.5 collective-permute-start.11
  41.6 1.5 %collective-permute-start.10 = (f32[4,4096]{1,0:T(4,128)S(1)}, f32[4,4096]{1,0:T(4,128)S(1)}, u32[]{:S(2)}, u32[]{:S(2)}) collective-permute-start(f32[4,4096]{1,0:T(4,128)S(1)} %get-tuple-element.31.refs_0_), channel_id=1, source_target_pairs={{0,4},{4,0},{8,12},{12,8},{16,20},{20,16},{24,28},{28,24},{1,5},{5... | collective-permute-start | bytes 196616 | tf_op jit(solution)/shard_map/ppermute | solution.py:391
  43.1 2.3 %collective-permute-done.12.refs_3_ = f32[4,4096]{1,0:T(4,128)S(1)} collective-permute-done((f32[4,4096]{1,0:T(4,128)S(1)}, f32[4,4096]{1,0:T(4,128)S(1)}, u32[]{:S(2)}, u32[]{:S(2)}) %collective-permute-start.12) | collective-permute-done | bytes 65568 | tf_op jit(solution)/shard_map/ppermute | solution.py:391
  45.4 0.0 collective-permute-done.11.refs_2_
  45.4 0.6 collective-permute-done.10.refs_1_
  46.1 2.7 %collective-permute-start.13 = (f32[4,4096]{1,0:T(4,128)S(1)}, f32[4,4096]{1,0:T(4,128)S(1)}, u32[]{:S(2)}, u32[]{:S(2)}) collective-permute-start(f32[4,4096]{1,0:T(4,128)S(1)} %shard_map.117.refs_0_), channel_id=1, source_target_pairs={{0,16},{4,20},{8,24},{12,28},{16,0},{20,4},{24,8},{28,12},{1,17},{... | collective-permute-start | bytes 196616 | tf_op jit(solution)/shard_map/ppermute | solution.py:391
  48.7 0.1 shard_map.118.refs_2_
  48.8 2.5 %collective-permute-done.13.refs_1_ = f32[4,4096]{1,0:T(4,128)S(1)} collective-permute-done((f32[4,4096]{1,0:T(4,128)S(1)}, f32[4,4096]{1,0:T(4,128)S(1)}, u32[]{:S(2)}, u32[]{:S(2)}) %collective-permute-start.13) | collective-permute-done | bytes 65568 | tf_op jit(solution)/shard_map/ppermute | solution.py:391
  51.3 6.2 %shard_map.119 = (f32[1,4096]{1,0:T(1,128)}, f32[3,1024]{1,0:T(4,128)S(1)}, f32[3,1024]{1,0:T(4,128)S(1)}, f32[3,1024]{1,0:T(4,128)S(1)}, f32[3,1024]{1,0:T(4,128)S(1)}) custom-call(f32[4,4096]{1,0:T(4,128)S(1)} %shard_map.117.refs_0_, f32[4,4096]{1,0:T(4,128)S(1)} %collective-permute-done.13.refs_1_, bf16[32,4096]{1,0:T(8,128)(2,1)S(1)} %shard_map.118.refs_2_, ...), custom_call_target="tpu_custom_call" | custom-call | tf_op jit(solution)/shard_map/pallas_call | solution.py:366
  57.4 0.1 collective-permute-start.14
  57.5 1.2 %collective-permute-start.15 = (f32[3,1024]{1,0:T(4,128)S(1)}, f32[3,1024]{1,0:T(4,128)S(1)}, u32[]{:S(2)}, u32[]{:S(2)}) collective-permute-start(f32[3,1024]{1,0:T(4,128)S(1)} %get-tuple-element.36), channel_id=1, source_target_pairs={{0,2},{1,3},{2,0},{3,1},{4,6},{5,7},{6,4},{7,5},{8,10},{9,11},{10,... | collective-permute-start | bytes 36872 | tf_op jit(solution)/shard_map/ppermute | solution.py:382
  58.7 0.6 %collective-permute-start.16 = (f32[3,1024]{1,0:T(4,128)S(1)}, f32[3,1024]{1,0:T(4,128)S(1)}, u32[]{:S(2)}, u32[]{:S(2)}) collective-permute-start(f32[3,1024]{1,0:T(4,128)S(1)} %get-tuple-element.37), channel_id=1, source_target_pairs={{0,1},{1,0},{2,3},{3,2},{4,5},{5,4},{6,7},{7,6},{8,9},{9,8},{10,11... | collective-permute-start | bytes 36872 | tf_op jit(solution)/shard_map/ppermute | solution.py:382
  59.4 0.7 %shard_map.120 = f32[3,4096]{1,0:T(4,128)} custom-call(f32[4,4096]{1,0:T(4,128)S(1)} %shard_map.117.refs_0_, f32[4,4096]{1,0:T(4,128)S(1)} %collective-permute-done.13.refs_1_, f32[10,4096]{1,0:T(8,128)S(1)} %convert_add_fusion.points.refs_8_.refs_4_.refs_2_, f32[3,1024]{1,0:T(4,128)S(1)} %get-tuple-element.34.refs_3_), custom_call_target="tpu_custom_call" | custom-call | tf_op jit(solution)/shard_map/pallas_call | solution.py:366
  60.0 0.6 %collective-permute-done.14 = f32[3,1024]{1,0:T(4,128)S(1)} collective-permute-done((f32[3,1024]{1,0:T(4,128)S(1)}, f32[3,1024]{1,0:T(4,128)S(1)}, u32[]{:S(2)}, u32[]{:S(2)}) %collective-permute-start.14) | collective-permute-done | bytes 12320 | tf_op jit(solution)/shard_map/ppermute | solution.py:382
  60.7 0.7 %collective-permute-done.15 = f32[3,1024]{1,0:T(4,128)S(1)} collective-permute-done((f32[3,1024]{1,0:T(4,128)S(1)}, f32[3,1024]{1,0:T(4,128)S(1)}, u32[]{:S(2)}, u32[]{:S(2)}) %collective-permute-start.15) | collective-permute-done | bytes 12320 | tf_op jit(solution)/shard_map/ppermute | solution.py:382
  61.3 0.0 collective-permute-done.16
  61.3 0.6 add_add_fusion
  (2 shorter events, 0.1 us)
Async XLA Ops:
  1.3 1.1 %copy-start = (s32[1,1,12]{2,1,0:T(1,128)S(1)}, s32[1,1,12]{2,1,0:T(1,128)}, u32[]{:S(2)}) copy-start(s32[1,1,12]{2,1,0:T(1,128)} %sources.1) | copy-start | bytes 148
  1.3 1.1 %copy-start.1 = (s32[1,1,12]{2,1,0:T(1,128)S(1)}, s32[1,1,12]{2,1,0:T(1,128)}, u32[]{:S(2)}) copy-start(s32[1,1,12]{2,1,0:T(1,128)} %targets.1) | copy-start | bytes 148
  5.6 3.9 %collective-permute-start.2 = (f32[1,4096]{1,0:T(1,128)S(1)}, f32[1,4096]{1,0:T(1,128)S(1)}, u32[]{:S(2)}, u32[]{:S(2)}) collective-permute-start(f32[1,4096]{1,0:T(1,128)S(1)} %get-tuple-element.21.refs_0_), channel_id=1, source_target_pairs={{0,3},{1,2},{2,1},{3,0},{4,7},{5,6},{6,5},{7,4},{8,11},{9,10},{10,... | collective-permute-start | bytes 49160 | tf_op jit(solution)/shard_map/ppermute | solution.py:382
  8.0 3.7 %collective-permute-start.1 = (f32[1,4096]{1,0:T(1,128)S(1)}, f32[1,4096]{1,0:T(1,128)S(1)}, u32[]{:S(2)}, u32[]{:S(2)}) collective-permute-start(f32[1,4096]{1,0:T(1,128)S(1)} %get-tuple-element.21.refs_0_), channel_id=1, source_target_pairs={{0,2},{1,3},{2,0},{3,1},{4,6},{5,7},{6,4},{7,5},{8,10},{9,11},{10,... | collective-permute-start | bytes 49160 | tf_op jit(solution)/shard_map/ppermute | solution.py:382
  8.7 3.1 %collective-permute-start = (f32[1,4096]{1,0:T(1,128)S(1)}, f32[1,4096]{1,0:T(1,128)S(1)}, u32[]{:S(2)}, u32[]{:S(2)}) collective-permute-start(f32[1,4096]{1,0:T(1,128)S(1)} %get-tuple-element.21.refs_0_), channel_id=1, source_target_pairs={{0,1},{1,0},{2,3},{3,2},{4,5},{5,4},{6,7},{7,6},{8,9},{9,8},{10,11... | collective-permute-start | bytes 49160 | tf_op jit(solution)/shard_map/ppermute | solution.py:382
  14.7 4.7 %collective-permute-start.5 = (f32[1,4096]{1,0:T(1,128)S(1)}, f32[1,4096]{1,0:T(1,128)S(1)}, u32[]{:S(2)}, u32[]{:S(2)}) collective-permute-start(f32[1,4096]{1,0:T(1,128)S(1)} %get-tuple-element.26.refs_0_), channel_id=1, source_target_pairs={{0,12},{4,8},{8,4},{12,0},{16,28},{20,24},{24,20},{28,16},{1,13},{... | collective-permute-start | bytes 49160 | tf_op jit(solution)/shard_map/ppermute | solution.py:391
  17.3 3.7 %collective-permute-start.4 = (f32[1,4096]{1,0:T(1,128)S(1)}, f32[1,4096]{1,0:T(1,128)S(1)}, u32[]{:S(2)}, u32[]{:S(2)}) collective-permute-start(f32[1,4096]{1,0:T(1,128)S(1)} %get-tuple-element.26.refs_0_), channel_id=1, source_target_pairs={{0,8},{4,12},{8,0},{12,4},{16,24},{20,28},{24,16},{28,20},{1,9},{5... | collective-permute-start | bytes 49160 | tf_op jit(solution)/shard_map/ppermute | solution.py:391
  17.8 3.7 %collective-permute-start.3 = (f32[1,4096]{1,0:T(1,128)S(1)}, f32[1,4096]{1,0:T(1,128)S(1)}, u32[]{:S(2)}, u32[]{:S(2)}) collective-permute-start(f32[1,4096]{1,0:T(1,128)S(1)} %get-tuple-element.26.refs_0_), channel_id=1, source_target_pairs={{0,4},{4,0},{8,12},{12,8},{16,20},{20,16},{24,28},{28,24},{1,5},{5... | collective-permute-start | bytes 49160 | tf_op jit(solution)/shard_map/ppermute | solution.py:391
  21.6 4.7 %collective-permute-start.6 = (f32[1,4096]{1,0:T(1,128)S(1)}, f32[1,4096]{1,0:T(1,128)S(1)}, u32[]{:S(2)}, u32[]{:S(2)}) collective-permute-start(f32[1,4096]{1,0:T(1,128)S(1)} %shard_map.113.refs_0_), channel_id=1, source_target_pairs={{0,16},{4,20},{8,24},{12,28},{16,0},{20,4},{24,8},{28,12},{1,17},{... | collective-permute-start | bytes 49160 | tf_op jit(solution)/shard_map/ppermute | solution.py:391
  29.1 3.2 %collective-permute-start.9 = (f32[1,4096]{1,0:T(1,128)S(1)}, f32[1,4096]{1,0:T(1,128)S(1)}, u32[]{:S(2)}, u32[]{:S(2)}) collective-permute-start(f32[1,4096]{1,0:T(1,128)S(1)} %shard_map.114.refs_0_), channel_id=1, source_target_pairs={{0,3},{1,2},{2,1},{3,0},{4,7},{5,6},{6,5},{7,4},{8,11},{9,10},{10,... | collective-permute-start | bytes 49160 | tf_op jit(solution)/shard_map/ppermute | solution.py:382
  29.2 3.8 %collective-permute-start.8 = (f32[1,4096]{1,0:T(1,128)S(1)}, f32[1,4096]{1,0:T(1,128)S(1)}, u32[]{:S(2)}, u32[]{:S(2)}) collective-permute-start(f32[1,4096]{1,0:T(1,128)S(1)} %shard_map.114.refs_0_), channel_id=1, source_target_pairs={{0,2},{1,3},{2,0},{3,1},{4,6},{5,7},{6,4},{7,5},{8,10},{9,11},{10,... | collective-permute-start | bytes 49160 | tf_op jit(solution)/shard_map/ppermute | solution.py:382
  29.9 3.1 %collective-permute-start.7 = (f32[1,4096]{1,0:T(1,128)S(1)}, f32[1,4096]{1,0:T(1,128)S(1)}, u32[]{:S(2)}, u32[]{:S(2)}) collective-permute-start(f32[1,4096]{1,0:T(1,128)S(1)} %shard_map.114.refs_0_), channel_id=1, source_target_pairs={{0,1},{1,0},{2,3},{3,2},{4,5},{5,4},{6,7},{7,6},{8,9},{9,8},{10,11... | collective-permute-start | bytes 49160 | tf_op jit(solution)/shard_map/ppermute | solution.py:382
  39.5 5.9 %collective-permute-start.12 = (f32[4,4096]{1,0:T(4,128)S(1)}, f32[4,4096]{1,0:T(4,128)S(1)}, u32[]{:S(2)}, u32[]{:S(2)}) collective-permute-start(f32[4,4096]{1,0:T(4,128)S(1)} %get-tuple-element.31.refs_0_), channel_id=1, source_target_pairs={{0,12},{4,8},{8,4},{12,0},{16,28},{20,24},{24,20},{28,16},{1,13},{... | collective-permute-start | bytes 196616 | tf_op jit(solution)/shard_map/ppermute | solution.py:391
  41.1 4.3 %collective-permute-start.11 = (f32[4,4096]{1,0:T(4,128)S(1)}, f32[4,4096]{1,0:T(4,128)S(1)}, u32[]{:S(2)}, u32[]{:S(2)}) collective-permute-start(f32[4,4096]{1,0:T(4,128)S(1)} %get-tuple-element.31.refs_0_), channel_id=1, source_target_pairs={{0,8},{4,12},{8,0},{12,4},{16,24},{20,28},{24,16},{28,20},{1,9},{5... | collective-permute-start | bytes 196616 | tf_op jit(solution)/shard_map/ppermute | solution.py:391
  41.6 4.4 %collective-permute-start.10 = (f32[4,4096]{1,0:T(4,128)S(1)}, f32[4,4096]{1,0:T(4,128)S(1)}, u32[]{:S(2)}, u32[]{:S(2)}) collective-permute-start(f32[4,4096]{1,0:T(4,128)S(1)} %get-tuple-element.31.refs_0_), channel_id=1, source_target_pairs={{0,4},{4,0},{8,12},{12,8},{16,20},{20,16},{24,28},{28,24},{1,5},{5... | collective-permute-start | bytes 196616 | tf_op jit(solution)/shard_map/ppermute | solution.py:391
  46.1 5.2 %collective-permute-start.13 = (f32[4,4096]{1,0:T(4,128)S(1)}, f32[4,4096]{1,0:T(4,128)S(1)}, u32[]{:S(2)}, u32[]{:S(2)}) collective-permute-start(f32[4,4096]{1,0:T(4,128)S(1)} %shard_map.117.refs_0_), channel_id=1, source_target_pairs={{0,16},{4,20},{8,24},{12,28},{16,0},{20,4},{24,8},{28,12},{1,17},{... | collective-permute-start | bytes 196616 | tf_op jit(solution)/shard_map/ppermute | solution.py:391
  57.4 3.2 %collective-permute-start.14 = (f32[3,1024]{1,0:T(4,128)S(1)}, f32[3,1024]{1,0:T(4,128)S(1)}, u32[]{:S(2)}, u32[]{:S(2)}) collective-permute-start(f32[3,1024]{1,0:T(4,128)S(1)} %get-tuple-element.35), channel_id=1, source_target_pairs={{0,3},{1,2},{2,1},{3,0},{4,7},{5,6},{6,5},{7,4},{8,11},{9,10},{10,... | collective-permute-start | bytes 36872 | tf_op jit(solution)/shard_map/ppermute | solution.py:382
  57.5 3.8 %collective-permute-start.15 = (f32[3,1024]{1,0:T(4,128)S(1)}, f32[3,1024]{1,0:T(4,128)S(1)}, u32[]{:S(2)}, u32[]{:S(2)}) collective-permute-start(f32[3,1024]{1,0:T(4,128)S(1)} %get-tuple-element.36), channel_id=1, source_target_pairs={{0,2},{1,3},{2,0},{3,1},{4,6},{5,7},{6,4},{7,5},{8,10},{9,11},{10,... | collective-permute-start | bytes 36872 | tf_op jit(solution)/shard_map/ppermute | solution.py:382
  58.7 2.6 %collective-permute-start.16 = (f32[3,1024]{1,0:T(4,128)S(1)}, f32[3,1024]{1,0:T(4,128)S(1)}, u32[]{:S(2)}, u32[]{:S(2)}) collective-permute-start(f32[3,1024]{1,0:T(4,128)S(1)} %get-tuple-element.37), channel_id=1, source_target_pairs={{0,1},{1,0},{2,3},{3,2},{4,5},{5,4},{6,7},{7,6},{8,9},{9,8},{10,11... | collective-permute-start | bytes 36872 | tf_op jit(solution)/shard_map/ppermute | solution.py:382
